TPU v7x, 32 devices: a whole 2x2x4 slice. The times are simulated.
32 devices in a mesh: seq: 4 (over y, x), tensor: 8 (over z, core).
Axes of the slice: x: 2, y: 2, z: 4, core: 2. Of those that a mesh axis runs over, the one named last changes fastest.
Arguments:
- states: bfloat16 [16, 2048], P('tensor'), may hold values from -6 to 6
- attn_gain: bfloat16 [2048], replicated, may hold values from 0.5 to 1.5
- w_qkv: bfloat16 [2048, 3, 2048], P(None, None, 'tensor'), may hold values from -0.125 to 0.125
- w_out: bfloat16 [2048, 2048], P('tensor'), may hold values from -0.125 to 0.125
- mlp_gain: bfloat16 [2048], replicated, may hold values from 0.5 to 1.5
- w_gate_up: bfloat16 [2048, 2, 8192], P(None, None, 'tensor'), may hold values from -0.125 to 0.125
- w_down: bfloat16 [8192, 2048], P('tensor'), may hold values from -0.0625 to 0.0625
- key_cache: bfloat16 [16, 2048, 4096], P('tensor', None, 'seq')
- value_cache: bfloat16 [16, 2048, 4096], P('tensor', None, 'seq')
- sink_keys: bfloat16 [16, 2048, 4], P('tensor'), may hold values from -8 to 8
- sink_values: bfloat16 [16, 2048, 4], P('tensor'), may hold values from -6 to 6
- cache_len: int32 [16], replicated, may hold values from 1 to 4096, as said below
- slot_mask: int32 [16, 4096], P('tensor', 'seq'), may hold values 0 or 1
- slot_pos: int32 [16, 4096], P('tensor', 'seq'), may hold values from 0 to 8191
- new_pos: int32 [16], replicated, may hold values from 4096 to 8191
Outputs:
- out_states: bfloat16 [16, 2048], P('tensor')
- new_keys: bfloat16 [16, 2048], P(None, 'tensor')
- new_values: bfloat16 [16, 2048], P(None, 'tensor')
Inputs may be any that keep to these rules, and one draw needn't show every extreme that they name: `cache_len`: at least one request has all 4096 slots filled in every draw.
All inputs are finite; a program needn't handle non-finite values. No bound on the sum of `slot_mask` on one device may be relied on, other than what follows from the above.
Results may differ from a plain program's by a relative error of at most 0.02.
The roundings to bfloat16 on the way count: a program that leaves them out, or rounds other values in their place, can miss the bound.
Values may be sent and summed in bfloat16 or wider, within the bound.
No kernel may reach another device: no remote copies, remote signals or barrier semaphores. Data moves between devices by JAX's collectives and lax.ppermute only.
A program may use at most 128 MiB of HBM per device.

v0:
```python
import jax
import jax.numpy as jnp
from jax import lax
from jax.sharding import PartitionSpec as P

HEAD_SIZE = 64
WINDOW = 4096


NEG = -1e30


def rms_norm(values, gain):
    meansq = jnp.mean(values * values, axis=-1, keepdims=True)
    return (values * lax.rsqrt(meansq + 1e-05) * gain.astype(jnp.float32)).astype(jnp.bfloat16)


def rotary(tensor, cosine, sine):
    half = tensor.shape[-1] // 2
    turned = jnp.concatenate([-tensor[..., half:], tensor[..., :half]], axis=-1)
    return tensor * cosine + turned * sine


def undo_round(weights):
    rounded = lax.optimization_barrier(weights.astype(jnp.bfloat16))
    return rounded.astype(jnp.float32)


def per_device(
    states,
    attn_gain,
    w_qkv,
    w_out,
    mlp_gain,
    w_gate_up,
    w_down,
    key_cache,
    value_cache,
    sink_keys,
    sink_values,
    cache_len,
    slot_mask,
    slot_pos,
    new_pos,
):
    rows = states.shape[0]
    width = states.shape[1]
    row_start = lax.axis_index("tensor") * rows
    floats = states.astype(jnp.float32)
    normed = rms_norm(floats, attn_gain)
    lanes = w_qkv.shape[2]
    heads_here = lanes // HEAD_SIZE
    qkv_matrix = w_qkv.reshape(width, 3 * lanes)
    projected = jnp.dot(
        lax.all_gather(normed, "tensor", axis=0, tiled=True),
        qkv_matrix,
        preferred_element_type=jnp.float32,
    )
    batch = projected.shape[0]
    projected = projected.reshape(batch, 3, heads_here, HEAD_SIZE)
    half = HEAD_SIZE // 2
    inverse = jnp.exp(
        -jnp.log(jnp.float32(130000.0)) * jnp.arange(half, dtype=jnp.float32) * (2.0 / HEAD_SIZE)
    )
    angle = new_pos.astype(jnp.float32)[:, None] * inverse[None, :]
    angle = jnp.concatenate([angle, angle], axis=-1)[:, None, :]
    cosine = jnp.cos(angle)
    sine = jnp.sin(angle)
    queries_all = rotary(projected[:, 0], cosine, sine).astype(jnp.bfloat16)
    keys_all = rotary(projected[:, 1], cosine, sine).astype(jnp.bfloat16)
    values_all = projected[:, 2].astype(jnp.bfloat16)
    stacked = jnp.stack([queries_all, keys_all, values_all], axis=1)
    mine = lax.all_to_all(stacked, "tensor", split_axis=0, concat_axis=2, tiled=True)
    queries = mine[:, 0]
    keys_new = mine[:, 1]
    values_new = mine[:, 2]
    all_heads = queries.shape[1]
    own_len = lax.dynamic_slice_in_dim(cache_len, row_start, rows, 0)
    own_pos = lax.dynamic_slice_in_dim(new_pos, row_start, rows, 0)
    window_here = key_cache.shape[2]
    seq_index = lax.axis_index("seq")
    slots = seq_index * window_here + jnp.arange(window_here, dtype=jnp.int32)
    live = (slots[None, :] < own_len[:, None]) & (slot_mask == 1)
    live = live & (slot_pos < own_pos[:, None]) & (own_pos[:, None] - slot_pos < WINDOW)
    live = live[:, None, :]
    first_shard = seq_index == 0
    kwin = key_cache.reshape(rows, all_heads, HEAD_SIZE, window_here)
    vwin = value_cache.reshape(rows, all_heads, HEAD_SIZE, window_here)
    sink_key_rows = sink_keys.reshape(rows, all_heads, HEAD_SIZE, sink_keys.shape[2])
    vsink = sink_values.reshape(rows, all_heads, HEAD_SIZE, sink_values.shape[2])
    score_win = (
        jnp.einsum("bhd,bhds->bhs", queries, kwin, preferred_element_type=jnp.float32) * 0.125
    )
    score_win = jnp.where(live, score_win, NEG)
    score_sink = (
        jnp.einsum("bhd,bhds->bhs", queries, sink_key_rows, preferred_element_type=jnp.float32)
        * 0.125
    )
    score_sink = jnp.where(first_shard, score_sink, NEG)
    score_new = jnp.sum(queries.astype(jnp.float32) * keys_new.astype(jnp.float32), axis=-1) * 0.125
    score_new = jnp.where(first_shard, score_new, NEG)
    local_top = jnp.maximum(
        jnp.maximum(jnp.max(score_win, axis=-1), jnp.max(score_sink, axis=-1)), score_new
    )
    top = lax.pmax(local_top, "seq")
    weight_win = jnp.where(live, jnp.exp(score_win - top[..., None]), 0.0)
    weight_sink = jnp.where(first_shard, jnp.exp(score_sink - top[..., None]), 0.0)
    weight_new = jnp.where(first_shard, jnp.exp(score_new - top), 0.0)
    total = jnp.sum(weight_win, axis=-1) + jnp.sum(weight_sink, axis=-1) + weight_new
    mixture = jnp.einsum(
        "bhs,bhds->bhd", weight_win.astype(jnp.bfloat16), vwin, preferred_element_type=jnp.float32
    )
    mixture = mixture + jnp.einsum(
        "bhs,bhds->bhd", weight_sink.astype(jnp.bfloat16), vsink, preferred_element_type=jnp.float32
    )
    mixture = mixture + undo_round(weight_new)[..., None] * values_new.astype(jnp.float32)
    total, mixture = (total, mixture)
    total, mixture = lax.psum((total, mixture), "seq")
    attended_own = (mixture / total[..., None]).astype(jnp.bfloat16)
    attended = lax.all_to_all(
        attended_own, "tensor", split_axis=1, concat_axis=0, tiled=True
    ).reshape(batch, lanes)
    units = w_gate_up.shape[2]
    gate_matrix = w_gate_up.reshape(width, 2 * units)
    block = attended
    projected_out = lax.psum_scatter(
        jnp.dot(block, w_out, preferred_element_type=jnp.float32).astype(jnp.bfloat16),
        "tensor",
        scatter_dimension=0,
        tiled=True,
    ).astype(jnp.float32)
    resid_part = (floats + projected_out).astype(jnp.bfloat16)
    normed2 = rms_norm(resid_part.astype(jnp.float32), mlp_gain)
    gate_up = jnp.dot(
        lax.all_gather(normed2, "tensor", axis=0, tiled=True),
        gate_matrix,
        preferred_element_type=jnp.float32,
    )
    hidden = (jax.nn.silu(gate_up[:, :units]) * gate_up[:, units:]).astype(jnp.bfloat16)
    block = hidden
    mlp_out = lax.psum_scatter(
        jnp.dot(block, w_down, preferred_element_type=jnp.float32).astype(jnp.bfloat16),
        "tensor",
        scatter_dimension=0,
        tiled=True,
    ).astype(jnp.float32)
    out_states = (resid_part.astype(jnp.float32) + mlp_out).astype(jnp.bfloat16)
    return (out_states, keys_all.reshape(batch, lanes), values_all.reshape(batch, lanes))


def solution(mesh):
    in_specs = (
        P("tensor", None),
        P(),
        P(None, None, "tensor"),
        P("tensor", None),
        P(),
        P(None, None, "tensor"),
        P("tensor", None),
        P("tensor", None, "seq"),
        P("tensor", None, "seq"),
        P("tensor", None, None),
        P("tensor", None, None),
        P(),
        P("tensor", "seq"),
        P("tensor", "seq"),
        P(),
    )
    out_specs = (P("tensor", None), P(None, "tensor"), P(None, "tensor"))
    return jax.shard_map(
        per_device, mesh=mesh, in_specs=in_specs, out_specs=out_specs, check_vma=False
    )
```

profile of v0, /device:TPU:0, one launch (start us, length us, event | category | flops | bytes accessed | tf_op | source)
XLA Modules:
  0.0 223.4 jit_solution(4022566736090589782)
XLA Ops:
  7.3 0.9 fusion.26
  8.2 0.7 convert_element_type.93
  8.9 0.8 fusion.35
  9.7 15.7 %all-gather = bf16[8,2,2048]{2,1,0:T(2,128)(2,1)S(1)} all-gather(bf16[1,2,2048]{2,1,0:T(2,128)(2,1)S(1)} %fusion.35), channel_id=1, replica_groups=mesh['seq'=4,'tensor'=8] {'tensor'}, dimensions={0}, use_global_device_ids=true | all-gather | bytes 73728 | tf_op jit(solution)/shard_map/all_gather | solution.py:55
  25.3 4.7 %copy.35 = bf16[2048,3,256]{0,2,1:T(8,128)(2,1)} copy(bf16[2048,3,256]{2,0,1:T(8,128)(2,1)} %param.17) | data formatting | bytes 6291456 | tf_op args[2]
  30.1 3.2 %fusion.8 = f32[16,3,4,64]{3,0,2,1:T(8,128)S(1)} fusion(bf16[3,4,64,2048]{3,2,1,0:T(8,128)(2,1)} %bitcast.109, bf16[16,2048,1,1]{1,0,2,3:T(8,128)(2,1)S(1)} %reshape.200), kind=kOutput, calls=%fused_computation.13 | convolution fusion | flops 50331648 | bytes 3260416 | tf_op jit(solution)/shard_map/dot_general | solution.py:54
  33.4 0.1 fusion.37
  33.7 0.1 fusion.17
  33.8 0.7 reshape.211
  34.5 4.6 %all-to-all-start = ((bf16[8,2,768]{2,1,0:T(2,128)(2,1)}), bf16[8,2,768]{2,1,0:T(2,128)(2,1)S(1)}, u32[]{:S(2)}, u32[]{:S(2)}) async-start(bf16[8,2,768]{2,1,0:T(2,128)(2,1)} %reshape.211), calls=%async_computation | async-start | bytes 49152 | tf_op jit(solution)/shard_map/all_to_all | solution.py:73
  39.4 0.1 compare_and_fusion
  39.5 0.1 reshape.189
  39.6 0.1 reshape.191
  39.7 5.1 %all-to-all-done = bf16[8,2,768]{2,1,0:T(2,128)(2,1)S(1)} async-done(((bf16[8,2,768]{2,1,0:T(2,128)(2,1)}), bf16[8,2,768]{2,1,0:T(2,128)(2,1)S(1)}, u32[]{:S(2)}, u32[]{:S(2)}) %all-to-all-start) | async-done | bytes 24608 | tf_op jit(solution)/shard_map/all_to_all | solution.py:73
  44.9 0.1 reshape.212
  45.0 0.1 fusion.21
  45.1 0.2 fusion.12
  45.3 0.1 copy.48
  45.4 4.6 %fusion.24 = f32[2,32,1,1024]{3,2,1,0:T(1,128)S(1)} fusion(bf16[2,32,64,1024]{3,2,1,0:T(8,128)(2,1)} %bitcast.108, bf16[2,32,64,1]{2,1,0,3:T(8,128)(2,1)S(1)} %slice_bitcast_fusion.4), kind=kOutput, calls=%fused_computation.40 | convolution fusion | flops 8388608 | bytes 8658944 | tf_op jit(solution)/shard_map/bhd,bhds->bhs/dot_general | solution.py:92
  50.0 0.1 fusion.5
  50.1 9.9 %pmax.7 = f32[2,32]{1,0:T(2,128)S(1)} all-reduce(f32[2,32]{1,0:T(2,128)S(1)} %maximum_maximum_fusion), channel_id=1, replica_groups=mesh['seq'=4,'tensor'=8] {'seq'}, use_global_device_ids=true, to_apply=%region_4.5 | all-reduce | flops 64 | bytes 512 | tf_op jit(solution)/shard_map/pmax | solution.py:105
  60.1 0.2 fusion.3
  60.3 0.1 copy.51
  60.4 5.6 %fusion.1 = f32[2,32,1,64]{3,2,1,0:T(1,128)S(1)} fusion(bf16[2,32,64,1024]{3,2,1,0:T(8,128)(2,1)} %bitcast.120, bf16[2,32,1024,1]{2,1,0,3:T(8,128)(2,1)S(1)} %get-tuple-element.8), kind=kOutput, calls=%fused_computation.4 | convolution fusion | flops 8388608 | bytes 8536064 | tf_op jit(solution)/shard_map/bhs,bhds->bhd/dot_general | solution.py:110
  66.1 0.2 fusion.10
  66.3 0.1 fusion.20
  66.4 14.8 %all-reduce.2 = (f32[2,32,64]{2,1,0:T(8,128)S(1)}, f32[2,32]{1,0:T(2,128)S(1)}) all-reduce(f32[2,32,64]{2,1,0:T(8,128)S(1)} %fusion.20, f32[2,32]{1,0:T(2,128)S(1)} %get-tuple-element.24), channel_id=1, replica_groups=mesh['seq'=4,'tensor'=8] {'seq'}, use_global_device_ids=true, to_apply=%region_5.6 | all-reduce | flops 4160 | bytes 33280 | tf_op jit(solution)/shard_map/psum | solution.py:118
  81.2 0.1 divide_convert_fusion
  81.3 0.1 reshape.213
  81.4 8.0 %all_to_all.33 = bf16[8,2,256]{2,1,0:T(2,128)(2,1)S(1)} all-to-all(bf16[8,2,256]{2,1,0:T(2,128)(2,1)S(1)} %reshape.213), channel_id=1, replica_groups=mesh['seq'=4,'tensor'=8] {'tensor'}, dimensions={0} | all-to-all | bytes 16384 | tf_op jit(solution)/shard_map/all_to_all | solution.py:120
  89.4 0.1 reshape.214
  89.5 0.1 reshape.192
  89.6 0.9 convolution_convert_fusion.1
  90.6 0.1 mul.204
  90.7 0.1 squeeze.17
  90.8 0.1 mul.208
  90.9 10.2 %copy.55 = bf16[256,8,2,1024]{3,1,2,0:T(8,128)(2,1)} copy(bf16[256,8,2,1024]{3,2,1,0:T(2,128)(2,1)} %bitcast.110) | data formatting | bytes 16777216
  101.1 0.6 dynamic-slice
  102.4 39.1 %all-reduce.6.cloned.1.call-done = bf16[16,2048]{1,0:T(8,128)(2,1)} async-done(((bf16[16,2048]{1,0:T(8,128)(2,1)}), bf16[16,2048]{1,0:T(8,128)(2,1)}) %all-reduce.6.cloned.1.call-update) | async-done | bytes 65552
  141.4 0.9 fusion.30
  142.3 0.1 fusion.34
  142.4 14.0 %all-gather.1 = bf16[8,2,2048]{2,1,0:T(2,128)(2,1)S(1)} all-gather(bf16[1,2,2048]{2,1,0:T(2,128)(2,1)S(1)} %fusion.34), channel_id=1, replica_groups=mesh['seq'=4,'tensor'=8] {'tensor'}, dimensions={0}, use_global_device_ids=true | all-gather | bytes 73728 | tf_op jit(solution)/shard_map/all_gather | solution.py:135
  156.4 4.7 %fusion.46 = f32[16,2048]{1,0:T(8,128)S(1)} fusion(bf16[16,2048]{1,0:T(8,128)(2,1)S(1)} %reshape.199, bf16[2048,2048]{1,0:T(8,128)(2,1)} %bitcast.107), kind=kOutput, calls=%fused_computation.89 | convolution fusion | flops 134217728 | bytes 8585216 | tf_op jit(solution)/shard_map/dot_general | solution.py:134
  161.2 1.3 convolution_convert_fusion
  162.5 0.6 add_convert_fusion
  163.1 0.7 convert_element_type.120
  163.8 51.4 %all-reduce.8.cloned.1.call-done = bf16[16,2048]{1,0:T(8,128)(2,1)} async-done(((bf16[16,2048]{1,0:T(8,128)(2,1)}), bf16[16,2048]{1,0:T(8,128)(2,1)}) %all-reduce.8.cloned.1.call-update) | async-done | bytes 65552
  215.2 1.4 fusion.33
  (57 shorter events, 0.9 us)
Async XLA Ops:
  7.2 82.4 %copy-start = (bf16[256,2048]{1,0:T(8,128)(2,1)S(1)}, bf16[256,2048]{1,0:T(8,128)(2,1)}, u32[]{:S(2)}) copy-start(bf16[256,2048]{1,0:T(8,128)(2,1)} %param.18) | copy-start | bytes 3145732
  7.2 26.1 %copy-start.8 = (s32[16]{0:T(128)S(1)}, s32[16]{0:T(128)}, u32[]{:S(2)}) copy-start(s32[16]{0:T(128)} %param.29) | copy-start | bytes 196
  7.2 32.1 %copy-start.9 = (s32[16]{0:T(128)S(1)}, s32[16]{0:T(128)}, u32[]{:S(2)}) copy-start(s32[16]{0:T(128)} %param.26) | copy-start | bytes 196
  7.2 32.2 %copy-start.5 = (s32[2,1024]{1,0:T(2,128)S(1)}, s32[2,1024]{1,0:T(2,128)}, u32[]{:S(2)}) copy-start(s32[2,1024]{1,0:T(2,128)} %param.28) | copy-start | bytes 24580
  7.2 32.2 %copy-start.6 = (s32[2,1024]{1,0:T(2,128)S(1)}, s32[2,1024]{1,0:T(2,128)}, u32[]{:S(2)}) copy-start(s32[2,1024]{1,0:T(2,128)} %param.27) | copy-start | bytes 24580
  7.2 32.3 %copy-start.3 = (bf16[2,2048,4]{1,2,0:T(4,128)(2,1)S(1)}, bf16[2,2048,4]{1,2,0:T(4,128)(2,1)}, u32[]{:S(2)}) copy-start(bf16[2,2048,4]{1,2,0:T(4,128)(2,1)} %param.24) | copy-start | bytes 98308
  7.2 32.4 %copy-start.4 = (bf16[2,2048,4]{1,2,0:T(4,128)(2,1)S(1)}, bf16[2,2048,4]{1,2,0:T(4,128)(2,1)}, u32[]{:S(2)}) copy-start(bf16[2,2048,4]{1,2,0:T(4,128)(2,1)} %param.25) | copy-start | bytes 98308
  34.5 10.3 %all-to-all-start = ((bf16[8,2,768]{2,1,0:T(2,128)(2,1)}), bf16[8,2,768]{2,1,0:T(2,128)(2,1)S(1)}, u32[]{:S(2)}, u32[]{:S(2)}) async-start(bf16[8,2,768]{2,1,0:T(2,128)(2,1)} %reshape.211), calls=%async_computation | async-start | bytes 49152 | tf_op jit(solution)/shard_map/all_to_all | solution.py:73
  39.2 102.3 %all-reduce.6.cloned.1.call-start = ((), (), s32[]{:S(2)}) async-start(), calls=%async_computation.2 | async-start | bytes 131072
  50.0 40.6 %copy-start.7 = (bf16[2048]{0:T(1024)(128)(2,1)S(1)}, bf16[2048]{0:T(1024)(128)(2,1)}, u32[]{:S(2)}) copy-start(bf16[2048]{0:T(1024)(128)(2,1)} %param.19) | copy-start | bytes 12292
  90.5 124.7 %all-reduce.8.cloned.1.call-start = ((), (), s32[]{:S(2)}) async-start(), calls=%async_computation.3 | async-start | bytes 131072
  90.9 10.2 %copy-start.10 = (u32[32]{0:T(128)S(1)}, u32[32]{0:T(128)}, u32[]{:S(2)}) copy-start(u32[32]{0:T(128)} %constant.52) | copy-start | bytes 388
  90.9 50.5 %copy-start.2 = (bf16[2,2048]{1,0:T(2,128)(2,1)S(1)}, bf16[2,2048]{1,0:T(2,128)(2,1)}, u32[]{:S(2)}) copy-start(bf16[2,2048]{1,0:T(2,128)(2,1)} %param.15) | copy-start | bytes 24580
  156.4 4.7 %copy-start.1 = (bf16[1024,2048]{1,0:T(8,128)(2,1)S(1)}, bf16[1024,2048]{1,0:T(8,128)(2,1)}, u32[]{:S(2)}) copy-start(bf16[1024,2048]{1,0:T(8,128)(2,1)} %param.21) | copy-start | bytes 12582916
Sparse Core Ops, SparseCore 0:
  90.6 50.7 all-reduce.5
  162.6 52.5 all-reduce.7
where the time goes:
time: 224 us; the launch traced here: 223 us
  waiting for transfers between devices  95.6 us (43%)
  blocking collectives  62.3 us (28%)
  matrix products  20.7 us (9%)
  local copies, waits for them, and re-layouts  18.3 us (8%)
  between operations  15 us (7%)
  other arithmetic  6.66 us (3%)
  starting transfers between devices  4.72 us (2%)
    unnamed x4, waiting for transfers between devices  90.5 us
    unnamed x31, local copies, waits for them, and re-layouts  16.6 us
    all_gather x1, blocking collectives, per_device(): lax.all_gather(normed, 'tensor', axis=0, tiled=True)  15.7 us
    psum x1, blocking collectives, per_device(): total, mixture = lax.psum((total, mixture), 'seq')  14.8 us
    all_gather x1, blocking collectives, per_device(): lax.all_gather(normed2, 'tensor', axis=0, tiled=True)  14 us
    pmax x1, blocking collectives, per_device(): top = lax.pmax(local_top, 'seq')  9.92 us
    all_to_all x1, blocking collectives, per_device(): lax.all_to_all(attended_own, 'tensor', split_axis=1, concat_axis=0, tiled...  7.96 us
    dot_general x1, matrix products, per_device(): jnp.einsum('bhs,bhds->bhd', weight_win.astype(jnp.bfloat16), vwin, prefer...  5.65 us
  transfers between devices with their start and end apart: 3, of which 3 were waited for; matrix products, arithmetic and copies ran while one was open for 6% of the time, Pallas kernels for 0%

commit v1 on v0

v1 whole, which is shorter than its diff:
```python
import functools

import jax
import jax.numpy as jnp
from jax import lax
from jax.experimental import pallas as pl
from jax.experimental.pallas import tpu as pltpu
from jax.sharding import PartitionSpec as P

HEAD_SIZE = 64
WINDOW = 4096
NEG = -1e30
LANE = 128
HEADS_BLOCK = 8
MIB = 2**20

VMEM_SPEC = pl.BlockSpec(memory_space=pltpu.VMEM)
SMEM_SPEC = pl.BlockSpec(memory_space=pltpu.SMEM)
F32 = jnp.float32
BF16 = jnp.bfloat16


def normed_rows(values, gain):
    meansq = jnp.mean(values * values, axis=-1, keepdims=True)
    return (values * lax.rsqrt(meansq + 1e-05) * gain).astype(BF16)


def swap_halves(tensor):
    width = tensor.shape[1]
    half = HEAD_SIZE // 2
    if width == HEAD_SIZE:
        return jnp.concatenate([tensor[:, half:], tensor[:, :half]], axis=1)
    lane = lax.broadcasted_iota(jnp.int32, tensor.shape, 1)
    upper = pltpu.roll(tensor, width - half, 1)
    lower = pltpu.roll(tensor, half, 1)
    return jnp.where(lane % HEAD_SIZE < half, upper, lower)


def wire_row(rows, lane_chunk, row):
    return lane_chunk * rows + row


def qkv_kernel(rows, x_ref, gain_ref, w_ref, cos_ref, sin_ref, q_ref, k_ref, v_ref, new_ref):
    lanes = w_ref.shape[2]
    normed = normed_rows(x_ref[...].astype(F32), gain_ref[...].astype(F32))
    cosine = cos_ref[...]
    sine = sin_ref[...]

    def project(part):
        return jnp.dot(normed, w_ref[part], preferred_element_type=F32)

    def turned(t):
        return (t * cosine + swap_halves(t) * sine).astype(BF16)

    queries = turned(project(0))
    keys = turned(project(1))
    values = project(2).astype(BF16)
    k_ref[...] = keys
    v_ref[...] = values
    queries = queries.astype(F32)
    head_in = lax.broadcasted_iota(jnp.int32, (lanes, lanes), 0) // HEAD_SIZE
    head_out = lax.broadcasted_iota(jnp.int32, (lanes, lanes), 1) // HEAD_SIZE
    same_head = (head_in == head_out).astype(F32)
    score = jnp.dot(
        queries * keys.astype(F32),
        same_head,
        preferred_element_type=F32,
        precision=lax.Precision.HIGHEST,
    ) * (HEAD_SIZE**-0.5)
    values = values.astype(F32)
    groups, half, chunk = q_ref.shape[0], q_ref.shape[1] // 2, q_ref.shape[2]
    q_ref[...] = jnp.zeros_like(q_ref)
    for group in range(groups):
        mine = slice(group * rows, (group + 1) * rows)
        for c in range(lanes // chunk):
            at = slice(c * chunk, (c + 1) * chunk)
            row = wire_row(rows, c, 0)
            q_ref[group, row : row + rows, :] = queries[mine, at]
            new_ref[group, row : row + rows, :] = values[mine, at]
            new_ref[group, half + row : half + row + rows, :] = score[mine, at]


def attention_kernel(
    lanes,
    len_ref,
    pos_ref,
    q_ref,
    k_ref,
    v_ref,
    sink_k_ref,
    sink_v_ref,
    mask_ref,
    slot_pos_ref,
    out_ref,
):
    rows, features, slots = k_ref.shape
    sinks = sink_k_ref.shape[1]
    copies = out_ref.shape[0]
    half, chunk = out_ref.shape[2] // 2, out_ref.shape[3]
    block = HEADS_BLOCK * HEAD_SIZE
    seq_index = lax.axis_index("seq")
    first_row = lax.axis_index("tensor") * rows
    head = lax.broadcasted_iota(jnp.int32, (HEADS_BLOCK, block), 0)
    own = head == lax.broadcasted_iota(jnp.int32, (HEADS_BLOCK, block), 1) // HEAD_SIZE
    slot = seq_index * slots + lax.broadcasted_iota(jnp.int32, (1, slots), 1)
    scale = HEAD_SIZE**-0.5
    for r in range(rows):
        own_len = len_ref[first_row + r]
        own_pos = pos_ref[first_row + r]
        slot_at = slot_pos_ref[r : r + 1, :]
        live = (slot < own_len) & (mask_ref[r : r + 1, :] == 1)
        live = live & (slot_at < own_pos) & (own_pos - slot_at < WINDOW)
        live = jnp.broadcast_to(live.astype(jnp.int32), (HEADS_BLOCK, slots)) == 1
        sink_keys = sink_k_ref[r].astype(F32)
        sink_values = sink_v_ref[r].astype(F32)
        for b in range(features // block):
            here = slice(b * block, (b + 1) * block)
            chunks = [divmod(b * (block // chunk) + f, lanes // chunk) for f in range(block // chunk)]
            query = jnp.concatenate(
                [
                    q_ref[t, wire_row(rows, c, r) : wire_row(rows, c, r) + 1, :]
                    for t, c in chunks
                ],
                axis=1,
            )
            query = jnp.where(own, jnp.broadcast_to(query, (HEADS_BLOCK, block)), 0.0)
            score = (
                jnp.dot(query.astype(BF16), k_ref[r, here, :], preferred_element_type=F32) * scale
            )
            score = jnp.where(live, score, NEG)
            top = jnp.max(score, axis=1, keepdims=True)
            sink_score = []
            for i in range(sinks):
                one = jnp.sum(query * sink_keys[i : i + 1, here], axis=1, keepdims=True) * scale
                one = jnp.where(seq_index == 0, one, NEG)
                sink_score.append(one)
                top = jnp.maximum(top, one)
            weight = jnp.where(live, jnp.exp(score - top), 0.0)
            total = jnp.sum(weight, axis=1, keepdims=True)
            mixture = lax.dot_general(
                weight.astype(BF16),
                v_ref[r, here, :],
                (((1,), (1,)), ((), ())),
                preferred_element_type=F32,
            )
            for i in range(sinks):
                one = jnp.where(seq_index == 0, jnp.exp(sink_score[i] - top), 0.0)
                total = total + one
                mixture = mixture + one.astype(BF16).astype(F32) * sink_values[i : i + 1, here]
            some = total > 0.0
            level = jnp.where(some, top + jnp.log(jnp.where(some, total, 1.0)), NEG)
            mixture = mixture / jnp.where(some, total, 1.0)
            mixture = jnp.sum(jnp.where(own, mixture, 0.0), axis=0, keepdims=True)
            level = jnp.sum(jnp.where(own, level, 0.0), axis=0, keepdims=True)
            for f, (t, c) in enumerate(chunks):
                row = wire_row(rows, c, r)
                at = slice(f * chunk, (f + 1) * chunk)
                for copy in range(copies):
                    out_ref[copy, t, row : row + 1, :] = mixture[:, at]
                    out_ref[copy, t, half + row : half + row + 1, :] = level[:, at]


def merge_kernel(rows, part_ref, new_ref, w_ref, mine_ref, other_ref, rows_ref, full_ref):
    copies, groups, wire_rows, chunk = part_ref.shape
    half = wire_rows // 2
    lanes = w_ref.shape[0]
    flat = groups * wire_rows
    parts = [part_ref[s].reshape(flat, chunk) for s in range(copies)]
    parts.append(new_ref[...].reshape(flat, chunk))
    levels = [pltpu.roll(part, flat - half, 0) for part in parts]
    top = functools.reduce(jnp.maximum, levels)
    mixture = jnp.zeros((flat, chunk), F32)
    total = jnp.zeros((flat, chunk), F32)
    for part, level in zip(parts, levels):
        share = jnp.exp(level - top)
        mixture = mixture + share * part
        total = total + share
    rows_ref[...] = mixture / total
    attended = []
    for c in range(lanes // chunk):
        start = wire_row(rows, c, 0)
        attended.append(
            jnp.concatenate(
                [
                    rows_ref[g * wire_rows + start : g * wire_rows + start + rows, :]
                    for g in range(groups)
                ],
                axis=0,
            )
        )
    attended = jnp.concatenate(attended, axis=1).astype(BF16)
    full_ref[...] = jnp.dot(attended, w_ref[...], preferred_element_type=F32)
    width = mine_ref.shape[1]
    core = lax.axis_index("tensor") % 2
    mine_ref[...] = full_ref[:, pl.ds(pl.multiple_of(core * width, LANE), width)]
    other_ref[...] = full_ref[:, pl.ds(pl.multiple_of((1 - core) * width, LANE), width)]


def mlp_kernel(mine_ref, other_ref, gain_ref, gate_up_ref, down_ref, out_ref, resid_ref, wide_ref):
    batch, width = mine_ref.shape
    units = gate_up_ref.shape[2]
    core = lax.axis_index("tensor") % 2
    first = jnp.where(core == 0, mine_ref[...].astype(F32), other_ref[...].astype(F32))
    second = jnp.where(core == 0, other_ref[...].astype(F32), mine_ref[...].astype(F32))
    resid = jnp.concatenate([first, second], axis=1)
    resid_ref[...] = resid.astype(BF16)
    normed = normed_rows(resid, gain_ref[...].astype(F32))
    step = 2 * LANE
    feature = lax.broadcasted_iota(jnp.int32, (step, 4 * step), 0)
    lane = lax.broadcasted_iota(jnp.int32, (step, 4 * step), 1)
    lane = jnp.where(lane < 2 * step, lane, lane - 2 * step - 1)
    spread = (2 * feature == lane).astype(F32).astype(BF16)
    pieces = 2 * width // step
    stacked = jnp.concatenate([normed[:, j * step : (j + 1) * step] for j in range(pieces)], axis=0)
    wide = jnp.dot(stacked, spread, preferred_element_type=F32).astype(BF16)
    for j in range(pieces):
        part = wide[j * batch : (j + 1) * batch, :]
        at = slice(j * 2 * step, (j + 1) * 2 * step)
        wide_ref[:batch, at] = part[:, : 2 * step]
        wide_ref[batch:, at] = part[:, 2 * step :]
    weights = gate_up_ref.reshape(4 * width, units)
    gate_up = jnp.dot(wide_ref[...], weights[...], preferred_element_type=F32)
    gate = gate_up[:batch]
    hidden = (gate * jax.nn.sigmoid(gate) * gate_up[batch:]).astype(BF16)
    out_ref[...] = jnp.dot(hidden, down_ref[...], preferred_element_type=F32).astype(BF16)


def call(kernel, out, inputs, specs=None, scratch=(), limit=16, name=None, flops=0):
    return pl.pallas_call(
        kernel,
        out_shape=out,
        in_specs=specs or [VMEM_SPEC] * len(inputs),
        out_specs=jax.tree.map(lambda _: VMEM_SPEC, out),
        scratch_shapes=scratch,
        compiler_params=pltpu.CompilerParams(vmem_limit_bytes=limit * MIB),
        name=name,
        cost_estimate=pl.CostEstimate(
            flops=flops,
            bytes_accessed=sum(a.size * a.dtype.itemsize for a in inputs),
            transcendentals=0,
        ),
    )(*inputs)


def per_device(
    shards,
    groups,
    states,
    attn_gain,
    w_qkv,
    w_out,
    mlp_gain,
    w_gate_up,
    w_down,
    key_cache,
    value_cache,
    sink_keys,
    sink_values,
    cache_len,
    slot_mask,
    slot_pos,
    new_pos,
):
    rows, width = states.shape
    batch = rows * groups
    lanes = w_qkv.shape[2]
    tensor = lax.axis_index("tensor")
    sds = jax.ShapeDtypeStruct
    chunk = min(lanes, LANE)
    wire_rows = max(8, 2 * rows * lanes // chunk)

    half = HEAD_SIZE // 2
    inverse = jnp.exp(-jnp.log(F32(130000.0)) * jnp.arange(half, dtype=F32) * (2.0 / HEAD_SIZE))
    angle = new_pos.astype(F32)[:, None] * inverse[None, :]
    cosine = jnp.cos(angle)
    sine = jnp.sin(angle)
    heads_here = lanes // HEAD_SIZE
    cosine = jnp.tile(cosine, (1, 2 * heads_here))
    sine = jnp.tile(jnp.concatenate([-sine, sine], axis=1), (1, heads_here))

    everyone = lax.all_to_all(
        jnp.broadcast_to(states[None], (groups, rows, width)), "tensor", 0, 0, tiled=True
    ).reshape(batch, width)
    wire = sds((groups, wire_rows, chunk), F32)
    flat = sds((batch, lanes), BF16)
    queries, new_keys, new_values, new_part = call(
        functools.partial(qkv_kernel, rows),
        (wire, flat, flat, wire),
        (everyone, attn_gain[None], jnp.transpose(w_qkv, (1, 0, 2)), cosine, sine),
        name="qkv",
        flops=2 * batch * width * 3 * lanes,
    )
    queries = lax.all_to_all(queries, "tensor", 0, 0, tiled=True)
    part = call(
        functools.partial(attention_kernel, lanes),
        sds((shards, groups, wire_rows, chunk), F32),
        (
            cache_len,
            new_pos,
            queries,
            key_cache,
            value_cache,
            jnp.transpose(sink_keys, (0, 2, 1)),
            jnp.transpose(sink_values, (0, 2, 1)),
            slot_mask,
            slot_pos,
        ),
        specs=[SMEM_SPEC] * 2 + [VMEM_SPEC] * 7,
        limit=28,
        name="attention",
        flops=4 * HEADS_BLOCK * key_cache.size,
    )
    part = lax.all_to_all(
        part.reshape(shards * groups, wire_rows, chunk), ("seq", "tensor"), 0, 0, tiled=True
    ).reshape(shards, groups, wire_rows, chunk)
    side = sds((batch, width // 2), F32)
    mine, other = call(
        functools.partial(merge_kernel, rows),
        (side, side),
        (part, new_part, w_out),
        scratch=[pltpu.VMEM((groups * wire_rows, chunk), F32), pltpu.VMEM((batch, width), F32)],
        name="merge",
        flops=2 * batch * lanes * width,
    )
    across = [(i, i ^ 1) for i in range(groups)]
    chip = (mine + lax.ppermute(other, "tensor", across)).astype(BF16)
    total = chip.astype(F32)
    for step in range(2, groups, 2):
        hop = [(i, (i + step) % groups) for i in range(groups)]
        total = total + lax.ppermute(chip, "tensor", hop).astype(F32)
    own_side = lax.dynamic_slice_in_dim(everyone, (tensor % 2) * (width // 2), width // 2, 1)
    side_resid = (own_side.astype(F32) + total).astype(BF16)
    other_resid = lax.ppermute(side_resid, "tensor", across)
    partial, resid = call(
        mlp_kernel,
        (sds((batch, width), BF16), sds((batch, width), BF16)),
        (side_resid, other_resid, mlp_gain[None], w_gate_up, w_down),
        scratch=[pltpu.VMEM((2 * batch, 2 * width), BF16)],
        limit=24,
        name="mlp",
        flops=6 * batch * width * w_gate_up.shape[2],
    )
    partial = lax.all_to_all(partial.reshape(groups, rows, width), "tensor", 0, 0, tiled=True)
    own_resid = lax.dynamic_slice_in_dim(resid, tensor * rows, rows, 0)
    out_states = (own_resid.astype(F32) + jnp.sum(partial.astype(F32), axis=0)).astype(BF16)
    return out_states, new_keys, new_values


def solution(mesh):
    in_specs = (
        P("tensor", None),
        P(),
        P(None, None, "tensor"),
        P("tensor", None),
        P(),
        P(None, None, "tensor"),
        P("tensor", None),
        P("tensor", None, "seq"),
        P("tensor", None, "seq"),
        P("tensor", None, None),
        P("tensor", None, None),
        P(),
        P("tensor", "seq"),
        P("tensor", "seq"),
        P(),
    )
    out_specs = (P("tensor", None), P(None, "tensor"), P(None, "tensor"))
    body = functools.partial(per_device, mesh.shape["seq"], mesh.shape["tensor"])
    return jax.shard_map(
        body, mesh=mesh, in_specs=in_specs, out_specs=out_specs, check_vma=False
    )
```

time: 224 us -> 82.8 us (0.37)
  waiting for transfers between devices: 95.6 us -> 17.5 us
  blocking collectives: 62.3 us -> 19 us
  matrix products: 20.7 us -> 0 us
  between operations: 15 us -> 0.72 us
  Pallas kernels: 0 us -> 9.26 us
  starting transfers between devices: 4.72 us -> 12.6 us
  other arithmetic: 6.66 us -> 1.58 us
  local copies, waits for them, and re-layouts: 18.3 us -> 21.4 us
    unnamed x4 -> x0, waiting for transfers between devices: 90.5 us -> none
    all_gather x2 -> x0, blocking collectives: 29.6 us -> none  [the longest x1 15.7 us: per_device(): lax.all_gather(normed, 'tensor', axis=0, tiled=True)]
    dot_general x8 -> x0, matrix products: 20.7 us -> none  [the longest x1 5.65 us: per_device(): jnp.einsum('bhs,bhds->bhd', weight_win.astype(jnp.bfloat16), vwin, prefer...]
    psum x1 -> x0, blocking collectives: 14.8 us -> none  [per_device(): total, mixture = lax.psum((total, mixture), 'seq')]
    all_to_all x1 -> x2, blocking collectives: 7.96 us -> 19 us  [the longest x1 10.9 us: per_device(): lax.all_to_all(part.reshape(shards * groups, wire_rows, chunk), ('seq', '...]
    pmax x1 -> x0, blocking collectives: 9.92 us -> none  [per_device(): top = lax.pmax(local_top, 'seq')]
    pallas_call x0 -> x4, Pallas kernels: none -> 9.26 us  [call(): pl.pallas_call(kernel, out_shape=out, in_specs=specs or [VMEM_SPEC] * len...]
    ppermute x0 -> x5, waiting for transfers between devices: none -> 7.45 us  [the longest x3 5.34 us: per_device(): total = total + lax.ppermute(chip, 'tensor', hop).astype(F32)]
  transfers between devices with their start and end apart: 3 -> 7, of which waited for: 3 -> 7; matrix products, arithmetic and copies ran while one was open for 6% -> 2% of each run, Pallas kernels for 0% -> 0%
where the time goes in v1:
time: 82.8 us; the launch traced here: 82 us
  local copies, waits for them, and re-layouts  21.4 us (26%)
  blocking collectives  19 us (23%)
  waiting for transfers between devices  17.5 us (21%)
  starting transfers between devices  12.6 us (15%)
  Pallas kernels  9.26 us (11%)
  other arithmetic  1.58 us (2%)
    unnamed x26, local copies, waits for them, and re-layouts  18.4 us
    all_to_all x1, blocking collectives, per_device(): lax.all_to_all(part.reshape(shards * groups, wire_rows, chunk), ('seq', '...  10.9 us
    pallas_call x4, Pallas kernels, call(): pl.pallas_call(kernel, out_shape=out, in_specs=specs or [VMEM_SPEC] * len...  9.26 us
    all_to_all x1, blocking collectives, per_device(): queries = lax.all_to_all(queries, 'tensor', 0, 0, tiled=True)  8.1 us
    all_to_all x1, starting transfers between devices, per_device(): lax.all_to_all(jnp.broadcast_to(states[None], (groups, rows, width)), 'te...  6.33 us
    all_to_all x1, waiting for transfers between devices, per_device(): lax.all_to_all(partial.reshape(groups, rows, width), 'tensor', 0, 0, tile...  5.85 us
    ppermute x3, waiting for transfers between devices, per_device(): total = total + lax.ppermute(chip, 'tensor', hop).astype(F32)  5.34 us
    all_to_all x1, waiting for transfers between devices, per_device(): lax.all_to_all(jnp.broadcast_to(states[None], (groups, rows, width)), 'te...  4.16 us
  transfers between devices with their start and end apart: 7, of which 7 were waited for; matrix products, arithmetic and copies ran while one was open for 2% of the time, Pallas kernels for 0%

profile of v1, /device:TPU:0, one launch (start us, length us, event | category | flops | bytes accessed | tf_op | source)
XLA Modules:
  0.0 82.0 jit_solution(14189385084456451925)
XLA Ops:
  0.6 1.4 %broadcast_in_dim.6 = bf16[8,2,2048]{2,1,0:T(2,128)(2,1)} broadcast(bf16[2,2048]{1,0:T(2,128)(2,1)} %param.15), dimensions={1,2} | broadcast | bytes 73728 | tf_op jit(solution)/shard_map/broadcast_in_dim | solution.py:282
  2.0 6.3 %all-to-all-start = ((bf16[8,2,2048]{2,1,0:T(2,128)(2,1)}), bf16[8,2,2048]{2,1,0:T(2,128)(2,1)S(1)}, u32[]{:S(2)}, u32[]{:S(2)}) async-start(bf16[8,2,2048]{2,1,0:T(2,128)(2,1)} %broadcast_in_dim.6), calls=%async_computation | async-start | bytes 131072 | tf_op jit(solution)/shard_map/all_to_all | solution.py:281
  8.3 0.7 convert_element_type.34
  9.0 0.1 fusion
  9.1 0.7 broadcast_in_dim.7.gain_ref
  9.8 0.1 tile.9.cos_ref
  9.9 0.1 pad_maximum_fusion
  10.0 0.1 tile.21.sin_ref
  10.1 4.2 %all-to-all-done = bf16[8,2,2048]{2,1,0:T(2,128)(2,1)S(1)} async-done(((bf16[8,2,2048]{2,1,0:T(2,128)(2,1)}), bf16[8,2,2048]{2,1,0:T(2,128)(2,1)S(1)}, u32[]{:S(2)}, u32[]{:S(2)}) %all-to-all-start) | async-done | bytes 65568 | tf_op jit(solution)/shard_map/all_to_all | solution.py:281
  14.3 0.0 copy-start.4
  14.3 1.9 %copy-done.4 = bf16[2048,3,256]{2,0,1:T(8,128)(2,1)S(1)} copy-done((bf16[2048,3,256]{2,0,1:T(8,128)(2,1)S(1)}, bf16[2048,3,256]{2,0,1:T(8,128)(2,1)}, u32[]{:S(2)}) %copy-start.4) | copy-done | bytes 3145752
  16.1 1.3 %qkv.1 = (f32[8,8,128]{2,1,0:T(8,128)S(1)}, bf16[16,256]{1,0:T(8,128)(2,1)}, bf16[16,256]{1,0:T(8,128)(2,1)}, f32[8,8,128]{2,1,0:T(8,128)S(1)}) custom-call(bf16[16,2048]{1,0:T(8,128)(2,1)S(1)} %reshape.58.x_ref, bf16[1,2048]{1,0:T(2,128)(2,1)S(1)} %broadcast_in_dim.7.gain_ref, bf16[3,2048,256]{2,1,0:T(8,128)(2,1)S(1)} %bitcast.5, ...), custom_call_target="tpu_custom_call" | custom-call | flops 50331648 | bytes 3248128 | tf_op jit(solution)/shard_map/qkv/pallas_call | solution.py:229
  17.5 8.1 %all_to_all.20.q_ref = f32[8,8,128]{2,1,0:T(8,128)S(1)} all-to-all(f32[8,8,128]{2,1,0:T(8,128)S(1)} %get-tuple-element.11), channel_id=1, replica_groups=mesh['seq'=4,'tensor'=8] {'tensor'}, dimensions={0} | all-to-all | bytes 65536 | tf_op jit(solution)/shard_map/all_to_all | solution.py:293
  25.6 0.0 copy-start
  25.6 3.4 %copy-done = bf16[2,2048,1024]{2,1,0:T(8,128)(2,1)S(1)} copy-done((bf16[2,2048,1024]{2,1,0:T(8,128)(2,1)S(1)}, bf16[2,2048,1024]{2,1,0:T(8,128)(2,1)}, u32[]{:S(2)}) %copy-start) | copy-done | bytes 8388632
  28.9 0.0 copy-start.1
  28.9 3.4 %copy-done.1 = bf16[2,2048,1024]{2,1,0:T(8,128)(2,1)S(1)} copy-done((bf16[2,2048,1024]{2,1,0:T(8,128)(2,1)S(1)}, bf16[2,2048,1024]{2,1,0:T(8,128)(2,1)}, u32[]{:S(2)}) %copy-start.1) | copy-done | bytes 8388632
  32.3 0.0 copy-start.6
  32.3 0.8 copy-done.6
  33.1 0.0 copy-start.7
  33.1 0.8 copy-done.7
  33.8 0.7 copy-done.8
  34.5 0.7 copy-done.9
  35.2 0.7 copy-done.10
  35.9 0.7 copy-done.11
  36.6 5.1 %attention.1 = f32[4,8,8,128]{3,2,1,0:T(8,128)S(1)} custom-call(s32[16]{0:T(128)S(1)} %copy-done.10, s32[16]{0:T(128)S(1)} %copy-done.11, f32[8,8,128]{2,1,0:T(8,128)S(1)} %all_to_all.20.q_ref, bf16[2,2048,1024]{2,1,0:T(8,128)(2,1)S(1)} %copy-done, bf16[2,2048,1024]{2,1,0:T(8,128)(2,1)S(1)} %copy-done.1, bf16[2,4,2048]{2,1,0:T(4,128)(2,1)S(1)} %bitcast.8, ...), custom_call_target="tpu_custom_call" | custom-call | flops 134217728 | bytes 16892032 | tf_op jit(solution)/shard_map/attention/pallas_call | solution.py:229
  41.6 10.9 %all_to_all.21 = f32[32,8,128]{2,1,0:T(8,128)S(1)} all-to-all(f32[32,8,128]{2,1,0:T(8,128)S(1)} %bitcast.6), channel_id=1, replica_groups=mesh['seq'=4,'tensor'=8] {'seq','tensor'}, dimensions={0} | all-to-all | bytes 262144 | tf_op jit(solution)/shard_map/all_to_all | solution.py:313
  52.5 0.0 copy-done.5
  52.5 0.3 merge.1
  52.8 0.4 collective-permute-start
  53.2 0.9 %collective-permute-done = f32[16,1024]{1,0:T(8,128)S(1)} collective-permute-done((f32[16,1024]{1,0:T(8,128)S(1)}, f32[16,1024]{1,0:T(8,128)S(1)}, u32[]{:S(2)}, u32[]{:S(2)}) %collective-permute-start) | collective-permute-done | bytes 65568 | tf_op jit(solution)/shard_map/ppermute | solution.py:326
  54.1 1.0 %collective-permute-start.3 = (bf16[16,1024]{1,0:T(8,128)(2,1)S(1)}, bf16[16,1024]{1,0:T(8,128)(2,1)S(1)}, u32[]{:S(2)}, u32[]{:S(2)}) collective-permute-start(bf16[16,1024]{1,0:T(8,128)(2,1)S(1)} %add_convert_fusion.1), channel_id=1, source_target_pairs={{0,6},{1,7},{2,0},{3,1},{4,2},{5,3},{6,4},{7,5},{8,14},{9,15},{10,... | collective-permute-start | bytes 98312 | tf_op jit(solution)/shard_map/ppermute | solution.py:330
  55.2 1.1 %collective-permute-start.2 = (bf16[16,1024]{1,0:T(8,128)(2,1)S(1)}, bf16[16,1024]{1,0:T(8,128)(2,1)S(1)}, u32[]{:S(2)}, u32[]{:S(2)}) collective-permute-start(bf16[16,1024]{1,0:T(8,128)(2,1)S(1)} %add_convert_fusion.1), channel_id=1, source_target_pairs={{0,4},{1,5},{2,6},{3,7},{4,0},{5,1},{6,2},{7,3},{8,12},{9,13},{10,... | collective-permute-start | bytes 98312 | tf_op jit(solution)/shard_map/ppermute | solution.py:330
  56.2 0.4 collective-permute-start.1
  56.6 1.5 %collective-permute-done.3 = bf16[16,1024]{1,0:T(8,128)(2,1)S(1)} collective-permute-done((bf16[16,1024]{1,0:T(8,128)(2,1)S(1)}, bf16[16,1024]{1,0:T(8,128)(2,1)S(1)}, u32[]{:S(2)}, u32[]{:S(2)}) %collective-permute-start.3) | collective-permute-done | bytes 32800 | tf_op jit(solution)/shard_map/ppermute | solution.py:330
  58.1 1.9 %collective-permute-done.2 = bf16[16,1024]{1,0:T(8,128)(2,1)S(1)} collective-permute-done((bf16[16,1024]{1,0:T(8,128)(2,1)S(1)}, bf16[16,1024]{1,0:T(8,128)(2,1)S(1)}, u32[]{:S(2)}, u32[]{:S(2)}) %collective-permute-start.2) | collective-permute-done | bytes 32800 | tf_op jit(solution)/shard_map/ppermute | solution.py:330
  60.0 2.0 %collective-permute-done.1 = bf16[16,1024]{1,0:T(8,128)(2,1)S(1)} collective-permute-done((bf16[16,1024]{1,0:T(8,128)(2,1)S(1)}, bf16[16,1024]{1,0:T(8,128)(2,1)S(1)}, u32[]{:S(2)}, u32[]{:S(2)}) %collective-permute-start.1) | collective-permute-done | bytes 32800 | tf_op jit(solution)/shard_map/ppermute | solution.py:330
  62.0 0.1 collective-permute-start.4
  62.1 0.0 copy-done.12
  62.1 1.2 %collective-permute-done.4.other_ref = bf16[16,1024]{1,0:T(8,128)(2,1)S(1)} collective-permute-done((bf16[16,1024]{1,0:T(8,128)(2,1)S(1)}, bf16[16,1024]{1,0:T(8,128)(2,1)S(1)}, u32[]{:S(2)}, u32[]{:S(2)}) %collective-permute-start.4) | collective-permute-done | bytes 32800 | tf_op jit(solution)/shard_map/ppermute | solution.py:333
  63.3 3.4 %copy-done.2 = bf16[2048,2,1024]{2,1,0:T(2,128)(2,1)S(1)} copy-done((bf16[2048,2,1024]{2,1,0:T(2,128)(2,1)S(1)}, bf16[2048,2,1024]{2,1,0:T(2,128)(2,1)}, u32[]{:S(2)}) %copy-start.2) | copy-done | bytes 8388632
  66.6 2.2 %copy-done.3 = bf16[1024,2048]{1,0:T(8,128)(2,1)S(1)} copy-done((bf16[1024,2048]{1,0:T(8,128)(2,1)S(1)}, bf16[1024,2048]{1,0:T(8,128)(2,1)}, u32[]{:S(2)}) %copy-start.3) | copy-done | bytes 4194328
  68.8 2.6 %mlp.1 = (bf16[16,2048]{1,0:T(8,128)(2,1)S(1)}, bf16[16,2048]{1,0:T(8,128)(2,1)S(1)}) custom-call(bf16[16,1024]{1,0:T(8,128)(2,1)S(1)} %add_convert_fusion.mine_ref, bf16[16,1024]{1,0:T(8,128)(2,1)S(1)} %collective-permute-done.4.other_ref, bf16[1,2048]{1,0:T(2,128)(2,1)S(1)} %broadcast_in_dim.16.gain_ref, bf16[2048,2,1024]{2,1,0:T(2,128)(2,1)S(1)} %copy-done.2, ...), custom_call_target="tpu_custom_call" | custom-call | flops 201326592 | bytes 12652544 | tf_op jit(solution)/shard_map/mlp/pallas_call | solution.py:229
  71.4 0.7 reshape.61
  72.1 3.3 %all-to-all-start.3 = ((bf16[8,2,2048]{2,1,0:T(2,128)(2,1)}), bf16[8,2,2048]{2,1,0:T(2,128)(2,1)S(1)}, u32[]{:S(2)}, u32[]{:S(2)}) async-start(bf16[8,2,2048]{2,1,0:T(2,128)(2,1)} %reshape.61), calls=%async_computation.3 | async-start | bytes 131072 | tf_op jit(solution)/shard_map/all_to_all | solution.py:343
  75.4 5.8 %all-to-all-done.3 = bf16[8,2,2048]{2,1,0:T(2,128)(2,1)S(1)} async-done(((bf16[8,2,2048]{2,1,0:T(2,128)(2,1)}), bf16[8,2,2048]{2,1,0:T(2,128)(2,1)S(1)}, u32[]{:S(2)}, u32[]{:S(2)}) %all-to-all-start.3) | async-done | bytes 65568 | tf_op jit(solution)/shard_map/all_to_all | solution.py:343
  81.3 0.1 convert_reduce_fusion
  81.4 0.6 add_convert_fusion.2
  (15 shorter events, 0.1 us)
Async XLA Ops:
  2.0 12.2 %all-to-all-start = ((bf16[8,2,2048]{2,1,0:T(2,128)(2,1)}), bf16[8,2,2048]{2,1,0:T(2,128)(2,1)S(1)}, u32[]{:S(2)}, u32[]{:S(2)}) async-start(bf16[8,2,2048]{2,1,0:T(2,128)(2,1)} %broadcast_in_dim.6), calls=%async_computation | async-start | bytes 131072 | tf_op jit(solution)/shard_map/all_to_all | solution.py:281
  14.3 1.9 %copy-start.4 = (bf16[2048,3,256]{2,0,1:T(8,128)(2,1)S(1)}, bf16[2048,3,256]{2,0,1:T(8,128)(2,1)}, u32[]{:S(2)}) copy-start(bf16[2048,3,256]{2,0,1:T(8,128)(2,1)} %param.17) | copy-start | bytes 9437188
  25.6 3.4 %copy-start = (bf16[2,2048,1024]{2,1,0:T(8,128)(2,1)S(1)}, bf16[2,2048,1024]{2,1,0:T(8,128)(2,1)}, u32[]{:S(2)}) copy-start(bf16[2,2048,1024]{2,1,0:T(8,128)(2,1)} %k_ref.1) | copy-start | bytes 25165828
  28.9 3.4 %copy-start.1 = (bf16[2,2048,1024]{2,1,0:T(8,128)(2,1)S(1)}, bf16[2,2048,1024]{2,1,0:T(8,128)(2,1)}, u32[]{:S(2)}) copy-start(bf16[2,2048,1024]{2,1,0:T(8,128)(2,1)} %v_ref.1) | copy-start | bytes 25165828
  32.3 0.8 copy-start.6
  33.1 0.8 copy-start.7
  33.8 0.7 copy-start.8
  34.5 0.7 copy-start.9
  35.2 0.7 copy-start.10
  35.9 0.7 copy-start.11
  36.6 16.0 %copy-start.5 = (bf16[256,2048]{1,0:T(8,128)(2,1)S(1)}, bf16[256,2048]{1,0:T(8,128)(2,1)}, u32[]{:S(2)}) copy-start(bf16[256,2048]{1,0:T(8,128)(2,1)} %w_ref.1) | copy-start | bytes 3145732
  36.6 25.5 %copy-start.12 = (bf16[2048]{0:T(1024)(128)(2,1)S(1)}, bf16[2048]{0:T(1024)(128)(2,1)}, u32[]{:S(2)}) copy-start(bf16[2048]{0:T(1024)(128)(2,1)} %param.19) | copy-start | bytes 12292
  52.8 1.3 %collective-permute-start = (f32[16,1024]{1,0:T(8,128)S(1)}, f32[16,1024]{1,0:T(8,128)S(1)}, u32[]{:S(2)}, u32[]{:S(2)}) collective-permute-start(f32[16,1024]{1,0:T(8,128)S(1)} %get-tuple-element.14), channel_id=1, source_target_pairs={{0,1},{1,0},{2,3},{3,2},{4,5},{5,4},{6,7},{7,6},{8,9},{9,8},{10,11... | collective-permute-start | bytes 196616 | tf_op jit(solution)/shard_map/ppermute | solution.py:326
  54.1 4.0 %collective-permute-start.3 = (bf16[16,1024]{1,0:T(8,128)(2,1)S(1)}, bf16[16,1024]{1,0:T(8,128)(2,1)S(1)}, u32[]{:S(2)}, u32[]{:S(2)}) collective-permute-start(bf16[16,1024]{1,0:T(8,128)(2,1)S(1)} %add_convert_fusion.1), channel_id=1, source_target_pairs={{0,6},{1,7},{2,0},{3,1},{4,2},{5,3},{6,4},{7,5},{8,14},{9,15},{10,... | collective-permute-start | bytes 98312 | tf_op jit(solution)/shard_map/ppermute | solution.py:330
  55.2 4.8 %collective-permute-start.2 = (bf16[16,1024]{1,0:T(8,128)(2,1)S(1)}, bf16[16,1024]{1,0:T(8,128)(2,1)S(1)}, u32[]{:S(2)}, u32[]{:S(2)}) collective-permute-start(bf16[16,1024]{1,0:T(8,128)(2,1)S(1)} %add_convert_fusion.1), channel_id=1, source_target_pairs={{0,4},{1,5},{2,6},{3,7},{4,0},{5,1},{6,2},{7,3},{8,12},{9,13},{10,... | collective-permute-start | bytes 98312 | tf_op jit(solution)/shard_map/ppermute | solution.py:330
  56.2 5.7 %collective-permute-start.1 = (bf16[16,1024]{1,0:T(8,128)(2,1)S(1)}, bf16[16,1024]{1,0:T(8,128)(2,1)S(1)}, u32[]{:S(2)}, u32[]{:S(2)}) collective-permute-start(bf16[16,1024]{1,0:T(8,128)(2,1)S(1)} %add_convert_fusion.1), channel_id=1, source_target_pairs={{0,2},{1,3},{2,4},{3,5},{4,6},{5,7},{6,0},{7,1},{8,10},{9,11},{10,... | collective-permute-start | bytes 98312 | tf_op jit(solution)/shard_map/ppermute | solution.py:330
  62.0 1.3 %collective-permute-start.4 = (bf16[16,1024]{1,0:T(8,128)(2,1)S(1)}, bf16[16,1024]{1,0:T(8,128)(2,1)S(1)}, u32[]{:S(2)}, u32[]{:S(2)}) collective-permute-start(bf16[16,1024]{1,0:T(8,128)(2,1)S(1)} %add_convert_fusion.mine_ref), channel_id=1, source_target_pairs={{0,1},{1,0},{2,3},{3,2},{4,5},{5,4},{6,7},{7,6},{8,9},{9,8},{10,11... | collective-permute-start | bytes 98312 | tf_op jit(solution)/shard_map/ppermute | solution.py:333
  63.3 3.4 %copy-start.2 = (bf16[2048,2,1024]{2,1,0:T(2,128)(2,1)S(1)}, bf16[2048,2,1024]{2,1,0:T(2,128)(2,1)}, u32[]{:S(2)}) copy-start(bf16[2048,2,1024]{2,1,0:T(2,128)(2,1)} %gate_up_ref.1) | copy-start | bytes 25165828
  66.6 2.2 %copy-start.3 = (bf16[1024,2048]{1,0:T(8,128)(2,1)S(1)}, bf16[1024,2048]{1,0:T(8,128)(2,1)}, u32[]{:S(2)}) copy-start(bf16[1024,2048]{1,0:T(8,128)(2,1)} %down_ref.1) | copy-start | bytes 12582916
  72.1 9.2 %all-to-all-start.3 = ((bf16[8,2,2048]{2,1,0:T(2,128)(2,1)}), bf16[8,2,2048]{2,1,0:T(2,128)(2,1)S(1)}, u32[]{:S(2)}, u32[]{:S(2)}) async-start(bf16[8,2,2048]{2,1,0:T(2,128)(2,1)} %reshape.61), calls=%async_computation.3 | async-start | bytes 131072 | tf_op jit(solution)/shard_map/all_to_all | solution.py:343

commit v2 on v1

--- a/solution.py
+++ b/solution.py
@@ -2,6 +2,7 @@
 
 import jax
 import jax.numpy as jnp
+import numpy as np
 from jax import lax
 from jax.experimental import pallas as pl
 from jax.experimental.pallas import tpu as pltpu
@@ -13,6 +14,10 @@
 LANE = 128
 HEADS_BLOCK = 8
 MIB = 2**20
+PREP_FLOPS = 20_000_000_000
+QKV_FLOPS = 20_000_000_000
+ATT_FLOPS = 10_000_000_000
+MERGE_FLOPS = 10_000_000_000
 
 VMEM_SPEC = pl.BlockSpec(memory_space=pltpu.VMEM)
 SMEM_SPEC = pl.BlockSpec(memory_space=pltpu.SMEM)
@@ -40,9 +45,36 @@
     return lane_chunk * rows + row
 
 
-def qkv_kernel(rows, x_ref, gain_ref, w_ref, cos_ref, sin_ref, q_ref, k_ref, v_ref, new_ref):
+def qkv_kernel(
+    rows,
+    same_ref,
+    peer_ref,
+    gain_ref,
+    w_ref,
+    cos_ref,
+    sin_ref,
+    q_ref,
+    k_ref,
+    v_ref,
+    new_ref,
+    side_ref,
+    by_ref,
+    flat_ref,
+):
     lanes = w_ref.shape[2]
-    normed = normed_rows(x_ref[...].astype(F32), gain_ref[...].astype(F32))
+    core = lax.axis_index("tensor") % 2
+    chip = lax.axis_index("tensor") // 2
+    chips = same_ref.shape[0]
+    for step in range(chips):
+        source = 2 * lax.rem(chip + chips - step, chips)
+        by_ref[source + core, :rows, :] = same_ref[step].astype(F32)
+        by_ref[source + 1 - core, :rows, :] = peer_ref[step].astype(F32)
+    for group in range(2 * chips):
+        flat_ref[group * rows : (group + 1) * rows, :] = by_ref[group, :rows, :]
+    values = flat_ref[...]
+    width = side_ref.shape[1]
+    side_ref[...] = flat_ref[:, pl.ds(pl.multiple_of(core * width, LANE), width)]
+    normed = normed_rows(values, gain_ref[...].astype(F32))
     cosine = cos_ref[...]
     sine = sin_ref[...]
 
@@ -82,15 +114,12 @@
 
 def attention_kernel(
     lanes,
-    len_ref,
-    pos_ref,
     q_ref,
     k_ref,
     v_ref,
     sink_k_ref,
     sink_v_ref,
-    mask_ref,
-    slot_pos_ref,
+    live_ref,
     out_ref,
 ):
     rows, features, slots = k_ref.shape
@@ -99,18 +128,11 @@
     half, chunk = out_ref.shape[2] // 2, out_ref.shape[3]
     block = HEADS_BLOCK * HEAD_SIZE
     seq_index = lax.axis_index("seq")
-    first_row = lax.axis_index("tensor") * rows
     head = lax.broadcasted_iota(jnp.int32, (HEADS_BLOCK, block), 0)
     own = head == lax.broadcasted_iota(jnp.int32, (HEADS_BLOCK, block), 1) // HEAD_SIZE
-    slot = seq_index * slots + lax.broadcasted_iota(jnp.int32, (1, slots), 1)
     scale = HEAD_SIZE**-0.5
     for r in range(rows):
-        own_len = len_ref[first_row + r]
-        own_pos = pos_ref[first_row + r]
-        slot_at = slot_pos_ref[r : r + 1, :]
-        live = (slot < own_len) & (mask_ref[r : r + 1, :] == 1)
-        live = live & (slot_at < own_pos) & (own_pos - slot_at < WINDOW)
-        live = jnp.broadcast_to(live.astype(jnp.int32), (HEADS_BLOCK, slots)) == 1
+        live = jnp.broadcast_to(live_ref[r : r + 1, :], (HEADS_BLOCK, slots)) == 1
         sink_keys = sink_k_ref[r].astype(F32)
         sink_values = sink_v_ref[r].astype(F32)
         for b in range(features // block):
@@ -196,14 +218,19 @@
     other_ref[...] = full_ref[:, pl.ds(pl.multiple_of((1 - core) * width, LANE), width)]
 
 
-def mlp_kernel(mine_ref, other_ref, gain_ref, gate_up_ref, down_ref, out_ref, resid_ref, wide_ref):
+def mlp_kernel(
+    rows, mine_ref, other_ref, gain_ref, gate_up_ref, down_ref, out_ref, resid_ref, wide_ref, by_ref
+):
     batch, width = mine_ref.shape
     units = gate_up_ref.shape[2]
     core = lax.axis_index("tensor") % 2
     first = jnp.where(core == 0, mine_ref[...].astype(F32), other_ref[...].astype(F32))
     second = jnp.where(core == 0, other_ref[...].astype(F32), mine_ref[...].astype(F32))
     resid = jnp.concatenate([first, second], axis=1)
-    resid_ref[...] = resid.astype(BF16)
+    groups = out_ref.shape[0]
+    for group in range(groups):
+        by_ref[group, :rows, :] = resid[group * rows : (group + 1) * rows, :]
+    resid_ref[...] = by_ref[lax.axis_index("tensor"), :rows, :]
     normed = normed_rows(resid, gain_ref[...].astype(F32))
     step = 2 * LANE
     feature = lax.broadcasted_iota(jnp.int32, (step, 4 * step), 0)
@@ -222,10 +249,41 @@
     gate_up = jnp.dot(wide_ref[...], weights[...], preferred_element_type=F32)
     gate = gate_up[:batch]
     hidden = (gate * jax.nn.sigmoid(gate) * gate_up[batch:]).astype(BF16)
-    out_ref[...] = jnp.dot(hidden, down_ref[...], preferred_element_type=F32).astype(BF16)
-
-
-def call(kernel, out, inputs, specs=None, scratch=(), limit=16, name=None, flops=0):
+    out = jnp.dot(hidden, down_ref[...], preferred_element_type=F32)
+    for group in range(groups):
+        out_ref[group] = out[group * rows : (group + 1) * rows, :].astype(BF16)
+
+
+def prepare_kernel(
+    len_ref, pos_ref, inverse_ref, mask_ref, slot_pos_ref, cos_ref, sin_ref, live_ref
+):
+    batch, width = cos_ref.shape
+    wide = inverse_ref.shape[1]
+    row = lax.broadcasted_iota(jnp.int32, (batch, wide), 0)
+    position = jnp.zeros((batch, wide), F32)
+    for i in range(batch):
+        position = jnp.where(row == i, pos_ref[i].astype(F32), position)
+    angle = position * inverse_ref[...]
+    cosine = jnp.cos(angle)
+    sine = jnp.sin(angle)
+    lane = lax.broadcasted_iota(jnp.int32, (batch, wide), 1)
+    sine = jnp.where(lane % HEAD_SIZE < HEAD_SIZE // 2, -sine, sine)
+    for start in range(0, width, wide):
+        cos_ref[:, start : start + wide] = cosine
+        sin_ref[:, start : start + wide] = sine
+    rows, slots = mask_ref.shape
+    slot = lax.axis_index("seq") * slots + lax.broadcasted_iota(jnp.int32, (1, slots), 1)
+    first_row = lax.axis_index("tensor") * rows
+    for r in range(rows):
+        own_len = len_ref[first_row + r]
+        own_pos = pos_ref[first_row + r]
+        slot_at = slot_pos_ref[r : r + 1, :]
+        live = (slot < own_len) & (mask_ref[r : r + 1, :] == 1)
+        live = live & (slot_at < own_pos) & (own_pos - slot_at < WINDOW)
+        live_ref[r : r + 1, :] = live.astype(jnp.int32)
+
+
+def call(kernel, out, inputs, specs=None, scratch=(), limit=6, name=None, flops=0):
     return pl.pallas_call(
         kernel,
         out_shape=out,
@@ -264,85 +322,77 @@
     rows, width = states.shape
     batch = rows * groups
     lanes = w_qkv.shape[2]
-    tensor = lax.axis_index("tensor")
     sds = jax.ShapeDtypeStruct
     chunk = min(lanes, LANE)
     wire_rows = max(8, 2 * rows * lanes // chunk)
 
     half = HEAD_SIZE // 2
-    inverse = jnp.exp(-jnp.log(F32(130000.0)) * jnp.arange(half, dtype=F32) * (2.0 / HEAD_SIZE))
-    angle = new_pos.astype(F32)[:, None] * inverse[None, :]
-    cosine = jnp.cos(angle)
-    sine = jnp.sin(angle)
-    heads_here = lanes // HEAD_SIZE
-    cosine = jnp.tile(cosine, (1, 2 * heads_here))
-    sine = jnp.tile(jnp.concatenate([-sine, sine], axis=1), (1, heads_here))
-
-    everyone = lax.all_to_all(
-        jnp.broadcast_to(states[None], (groups, rows, width)), "tensor", 0, 0, tiled=True
-    ).reshape(batch, width)
+    inverse = np.exp(-np.log(130000.0) * np.arange(half) * (2.0 / HEAD_SIZE))
+    inverse = jnp.asarray(np.tile(inverse, 2 * chunk // HEAD_SIZE)[None], F32)
+    turn = sds((batch, lanes), F32)
+    cosine, sine, live = call(
+        prepare_kernel,
+        (turn, turn, sds(slot_mask.shape, jnp.int32)),
+        (cache_len, new_pos, inverse, slot_mask, slot_pos),
+        specs=[SMEM_SPEC] * 2 + [VMEM_SPEC] * 3,
+        name="prepare",
+        flops=PREP_FLOPS,
+    )
+    across = [(i, i ^ 1) for i in range(groups)]
+    hops = [[(i, (i + step) % groups) for i in range(groups)] for step in range(2, groups, 2)]
+    same = jnp.stack([states] + [lax.ppermute(states, "tensor", hop) for hop in hops])
+    peer = lax.ppermute(same, "tensor", across)
+    w_qkv = jnp.transpose(w_qkv, (1, 0, 2))
+    side = sds((batch, width // 2), F32)
     wire = sds((groups, wire_rows, chunk), F32)
     flat = sds((batch, lanes), BF16)
-    queries, new_keys, new_values, new_part = call(
+    queries, new_keys, new_values, new_part, own_side = call(
         functools.partial(qkv_kernel, rows),
-        (wire, flat, flat, wire),
-        (everyone, attn_gain[None], jnp.transpose(w_qkv, (1, 0, 2)), cosine, sine),
+        (wire, flat, flat, wire, side),
+        (same, peer, attn_gain[None], w_qkv, cosine, sine),
+        scratch=[pltpu.VMEM((groups, 8, width), F32), pltpu.VMEM((batch, width), F32)],
         name="qkv",
-        flops=2 * batch * width * 3 * lanes,
+        flops=QKV_FLOPS,
     )
     queries = lax.all_to_all(queries, "tensor", 0, 0, tiled=True)
+    sink_keys = jnp.transpose(sink_keys, (0, 2, 1))
+    sink_values = jnp.transpose(sink_values, (0, 2, 1))
     part = call(
         functools.partial(attention_kernel, lanes),
         sds((shards, groups, wire_rows, chunk), F32),
-        (
-            cache_len,
-            new_pos,
-            queries,
-            key_cache,
-            value_cache,
-            jnp.transpose(sink_keys, (0, 2, 1)),
-            jnp.transpose(sink_values, (0, 2, 1)),
-            slot_mask,
-            slot_pos,
-        ),
-        specs=[SMEM_SPEC] * 2 + [VMEM_SPEC] * 7,
-        limit=28,
+        (queries, key_cache, value_cache, sink_keys, sink_values, live),
+        limit=8,
         name="attention",
-        flops=4 * HEADS_BLOCK * key_cache.size,
+        flops=ATT_FLOPS,
     )
     part = lax.all_to_all(
         part.reshape(shards * groups, wire_rows, chunk), ("seq", "tensor"), 0, 0, tiled=True
     ).reshape(shards, groups, wire_rows, chunk)
-    side = sds((batch, width // 2), F32)
     mine, other = call(
         functools.partial(merge_kernel, rows),
         (side, side),
         (part, new_part, w_out),
         scratch=[pltpu.VMEM((groups * wire_rows, chunk), F32), pltpu.VMEM((batch, width), F32)],
         name="merge",
-        flops=2 * batch * lanes * width,
-    )
-    across = [(i, i ^ 1) for i in range(groups)]
+        flops=MERGE_FLOPS,
+    )
     chip = (mine + lax.ppermute(other, "tensor", across)).astype(BF16)
     total = chip.astype(F32)
-    for step in range(2, groups, 2):
-        hop = [(i, (i + step) % groups) for i in range(groups)]
+    for hop in hops:
         total = total + lax.ppermute(chip, "tensor", hop).astype(F32)
-    own_side = lax.dynamic_slice_in_dim(everyone, (tensor % 2) * (width // 2), width // 2, 1)
-    side_resid = (own_side.astype(F32) + total).astype(BF16)
+    side_resid = (own_side + total).astype(BF16)
     other_resid = lax.ppermute(side_resid, "tensor", across)
-    partial, resid = call(
-        mlp_kernel,
-        (sds((batch, width), BF16), sds((batch, width), BF16)),
+    partial, own_resid = call(
+        functools.partial(mlp_kernel, rows),
+        (sds((groups, rows, width), BF16), sds((rows, width), F32)),
         (side_resid, other_resid, mlp_gain[None], w_gate_up, w_down),
-        scratch=[pltpu.VMEM((2 * batch, 2 * width), BF16)],
-        limit=24,
+        scratch=[pltpu.VMEM((2 * batch, 2 * width), BF16), pltpu.VMEM((groups, 8, width), F32)],
+        limit=8,
         name="mlp",
         flops=6 * batch * width * w_gate_up.shape[2],
     )
-    partial = lax.all_to_all(partial.reshape(groups, rows, width), "tensor", 0, 0, tiled=True)
-    own_resid = lax.dynamic_slice_in_dim(resid, tensor * rows, rows, 0)
-    out_states = (own_resid.astype(F32) + jnp.sum(partial.astype(F32), axis=0)).astype(BF16)
+    partial = lax.all_to_all(partial, "tensor", 0, 0, tiled=True)
+    out_states = (own_resid + jnp.sum(partial.astype(F32), axis=0)).astype(BF16)
     return out_states, new_keys, new_values
 
 

time: 82.8 us -> 65.7 us (0.79)
  local copies, waits for them, and re-layouts: 21.4 us -> 3.66 us
  blocking collectives: 19 us -> 31.1 us
  waiting for transfers between devices: 17.5 us -> 7.27 us
  starting transfers between devices: 12.6 us -> 11.4 us
    unnamed x26 -> x36, local copies, waits for them, and re-layouts: 18.4 us -> 3.64 us
    all_to_all x0 -> x1, blocking collectives: none -> 10 us  [per_device(): partial = lax.all_to_all(partial, 'tensor', 0, 0, tiled=True)]
    all_to_all x2 -> x0, waiting for transfers between devices: 10 us -> none  [the longest x1 5.85 us: per_device(): lax.all_to_all(partial.reshape(groups, rows, width), 'tensor', 0, 0, tile...]
    all_to_all x2 -> x0, starting transfers between devices: 9.67 us -> none  [the longest x1 6.33 us: per_device(): lax.all_to_all(jnp.broadcast_to(states[None], (groups, rows, width)), 'te...]
    ppermute x0 -> x4, starting transfers between devices: none -> 7.08 us  [the longest x3 7.01 us: per_device(): lax.ppermute(states, 'tensor', hop)]
    ppermute x3, waiting for transfers between devices: 5.34 us -> 2.65 us  [per_device(): total = total + lax.ppermute(chip, 'tensor', hop).astype(F32)]
    ppermute x0 -> x4, waiting for transfers between devices: none -> 2.51 us  [the longest x3 2.51 us: per_device(): lax.ppermute(states, 'tensor', hop)]
    all_to_all x1, blocking collectives: 8.1 us -> 10.2 us  [per_device(): queries = lax.all_to_all(queries, 'tensor', 0, 0, tiled=True)]
  transfers between devices with their start and end apart: 7 -> 9, of which waited for: 7 -> 6; matrix products, arithmetic and copies ran while one was open for 2% -> 0% of each run, Pallas kernels for 0% -> 1%
where the time goes in v2:
time: 65.7 us; the launch traced here: 65.3 us
  blocking collectives  31.1 us (47%)
  starting transfers between devices  11.4 us (17%)
  Pallas kernels  9.5 us (14%)
  waiting for transfers between devices  7.27 us (11%)
  local copies, waits for them, and re-layouts  3.66 us (6%)
  other arithmetic  1.46 us (2%)
  between operations  0.84 us (1%)
    all_to_all x1, blocking collectives, per_device(): lax.all_to_all(part.reshape(shards * groups, wire_rows, chunk), ('seq', '...  10.9 us
    all_to_all x1, blocking collectives, per_device(): queries = lax.all_to_all(queries, 'tensor', 0, 0, tiled=True)  10.2 us
    all_to_all x1, blocking collectives, per_device(): partial = lax.all_to_all(partial, 'tensor', 0, 0, tiled=True)  10 us
    pallas_call x5, Pallas kernels, call(): pl.pallas_call(kernel, out_shape=out, in_specs=specs or [VMEM_SPEC] * len...  9.5 us
    ppermute x3, starting transfers between devices, per_device(): lax.ppermute(states, 'tensor', hop)  7.01 us
    ppermute x3, starting transfers between devices, per_device(): total = total + lax.ppermute(chip, 'tensor', hop).astype(F32)  3.88 us
    unnamed x36, local copies, waits for them, and re-layouts  3.64 us
    ppermute x3, waiting for transfers between devices, per_device(): total = total + lax.ppermute(chip, 'tensor', hop).astype(F32)  2.65 us
  transfers between devices with their start and end apart: 9, of which 6 were waited for; matrix products, arithmetic and copies ran while one was open for 0% of the time, Pallas kernels for 1%

profile of v2, /device:TPU:0, one launch (start us, length us, event | category | flops | bytes accessed | tf_op | source)
XLA Modules:
  0.0 65.3 jit_solution(8479649769856410858)
XLA Ops:
  0.6 3.1 %collective-permute-start = (bf16[2,2048]{1,0:T(2,128)(2,1)}, bf16[2,2048]{1,0:T(2,128)(2,1)S(1)}, u32[]{:S(2)}, u32[]{:S(2)}) collective-permute-start(bf16[2,2048]{1,0:T(2,128)(2,1)} %param.16), channel_id=1, source_target_pairs={{0,2},{1,3},{2,4},{3,5},{4,6},{5,7},{6,0},{7,1},{8,10},{9,11},{10,... | collective-permute-start | bytes 24584 | tf_op jit(solution)/shard_map/ppermute | solution.py:343
  3.7 2.6 %collective-permute-start.1 = (bf16[2,2048]{1,0:T(2,128)(2,1)}, bf16[2,2048]{1,0:T(2,128)(2,1)S(1)}, u32[]{:S(2)}, u32[]{:S(2)}) collective-permute-start(bf16[2,2048]{1,0:T(2,128)(2,1)} %param.16), channel_id=1, source_target_pairs={{0,4},{1,5},{2,6},{3,7},{4,0},{5,1},{6,2},{7,3},{8,12},{9,13},{10,... | collective-permute-start | bytes 24584 | tf_op jit(solution)/shard_map/ppermute | solution.py:343
  6.3 1.3 %collective-permute-start.2 = (bf16[2,2048]{1,0:T(2,128)(2,1)}, bf16[2,2048]{1,0:T(2,128)(2,1)S(1)}, u32[]{:S(2)}, u32[]{:S(2)}) collective-permute-start(bf16[2,2048]{1,0:T(2,128)(2,1)} %param.16), channel_id=1, source_target_pairs={{0,6},{1,7},{2,0},{3,1},{4,2},{5,3},{6,4},{7,5},{8,14},{9,15},{10,... | collective-permute-start | bytes 24584 | tf_op jit(solution)/shard_map/ppermute | solution.py:343
  7.6 0.0 collective-permute-done
  7.6 0.9 %collective-permute-done.1 = bf16[2,2048]{1,0:T(2,128)(2,1)S(1)} collective-permute-done((bf16[2,2048]{1,0:T(2,128)(2,1)}, bf16[2,2048]{1,0:T(2,128)(2,1)S(1)}, u32[]{:S(2)}, u32[]{:S(2)}) %collective-permute-start.1) | collective-permute-done | bytes 8224 | tf_op jit(solution)/shard_map/ppermute | solution.py:343
  8.6 1.6 %collective-permute-done.2 = bf16[2,2048]{1,0:T(2,128)(2,1)S(1)} collective-permute-done((bf16[2,2048]{1,0:T(2,128)(2,1)}, bf16[2,2048]{1,0:T(2,128)(2,1)S(1)}, u32[]{:S(2)}, u32[]{:S(2)}) %collective-permute-start.2) | collective-permute-done | bytes 8224 | tf_op jit(solution)/shard_map/ppermute | solution.py:343
  10.2 0.8 %pad_maximum_fusion.same_ref = bf16[4,2,2048]{2,1,0:T(2,128)(2,1)S(1)} fusion(bf16[1,2,2048]{2,1,0:T(2,128)(2,1)S(1)} %bitcast.23, bf16[1,2,2048]{2,1,0:T(2,128)(2,1)S(1)} %bitcast.22, bf16[1,2,2048]{2,1,0:T(2,128)(2,1)S(1)} %bitcast.21, bf16[1,2,2048]{2,1,0:T(2,128)(2,1)} %bitcast.20), kind=kLoop, calls=%fused_computation.3 | loop fusion | flops 49152 | bytes 65536 | tf_op jit(solution)/shard_map/stack | solution.py:343
  10.9 0.0 copy-start.1
  10.9 0.1 collective-permute-start.3
  11.0 0.0 copy-start.5
  11.0 0.8 %copy-done.5 = s32[2,1024]{1,0:T(2,128)S(1)} copy-done((s32[2,1024]{1,0:T(2,128)S(1)}, s32[2,1024]{1,0:T(2,128)}, u32[]{:S(2)}) %copy-start.5) | copy-done | bytes 8216
  11.9 0.7 %copy-done.6 = s32[2,1024]{1,0:T(2,128)S(1)} copy-done((s32[2,1024]{1,0:T(2,128)S(1)}, s32[2,1024]{1,0:T(2,128)}, u32[]{:S(2)}) %copy-start.6) | copy-done | bytes 8216
  12.6 0.7 %copy-done.7 = s32[16]{0:T(128)S(1)} copy-done((s32[16]{0:T(128)S(1)}, s32[16]{0:T(128)}, u32[]{:S(2)}) %copy-start.7) | copy-done | bytes 88
  13.2 0.7 %copy-done.8 = s32[16]{0:T(128)S(1)} copy-done((s32[16]{0:T(128)S(1)}, s32[16]{0:T(128)}, u32[]{:S(2)}) %copy-start.8) | copy-done | bytes 88
  13.9 0.7 %copy-done.9 = f32[1,128]{1,0:T(1,128)S(1)} copy-done((f32[1,128]{1,0:T(1,128)S(1)}, f32[1,128]{1,0:T(1,128)}, u32[]{:S(2)}) %copy-start.9) | copy-done | bytes 536
  14.5 0.6 prepare.1
  15.2 0.0 copy-done.10
  15.2 0.0 collective-permute-done.3.peer_ref
  15.2 0.0 copy-done.1
  15.3 0.0 slice-start.3
  15.3 0.0 slice-start.5
  15.3 0.0 copy-start.3
  15.3 0.0 copy-start.4
  15.3 1.4 %qkv.1 = (f32[8,8,128]{2,1,0:T(8,128)S(1)}, bf16[16,256]{1,0:T(8,128)(2,1)}, bf16[16,256]{1,0:T(8,128)(2,1)}, f32[8,8,128]{2,1,0:T(8,128)S(1)}, f32[16,1024]{1,0:T(8,128)S(1)}) custom-call(bf16[4,2,2048]{2,1,0:T(2,128)(2,1)S(1)} %pad_maximum_fusion.same_ref, bf16[4,2,2048]{2,1,0:T(2,128)(2,1)S(1)} %collective-permute-done.3.peer_ref, ...), custom_call_target="tpu_custom_call" | custom-call | flops 20000000000 | bytes 3248128 | tf_op jit(solution)/shard_map/qkv/pallas_call | solution.py:287
  16.7 10.2 %all_to_all.15.q_ref = f32[8,8,128]{2,1,0:T(8,128)S(1)} all-to-all(f32[8,8,128]{2,1,0:T(8,128)S(1)} %get-tuple-element.18), channel_id=1, replica_groups=mesh['seq'=4,'tensor'=8] {'tensor'}, dimensions={0} | all-to-all | bytes 65536 | tf_op jit(solution)/shard_map/all_to_all | solution.py:357
  26.9 0.0 slice-done.2
  27.0 0.0 slice-done.3
  27.0 0.0 copy-start.2
  27.0 0.0 slice-start
  27.0 4.5 %attention.1 = f32[4,8,8,128]{3,2,1,0:T(8,128)S(1)} custom-call(f32[8,8,128]{2,1,0:T(8,128)S(1)} %all_to_all.15.q_ref, bf16[2,2048,1024]{2,1,0:T(8,128)(2,1)S(1)} %bitcast.14, bf16[2,2048,1024]{2,1,0:T(8,128)(2,1)S(1)} %bitcast.16, bf16[2,4,2048]{2,1,0:T(4,128)(2,1)S(1)} %bitcast.18, bf16[2,4,2048]{2,1,0:T(4,128)(2,1)S(1)} %bitcast.19, ...), custom_call_target="tpu_custom_call" | custom-call | flops 10000000000 | bytes 16883712 | tf_op jit(solution)/shard_map/attention/pallas_call | solution.py:287
  31.6 10.9 %all_to_all.16 = f32[32,8,128]{2,1,0:T(8,128)S(1)} all-to-all(f32[32,8,128]{2,1,0:T(8,128)S(1)} %bitcast.12), channel_id=1, replica_groups=mesh['seq'=4,'tensor'=8] {'seq','tensor'}, dimensions={0} | all-to-all | bytes 262144 | tf_op jit(solution)/shard_map/all_to_all | solution.py:368
  42.5 0.0 copy-done.2
  42.5 0.3 merge.1
  42.8 0.4 collective-permute-start.4
  43.1 0.9 %collective-permute-done.4 = f32[16,1024]{1,0:T(8,128)S(1)} collective-permute-done((f32[16,1024]{1,0:T(8,128)S(1)}, f32[16,1024]{1,0:T(8,128)S(1)}, u32[]{:S(2)}, u32[]{:S(2)}) %collective-permute-start.4) | collective-permute-done | bytes 65568 | tf_op jit(solution)/shard_map/ppermute | solution.py:379
  44.1 0.6 collective-permute-start.5
  44.7 1.0 %collective-permute-start.6 = (bf16[16,1024]{1,0:T(8,128)(2,1)S(1)}, bf16[16,1024]{1,0:T(8,128)(2,1)S(1)}, u32[]{:S(2)}, u32[]{:S(2)}) collective-permute-start(bf16[16,1024]{1,0:T(8,128)(2,1)S(1)} %add_convert_fusion.1), channel_id=1, source_target_pairs={{0,4},{1,5},{2,6},{3,7},{4,0},{5,1},{6,2},{7,3},{8,12},{9,13},{10,... | collective-permute-start | bytes 98312 | tf_op jit(solution)/shard_map/ppermute | solution.py:382
  45.7 2.3 %collective-permute-start.7 = (bf16[16,1024]{1,0:T(8,128)(2,1)S(1)}, bf16[16,1024]{1,0:T(8,128)(2,1)S(1)}, u32[]{:S(2)}, u32[]{:S(2)}) collective-permute-start(bf16[16,1024]{1,0:T(8,128)(2,1)S(1)} %add_convert_fusion.1), channel_id=1, source_target_pairs={{0,6},{1,7},{2,0},{3,1},{4,2},{5,3},{6,4},{7,5},{8,14},{9,15},{10,... | collective-permute-start | bytes 98312 | tf_op jit(solution)/shard_map/ppermute | solution.py:382
  48.0 2.2 %collective-permute-done.5 = bf16[16,1024]{1,0:T(8,128)(2,1)S(1)} collective-permute-done((bf16[16,1024]{1,0:T(8,128)(2,1)S(1)}, bf16[16,1024]{1,0:T(8,128)(2,1)S(1)}, u32[]{:S(2)}, u32[]{:S(2)}) %collective-permute-start.5) | collective-permute-done | bytes 32800 | tf_op jit(solution)/shard_map/ppermute | solution.py:382
  50.2 0.5 collective-permute-done.6
  50.6 0.0 collective-permute-done.7
  50.7 0.1 collective-permute-start.8
  50.8 1.2 %collective-permute-done.8.other_ref = bf16[16,1024]{1,0:T(8,128)(2,1)S(1)} collective-permute-done((bf16[16,1024]{1,0:T(8,128)(2,1)S(1)}, bf16[16,1024]{1,0:T(8,128)(2,1)S(1)}, u32[]{:S(2)}, u32[]{:S(2)}) %collective-permute-start.8) | collective-permute-done | bytes 32800 | tf_op jit(solution)/shard_map/ppermute | solution.py:384
  51.9 0.0 slice-done
  52.0 2.6 %mlp.1 = (bf16[8,2,2048]{2,1,0:T(2,128)(2,1)S(1)}, f32[2,2048]{1,0:T(2,128)S(1)}) custom-call(bf16[16,1024]{1,0:T(8,128)(2,1)S(1)} %add_convert_fusion.mine_ref, bf16[16,1024]{1,0:T(8,128)(2,1)S(1)} %collective-permute-done.8.other_ref, bf16[1,2048]{1,0:T(2,128)(2,1)S(1)} %broadcast_in_dim.7.gain_ref, bf16[2048,2,1024]{2,1,0:T(2,128)(2,1)S(1)} %bitcast.10, ...), custom_call_target="tpu_custom_call" | custom-call | flops 201326592 | bytes 12652544 | tf_op jit(solution)/shard_map/mlp/pallas_call | solution.py:287
  54.6 10.0 %all_to_all.17 = bf16[8,2,2048]{2,1,0:T(2,128)(2,1)S(1)} all-to-all(bf16[8,2,2048]{2,1,0:T(2,128)(2,1)S(1)} %get-tuple-element.24), channel_id=1, replica_groups=mesh['seq'=4,'tensor'=8] {'tensor'}, dimensions={0} | all-to-all | bytes 131072 | tf_op jit(solution)/shard_map/all_to_all | solution.py:394
  64.6 0.1 convert_reduce_fusion
  64.7 0.6 add_convert_fusion.2
  (24 shorter events, 0.1 us)
Async XLA Ops:
  0.6 7.0 %collective-permute-start = (bf16[2,2048]{1,0:T(2,128)(2,1)}, bf16[2,2048]{1,0:T(2,128)(2,1)S(1)}, u32[]{:S(2)}, u32[]{:S(2)}) collective-permute-start(bf16[2,2048]{1,0:T(2,128)(2,1)} %param.16), channel_id=1, source_target_pairs={{0,2},{1,3},{2,4},{3,5},{4,6},{5,7},{6,0},{7,1},{8,10},{9,11},{10,... | collective-permute-start | bytes 24584 | tf_op jit(solution)/shard_map/ppermute | solution.py:343
  3.7 4.8 %collective-permute-start.1 = (bf16[2,2048]{1,0:T(2,128)(2,1)}, bf16[2,2048]{1,0:T(2,128)(2,1)S(1)}, u32[]{:S(2)}, u32[]{:S(2)}) collective-permute-start(bf16[2,2048]{1,0:T(2,128)(2,1)} %param.16), channel_id=1, source_target_pairs={{0,4},{1,5},{2,6},{3,7},{4,0},{5,1},{6,2},{7,3},{8,12},{9,13},{10,... | collective-permute-start | bytes 24584 | tf_op jit(solution)/shard_map/ppermute | solution.py:343
  6.3 3.9 %collective-permute-start.2 = (bf16[2,2048]{1,0:T(2,128)(2,1)}, bf16[2,2048]{1,0:T(2,128)(2,1)S(1)}, u32[]{:S(2)}, u32[]{:S(2)}) collective-permute-start(bf16[2,2048]{1,0:T(2,128)(2,1)} %param.16), channel_id=1, source_target_pairs={{0,6},{1,7},{2,0},{3,1},{4,2},{5,3},{6,4},{7,5},{8,14},{9,15},{10,... | collective-permute-start | bytes 24584 | tf_op jit(solution)/shard_map/ppermute | solution.py:343
  10.9 4.3 %copy-start.1 = (bf16[2048,3,256]{2,0,1:T(8,128)(2,1)S(1)}, bf16[2048,3,256]{2,0,1:T(8,128)(2,1)}, u32[]{:S(2)}) copy-start(bf16[2048,3,256]{2,0,1:T(8,128)(2,1)} %param.18) | copy-start | bytes 9437188
  10.9 4.3 %collective-permute-start.3 = (bf16[4,2,2048]{2,1,0:T(2,128)(2,1)S(1)}, bf16[4,2,2048]{2,1,0:T(2,128)(2,1)S(1)}, u32[]{:S(2)}, u32[]{:S(2)}) collective-permute-start(bf16[4,2,2048]{2,1,0:T(2,128)(2,1)S(1)} %pad_maximum_fusion.same_ref), channel_id=1, source_target_pairs={{0,1},{1,0},{2,3},{3,2},{4,5},{5,4},{6,7},{7,6},{8,9},{9,8},{10,11... | collective-permute-start | bytes 98312 | tf_op jit(solution)/shard_map/ppermute | solution.py:344
  11.0 0.8 %copy-start.5 = (s32[2,1024]{1,0:T(2,128)S(1)}, s32[2,1024]{1,0:T(2,128)}, u32[]{:S(2)}) copy-start(s32[2,1024]{1,0:T(2,128)} %mask_ref.1) | copy-start | bytes 24580
  11.9 0.7 %copy-start.6 = (s32[2,1024]{1,0:T(2,128)S(1)}, s32[2,1024]{1,0:T(2,128)}, u32[]{:S(2)}) copy-start(s32[2,1024]{1,0:T(2,128)} %slot_pos_ref.1) | copy-start | bytes 24580
  12.6 0.7 %copy-start.7 = (s32[16]{0:T(128)S(1)}, s32[16]{0:T(128)}, u32[]{:S(2)}) copy-start(s32[16]{0:T(128)} %len_ref.1) | copy-start | bytes 196
  13.2 0.7 %copy-start.8 = (s32[16]{0:T(128)S(1)}, s32[16]{0:T(128)}, u32[]{:S(2)}) copy-start(s32[16]{0:T(128)} %pos_ref.1) | copy-start | bytes 196
  13.9 0.7 %copy-start.9 = (f32[1,128]{1,0:T(1,128)S(1)}, f32[1,128]{1,0:T(1,128)}, u32[]{:S(2)}) copy-start(f32[1,128]{1,0:T(1,128)} %constant.4.clone.inverse_ref) | copy-start | bytes 1540
  14.5 0.7 %copy-start.10 = (bf16[2048]{0:T(1024)(128)(2,1)S(1)}, bf16[2048]{0:T(1024)(128)(2,1)}, u32[]{:S(2)}) copy-start(bf16[2048]{0:T(1024)(128)(2,1)} %param.17) | copy-start | bytes 12292
  14.5 12.4 %slice-start.2 = ((s8[8388608]{0:T(1024)(128)(4,1)}), s8[4194304]{0:T(1024)(128)(4,1)S(1)}, s32[]{:S(2)}) async-start(s8[8388608]{0:T(1024)(128)(4,1)} %bitcast.13), calls=%async_computation.5 | async-start | bytes 8388608
  14.5 12.4 %slice-start.4 = ((s8[8388608]{0:T(1024)(128)(4,1)}), s8[4194304]{0:T(1024)(128)(4,1)S(1)}, s32[]{:S(2)}) async-start(s8[8388608]{0:T(1024)(128)(4,1)} %bitcast.15), calls=%async_computation.7 | async-start | bytes 8388608
  15.3 11.7 %slice-start.3 = ((s8[8388608]{0:T(1024)(128)(4,1)}), s8[4194304]{0:T(1024)(128)(4,1)S(1)}, s32[]{:S(2)}) async-start(s8[8388608]{0:T(1024)(128)(4,1)} %bitcast.13), calls=%async_computation.6 | async-start | bytes 8388608
  15.3 11.7 %slice-start.5 = ((s8[8388608]{0:T(1024)(128)(4,1)}), s8[4194304]{0:T(1024)(128)(4,1)S(1)}, s32[]{:S(2)}) async-start(s8[8388608]{0:T(1024)(128)(4,1)} %bitcast.15), calls=%async_computation.8 | async-start | bytes 8388608
  15.3 11.7 %copy-start.3 = (bf16[2,2048,4]{1,2,0:T(4,128)(2,1)S(1)}, bf16[2,2048,4]{1,2,0:T(4,128)(2,1)}, u32[]{:S(2)}) copy-start(bf16[2,2048,4]{1,2,0:T(4,128)(2,1)} %param.25) | copy-start | bytes 98308
  15.3 11.7 %copy-start.4 = (bf16[2,2048,4]{1,2,0:T(4,128)(2,1)S(1)}, bf16[2,2048,4]{1,2,0:T(4,128)(2,1)}, u32[]{:S(2)}) copy-start(bf16[2,2048,4]{1,2,0:T(4,128)(2,1)} %param.26) | copy-start | bytes 98308
  27.0 15.5 %copy-start.2 = (bf16[256,2048]{1,0:T(8,128)(2,1)S(1)}, bf16[256,2048]{1,0:T(8,128)(2,1)}, u32[]{:S(2)}) copy-start(bf16[256,2048]{1,0:T(8,128)(2,1)} %w_ref.1) | copy-start | bytes 3145732
  27.0 24.9 %slice-start = ((s8[8388608]{0:T(1024)(128)(4,1)}), s8[4194304]{0:T(1024)(128)(4,1)S(1)}, s32[]{:S(2)}) async-start(s8[8388608]{0:T(1024)(128)(4,1)} %bitcast.9), calls=%async_computation.3 | async-start | bytes 8388608
  42.5 8.3 %copy-start.11 = (bf16[2048]{0:T(1024)(128)(2,1)S(1)}, bf16[2048]{0:T(1024)(128)(2,1)}, u32[]{:S(2)}) copy-start(bf16[2048]{0:T(1024)(128)(2,1)} %param.20) | copy-start | bytes 12292
  42.5 9.5 %slice-start.1 = ((s8[8388608]{0:T(1024)(128)(4,1)}), s8[4194304]{0:T(1024)(128)(4,1)S(1)}, s32[]{:S(2)}) async-start(s8[8388608]{0:T(1024)(128)(4,1)} %bitcast.9), calls=%async_computation.4 | async-start | bytes 8388608
  42.5 9.5 %copy-start = (bf16[1024,2048]{1,0:T(8,128)(2,1)S(1)}, bf16[1024,2048]{1,0:T(8,128)(2,1)}, u32[]{:S(2)}) copy-start(bf16[1024,2048]{1,0:T(8,128)(2,1)} %down_ref.1) | copy-start | bytes 12582916
  42.8 1.3 %collective-permute-start.4 = (f32[16,1024]{1,0:T(8,128)S(1)}, f32[16,1024]{1,0:T(8,128)S(1)}, u32[]{:S(2)}, u32[]{:S(2)}) collective-permute-start(f32[16,1024]{1,0:T(8,128)S(1)} %get-tuple-element.22), channel_id=1, source_target_pairs={{0,1},{1,0},{2,3},{3,2},{4,5},{5,4},{6,7},{7,6},{8,9},{9,8},{10,11... | collective-permute-start | bytes 196616 | tf_op jit(solution)/shard_map/ppermute | solution.py:379
  44.1 6.1 %collective-permute-start.5 = (bf16[16,1024]{1,0:T(8,128)(2,1)S(1)}, bf16[16,1024]{1,0:T(8,128)(2,1)S(1)}, u32[]{:S(2)}, u32[]{:S(2)}) collective-permute-start(bf16[16,1024]{1,0:T(8,128)(2,1)S(1)} %add_convert_fusion.1), channel_id=1, source_target_pairs={{0,2},{1,3},{2,4},{3,5},{4,6},{5,7},{6,0},{7,1},{8,10},{9,11},{10,... | collective-permute-start | bytes 98312 | tf_op jit(solution)/shard_map/ppermute | solution.py:382
  44.7 5.9 %collective-permute-start.6 = (bf16[16,1024]{1,0:T(8,128)(2,1)S(1)}, bf16[16,1024]{1,0:T(8,128)(2,1)S(1)}, u32[]{:S(2)}, u32[]{:S(2)}) collective-permute-start(bf16[16,1024]{1,0:T(8,128)(2,1)S(1)} %add_convert_fusion.1), channel_id=1, source_target_pairs={{0,4},{1,5},{2,6},{3,7},{4,0},{5,1},{6,2},{7,3},{8,12},{9,13},{10,... | collective-permute-start | bytes 98312 | tf_op jit(solution)/shard_map/ppermute | solution.py:382
  45.7 4.9 %collective-permute-start.7 = (bf16[16,1024]{1,0:T(8,128)(2,1)S(1)}, bf16[16,1024]{1,0:T(8,128)(2,1)S(1)}, u32[]{:S(2)}, u32[]{:S(2)}) collective-permute-start(bf16[16,1024]{1,0:T(8,128)(2,1)S(1)} %add_convert_fusion.1), channel_id=1, source_target_pairs={{0,6},{1,7},{2,0},{3,1},{4,2},{5,3},{6,4},{7,5},{8,14},{9,15},{10,... | collective-permute-start | bytes 98312 | tf_op jit(solution)/shard_map/ppermute | solution.py:382
  50.7 1.3 %collective-permute-start.8 = (bf16[16,1024]{1,0:T(8,128)(2,1)S(1)}, bf16[16,1024]{1,0:T(8,128)(2,1)S(1)}, u32[]{:S(2)}, u32[]{:S(2)}) collective-permute-start(bf16[16,1024]{1,0:T(8,128)(2,1)S(1)} %add_convert_fusion.mine_ref), channel_id=1, source_target_pairs={{0,1},{1,0},{2,3},{3,2},{4,5},{5,4},{6,7},{7,6},{8,9},{9,8},{10,11... | collective-permute-start | bytes 98312 | tf_op jit(solution)/shard_map/ppermute | solution.py:384

commit v3 on v2

--- a/solution.py
+++ b/solution.py
@@ -10,12 +10,12 @@
 
 HEAD_SIZE = 64
 WINDOW = 4096
+ROTARY_BASE = 130000.0
 NEG = -1e30
 LANE = 128
-HEADS_BLOCK = 8
 MIB = 2**20
 PREP_FLOPS = 20_000_000_000
-QKV_FLOPS = 20_000_000_000
+QKV_FLOPS = 2_000_000_000
 ATT_FLOPS = 10_000_000_000
 MERGE_FLOPS = 10_000_000_000
 
@@ -45,22 +45,54 @@
     return lane_chunk * rows + row
 
 
-def qkv_kernel(
+def query_kernel(rows, chips, *refs):
+    states, refs = refs[:chips], refs[chips:]
+    gain_ref, own_ref, peer_ref, cos_ref, sin_ref = refs[:5]
+    outs = refs[5:]
+    core = lax.axis_index("tensor") % 2
+    values = jnp.concatenate([ref[...].astype(F32) for ref in states], axis=0)
+    normed = normed_rows(values, gain_ref[...].astype(F32))
+    own = jnp.dot(normed, own_ref[...], preferred_element_type=F32)
+    peer = jnp.dot(normed, peer_ref[...], preferred_element_type=F32)
+    queries = jnp.concatenate(
+        [jnp.where(core == 0, own, peer), jnp.where(core == 0, peer, own)], axis=1
+    )
+    repeat = queries.shape[1] // cos_ref.shape[1]
+    cosine = jnp.concatenate([cos_ref[...]] * repeat, axis=1)
+    sine = jnp.concatenate([sin_ref[...]] * repeat, axis=1)
+    queries = (queries * cosine + swap_halves(queries) * sine).astype(BF16).astype(F32)
+    for step in range(chips):
+        first = (chips - step) % chips * rows
+        out = outs[step]
+        if rows * queries.shape[1] // LANE < out.shape[0]:
+            out[...] = jnp.zeros_like(out)
+        for c in range(queries.shape[1] // LANE):
+            at = slice(c * LANE, (c + 1) * LANE)
+            row = wire_row(rows, c, 0)
+            out[row : row + rows, :] = queries[first : first + rows, at]
+
+
+def new_token_kernel(
     rows,
+    len_ref,
+    pos_ref,
+    mask_ref,
+    slot_pos_ref,
     same_ref,
     peer_ref,
     gain_ref,
     w_ref,
     cos_ref,
     sin_ref,
-    q_ref,
     k_ref,
     v_ref,
     new_ref,
     side_ref,
+    live_ref,
     by_ref,
     flat_ref,
 ):
+    mark_live(len_ref, pos_ref, mask_ref, slot_pos_ref, live_ref)
     lanes = w_ref.shape[2]
     core = lax.axis_index("tensor") % 2
     chip = lax.axis_index("tensor") // 2
@@ -75,8 +107,9 @@
     width = side_ref.shape[1]
     side_ref[...] = flat_ref[:, pl.ds(pl.multiple_of(core * width, LANE), width)]
     normed = normed_rows(values, gain_ref[...].astype(F32))
-    cosine = cos_ref[...]
-    sine = sin_ref[...]
+    repeat = lanes // cos_ref.shape[1]
+    cosine = jnp.concatenate([cos_ref[...]] * repeat, axis=1)
+    sine = jnp.concatenate([sin_ref[...]] * repeat, axis=1)
 
     def project(part):
         return jnp.dot(normed, w_ref[part], preferred_element_type=F32)
@@ -100,52 +133,45 @@
         precision=lax.Precision.HIGHEST,
     ) * (HEAD_SIZE**-0.5)
     values = values.astype(F32)
-    groups, half, chunk = q_ref.shape[0], q_ref.shape[1] // 2, q_ref.shape[2]
-    q_ref[...] = jnp.zeros_like(q_ref)
+    groups, half, chunk = new_ref.shape[0], new_ref.shape[1] // 2, new_ref.shape[2]
     for group in range(groups):
         mine = slice(group * rows, (group + 1) * rows)
         for c in range(lanes // chunk):
             at = slice(c * chunk, (c + 1) * chunk)
             row = wire_row(rows, c, 0)
-            q_ref[group, row : row + rows, :] = queries[mine, at]
             new_ref[group, row : row + rows, :] = values[mine, at]
             new_ref[group, half + row : half + row + rows, :] = score[mine, at]
 
 
-def attention_kernel(
-    lanes,
-    q_ref,
-    k_ref,
-    v_ref,
-    sink_k_ref,
-    sink_v_ref,
-    live_ref,
-    out_ref,
-):
+def attention_kernel(lanes, chips, *refs):
+    queries, refs = refs[:chips], refs[chips:]
+    k_ref, v_ref, sink_k_ref, sink_v_ref, live_ref, out_ref = refs
     rows, features, slots = k_ref.shape
     sinks = sink_k_ref.shape[1]
     copies = out_ref.shape[0]
     half, chunk = out_ref.shape[2] // 2, out_ref.shape[3]
-    block = HEADS_BLOCK * HEAD_SIZE
+    block = 2 * lanes
+    heads = max(8, block // HEAD_SIZE)
     seq_index = lax.axis_index("seq")
-    head = lax.broadcasted_iota(jnp.int32, (HEADS_BLOCK, block), 0)
-    own = head == lax.broadcasted_iota(jnp.int32, (HEADS_BLOCK, block), 1) // HEAD_SIZE
+    chip = lax.axis_index("tensor") // 2
+    head = lax.broadcasted_iota(jnp.int32, (heads, block), 0)
+    own = head == lax.broadcasted_iota(jnp.int32, (heads, block), 1) // HEAD_SIZE
     scale = HEAD_SIZE**-0.5
     for r in range(rows):
-        live = jnp.broadcast_to(live_ref[r : r + 1, :], (HEADS_BLOCK, slots)) == 1
-        sink_keys = sink_k_ref[r].astype(F32)
-        sink_values = sink_v_ref[r].astype(F32)
-        for b in range(features // block):
-            here = slice(b * block, (b + 1) * block)
-            chunks = [divmod(b * (block // chunk) + f, lanes // chunk) for f in range(block // chunk)]
+        live = jnp.broadcast_to(live_ref[r : r + 1, :], (heads, slots)) == 1
+        for step in range(chips):
+            source = lax.rem(chip + chips - step, chips)
+            here = pl.ds(pl.multiple_of(source * block, block), block)
+            sink_keys = sink_k_ref[r, :, here].astype(F32)
+            sink_values = sink_v_ref[r, :, here].astype(F32)
             query = jnp.concatenate(
                 [
-                    q_ref[t, wire_row(rows, c, r) : wire_row(rows, c, r) + 1, :]
-                    for t, c in chunks
+                    queries[step][wire_row(rows, c, r) : wire_row(rows, c, r) + 1, :]
+                    for c in range(block // LANE)
                 ],
                 axis=1,
             )
-            query = jnp.where(own, jnp.broadcast_to(query, (HEADS_BLOCK, block)), 0.0)
+            query = jnp.where(own, jnp.broadcast_to(query, (heads, block)), 0.0)
             score = (
                 jnp.dot(query.astype(BF16), k_ref[r, here, :], preferred_element_type=F32) * scale
             )
@@ -153,7 +179,7 @@
             top = jnp.max(score, axis=1, keepdims=True)
             sink_score = []
             for i in range(sinks):
-                one = jnp.sum(query * sink_keys[i : i + 1, here], axis=1, keepdims=True) * scale
+                one = jnp.sum(query * sink_keys[i : i + 1, :], axis=1, keepdims=True) * scale
                 one = jnp.where(seq_index == 0, one, NEG)
                 sink_score.append(one)
                 top = jnp.maximum(top, one)
@@ -168,18 +194,19 @@
             for i in range(sinks):
                 one = jnp.where(seq_index == 0, jnp.exp(sink_score[i] - top), 0.0)
                 total = total + one
-                mixture = mixture + one.astype(BF16).astype(F32) * sink_values[i : i + 1, here]
+                mixture = mixture + one.astype(BF16).astype(F32) * sink_values[i : i + 1, :]
             some = total > 0.0
             level = jnp.where(some, top + jnp.log(jnp.where(some, total, 1.0)), NEG)
             mixture = mixture / jnp.where(some, total, 1.0)
             mixture = jnp.sum(jnp.where(own, mixture, 0.0), axis=0, keepdims=True)
             level = jnp.sum(jnp.where(own, level, 0.0), axis=0, keepdims=True)
-            for f, (t, c) in enumerate(chunks):
+            for f in range(block // chunk):
+                t, c = divmod(f, lanes // chunk)
                 row = wire_row(rows, c, r)
                 at = slice(f * chunk, (f + 1) * chunk)
                 for copy in range(copies):
-                    out_ref[copy, t, row : row + 1, :] = mixture[:, at]
-                    out_ref[copy, t, half + row : half + row + 1, :] = level[:, at]
+                    out_ref[copy, 2 * source + t, row : row + 1, :] = mixture[:, at]
+                    out_ref[copy, 2 * source + t, half + row : half + row + 1, :] = level[:, at]
 
 
 def merge_kernel(rows, part_ref, new_ref, w_ref, mine_ref, other_ref, rows_ref, full_ref):
@@ -254,23 +281,39 @@
         out_ref[group] = out[group * rows : (group + 1) * rows, :].astype(BF16)
 
 
-def prepare_kernel(
-    len_ref, pos_ref, inverse_ref, mask_ref, slot_pos_ref, cos_ref, sin_ref, live_ref
-):
-    batch, width = cos_ref.shape
-    wide = inverse_ref.shape[1]
-    row = lax.broadcasted_iota(jnp.int32, (batch, wide), 0)
-    position = jnp.zeros((batch, wide), F32)
-    for i in range(batch):
-        position = jnp.where(row == i, pos_ref[i].astype(F32), position)
-    angle = position * inverse_ref[...]
-    cosine = jnp.cos(angle)
-    sine = jnp.sin(angle)
-    lane = lax.broadcasted_iota(jnp.int32, (batch, wide), 1)
-    sine = jnp.where(lane % HEAD_SIZE < HEAD_SIZE // 2, -sine, sine)
-    for start in range(0, width, wide):
-        cos_ref[:, start : start + wide] = cosine
-        sin_ref[:, start : start + wide] = sine
+def prepare_kernel(rows, pos_ref, cos_ref, sin_ref, query_cos_ref, query_sin_ref):
+    core = lax.axis_index("tensor") % 2
+    chip = lax.axis_index("tensor") // 2
+    chips = query_cos_ref.shape[0] // rows
+    wide = cos_ref.shape[1]
+    half = HEAD_SIZE // 2
+    pair = lax.broadcasted_iota(jnp.int32, (1, wide), 1) % half
+    inverse = jnp.zeros((1, wide), F32)
+    for i in range(half):
+        inverse = jnp.where(pair == i, np.float32(ROTARY_BASE ** (-2 * i / HEAD_SIZE)), inverse)
+
+    def turn(positions, to_cos, to_sin):
+        shape = to_cos.shape
+        row = lax.broadcasted_iota(jnp.int32, shape, 0)
+        position = jnp.zeros(shape, F32)
+        for i, one in enumerate(positions):
+            position = jnp.where(row == i, one.astype(F32), position)
+        angle = position * inverse
+        sine = jnp.sin(angle)
+        lane = lax.broadcasted_iota(jnp.int32, shape, 1)
+        to_cos[...] = jnp.cos(angle)
+        to_sin[...] = jnp.where(lane % HEAD_SIZE < half, -sine, sine)
+
+    turn([pos_ref[i] for i in range(cos_ref.shape[0])], cos_ref, sin_ref)
+    sources = [2 * lax.rem(chip + chips - step, chips) + core for step in range(chips)]
+    turn(
+        [pos_ref[source * rows + r] for source in sources for r in range(rows)],
+        query_cos_ref,
+        query_sin_ref,
+    )
+
+
+def mark_live(len_ref, pos_ref, mask_ref, slot_pos_ref, live_ref):
     rows, slots = mask_ref.shape
     slot = lax.axis_index("seq") * slots + lax.broadcasted_iota(jnp.int32, (1, slots), 1)
     first_row = lax.axis_index("tensor") * rows
@@ -326,41 +369,55 @@
     chunk = min(lanes, LANE)
     wire_rows = max(8, 2 * rows * lanes // chunk)
 
-    half = HEAD_SIZE // 2
-    inverse = np.exp(-np.log(130000.0) * np.arange(half) * (2.0 / HEAD_SIZE))
-    inverse = jnp.asarray(np.tile(inverse, 2 * chunk // HEAD_SIZE)[None], F32)
-    turn = sds((batch, lanes), F32)
-    cosine, sine, live = call(
-        prepare_kernel,
-        (turn, turn, sds(slot_mask.shape, jnp.int32)),
-        (cache_len, new_pos, inverse, slot_mask, slot_pos),
-        specs=[SMEM_SPEC] * 2 + [VMEM_SPEC] * 3,
+    chips = groups // 2
+    turn = sds((batch, chunk), F32)
+    query_turn = sds((batch // 2, chunk), F32)
+    cosine, sine, query_cos, query_sin = call(
+        functools.partial(prepare_kernel, rows),
+        (turn, turn, query_turn, query_turn),
+        (new_pos,),
+        specs=[SMEM_SPEC],
         name="prepare",
         flops=PREP_FLOPS,
     )
     across = [(i, i ^ 1) for i in range(groups)]
     hops = [[(i, (i + step) % groups) for i in range(groups)] for step in range(2, groups, 2)]
-    same = jnp.stack([states] + [lax.ppermute(states, "tensor", hop) for hop in hops])
+    column = [states] + [lax.ppermute(states, "tensor", hop) for hop in hops]
+    w_qkv = jnp.transpose(w_qkv, (1, 0, 2))
+    w_query = w_qkv[0]
+    w_query_peer = lax.ppermute(w_query, "tensor", across)
+    query_wire = sds((max(8, 2 * rows * lanes // LANE), LANE), F32)
+    queries = call(
+        functools.partial(query_kernel, rows, chips),
+        (query_wire,) * chips,
+        (*column, attn_gain[None], w_query, w_query_peer, query_cos, query_sin),
+        name="query",
+        flops=QKV_FLOPS,
+    )
+    queries = [queries[0]] + [
+        lax.ppermute(query, "tensor", hop) for query, hop in zip(queries[1:], hops)
+    ]
+    same = jnp.stack(column)
     peer = lax.ppermute(same, "tensor", across)
-    w_qkv = jnp.transpose(w_qkv, (1, 0, 2))
     side = sds((batch, width // 2), F32)
     wire = sds((groups, wire_rows, chunk), F32)
     flat = sds((batch, lanes), BF16)
-    queries, new_keys, new_values, new_part, own_side = call(
-        functools.partial(qkv_kernel, rows),
-        (wire, flat, flat, wire, side),
-        (same, peer, attn_gain[None], w_qkv, cosine, sine),
+    new_keys, new_values, new_part, own_side, live = call(
+        functools.partial(new_token_kernel, rows),
+        (flat, flat, wire, side, sds(slot_mask.shape, jnp.int32)),
+        (cache_len, new_pos, slot_mask, slot_pos, same, peer, attn_gain[None], w_qkv, cosine, sine),
+        specs=[SMEM_SPEC] * 2 + [VMEM_SPEC] * 8,
         scratch=[pltpu.VMEM((groups, 8, width), F32), pltpu.VMEM((batch, width), F32)],
-        name="qkv",
+        name="new_token",
         flops=QKV_FLOPS,
     )
-    queries = lax.all_to_all(queries, "tensor", 0, 0, tiled=True)
+    queries, new_part = lax.optimization_barrier((queries, new_part))
     sink_keys = jnp.transpose(sink_keys, (0, 2, 1))
     sink_values = jnp.transpose(sink_values, (0, 2, 1))
     part = call(
-        functools.partial(attention_kernel, lanes),
+        functools.partial(attention_kernel, lanes, chips),
         sds((shards, groups, wire_rows, chunk), F32),
-        (queries, key_cache, value_cache, sink_keys, sink_values, live),
+        (*queries, key_cache, value_cache, sink_keys, sink_values, live),
         limit=8,
         name="attention",
         flops=ATT_FLOPS,

time: 65.7 us -> 61.1 us (0.930)
  blocking collectives: 31.1 us -> 21.8 us
  starting transfers between devices: 11.4 us -> 15 us
  Pallas kernels: 9.5 us -> 10.6 us
  waiting for transfers between devices: 7.27 us -> 7.96 us
  other arithmetic: 1.46 us -> 0.77 us
    all_to_all x1 -> x0, blocking collectives: 10.2 us -> none  [per_device(): queries = lax.all_to_all(queries, 'tensor', 0, 0, tiled=True)]
    ppermute x3 -> x7, starting transfers between devices: 7.01 us -> 11 us  [the longest x3 7.01 us: per_device(): column = [states] + [lax.ppermute(states, 'tensor', hop) for hop in hops]]
    ppermute x3, waiting for transfers between devices: 2.65 us -> 5.71 us  [per_device(): total = total + lax.ppermute(chip, 'tensor', hop).astype(F32)]
    all_to_all x1, blocking collectives: 10.9 us -> 13.5 us  [per_device(): lax.all_to_all(part.reshape(shards * groups, wire_rows, chunk), ('seq', '...]
    ppermute x3 -> x7, waiting for transfers between devices: 2.51 us -> 0.14 us  [the longest x3 0.13 us: per_device(): lax.ppermute(query, 'tensor', hop)]
    all_to_all x1, blocking collectives: 10 us -> 8.29 us  [per_device(): partial = lax.all_to_all(partial, 'tensor', 0, 0, tiled=True)]
    squeeze x0 -> x1, local copies, waits for them, and re-layouts: none -> 1.44 us  [per_device(): w_query = w_qkv[0]]
    unnamed x36 -> x38, local copies, waits for them, and re-layouts: 3.64 us -> 2.41 us
  transfers between devices with their start and end apart: 9 -> 13, of which waited for: 6 -> 5; matrix products, arithmetic and copies ran while one was open for 0% -> 2% of each run, Pallas kernels for 1% -> 5%
where the time goes in v3:
time: 61.1 us; the launch traced here: 60.9 us
  blocking collectives  21.8 us (36%)
  starting transfers between devices  15 us (25%)
  Pallas kernels  10.6 us (17%)
  waiting for transfers between devices  7.96 us (13%)
  local copies, waits for them, and re-layouts  3.87 us (6%)
  between operations  0.92 us (2%)
  other arithmetic  0.77 us (1%)
    all_to_all x1, blocking collectives, per_device(): lax.all_to_all(part.reshape(shards * groups, wire_rows, chunk), ('seq', '...  13.5 us
    pallas_call x6, Pallas kernels, call(): pl.pallas_call(kernel, out_shape=out, in_specs=specs or [VMEM_SPEC] * len...  10.6 us
    all_to_all x1, blocking collectives, per_device(): partial = lax.all_to_all(partial, 'tensor', 0, 0, tiled=True)  8.29 us
    ppermute x3, starting transfers between devices, per_device(): column = [states] + [lax.ppermute(states, 'tensor', hop) for hop in hops]  7.01 us
    ppermute x3, waiting for transfers between devices, per_device(): total = total + lax.ppermute(chip, 'tensor', hop).astype(F32)  5.71 us
    ppermute x3, starting transfers between devices, per_device(): lax.ppermute(query, 'tensor', hop)  3.88 us
    ppermute x3, starting transfers between devices, per_device(): total = total + lax.ppermute(chip, 'tensor', hop).astype(F32)  3.01 us
    unnamed x38, local copies, waits for them, and re-layouts  2.41 us
  transfers between devices with their start and end apart: 13, of which 5 were waited for; matrix products, arithmetic and copies ran while one was open for 2% of the time, Pallas kernels for 5%

profile of v3, /device:TPU:0, one launch (start us, length us, event | category | flops | bytes accessed | tf_op | source)
XLA Modules:
  0.0 60.9 jit_solution(3499791098341063371)
XLA Ops:
  0.6 3.1 %collective-permute-start = (bf16[2,2048]{1,0:T(2,128)(2,1)}, bf16[2,2048]{1,0:T(2,128)(2,1)S(1)}, u32[]{:S(2)}, u32[]{:S(2)}) collective-permute-start(bf16[2,2048]{1,0:T(2,128)(2,1)} %refs_0_.1), channel_id=1, source_target_pairs={{0,2},{1,3},{2,4},{3,5},{4,6},{5,7},{6,0},{7,1},{8,10},{9,11},{10,... | collective-permute-start | bytes 24584 | tf_op jit(solution)/shard_map/ppermute | solution.py:385
  3.7 2.6 %collective-permute-start.1 = (bf16[2,2048]{1,0:T(2,128)(2,1)}, bf16[2,2048]{1,0:T(2,128)(2,1)S(1)}, u32[]{:S(2)}, u32[]{:S(2)}) collective-permute-start(bf16[2,2048]{1,0:T(2,128)(2,1)} %refs_0_.1), channel_id=1, source_target_pairs={{0,4},{1,5},{2,6},{3,7},{4,0},{5,1},{6,2},{7,3},{8,12},{9,13},{10,... | collective-permute-start | bytes 24584 | tf_op jit(solution)/shard_map/ppermute | solution.py:385
  6.3 1.3 %collective-permute-start.2 = (bf16[2,2048]{1,0:T(2,128)(2,1)}, bf16[2,2048]{1,0:T(2,128)(2,1)S(1)}, u32[]{:S(2)}, u32[]{:S(2)}) collective-permute-start(bf16[2,2048]{1,0:T(2,128)(2,1)} %refs_0_.1), channel_id=1, source_target_pairs={{0,6},{1,7},{2,0},{3,1},{4,2},{5,3},{6,4},{7,5},{8,14},{9,15},{10,... | collective-permute-start | bytes 24584 | tf_op jit(solution)/shard_map/ppermute | solution.py:385
  7.6 1.4 %slice_bitcast_fusion.refs_5_ = bf16[2048,256]{1,0:T(8,128)(2,1)S(1)} fusion(bf16[3,2048,256]{2,1,0:T(8,128)(2,1)} %bitcast.13), kind=kLoop, calls=%fused_computation | loop fusion | bytes 2097152 | tf_op jit(solution)/shard_map/squeeze | solution.py:387
  9.1 0.0 copy-start.2
  9.1 0.0 copy-start.1
  9.1 0.0 copy-start.6
  9.1 0.0 copy-start.7
  9.1 0.0 copy-start.8
  9.2 0.0 slice-start.3
  9.2 0.0 slice-start.5
  9.2 0.1 collective-permute-start.4
  9.3 0.0 copy-start.9
  9.3 1.4 %copy-done.9 = s32[16]{0:T(128)S(1)} copy-done((s32[16]{0:T(128)S(1)}, s32[16]{0:T(128)}, u32[]{:S(2)}) %copy-start.9) | copy-done | bytes 88
  10.7 0.6 %prepare.1 = (f32[16,128]{1,0:T(8,128)S(1)}, f32[16,128]{1,0:T(8,128)S(1)}, f32[8,128]{1,0:T(8,128)S(1)}, f32[8,128]{1,0:T(8,128)S(1)}) custom-call(s32[16]{0:T(128)S(1)} %copy-done.9), custom_call_target="tpu_custom_call" | custom-call | flops 20000000000 | bytes 64 | tf_op jit(solution)/shard_map/prepare/pallas_call | solution.py:330
  11.3 0.9 %copy-done.11 = bf16[2048]{0:T(1024)(128)(2,1)S(1)} copy-done((bf16[2048]{0:T(1024)(128)(2,1)S(1)}, bf16[2048]{0:T(1024)(128)(2,1)}, u32[]{:S(2)}) %copy-start.11) | copy-done | bytes 4120
  12.2 0.0 collective-permute-done.refs_1_
  12.2 0.0 collective-permute-done.1.refs_2_
  12.3 0.0 collective-permute-done.2.refs_3_
  12.3 0.1 pad_maximum_fusion.same_ref
  12.3 0.6 collective-permute-start.3
  12.9 0.0 collective-permute-done.4.refs_6_
  12.9 0.6 query.1
  13.5 0.7 %collective-permute-start.5 = (f32[8,128]{1,0:T(8,128)S(1)}, f32[8,128]{1,0:T(8,128)S(1)}, u32[]{:S(2)}, u32[]{:S(2)}) collective-permute-start(f32[8,128]{1,0:T(8,128)S(1)} %get-tuple-element.31), channel_id=1, source_target_pairs={{0,2},{1,3},{2,4},{3,5},{4,6},{5,7},{6,0},{7,1},{8,10},{9,11},{10,... | collective-permute-start | bytes 12296 | tf_op jit(solution)/shard_map/ppermute | solution.py:398
  14.2 0.4 collective-permute-start.6
  14.6 2.7 %collective-permute-start.7 = (f32[8,128]{1,0:T(8,128)S(1)}, f32[8,128]{1,0:T(8,128)S(1)}, u32[]{:S(2)}, u32[]{:S(2)}) collective-permute-start(f32[8,128]{1,0:T(8,128)S(1)} %get-tuple-element.33), channel_id=1, source_target_pairs={{0,6},{1,7},{2,0},{3,1},{4,2},{5,3},{6,4},{7,5},{8,14},{9,15},{10,... | collective-permute-start | bytes 12296 | tf_op jit(solution)/shard_map/ppermute | solution.py:398
  17.4 0.0 collective-permute-done.3.peer_ref
  17.4 2.0 %new_token.1 = (bf16[16,256]{1,0:T(8,128)(2,1)}, bf16[16,256]{1,0:T(8,128)(2,1)}, f32[8,8,128]{2,1,0:T(8,128)S(1)}, f32[16,1024]{1,0:T(8,128)S(1)}, s32[2,1024]{1,0:T(2,128)S(1)}) custom-call(s32[16]{0:T(128)S(1)} %copy-done.8, s32[16]{0:T(128)S(1)} %copy-done.10, s32[2,1024]{1,0:T(2,128)S(1)} %copy-done.6, s32[2,1024]{1,0:T(2,128)S(1)} %copy-done.7, ...), custom_call_target="tpu_custom_call" | custom-call | flops 2000000000 | bytes 3248256 | tf_op jit(solution)/shard_map/new_token/pallas_call | solution.py:330
  19.4 0.0 collective-permute-done.5.refs_1_
  19.4 0.0 collective-permute-done.6.refs_2_
  19.4 0.1 collective-permute-done.7.refs_3_
  19.6 0.0 copy-start.3
  19.6 0.0 slice-start
  19.6 4.6 %attention.1 = f32[4,8,8,128]{3,2,1,0:T(8,128)S(1)} custom-call(f32[8,128]{1,0:T(8,128)S(1)} %get-tuple-element.35.refs_0_, f32[8,128]{1,0:T(8,128)S(1)} %collective-permute-done.5.refs_1_, f32[8,128]{1,0:T(8,128)S(1)} %collective-permute-done.6.refs_2_, f32[8,128]{1,0:T(8,128)S(1)} %collective-permute-done.7.refs_3_, bf16[2,2048,1024]{2,1,0:T(8,128)(2,1)S(1)} %bitcast.22, ...), custom_call_target="tpu_custom_call" | custom-call | flops 10000000000 | bytes 16867328 | tf_op jit(solution)/shard_map/attention/pallas_call | solution.py:330
  24.1 13.5 %all_to_all.10 = f32[32,8,128]{2,1,0:T(8,128)S(1)} all-to-all(f32[32,8,128]{2,1,0:T(8,128)S(1)} %bitcast.15), channel_id=1, replica_groups=mesh['seq'=4,'tensor'=8] {'seq','tensor'}, dimensions={0} | all-to-all | bytes 262144 | tf_op jit(solution)/shard_map/all_to_all | solution.py:425
  37.6 0.3 merge.1
  37.9 0.4 collective-permute-start.8
  38.3 0.9 %collective-permute-done.8 = f32[16,1024]{1,0:T(8,128)S(1)} collective-permute-done((f32[16,1024]{1,0:T(8,128)S(1)}, f32[16,1024]{1,0:T(8,128)S(1)}, u32[]{:S(2)}, u32[]{:S(2)}) %collective-permute-start.8) | collective-permute-done | bytes 65568 | tf_op jit(solution)/shard_map/ppermute | solution.py:436
  39.3 0.5 collective-permute-start.10
  39.7 2.6 %collective-permute-start.11 = (bf16[16,1024]{1,0:T(8,128)(2,1)S(1)}, bf16[16,1024]{1,0:T(8,128)(2,1)S(1)}, u32[]{:S(2)}, u32[]{:S(2)}) collective-permute-start(bf16[16,1024]{1,0:T(8,128)(2,1)S(1)} %add_convert_fusion.1), channel_id=1, source_target_pairs={{0,6},{1,7},{2,0},{3,1},{4,2},{5,3},{6,4},{7,5},{8,14},{9,15},{10,... | collective-permute-start | bytes 98312 | tf_op jit(solution)/shard_map/ppermute | solution.py:439
  42.3 2.5 %collective-permute-done.10 = bf16[16,1024]{1,0:T(8,128)(2,1)S(1)} collective-permute-done((bf16[16,1024]{1,0:T(8,128)(2,1)S(1)}, bf16[16,1024]{1,0:T(8,128)(2,1)S(1)}, u32[]{:S(2)}, u32[]{:S(2)}) %collective-permute-start.10) | collective-permute-done | bytes 32800 | tf_op jit(solution)/shard_map/ppermute | solution.py:439
  44.8 3.2 %collective-permute-done.9 = bf16[16,1024]{1,0:T(8,128)(2,1)S(1)} collective-permute-done((bf16[16,1024]{1,0:T(8,128)(2,1)S(1)}, bf16[16,1024]{1,0:T(8,128)(2,1)S(1)}, u32[]{:S(2)}, u32[]{:S(2)}) %collective-permute-start.9) | collective-permute-done | bytes 32800 | tf_op jit(solution)/shard_map/ppermute | solution.py:439
  48.0 0.1 collective-permute-start.12
  48.1 1.2 %collective-permute-done.12.other_ref = bf16[16,1024]{1,0:T(8,128)(2,1)S(1)} collective-permute-done((bf16[16,1024]{1,0:T(8,128)(2,1)S(1)}, bf16[16,1024]{1,0:T(8,128)(2,1)S(1)}, u32[]{:S(2)}, u32[]{:S(2)}) %collective-permute-start.12) | collective-permute-done | bytes 32800 | tf_op jit(solution)/shard_map/ppermute | solution.py:441
  49.3 2.6 %mlp.1 = (bf16[8,2,2048]{2,1,0:T(2,128)(2,1)S(1)}, f32[2,2048]{1,0:T(2,128)S(1)}) custom-call(bf16[16,1024]{1,0:T(8,128)(2,1)S(1)} %add_convert_fusion.mine_ref, bf16[16,1024]{1,0:T(8,128)(2,1)S(1)} %collective-permute-done.12.other_ref, bf16[1,2048]{1,0:T(2,128)(2,1)S(1)} %broadcast_in_dim.8.gain_ref, bf16[2048,2,1024]{2,1,0:T(2,128)(2,1)S(1)} %bitcast.12, ...), custom_call_target="tpu_custom_call" | custom-call | flops 201326592 | bytes 12652544 | tf_op jit(solution)/shard_map/mlp/pallas_call | solution.py:330
  51.9 8.3 %all_to_all.11 = bf16[8,2,2048]{2,1,0:T(2,128)(2,1)S(1)} all-to-all(bf16[8,2,2048]{2,1,0:T(2,128)(2,1)S(1)} %get-tuple-element.44), channel_id=1, replica_groups=mesh['seq'=4,'tensor'=8] {'tensor'}, dimensions={0} | all-to-all | bytes 131072 | tf_op jit(solution)/shard_map/all_to_all | solution.py:451
  60.2 0.1 convert_reduce_fusion
  60.3 0.6 add_convert_fusion.2
  (35 shorter events, 0.1 us)
Async XLA Ops:
  0.6 11.6 %collective-permute-start = (bf16[2,2048]{1,0:T(2,128)(2,1)}, bf16[2,2048]{1,0:T(2,128)(2,1)S(1)}, u32[]{:S(2)}, u32[]{:S(2)}) collective-permute-start(bf16[2,2048]{1,0:T(2,128)(2,1)} %refs_0_.1), channel_id=1, source_target_pairs={{0,2},{1,3},{2,4},{3,5},{4,6},{5,7},{6,0},{7,1},{8,10},{9,11},{10,... | collective-permute-start | bytes 24584 | tf_op jit(solution)/shard_map/ppermute | solution.py:385
  3.7 8.5 %collective-permute-start.1 = (bf16[2,2048]{1,0:T(2,128)(2,1)}, bf16[2,2048]{1,0:T(2,128)(2,1)S(1)}, u32[]{:S(2)}, u32[]{:S(2)}) collective-permute-start(bf16[2,2048]{1,0:T(2,128)(2,1)} %refs_0_.1), channel_id=1, source_target_pairs={{0,4},{1,5},{2,6},{3,7},{4,0},{5,1},{6,2},{7,3},{8,12},{9,13},{10,... | collective-permute-start | bytes 24584 | tf_op jit(solution)/shard_map/ppermute | solution.py:385
  6.3 6.0 %collective-permute-start.2 = (bf16[2,2048]{1,0:T(2,128)(2,1)}, bf16[2,2048]{1,0:T(2,128)(2,1)S(1)}, u32[]{:S(2)}, u32[]{:S(2)}) collective-permute-start(bf16[2,2048]{1,0:T(2,128)(2,1)} %refs_0_.1), channel_id=1, source_target_pairs={{0,6},{1,7},{2,0},{3,1},{4,2},{5,3},{6,4},{7,5},{8,14},{9,15},{10,... | collective-permute-start | bytes 24584 | tf_op jit(solution)/shard_map/ppermute | solution.py:385
  7.6 11.9 %slice-start.2 = ((s8[8388608]{0:T(1024)(128)(4,1)}), s8[4194304]{0:T(1024)(128)(4,1)S(1)}, s32[]{:S(2)}) async-start(s8[8388608]{0:T(1024)(128)(4,1)} %bitcast.21), calls=%async_computation.4 | async-start | bytes 8388608
  7.6 11.9 %slice-start.4 = ((s8[8388608]{0:T(1024)(128)(4,1)}), s8[4194304]{0:T(1024)(128)(4,1)S(1)}, s32[]{:S(2)}) async-start(s8[8388608]{0:T(1024)(128)(4,1)} %bitcast.23), calls=%async_computation.6 | async-start | bytes 8388608
  9.1 3.2 %copy-start.2 = (bf16[2,2048]{1,0:T(2,128)(2,1)S(1)}, bf16[2,2048]{1,0:T(2,128)(2,1)}, u32[]{:S(2)}) copy-start(bf16[2,2048]{1,0:T(2,128)(2,1)} %refs_0_.1) | copy-start | bytes 24580
  9.1 8.3 %copy-start.1 = (bf16[2048,3,256]{2,0,1:T(8,128)(2,1)S(1)}, bf16[2048,3,256]{2,0,1:T(8,128)(2,1)}, u32[]{:S(2)}) copy-start(bf16[2048,3,256]{2,0,1:T(8,128)(2,1)} %param.17) | copy-start | bytes 9437188
  9.1 8.2 %copy-start.6 = (s32[2,1024]{1,0:T(2,128)S(1)}, s32[2,1024]{1,0:T(2,128)}, u32[]{:S(2)}) copy-start(s32[2,1024]{1,0:T(2,128)} %mask_ref.1) | copy-start | bytes 24580
  9.1 8.2 %copy-start.7 = (s32[2,1024]{1,0:T(2,128)S(1)}, s32[2,1024]{1,0:T(2,128)}, u32[]{:S(2)}) copy-start(s32[2,1024]{1,0:T(2,128)} %slot_pos_ref.1) | copy-start | bytes 24580
  9.1 8.2 %copy-start.8 = (s32[16]{0:T(128)S(1)}, s32[16]{0:T(128)}, u32[]{:S(2)}) copy-start(s32[16]{0:T(128)} %len_ref.1) | copy-start | bytes 196
  9.2 10.3 %slice-start.3 = ((s8[8388608]{0:T(1024)(128)(4,1)}), s8[4194304]{0:T(1024)(128)(4,1)S(1)}, s32[]{:S(2)}) async-start(s8[8388608]{0:T(1024)(128)(4,1)} %bitcast.21), calls=%async_computation.5 | async-start | bytes 8388608
  9.2 10.3 %slice-start.5 = ((s8[8388608]{0:T(1024)(128)(4,1)}), s8[4194304]{0:T(1024)(128)(4,1)S(1)}, s32[]{:S(2)}) async-start(s8[8388608]{0:T(1024)(128)(4,1)} %bitcast.23), calls=%async_computation.7 | async-start | bytes 8388608
  9.2 3.7 %collective-permute-start.4 = (bf16[2048,256]{1,0:T(8,128)(2,1)S(1)}, bf16[2048,256]{1,0:T(8,128)(2,1)S(1)}, u32[]{:S(2)}, u32[]{:S(2)}) collective-permute-start(bf16[2048,256]{1,0:T(8,128)(2,1)S(1)} %slice_bitcast_fusion.refs_5_), channel_id=1, source_target_pairs={{0,1},{1,0},{2,3},{3,2},{4,5},{5,4},{6,7},{7,6},{8,9},{9,8},{10,11... | collective-permute-start | bytes 3145736 | tf_op jit(solution)/shard_map/ppermute | solution.py:388
  9.3 1.4 %copy-start.9 = (s32[16]{0:T(128)S(1)}, s32[16]{0:T(128)}, u32[]{:S(2)}) copy-start(s32[16]{0:T(128)} %pos_ref.3) | copy-start | bytes 196
  10.7 1.5 %copy-start.11 = (bf16[2048]{0:T(1024)(128)(2,1)S(1)}, bf16[2048]{0:T(1024)(128)(2,1)}, u32[]{:S(2)}) copy-start(bf16[2048]{0:T(1024)(128)(2,1)} %param.16) | copy-start | bytes 12292
  10.7 6.7 %copy-start.10 = (s32[16]{0:T(128)S(1)}, s32[16]{0:T(128)}, u32[]{:S(2)}) copy-start(s32[16]{0:T(128)} %pos_ref.3) | copy-start | bytes 196
  12.2 7.3 %copy-start.4 = (bf16[2,2048,4]{1,2,0:T(4,128)(2,1)S(1)}, bf16[2,2048,4]{1,2,0:T(4,128)(2,1)}, u32[]{:S(2)}) copy-start(bf16[2,2048,4]{1,2,0:T(4,128)(2,1)} %param.24) | copy-start | bytes 98308
  12.2 7.3 %copy-start.5 = (bf16[2,2048,4]{1,2,0:T(4,128)(2,1)S(1)}, bf16[2,2048,4]{1,2,0:T(4,128)(2,1)}, u32[]{:S(2)}) copy-start(bf16[2,2048,4]{1,2,0:T(4,128)(2,1)} %param.25) | copy-start | bytes 98308
  12.3 5.0 %collective-permute-start.3 = (bf16[4,2,2048]{2,1,0:T(2,128)(2,1)S(1)}, bf16[4,2,2048]{2,1,0:T(2,128)(2,1)S(1)}, u32[]{:S(2)}, u32[]{:S(2)}) collective-permute-start(bf16[4,2,2048]{2,1,0:T(2,128)(2,1)S(1)} %pad_maximum_fusion.same_ref), channel_id=1, source_target_pairs={{0,1},{1,0},{2,3},{3,2},{4,5},{5,4},{6,7},{7,6},{8,9},{9,8},{10,11... | collective-permute-start | bytes 98312 | tf_op jit(solution)/shard_map/ppermute | solution.py:401
  13.5 5.9 %collective-permute-start.5 = (f32[8,128]{1,0:T(8,128)S(1)}, f32[8,128]{1,0:T(8,128)S(1)}, u32[]{:S(2)}, u32[]{:S(2)}) collective-permute-start(f32[8,128]{1,0:T(8,128)S(1)} %get-tuple-element.31), channel_id=1, source_target_pairs={{0,2},{1,3},{2,4},{3,5},{4,6},{5,7},{6,0},{7,1},{8,10},{9,11},{10,... | collective-permute-start | bytes 12296 | tf_op jit(solution)/shard_map/ppermute | solution.py:398
  14.2 5.2 %collective-permute-start.6 = (f32[8,128]{1,0:T(8,128)S(1)}, f32[8,128]{1,0:T(8,128)S(1)}, u32[]{:S(2)}, u32[]{:S(2)}) collective-permute-start(f32[8,128]{1,0:T(8,128)S(1)} %get-tuple-element.32), channel_id=1, source_target_pairs={{0,4},{1,5},{2,6},{3,7},{4,0},{5,1},{6,2},{7,3},{8,12},{9,13},{10,... | collective-permute-start | bytes 12296 | tf_op jit(solution)/shard_map/ppermute | solution.py:398
  14.6 4.8 %collective-permute-start.7 = (f32[8,128]{1,0:T(8,128)S(1)}, f32[8,128]{1,0:T(8,128)S(1)}, u32[]{:S(2)}, u32[]{:S(2)}) collective-permute-start(f32[8,128]{1,0:T(8,128)S(1)} %get-tuple-element.33), channel_id=1, source_target_pairs={{0,6},{1,7},{2,0},{3,1},{4,2},{5,3},{6,4},{7,5},{8,14},{9,15},{10,... | collective-permute-start | bytes 12296 | tf_op jit(solution)/shard_map/ppermute | solution.py:398
  19.6 18.1 %copy-start.3 = (bf16[256,2048]{1,0:T(8,128)(2,1)S(1)}, bf16[256,2048]{1,0:T(8,128)(2,1)}, u32[]{:S(2)}) copy-start(bf16[256,2048]{1,0:T(8,128)(2,1)} %w_ref.1) | copy-start | bytes 3145732
  19.6 29.7 %slice-start = ((s8[8388608]{0:T(1024)(128)(4,1)}), s8[4194304]{0:T(1024)(128)(4,1)S(1)}, s32[]{:S(2)}) async-start(s8[8388608]{0:T(1024)(128)(4,1)} %bitcast.11), calls=%async_computation.2 | async-start | bytes 8388608
  37.6 10.5 %copy-start.12 = (bf16[2048]{0:T(1024)(128)(2,1)S(1)}, bf16[2048]{0:T(1024)(128)(2,1)}, u32[]{:S(2)}) copy-start(bf16[2048]{0:T(1024)(128)(2,1)} %param.19) | copy-start | bytes 12292
  37.6 11.7 %slice-start.1 = ((s8[8388608]{0:T(1024)(128)(4,1)}), s8[4194304]{0:T(1024)(128)(4,1)S(1)}, s32[]{:S(2)}) async-start(s8[8388608]{0:T(1024)(128)(4,1)} %bitcast.11), calls=%async_computation.3 | async-start | bytes 8388608
  37.6 11.7 %copy-start = (bf16[1024,2048]{1,0:T(8,128)(2,1)S(1)}, bf16[1024,2048]{1,0:T(8,128)(2,1)}, u32[]{:S(2)}) copy-start(bf16[1024,2048]{1,0:T(8,128)(2,1)} %down_ref.1) | copy-start | bytes 12582916
  37.9 1.3 %collective-permute-start.8 = (f32[16,1024]{1,0:T(8,128)S(1)}, f32[16,1024]{1,0:T(8,128)S(1)}, u32[]{:S(2)}, u32[]{:S(2)}) collective-permute-start(f32[16,1024]{1,0:T(8,128)S(1)} %get-tuple-element.42), channel_id=1, source_target_pairs={{0,1},{1,0},{2,3},{3,2},{4,5},{5,4},{6,7},{7,6},{8,9},{9,8},{10,11... | collective-permute-start | bytes 196616 | tf_op jit(solution)/shard_map/ppermute | solution.py:436
  39.3 5.5 %collective-permute-start.10 = (bf16[16,1024]{1,0:T(8,128)(2,1)S(1)}, bf16[16,1024]{1,0:T(8,128)(2,1)S(1)}, u32[]{:S(2)}, u32[]{:S(2)}) collective-permute-start(bf16[16,1024]{1,0:T(8,128)(2,1)S(1)} %add_convert_fusion.1), channel_id=1, source_target_pairs={{0,4},{1,5},{2,6},{3,7},{4,0},{5,1},{6,2},{7,3},{8,12},{9,13},{10,... | collective-permute-start | bytes 98312 | tf_op jit(solution)/shard_map/ppermute | solution.py:439
  39.7 5.0 %collective-permute-start.11 = (bf16[16,1024]{1,0:T(8,128)(2,1)S(1)}, bf16[16,1024]{1,0:T(8,128)(2,1)S(1)}, u32[]{:S(2)}, u32[]{:S(2)}) collective-permute-start(bf16[16,1024]{1,0:T(8,128)(2,1)S(1)} %add_convert_fusion.1), channel_id=1, source_target_pairs={{0,6},{1,7},{2,0},{3,1},{4,2},{5,3},{6,4},{7,5},{8,14},{9,15},{10,... | collective-permute-start | bytes 98312 | tf_op jit(solution)/shard_map/ppermute | solution.py:439
  42.3 5.7 %collective-permute-start.9 = (bf16[16,1024]{1,0:T(8,128)(2,1)S(1)}, bf16[16,1024]{1,0:T(8,128)(2,1)S(1)}, u32[]{:S(2)}, u32[]{:S(2)}) collective-permute-start(bf16[16,1024]{1,0:T(8,128)(2,1)S(1)} %add_convert_fusion.1), channel_id=1, source_target_pairs={{0,2},{1,3},{2,4},{3,5},{4,6},{5,7},{6,0},{7,1},{8,10},{9,11},{10,... | collective-permute-start | bytes 98312 | tf_op jit(solution)/shard_map/ppermute | solution.py:439
  48.0 1.3 %collective-permute-start.12 = (bf16[16,1024]{1,0:T(8,128)(2,1)S(1)}, bf16[16,1024]{1,0:T(8,128)(2,1)S(1)}, u32[]{:S(2)}, u32[]{:S(2)}) collective-permute-start(bf16[16,1024]{1,0:T(8,128)(2,1)S(1)} %add_convert_fusion.mine_ref), channel_id=1, source_target_pairs={{0,1},{1,0},{2,3},{3,2},{4,5},{5,4},{6,7},{7,6},{8,9},{9,8},{10,11... | collective-permute-start | bytes 98312 | tf_op jit(solution)/shard_map/ppermute | solution.py:441

commit v4 on v3

--- a/solution.py
+++ b/solution.py
@@ -14,6 +14,7 @@
 NEG = -1e30
 LANE = 128
 MIB = 2**20
+AHEAD = 1
 PREP_FLOPS = 20_000_000_000
 QKV_FLOPS = 2_000_000_000
 ATT_FLOPS = 10_000_000_000
@@ -51,9 +52,9 @@
     outs = refs[5:]
     core = lax.axis_index("tensor") % 2
     values = jnp.concatenate([ref[...].astype(F32) for ref in states], axis=0)
-    normed = normed_rows(values, gain_ref[...].astype(F32))
-    own = jnp.dot(normed, own_ref[...], preferred_element_type=F32)
-    peer = jnp.dot(normed, peer_ref[...], preferred_element_type=F32)
+    normed = normed_rows(values, gain_ref[...].astype(F32).reshape(1, -1))
+    own = jnp.dot(normed, own_ref[0], preferred_element_type=F32)
+    peer = jnp.dot(normed, peer_ref[0], preferred_element_type=F32)
     queries = jnp.concatenate(
         [jnp.where(core == 0, own, peer), jnp.where(core == 0, peer, own)], axis=1
     )
@@ -106,7 +107,7 @@
     values = flat_ref[...]
     width = side_ref.shape[1]
     side_ref[...] = flat_ref[:, pl.ds(pl.multiple_of(core * width, LANE), width)]
-    normed = normed_rows(values, gain_ref[...].astype(F32))
+    normed = normed_rows(values, gain_ref[...].astype(F32).reshape(1, -1))
     repeat = lanes // cos_ref.shape[1]
     cosine = jnp.concatenate([cos_ref[...]] * repeat, axis=1)
     sine = jnp.concatenate([sin_ref[...]] * repeat, axis=1)
@@ -157,56 +158,71 @@
     head = lax.broadcasted_iota(jnp.int32, (heads, block), 0)
     own = head == lax.broadcasted_iota(jnp.int32, (heads, block), 1) // HEAD_SIZE
     scale = HEAD_SIZE**-0.5
-    for r in range(rows):
-        live = jnp.broadcast_to(live_ref[r : r + 1, :], (heads, slots)) == 1
-        for step in range(chips):
-            source = lax.rem(chip + chips - step, chips)
-            here = pl.ds(pl.multiple_of(source * block, block), block)
-            sink_keys = sink_k_ref[r, :, here].astype(F32)
-            sink_values = sink_v_ref[r, :, here].astype(F32)
-            query = jnp.concatenate(
-                [
-                    queries[step][wire_row(rows, c, r) : wire_row(rows, c, r) + 1, :]
-                    for c in range(block // LANE)
-                ],
-                axis=1,
-            )
-            query = jnp.where(own, jnp.broadcast_to(query, (heads, block)), 0.0)
-            score = (
-                jnp.dot(query.astype(BF16), k_ref[r, here, :], preferred_element_type=F32) * scale
-            )
-            score = jnp.where(live, score, NEG)
-            top = jnp.max(score, axis=1, keepdims=True)
-            sink_score = []
-            for i in range(sinks):
-                one = jnp.sum(query * sink_keys[i : i + 1, :], axis=1, keepdims=True) * scale
-                one = jnp.where(seq_index == 0, one, NEG)
-                sink_score.append(one)
-                top = jnp.maximum(top, one)
-            weight = jnp.where(live, jnp.exp(score - top), 0.0)
-            total = jnp.sum(weight, axis=1, keepdims=True)
-            mixture = lax.dot_general(
-                weight.astype(BF16),
-                v_ref[r, here, :],
-                (((1,), (1,)), ((), ())),
-                preferred_element_type=F32,
-            )
-            for i in range(sinks):
-                one = jnp.where(seq_index == 0, jnp.exp(sink_score[i] - top), 0.0)
-                total = total + one
-                mixture = mixture + one.astype(BF16).astype(F32) * sink_values[i : i + 1, :]
-            some = total > 0.0
-            level = jnp.where(some, top + jnp.log(jnp.where(some, total, 1.0)), NEG)
-            mixture = mixture / jnp.where(some, total, 1.0)
-            mixture = jnp.sum(jnp.where(own, mixture, 0.0), axis=0, keepdims=True)
-            level = jnp.sum(jnp.where(own, level, 0.0), axis=0, keepdims=True)
-            for f in range(block // chunk):
-                t, c = divmod(f, lanes // chunk)
-                row = wire_row(rows, c, r)
-                at = slice(f * chunk, (f + 1) * chunk)
-                for copy in range(copies):
-                    out_ref[copy, 2 * source + t, row : row + 1, :] = mixture[:, at]
-                    out_ref[copy, 2 * source + t, half + row : half + row + 1, :] = level[:, at]
+    lives = [
+        jnp.broadcast_to(live_ref[r : r + 1, :], (heads, slots)) == 1 for r in range(rows)
+    ]
+    first_shard = seq_index == 0
+
+    def place(step):
+        source = lax.rem(chip + chips - step, chips)
+        return source, pl.ds(pl.multiple_of(source * block, block), block)
+
+    def scores(r, step):
+        _, here = place(step)
+        query = jnp.concatenate(
+            [
+                queries[step][wire_row(rows, c, r) : wire_row(rows, c, r) + 1, :]
+                for c in range(block // LANE)
+            ],
+            axis=1,
+        )
+        query = jnp.where(own, jnp.broadcast_to(query, (heads, block)), 0.0)
+        score = jnp.dot(query.astype(BF16), k_ref[r, here, :], preferred_element_type=F32)
+        return query, score
+
+    def mix(r, step, query, score):
+        source, here = place(step)
+        sink_keys = sink_k_ref[r, :, here].astype(F32)
+        sink_values = sink_v_ref[r, :, here].astype(F32)
+        score = jnp.where(lives[r], score * scale, NEG)
+        top = jnp.max(score, axis=1, keepdims=True)
+        sink_score = []
+        for i in range(sinks):
+            one = jnp.sum(query * sink_keys[i : i + 1, :], axis=1, keepdims=True) * scale
+            one = jnp.where(first_shard, one, NEG)
+            sink_score.append(one)
+            top = jnp.maximum(top, one)
+        weight = jnp.where(lives[r], jnp.exp(score - top), 0.0)
+        mixture = lax.dot_general(
+            weight.astype(BF16),
+            v_ref[r, here, :],
+            (((1,), (1,)), ((), ())),
+            preferred_element_type=F32,
+        )
+        total = jnp.sum(weight, axis=1, keepdims=True)
+        for i in range(sinks):
+            one = jnp.where(first_shard, jnp.exp(sink_score[i] - top), 0.0)
+            total = total + one
+            mixture = mixture + one.astype(BF16).astype(F32) * sink_values[i : i + 1, :]
+        some = total > 0.0
+        level = jnp.where(some, top + jnp.log(jnp.where(some, total, 1.0)), NEG)
+        mixture = mixture / jnp.where(some, total, 1.0)
+        mixture = jnp.sum(jnp.where(own, mixture, 0.0), axis=0, keepdims=True)
+        level = jnp.sum(jnp.where(own, level, 0.0), axis=0, keepdims=True)
+        for f in range(block // chunk):
+            t, c = divmod(f, lanes // chunk)
+            row = wire_row(rows, c, r)
+            at = slice(f * chunk, (f + 1) * chunk)
+            for copy in range(copies):
+                out_ref[copy, 2 * source + t, row : row + 1, :] = mixture[:, at]
+                out_ref[copy, 2 * source + t, half + row : half + row + 1, :] = level[:, at]
+
+    todo = [(r, step) for r in range(rows) for step in range(chips)]
+    ahead = [scores(*one) for one in todo[:AHEAD]]
+    for i, one in enumerate(todo):
+        if i + AHEAD < len(todo):
+            ahead.append(scores(*todo[i + AHEAD]))
+        mix(*one, *ahead[i])
 
 
 def merge_kernel(rows, part_ref, new_ref, w_ref, mine_ref, other_ref, rows_ref, full_ref):
@@ -245,40 +261,75 @@
     other_ref[...] = full_ref[:, pl.ds(pl.multiple_of((1 - core) * width, LANE), width)]
 
 
-def mlp_kernel(
-    rows, mine_ref, other_ref, gain_ref, gate_up_ref, down_ref, out_ref, resid_ref, wide_ref, by_ref
-):
-    batch, width = mine_ref.shape
-    units = gate_up_ref.shape[2]
-    core = lax.axis_index("tensor") % 2
-    first = jnp.where(core == 0, mine_ref[...].astype(F32), other_ref[...].astype(F32))
-    second = jnp.where(core == 0, other_ref[...].astype(F32), mine_ref[...].astype(F32))
-    resid = jnp.concatenate([first, second], axis=1)
-    groups = out_ref.shape[0]
-    for group in range(groups):
-        by_ref[group, :rows, :] = resid[group * rows : (group + 1) * rows, :]
-    resid_ref[...] = by_ref[lax.axis_index("tensor"), :rows, :]
-    normed = normed_rows(resid, gain_ref[...].astype(F32))
+def spread_rows(values, wide_ref):
+    batch, width = values.shape
     step = 2 * LANE
     feature = lax.broadcasted_iota(jnp.int32, (step, 4 * step), 0)
     lane = lax.broadcasted_iota(jnp.int32, (step, 4 * step), 1)
     lane = jnp.where(lane < 2 * step, lane, lane - 2 * step - 1)
     spread = (2 * feature == lane).astype(F32).astype(BF16)
-    pieces = 2 * width // step
-    stacked = jnp.concatenate([normed[:, j * step : (j + 1) * step] for j in range(pieces)], axis=0)
+    pieces = width // step
+    stacked = jnp.concatenate([values[:, j * step : (j + 1) * step] for j in range(pieces)], axis=0)
     wide = jnp.dot(stacked, spread, preferred_element_type=F32).astype(BF16)
     for j in range(pieces):
         part = wide[j * batch : (j + 1) * batch, :]
         at = slice(j * 2 * step, (j + 1) * 2 * step)
         wide_ref[:batch, at] = part[:, : 2 * step]
         wide_ref[batch:, at] = part[:, 2 * step :]
+
+
+def half_gate_up(side, half, gain_ref, gate_up_ref, wide_ref):
+    width = side.shape[1]
+    units = gate_up_ref.shape[2]
+    gain = gain_ref[...].astype(F32).reshape(1, -1)
+    gain = jnp.where(half == 0, gain[:, :width], gain[:, width:])
+    spread_rows((side * gain).astype(BF16), wide_ref)
     weights = gate_up_ref.reshape(4 * width, units)
-    gate_up = jnp.dot(wide_ref[...], weights[...], preferred_element_type=F32)
-    gate = gate_up[:batch]
-    hidden = (gate * jax.nn.sigmoid(gate) * gate_up[batch:]).astype(BF16)
+    weights = weights[pl.ds(pl.multiple_of(half * 2 * width, 2 * width), 2 * width), :]
+    gate_up = jnp.dot(wide_ref[...], weights, preferred_element_type=F32)
+    return gate_up, jnp.sum(side * side, axis=1, keepdims=True)
+
+
+def first_half_kernel(side_ref, gain_ref, gate_up_ref, out_ref, square_ref, wide_ref):
+    core = lax.axis_index("tensor") % 2
+    side = side_ref[...].astype(F32)
+    out_ref[...], square = half_gate_up(side, core, gain_ref, gate_up_ref, wide_ref)
+    square_ref[...] = jnp.broadcast_to(square, square_ref.shape)
+
+
+def mlp_kernel(
+    rows,
+    mine_ref,
+    other_ref,
+    gain_ref,
+    gate_up_ref,
+    down_ref,
+    first_ref,
+    square_ref,
+    out_ref,
+    resid_ref,
+    wide_ref,
+    by_ref,
+):
+    batch, width = mine_ref.shape
+    core = lax.axis_index("tensor") % 2
+    mine = mine_ref[...].astype(F32)
+    other = other_ref[...].astype(F32)
+    gate_up, square = half_gate_up(other, 1 - core, gain_ref, gate_up_ref, wide_ref)
+    meansq = (square + square_ref[:, :1]) / (2 * width)
+    scale = lax.rsqrt(meansq + 1e-05)
+    gate_up = gate_up + first_ref[...]
+    gate = gate_up[:batch] * scale
+    hidden = (gate * jax.nn.sigmoid(gate) * (gate_up[batch:] * scale)).astype(BF16)
     out = jnp.dot(hidden, down_ref[...], preferred_element_type=F32)
+    resid = jnp.concatenate(
+        [jnp.where(core == 0, mine, other), jnp.where(core == 0, other, mine)], axis=1
+    )
+    groups = out_ref.shape[0]
     for group in range(groups):
+        by_ref[group, :rows, :] = resid[group * rows : (group + 1) * rows, :]
         out_ref[group] = out[group * rows : (group + 1) * rows, :].astype(BF16)
+    resid_ref[...] = by_ref[lax.axis_index("tensor"), :rows, :]
 
 
 def prepare_kernel(rows, pos_ref, cos_ref, sin_ref, query_cos_ref, query_sin_ref):
@@ -384,13 +435,12 @@
     hops = [[(i, (i + step) % groups) for i in range(groups)] for step in range(2, groups, 2)]
     column = [states] + [lax.ppermute(states, "tensor", hop) for hop in hops]
     w_qkv = jnp.transpose(w_qkv, (1, 0, 2))
-    w_query = w_qkv[0]
-    w_query_peer = lax.ppermute(w_query, "tensor", across)
+    w_peer = lax.ppermute(w_qkv, "tensor", across)
     query_wire = sds((max(8, 2 * rows * lanes // LANE), LANE), F32)
     queries = call(
         functools.partial(query_kernel, rows, chips),
         (query_wire,) * chips,
-        (*column, attn_gain[None], w_query, w_query_peer, query_cos, query_sin),
+        (*column, attn_gain, w_qkv, w_peer, query_cos, query_sin),
         name="query",
         flops=QKV_FLOPS,
     )
@@ -405,7 +455,7 @@
     new_keys, new_values, new_part, own_side, live = call(
         functools.partial(new_token_kernel, rows),
         (flat, flat, wire, side, sds(slot_mask.shape, jnp.int32)),
-        (cache_len, new_pos, slot_mask, slot_pos, same, peer, attn_gain[None], w_qkv, cosine, sine),
+        (cache_len, new_pos, slot_mask, slot_pos, same, peer, attn_gain, w_qkv, cosine, sine),
         specs=[SMEM_SPEC] * 2 + [VMEM_SPEC] * 8,
         scratch=[pltpu.VMEM((groups, 8, width), F32), pltpu.VMEM((batch, width), F32)],
         name="new_token",
@@ -439,14 +489,24 @@
         total = total + lax.ppermute(chip, "tensor", hop).astype(F32)
     side_resid = (own_side + total).astype(BF16)
     other_resid = lax.ppermute(side_resid, "tensor", across)
+    units = w_gate_up.shape[2]
+    first_half, square = call(
+        first_half_kernel,
+        (sds((2 * batch, units), F32), sds((batch, LANE), F32)),
+        (side_resid, mlp_gain, w_gate_up),
+        scratch=[pltpu.VMEM((2 * batch, width), BF16)],
+        limit=8,
+        name="first_half",
+        flops=2 * batch * width * units,
+    )
     partial, own_resid = call(
         functools.partial(mlp_kernel, rows),
         (sds((groups, rows, width), BF16), sds((rows, width), F32)),
-        (side_resid, other_resid, mlp_gain[None], w_gate_up, w_down),
-        scratch=[pltpu.VMEM((2 * batch, 2 * width), BF16), pltpu.VMEM((groups, 8, width), F32)],
+        (side_resid, other_resid, mlp_gain, w_gate_up, w_down, first_half, square),
+        scratch=[pltpu.VMEM((2 * batch, width), BF16), pltpu.VMEM((groups, 8, width), F32)],
         limit=8,
         name="mlp",
-        flops=6 * batch * width * w_gate_up.shape[2],
+        flops=4 * batch * width * units,
     )
     partial = lax.all_to_all(partial, "tensor", 0, 0, tiled=True)
     out_states = (own_resid + jnp.sum(partial.astype(F32), axis=0)).astype(BF16)

time: 61.1 us -> 56.5 us (0.925)
  local copies, waits for them, and re-layouts: 3.87 us -> 0.74 us
  blocking collectives: 21.8 us -> 20.4 us
  Pallas kernels: 10.6 us -> 9.61 us
    unnamed x38, local copies, waits for them, and re-layouts: 2.41 us -> 0.74 us
    ppermute x3, waiting for transfers between devices: 0.13 us -> 1.59 us  [per_device(): lax.ppermute(query, 'tensor', hop)]
    squeeze x1 -> x0, local copies, waits for them, and re-layouts: 1.44 us -> none  [per_device(): w_query = w_qkv[0]]
    all_to_all x1, blocking collectives: 13.5 us -> 12.1 us  [per_device(): lax.all_to_all(part.reshape(shards * groups, wire_rows, chunk), ('seq', '...]
    ppermute x1, waiting for transfers between devices: 1.17 us -> 0.1 us  [per_device(): other_resid = lax.ppermute(side_resid, 'tensor', across)]
    pallas_call x6 -> x7, Pallas kernels: 10.6 us -> 9.61 us  [call(): pl.pallas_call(kernel, out_shape=out, in_specs=specs or [VMEM_SPEC] * len...]
  transfers between devices with their start and end apart: 13 -> 13, of which waited for: 5 -> 7; matrix products, arithmetic and copies ran while one was open for 2% -> 0% of each run, Pallas kernels for 5% -> 7%
where the time goes in v4:
time: 56.5 us; the launch traced here: 56.3 us
  blocking collectives  20.4 us (36%)
  starting transfers between devices  15.4 us (27%)
  Pallas kernels  9.61 us (17%)
  waiting for transfers between devices  8.49 us (15%)
  between operations  0.95 us (2%)
  other arithmetic  0.76 us (1%)
  local copies, waits for them, and re-layouts  0.74 us (1%)
    all_to_all x1, blocking collectives, per_device(): lax.all_to_all(part.reshape(shards * groups, wire_rows, chunk), ('seq', '...  12.1 us
    pallas_call x7, Pallas kernels, call(): pl.pallas_call(kernel, out_shape=out, in_specs=specs or [VMEM_SPEC] * len...  9.61 us
    all_to_all x1, blocking collectives, per_device(): partial = lax.all_to_all(partial, 'tensor', 0, 0, tiled=True)  8.29 us
    ppermute x3, starting transfers between devices, per_device(): column = [states] + [lax.ppermute(states, 'tensor', hop) for hop in hops]  7.49 us
    ppermute x3, waiting for transfers between devices, per_device(): total = total + lax.ppermute(chip, 'tensor', hop).astype(F32)  5.34 us
    ppermute x3, starting transfers between devices, per_device(): lax.ppermute(query, 'tensor', hop)  4.44 us
    ppermute x3, starting transfers between devices, per_device(): total = total + lax.ppermute(chip, 'tensor', hop).astype(F32)  2.46 us
    ppermute x3, waiting for transfers between devices, per_device(): lax.ppermute(query, 'tensor', hop)  1.59 us
  transfers between devices with their start and end apart: 13, of which 7 were waited for; matrix products, arithmetic and copies ran while one was open for 0% of the time, Pallas kernels for 7%

profile of v4, /device:TPU:0, one launch (start us, length us, event | category | flops | bytes accessed | tf_op | source)
XLA Modules:
  0.0 56.3 jit_solution(14651895415412396450)
XLA Ops:
  0.6 0.0 slice-start.2
  0.6 0.0 slice-start.4
  0.7 0.0 slice-start.3
  0.7 0.0 slice-start.5
  0.7 0.5 collective-permute-start.4
  1.3 3.7 %collective-permute-start.1 = (bf16[2,2048]{1,0:T(2,128)(2,1)}, bf16[2,2048]{1,0:T(2,128)(2,1)S(1)}, u32[]{:S(2)}, u32[]{:S(2)}) collective-permute-start(bf16[2,2048]{1,0:T(2,128)(2,1)} %refs_0_.1), channel_id=1, source_target_pairs={{0,4},{1,5},{2,6},{3,7},{4,0},{5,1},{6,2},{7,3},{8,12},{9,13},{10,... | collective-permute-start | bytes 24584 | tf_op jit(solution)/shard_map/ppermute | solution.py:436
  4.9 1.6 %collective-permute-start = (bf16[2,2048]{1,0:T(2,128)(2,1)}, bf16[2,2048]{1,0:T(2,128)(2,1)S(1)}, u32[]{:S(2)}, u32[]{:S(2)}) collective-permute-start(bf16[2,2048]{1,0:T(2,128)(2,1)} %refs_0_.1), channel_id=1, source_target_pairs={{0,2},{1,3},{2,4},{3,5},{4,6},{5,7},{6,0},{7,1},{8,10},{9,11},{10,... | collective-permute-start | bytes 24584 | tf_op jit(solution)/shard_map/ppermute | solution.py:436
  6.5 2.2 %collective-permute-start.2 = (bf16[2,2048]{1,0:T(2,128)(2,1)}, bf16[2,2048]{1,0:T(2,128)(2,1)S(1)}, u32[]{:S(2)}, u32[]{:S(2)}) collective-permute-start(bf16[2,2048]{1,0:T(2,128)(2,1)} %refs_0_.1), channel_id=1, source_target_pairs={{0,6},{1,7},{2,0},{3,1},{4,2},{5,3},{6,4},{7,5},{8,14},{9,15},{10,... | collective-permute-start | bytes 24584 | tf_op jit(solution)/shard_map/ppermute | solution.py:436
  8.7 0.7 %copy-done.11 = s32[16]{0:T(128)S(1)} copy-done((s32[16]{0:T(128)S(1)}, s32[16]{0:T(128)}, u32[]{:S(2)}) %copy-start.11) | copy-done | bytes 88
  9.4 0.6 %prepare.1 = (f32[16,128]{1,0:T(8,128)S(1)}, f32[16,128]{1,0:T(8,128)S(1)}, f32[8,128]{1,0:T(8,128)S(1)}, f32[8,128]{1,0:T(8,128)S(1)}) custom-call(s32[16]{0:T(128)S(1)} %copy-done.11), custom_call_target="tpu_custom_call" | custom-call | flops 20000000000 | bytes 64 | tf_op jit(solution)/shard_map/prepare/pallas_call | solution.py:381
  10.0 0.0 copy-start.5
  10.0 0.0 copy-start.6
  10.1 0.0 collective-permute-done.1.refs_2_
  10.1 0.5 collective-permute-done.refs_1_
  10.6 0.0 collective-permute-done.2.refs_3_
  10.6 0.1 pad_maximum_fusion.same_ref
  10.6 0.1 collective-permute-start.3
  10.7 0.0 collective-permute-done.4.refs_6_
  10.8 0.6 query.1
  11.3 0.1 collective-permute-start.5
  11.4 4.3 %collective-permute-start.6 = (f32[8,128]{1,0:T(8,128)S(1)}, f32[8,128]{1,0:T(8,128)S(1)}, u32[]{:S(2)}, u32[]{:S(2)}) collective-permute-start(f32[8,128]{1,0:T(8,128)S(1)} %get-tuple-element.34), channel_id=1, source_target_pairs={{0,4},{1,5},{2,6},{3,7},{4,0},{5,1},{6,2},{7,3},{8,12},{9,13},{10,... | collective-permute-start | bytes 12296 | tf_op jit(solution)/shard_map/ppermute | solution.py:448
  15.8 0.0 collective-permute-start.7
  15.8 0.0 collective-permute-done.3.peer_ref
  15.8 2.0 %new_token.1 = (bf16[16,256]{1,0:T(8,128)(2,1)}, bf16[16,256]{1,0:T(8,128)(2,1)}, f32[8,8,128]{2,1,0:T(8,128)S(1)}, f32[16,1024]{1,0:T(8,128)S(1)}, s32[2,1024]{1,0:T(2,128)S(1)}) custom-call(s32[16]{0:T(128)S(1)} %copy-done.10, s32[16]{0:T(128)S(1)} %copy-done.12, s32[2,1024]{1,0:T(2,128)S(1)} %copy-done.7, s32[2,1024]{1,0:T(2,128)S(1)} %copy-done.8, ...), custom_call_target="tpu_custom_call" | custom-call | flops 2000000000 | bytes 3248256 | tf_op jit(solution)/shard_map/new_token/pallas_call | solution.py:381
  17.8 0.0 collective-permute-done.5.refs_1_
  17.8 0.0 collective-permute-done.6.refs_2_
  17.8 1.6 %collective-permute-done.7.refs_3_ = f32[8,128]{1,0:T(8,128)S(1)} collective-permute-done((f32[8,128]{1,0:T(8,128)S(1)}, f32[8,128]{1,0:T(8,128)S(1)}, u32[]{:S(2)}, u32[]{:S(2)}) %collective-permute-start.7) | collective-permute-done | bytes 4128 | tf_op jit(solution)/shard_map/ppermute | solution.py:448
  19.4 0.0 copy-start.4
  19.4 0.0 slice-start
  19.4 3.5 %attention.1 = f32[4,8,8,128]{3,2,1,0:T(8,128)S(1)} custom-call(f32[8,128]{1,0:T(8,128)S(1)} %get-tuple-element.37.refs_0_, f32[8,128]{1,0:T(8,128)S(1)} %collective-permute-done.5.refs_1_, f32[8,128]{1,0:T(8,128)S(1)} %collective-permute-done.6.refs_2_, f32[8,128]{1,0:T(8,128)S(1)} %collective-permute-done.7.refs_3_, bf16[2,2048,1024]{2,1,0:T(8,128)(2,1)S(1)} %bitcast.18, ...), custom_call_target="tpu_custom_call" | custom-call | flops 10000000000 | bytes 16867328 | tf_op jit(solution)/shard_map/attention/pallas_call | solution.py:381
  22.9 12.1 %all_to_all.10 = f32[32,8,128]{2,1,0:T(8,128)S(1)} all-to-all(f32[32,8,128]{2,1,0:T(8,128)S(1)} %bitcast.11), channel_id=1, replica_groups=mesh['seq'=4,'tensor'=8] {'seq','tensor'}, dimensions={0} | all-to-all | bytes 262144 | tf_op jit(solution)/shard_map/all_to_all | solution.py:475
  35.0 0.0 copy-done.4
  35.0 0.3 merge.1
  35.3 0.4 collective-permute-start.8
  35.7 0.9 %collective-permute-done.8 = f32[16,1024]{1,0:T(8,128)S(1)} collective-permute-done((f32[16,1024]{1,0:T(8,128)S(1)}, f32[16,1024]{1,0:T(8,128)S(1)}, u32[]{:S(2)}, u32[]{:S(2)}) %collective-permute-start.8) | collective-permute-done | bytes 65568 | tf_op jit(solution)/shard_map/ppermute | solution.py:486
  36.6 1.0 %collective-permute-start.11 = (bf16[16,1024]{1,0:T(8,128)(2,1)S(1)}, bf16[16,1024]{1,0:T(8,128)(2,1)S(1)}, u32[]{:S(2)}, u32[]{:S(2)}) collective-permute-start(bf16[16,1024]{1,0:T(8,128)(2,1)S(1)} %add_convert_fusion.1), channel_id=1, source_target_pairs={{0,6},{1,7},{2,0},{3,1},{4,2},{5,3},{6,4},{7,5},{8,14},{9,15},{10,... | collective-permute-start | bytes 98312 | tf_op jit(solution)/shard_map/ppermute | solution.py:489
  37.7 1.1 %collective-permute-start.10 = (bf16[16,1024]{1,0:T(8,128)(2,1)S(1)}, bf16[16,1024]{1,0:T(8,128)(2,1)S(1)}, u32[]{:S(2)}, u32[]{:S(2)}) collective-permute-start(bf16[16,1024]{1,0:T(8,128)(2,1)S(1)} %add_convert_fusion.1), channel_id=1, source_target_pairs={{0,4},{1,5},{2,6},{3,7},{4,0},{5,1},{6,2},{7,3},{8,12},{9,13},{10,... | collective-permute-start | bytes 98312 | tf_op jit(solution)/shard_map/ppermute | solution.py:489
  38.7 0.4 collective-permute-start.9
  39.1 1.5 %collective-permute-done.11 = bf16[16,1024]{1,0:T(8,128)(2,1)S(1)} collective-permute-done((bf16[16,1024]{1,0:T(8,128)(2,1)S(1)}, bf16[16,1024]{1,0:T(8,128)(2,1)S(1)}, u32[]{:S(2)}, u32[]{:S(2)}) %collective-permute-start.11) | collective-permute-done | bytes 32800 | tf_op jit(solution)/shard_map/ppermute | solution.py:489
  40.6 1.9 %collective-permute-done.10 = bf16[16,1024]{1,0:T(8,128)(2,1)S(1)} collective-permute-done((bf16[16,1024]{1,0:T(8,128)(2,1)S(1)}, bf16[16,1024]{1,0:T(8,128)(2,1)S(1)}, u32[]{:S(2)}, u32[]{:S(2)}) %collective-permute-start.10) | collective-permute-done | bytes 32800 | tf_op jit(solution)/shard_map/ppermute | solution.py:489
  42.5 2.0 %collective-permute-done.9 = bf16[16,1024]{1,0:T(8,128)(2,1)S(1)} collective-permute-done((bf16[16,1024]{1,0:T(8,128)(2,1)S(1)}, bf16[16,1024]{1,0:T(8,128)(2,1)S(1)}, u32[]{:S(2)}, u32[]{:S(2)}) %collective-permute-start.9) | collective-permute-done | bytes 32800 | tf_op jit(solution)/shard_map/ppermute | solution.py:489
  44.5 0.1 collective-permute-start.12
  44.6 1.1 %first_half.1 = (f32[32,1024]{1,0:T(8,128)S(1)}, f32[16,128]{1,0:T(8,128)S(1)}) custom-call(bf16[16,1024]{1,0:T(8,128)(2,1)S(1)} %add_convert_fusion.side_ref.mine_ref, bf16[2048]{0:T(1024)(128)(2,1)S(1)} %copy-done.1, bf16[2048,2,1024]{2,1,0:T(2,128)(2,1)S(1)} %bitcast.10), custom_call_target="tpu_custom_call" | custom-call | flops 67108864 | bytes 8425472 | tf_op jit(solution)/shard_map/first_half/pallas_call | solution.py:381
  45.6 0.1 collective-permute-done.12.other_ref
  45.7 1.6 %mlp.1 = (bf16[8,2,2048]{2,1,0:T(2,128)(2,1)S(1)}, f32[2,2048]{1,0:T(2,128)S(1)}) custom-call(bf16[16,1024]{1,0:T(8,128)(2,1)S(1)} %add_convert_fusion.side_ref.mine_ref, bf16[16,1024]{1,0:T(8,128)(2,1)S(1)} %collective-permute-done.12.other_ref, bf16[2048]{0:T(1024)(128)(2,1)S(1)} %copy-done.1, bf16[2048,2,1024]{2,1,0:T(2,128)(2,1)S(1)} %bitcast.10, ...), custom_call_target="tpu_custom_call" | custom-call | flops 134217728 | bytes 12791808 | tf_op jit(solution)/shard_map/mlp/pallas_call | solution.py:381
  47.4 8.3 %all_to_all.11 = bf16[8,2,2048]{2,1,0:T(2,128)(2,1)S(1)} all-to-all(bf16[8,2,2048]{2,1,0:T(2,128)(2,1)S(1)} %get-tuple-element.48), channel_id=1, replica_groups=mesh['seq'=4,'tensor'=8] {'tensor'}, dimensions={0} | all-to-all | bytes 131072 | tf_op jit(solution)/shard_map/all_to_all | solution.py:511
  55.7 0.1 convert_reduce_fusion
  55.7 0.6 %add_convert_fusion.2 = bf16[2,2048]{1,0:T(2,128)(2,1)} fusion(f32[2,2048]{1,0:T(2,128)S(1)} %get-tuple-element.47, f32[2,2048]{1,0:T(2,128)S(1)} %convert_reduce_fusion), kind=kLoop, calls=%fused_computation.4 | loop fusion | flops 8192 | bytes 40960 | tf_op jit(solution)/shard_map/convert_element_type | solution.py:512
  (33 shorter events, 0.1 us)
Async XLA Ops:
  0.6 18.7 %slice-start.2 = ((s8[8388608]{0:T(1024)(128)(4,1)}), s8[4194304]{0:T(1024)(128)(4,1)S(1)}, s32[]{:S(2)}) async-start(s8[8388608]{0:T(1024)(128)(4,1)} %bitcast.17), calls=%async_computation.4 | async-start | bytes 8388608
  0.6 18.7 %slice-start.4 = ((s8[8388608]{0:T(1024)(128)(4,1)}), s8[4194304]{0:T(1024)(128)(4,1)S(1)}, s32[]{:S(2)}) async-start(s8[8388608]{0:T(1024)(128)(4,1)} %bitcast.19), calls=%async_computation.6 | async-start | bytes 8388608
  0.7 9.9 %copy-start.2 = (bf16[2,2048]{1,0:T(2,128)(2,1)S(1)}, bf16[2,2048]{1,0:T(2,128)(2,1)}, u32[]{:S(2)}) copy-start(bf16[2,2048]{1,0:T(2,128)(2,1)} %refs_0_.1) | copy-start | bytes 24580
  0.7 10.1 %copy-start.3 = (bf16[2048,3,256]{2,0,1:T(8,128)(2,1)S(1)}, bf16[2048,3,256]{2,0,1:T(8,128)(2,1)}, u32[]{:S(2)}) copy-start(bf16[2048,3,256]{2,0,1:T(8,128)(2,1)} %param.17) | copy-start | bytes 9437188
  0.7 10.1 %copy-start.9 = (bf16[2048]{0:T(1024)(128)(2,1)S(1)}, bf16[2048]{0:T(1024)(128)(2,1)}, u32[]{:S(2)}) copy-start(bf16[2048]{0:T(1024)(128)(2,1)} %refs_4_.2) | copy-start | bytes 12292
  0.7 15.1 %copy-start.7 = (s32[2,1024]{1,0:T(2,128)S(1)}, s32[2,1024]{1,0:T(2,128)}, u32[]{:S(2)}) copy-start(s32[2,1024]{1,0:T(2,128)} %mask_ref.1) | copy-start | bytes 24580
  0.7 15.1 %copy-start.8 = (s32[2,1024]{1,0:T(2,128)S(1)}, s32[2,1024]{1,0:T(2,128)}, u32[]{:S(2)}) copy-start(s32[2,1024]{1,0:T(2,128)} %slot_pos_ref.1) | copy-start | bytes 24580
  0.7 15.1 %copy-start.10 = (s32[16]{0:T(128)S(1)}, s32[16]{0:T(128)}, u32[]{:S(2)}) copy-start(s32[16]{0:T(128)} %len_ref.1) | copy-start | bytes 196
  0.7 18.7 %slice-start.3 = ((s8[8388608]{0:T(1024)(128)(4,1)}), s8[4194304]{0:T(1024)(128)(4,1)S(1)}, s32[]{:S(2)}) async-start(s8[8388608]{0:T(1024)(128)(4,1)} %bitcast.17), calls=%async_computation.5 | async-start | bytes 8388608
  0.7 18.6 %slice-start.5 = ((s8[8388608]{0:T(1024)(128)(4,1)}), s8[4194304]{0:T(1024)(128)(4,1)S(1)}, s32[]{:S(2)}) async-start(s8[8388608]{0:T(1024)(128)(4,1)} %bitcast.19), calls=%async_computation.7 | async-start | bytes 8388608
  0.7 10.0 %collective-permute-start.4 = (bf16[3,2048,256]{2,1,0:T(8,128)(2,1)}, bf16[3,2048,256]{2,1,0:T(8,128)(2,1)S(1)}, u32[]{:S(2)}, u32[]{:S(2)}) collective-permute-start(bf16[3,2048,256]{2,1,0:T(8,128)(2,1)} %bitcast.21), channel_id=1, source_target_pairs={{0,1},{1,0},{2,3},{3,2},{4,5},{5,4},{6,7},{7,6},{8,9},{9,8},{10,11... | collective-permute-start | bytes 9437192 | tf_op jit(solution)/shard_map/ppermute | solution.py:438
  1.3 8.8 %collective-permute-start.1 = (bf16[2,2048]{1,0:T(2,128)(2,1)}, bf16[2,2048]{1,0:T(2,128)(2,1)S(1)}, u32[]{:S(2)}, u32[]{:S(2)}) collective-permute-start(bf16[2,2048]{1,0:T(2,128)(2,1)} %refs_0_.1), channel_id=1, source_target_pairs={{0,4},{1,5},{2,6},{3,7},{4,0},{5,1},{6,2},{7,3},{8,12},{9,13},{10,... | collective-permute-start | bytes 24584 | tf_op jit(solution)/shard_map/ppermute | solution.py:436
  4.9 5.7 %collective-permute-start = (bf16[2,2048]{1,0:T(2,128)(2,1)}, bf16[2,2048]{1,0:T(2,128)(2,1)S(1)}, u32[]{:S(2)}, u32[]{:S(2)}) collective-permute-start(bf16[2,2048]{1,0:T(2,128)(2,1)} %refs_0_.1), channel_id=1, source_target_pairs={{0,2},{1,3},{2,4},{3,5},{4,6},{5,7},{6,0},{7,1},{8,10},{9,11},{10,... | collective-permute-start | bytes 24584 | tf_op jit(solution)/shard_map/ppermute | solution.py:436
  6.5 4.1 %collective-permute-start.2 = (bf16[2,2048]{1,0:T(2,128)(2,1)}, bf16[2,2048]{1,0:T(2,128)(2,1)S(1)}, u32[]{:S(2)}, u32[]{:S(2)}) collective-permute-start(bf16[2,2048]{1,0:T(2,128)(2,1)} %refs_0_.1), channel_id=1, source_target_pairs={{0,6},{1,7},{2,0},{3,1},{4,2},{5,3},{6,4},{7,5},{8,14},{9,15},{10,... | collective-permute-start | bytes 24584 | tf_op jit(solution)/shard_map/ppermute | solution.py:436
  8.7 0.7 %copy-start.11 = (s32[16]{0:T(128)S(1)}, s32[16]{0:T(128)}, u32[]{:S(2)}) copy-start(s32[16]{0:T(128)} %pos_ref.3) | copy-start | bytes 196
  9.4 6.4 %copy-start.12 = (s32[16]{0:T(128)S(1)}, s32[16]{0:T(128)}, u32[]{:S(2)}) copy-start(s32[16]{0:T(128)} %pos_ref.3) | copy-start | bytes 196
  10.0 9.4 %copy-start.5 = (bf16[2,2048,4]{1,2,0:T(4,128)(2,1)S(1)}, bf16[2,2048,4]{1,2,0:T(4,128)(2,1)}, u32[]{:S(2)}) copy-start(bf16[2,2048,4]{1,2,0:T(4,128)(2,1)} %param.24) | copy-start | bytes 98308
  10.0 9.4 %copy-start.6 = (bf16[2,2048,4]{1,2,0:T(4,128)(2,1)S(1)}, bf16[2,2048,4]{1,2,0:T(4,128)(2,1)}, u32[]{:S(2)}) copy-start(bf16[2,2048,4]{1,2,0:T(4,128)(2,1)} %param.25) | copy-start | bytes 98308
  10.6 5.1 %collective-permute-start.3 = (bf16[4,2,2048]{2,1,0:T(2,128)(2,1)S(1)}, bf16[4,2,2048]{2,1,0:T(2,128)(2,1)S(1)}, u32[]{:S(2)}, u32[]{:S(2)}) collective-permute-start(bf16[4,2,2048]{2,1,0:T(2,128)(2,1)S(1)} %pad_maximum_fusion.same_ref), channel_id=1, source_target_pairs={{0,1},{1,0},{2,3},{3,2},{4,5},{5,4},{6,7},{7,6},{8,9},{9,8},{10,11... | collective-permute-start | bytes 98312 | tf_op jit(solution)/shard_map/ppermute | solution.py:451
  11.3 6.5 %collective-permute-start.5 = (f32[8,128]{1,0:T(8,128)S(1)}, f32[8,128]{1,0:T(8,128)S(1)}, u32[]{:S(2)}, u32[]{:S(2)}) collective-permute-start(f32[8,128]{1,0:T(8,128)S(1)} %get-tuple-element.33), channel_id=1, source_target_pairs={{0,2},{1,3},{2,4},{3,5},{4,6},{5,7},{6,0},{7,1},{8,10},{9,11},{10,... | collective-permute-start | bytes 12296 | tf_op jit(solution)/shard_map/ppermute | solution.py:448
  11.4 6.4 %collective-permute-start.6 = (f32[8,128]{1,0:T(8,128)S(1)}, f32[8,128]{1,0:T(8,128)S(1)}, u32[]{:S(2)}, u32[]{:S(2)}) collective-permute-start(f32[8,128]{1,0:T(8,128)S(1)} %get-tuple-element.34), channel_id=1, source_target_pairs={{0,4},{1,5},{2,6},{3,7},{4,0},{5,1},{6,2},{7,3},{8,12},{9,13},{10,... | collective-permute-start | bytes 12296 | tf_op jit(solution)/shard_map/ppermute | solution.py:448
  15.8 3.6 %collective-permute-start.7 = (f32[8,128]{1,0:T(8,128)S(1)}, f32[8,128]{1,0:T(8,128)S(1)}, u32[]{:S(2)}, u32[]{:S(2)}) collective-permute-start(f32[8,128]{1,0:T(8,128)S(1)} %get-tuple-element.35), channel_id=1, source_target_pairs={{0,6},{1,7},{2,0},{3,1},{4,2},{5,3},{6,4},{7,5},{8,14},{9,15},{10,... | collective-permute-start | bytes 12296 | tf_op jit(solution)/shard_map/ppermute | solution.py:448
  19.4 15.6 %copy-start.4 = (bf16[256,2048]{1,0:T(8,128)(2,1)S(1)}, bf16[256,2048]{1,0:T(8,128)(2,1)}, u32[]{:S(2)}) copy-start(bf16[256,2048]{1,0:T(8,128)(2,1)} %w_ref.1) | copy-start | bytes 3145732
  19.4 25.1 %slice-start = ((s8[8388608]{0:T(1024)(128)(4,1)}), s8[4194304]{0:T(1024)(128)(4,1)S(1)}, s32[]{:S(2)}) async-start(s8[8388608]{0:T(1024)(128)(4,1)} %bitcast.9), calls=%async_computation.2 | async-start | bytes 8388608
  35.0 9.6 %slice-start.1 = ((s8[8388608]{0:T(1024)(128)(4,1)}), s8[4194304]{0:T(1024)(128)(4,1)S(1)}, s32[]{:S(2)}) async-start(s8[8388608]{0:T(1024)(128)(4,1)} %bitcast.9), calls=%async_computation.3 | async-start | bytes 8388608
  35.0 9.6 %copy-start.1 = (bf16[2048]{0:T(1024)(128)(2,1)S(1)}, bf16[2048]{0:T(1024)(128)(2,1)}, u32[]{:S(2)}) copy-start(bf16[2048]{0:T(1024)(128)(2,1)} %gain_ref.5) | copy-start | bytes 12292
  35.3 10.5 %copy-start = (bf16[1024,2048]{1,0:T(8,128)(2,1)S(1)}, bf16[1024,2048]{1,0:T(8,128)(2,1)}, u32[]{:S(2)}) copy-start(bf16[1024,2048]{1,0:T(8,128)(2,1)} %down_ref.1) | copy-start | bytes 12582916
  35.3 1.3 %collective-permute-start.8 = (f32[16,1024]{1,0:T(8,128)S(1)}, f32[16,1024]{1,0:T(8,128)S(1)}, u32[]{:S(2)}, u32[]{:S(2)}) collective-permute-start(f32[16,1024]{1,0:T(8,128)S(1)} %get-tuple-element.44), channel_id=1, source_target_pairs={{0,1},{1,0},{2,3},{3,2},{4,5},{5,4},{6,7},{7,6},{8,9},{9,8},{10,11... | collective-permute-start | bytes 196616 | tf_op jit(solution)/shard_map/ppermute | solution.py:486
  36.6 4.0 %collective-permute-start.11 = (bf16[16,1024]{1,0:T(8,128)(2,1)S(1)}, bf16[16,1024]{1,0:T(8,128)(2,1)S(1)}, u32[]{:S(2)}, u32[]{:S(2)}) collective-permute-start(bf16[16,1024]{1,0:T(8,128)(2,1)S(1)} %add_convert_fusion.1), channel_id=1, source_target_pairs={{0,6},{1,7},{2,0},{3,1},{4,2},{5,3},{6,4},{7,5},{8,14},{9,15},{10,... | collective-permute-start | bytes 98312 | tf_op jit(solution)/shard_map/ppermute | solution.py:489
  37.7 4.8 %collective-permute-start.10 = (bf16[16,1024]{1,0:T(8,128)(2,1)S(1)}, bf16[16,1024]{1,0:T(8,128)(2,1)S(1)}, u32[]{:S(2)}, u32[]{:S(2)}) collective-permute-start(bf16[16,1024]{1,0:T(8,128)(2,1)S(1)} %add_convert_fusion.1), channel_id=1, source_target_pairs={{0,4},{1,5},{2,6},{3,7},{4,0},{5,1},{6,2},{7,3},{8,12},{9,13},{10,... | collective-permute-start | bytes 98312 | tf_op jit(solution)/shard_map/ppermute | solution.py:489
  38.7 5.7 %collective-permute-start.9 = (bf16[16,1024]{1,0:T(8,128)(2,1)S(1)}, bf16[16,1024]{1,0:T(8,128)(2,1)S(1)}, u32[]{:S(2)}, u32[]{:S(2)}) collective-permute-start(bf16[16,1024]{1,0:T(8,128)(2,1)S(1)} %add_convert_fusion.1), channel_id=1, source_target_pairs={{0,2},{1,3},{2,4},{3,5},{4,6},{5,7},{6,0},{7,1},{8,10},{9,11},{10,... | collective-permute-start | bytes 98312 | tf_op jit(solution)/shard_map/ppermute | solution.py:489
  44.5 1.3 %collective-permute-start.12 = (bf16[16,1024]{1,0:T(8,128)(2,1)S(1)}, bf16[16,1024]{1,0:T(8,128)(2,1)S(1)}, u32[]{:S(2)}, u32[]{:S(2)}) collective-permute-start(bf16[16,1024]{1,0:T(8,128)(2,1)S(1)} %add_convert_fusion.side_ref.mine_ref), channel_id=1, source_target_pairs={{0,1},{1,0},{2,3},{3,2},{4,5},{5,4},{6,7},{7,6},{8,9},{9,8},{10,11... | collective-permute-start | bytes 98312 | tf_op jit(solution)/shard_map/ppermute | solution.py:491

commit v5 on v4

--- a/solution.py
+++ b/solution.py
@@ -58,9 +58,9 @@
     queries = jnp.concatenate(
         [jnp.where(core == 0, own, peer), jnp.where(core == 0, peer, own)], axis=1
     )
-    repeat = queries.shape[1] // cos_ref.shape[1]
-    cosine = jnp.concatenate([cos_ref[...]] * repeat, axis=1)
-    sine = jnp.concatenate([sin_ref[...]] * repeat, axis=1)
+    count, repeat = queries.shape[0], queries.shape[1] // cos_ref.shape[1]
+    cosine = jnp.concatenate([cos_ref[:count, :]] * repeat, axis=1)
+    sine = jnp.concatenate([sin_ref[:count, :]] * repeat, axis=1)
     queries = (queries * cosine + swap_halves(queries) * sine).astype(BF16).astype(F32)
     for step in range(chips):
         first = (chips - step) % chips * rows
@@ -71,6 +71,10 @@
             at = slice(c * LANE, (c + 1) * LANE)
             row = wire_row(rows, c, 0)
             out[row : row + rows, :] = queries[first : first + rows, at]
+
+
+def chip_away(step, chips):
+    return lax.rem(lax.axis_index("tensor") // 2 + chips - step, chips)
 
 
 def new_token_kernel(
@@ -85,28 +89,17 @@
     w_ref,
     cos_ref,
     sin_ref,
-    k_ref,
-    v_ref,
     new_ref,
-    side_ref,
+    key_ref,
     live_ref,
-    by_ref,
-    flat_ref,
 ):
     mark_live(len_ref, pos_ref, mask_ref, slot_pos_ref, live_ref)
     lanes = w_ref.shape[2]
     core = lax.axis_index("tensor") % 2
-    chip = lax.axis_index("tensor") // 2
     chips = same_ref.shape[0]
-    for step in range(chips):
-        source = 2 * lax.rem(chip + chips - step, chips)
-        by_ref[source + core, :rows, :] = same_ref[step].astype(F32)
-        by_ref[source + 1 - core, :rows, :] = peer_ref[step].astype(F32)
-    for group in range(2 * chips):
-        flat_ref[group * rows : (group + 1) * rows, :] = by_ref[group, :rows, :]
-    values = flat_ref[...]
-    width = side_ref.shape[1]
-    side_ref[...] = flat_ref[:, pl.ds(pl.multiple_of(core * width, LANE), width)]
+    values = jnp.concatenate(
+        [ref[step].astype(F32) for ref in (same_ref, peer_ref) for step in range(chips)], axis=0
+    )
     normed = normed_rows(values, gain_ref[...].astype(F32).reshape(1, -1))
     repeat = lanes // cos_ref.shape[1]
     cosine = jnp.concatenate([cos_ref[...]] * repeat, axis=1)
@@ -116,37 +109,60 @@
         return jnp.dot(normed, w_ref[part], preferred_element_type=F32)
 
     def turned(t):
-        return (t * cosine + swap_halves(t) * sine).astype(BF16)
+        return (t * cosine + swap_halves(t) * sine).astype(BF16).astype(F32)
 
     queries = turned(project(0))
     keys = turned(project(1))
-    values = project(2).astype(BF16)
-    k_ref[...] = keys
-    v_ref[...] = values
-    queries = queries.astype(F32)
+    values = project(2).astype(BF16).astype(F32)
     head_in = lax.broadcasted_iota(jnp.int32, (lanes, lanes), 0) // HEAD_SIZE
     head_out = lax.broadcasted_iota(jnp.int32, (lanes, lanes), 1) // HEAD_SIZE
     same_head = (head_in == head_out).astype(F32)
     score = jnp.dot(
-        queries * keys.astype(F32),
+        queries * keys,
         same_head,
         preferred_element_type=F32,
         precision=lax.Precision.HIGHEST,
     ) * (HEAD_SIZE**-0.5)
-    values = values.astype(F32)
-    groups, half, chunk = new_ref.shape[0], new_ref.shape[1] // 2, new_ref.shape[2]
-    for group in range(groups):
-        mine = slice(group * rows, (group + 1) * rows)
+    half, chunk = new_ref.shape[1] // 2, new_ref.shape[2]
+    for i in range(2 * chips):
+        group = 2 * chip_away(i % chips, chips) + (core if i < chips else 1 - core)
+        mine = slice(i * rows, (i + 1) * rows)
         for c in range(lanes // chunk):
             at = slice(c * chunk, (c + 1) * chunk)
             row = wire_row(rows, c, 0)
             new_ref[group, row : row + rows, :] = values[mine, at]
             new_ref[group, half + row : half + row + rows, :] = score[mine, at]
-
-
-def attention_kernel(lanes, chips, *refs):
-    queries, refs = refs[:chips], refs[chips:]
-    k_ref, v_ref, sink_k_ref, sink_v_ref, live_ref, out_ref = refs
+            key_ref[group, row : row + rows, :] = keys[mine, at]
+
+
+def outputs_kernel(same_ref, peer_ref, new_ref, key_ref, k_ref, v_ref, side_ref, by_ref, flat_ref):
+    chips, rows, _ = same_ref.shape
+    core = lax.axis_index("tensor") % 2
+    for step in range(chips):
+        source = 2 * chip_away(step, chips)
+        by_ref[source + core, :rows, :] = same_ref[step].astype(F32)
+        by_ref[source + 1 - core, :rows, :] = peer_ref[step].astype(F32)
+    for group in range(2 * chips):
+        flat_ref[group * rows : (group + 1) * rows, :] = by_ref[group, :rows, :]
+    width = side_ref.shape[1]
+    side_ref[...] = flat_ref[:, pl.ds(pl.multiple_of(core * width, LANE), width)]
+    lanes, chunk = k_ref.shape[1], new_ref.shape[2]
+    for from_ref, to_ref in ((key_ref, k_ref), (new_ref, v_ref)):
+        parts = []
+        for c in range(lanes // chunk):
+            row = wire_row(rows, c, 0)
+            parts.append(
+                jnp.concatenate(
+                    [from_ref[group, row : row + rows, :] for group in range(2 * chips)], axis=0
+                )
+            )
+        to_ref[...] = jnp.concatenate(parts, axis=1).astype(BF16)
+
+
+def attention_kernel(lanes, chips, steps, *refs):
+    queries, refs = dict(zip(steps, refs)), refs[len(steps) :]
+    k_ref, v_ref, sink_k_ref, sink_v_ref, live_ref = refs[:5]
+    out_ref = refs[-1]
     rows, features, slots = k_ref.shape
     sinks = sink_k_ref.shape[1]
     copies = out_ref.shape[0]
@@ -217,7 +233,7 @@
                 out_ref[copy, 2 * source + t, row : row + 1, :] = mixture[:, at]
                 out_ref[copy, 2 * source + t, half + row : half + row + 1, :] = level[:, at]
 
-    todo = [(r, step) for r in range(rows) for step in range(chips)]
+    todo = [(r, step) for step in steps for r in range(rows)]
     ahead = [scores(*one) for one in todo[:AHEAD]]
     for i, one in enumerate(todo):
         if i + AHEAD < len(todo):
@@ -332,10 +348,9 @@
     resid_ref[...] = by_ref[lax.axis_index("tensor"), :rows, :]
 
 
-def prepare_kernel(rows, pos_ref, cos_ref, sin_ref, query_cos_ref, query_sin_ref):
-    core = lax.axis_index("tensor") % 2
-    chip = lax.axis_index("tensor") // 2
-    chips = query_cos_ref.shape[0] // rows
+def prepare_kernel(rows, pos_ref, cos_ref, sin_ref):
+    core = lax.axis_index("tensor") % 2
+    chips = cos_ref.shape[0] // (2 * rows)
     wide = cos_ref.shape[1]
     half = HEAD_SIZE // 2
     pair = lax.broadcasted_iota(jnp.int32, (1, wide), 1) % half
@@ -343,25 +358,19 @@
     for i in range(half):
         inverse = jnp.where(pair == i, np.float32(ROTARY_BASE ** (-2 * i / HEAD_SIZE)), inverse)
 
-    def turn(positions, to_cos, to_sin):
-        shape = to_cos.shape
-        row = lax.broadcasted_iota(jnp.int32, shape, 0)
-        position = jnp.zeros(shape, F32)
-        for i, one in enumerate(positions):
-            position = jnp.where(row == i, one.astype(F32), position)
-        angle = position * inverse
-        sine = jnp.sin(angle)
-        lane = lax.broadcasted_iota(jnp.int32, shape, 1)
-        to_cos[...] = jnp.cos(angle)
-        to_sin[...] = jnp.where(lane % HEAD_SIZE < half, -sine, sine)
-
-    turn([pos_ref[i] for i in range(cos_ref.shape[0])], cos_ref, sin_ref)
-    sources = [2 * lax.rem(chip + chips - step, chips) + core for step in range(chips)]
-    turn(
-        [pos_ref[source * rows + r] for source in sources for r in range(rows)],
-        query_cos_ref,
-        query_sin_ref,
-    )
+    shape = cos_ref.shape
+    row = lax.broadcasted_iota(jnp.int32, shape, 0)
+    position = jnp.zeros(shape, F32)
+    for i in range(shape[0]):
+        group, r = divmod(i, rows)
+        parity = core if group < chips else 1 - core
+        request = (2 * chip_away(group % chips, chips) + parity) * rows + r
+        position = jnp.where(row == i, pos_ref[request].astype(F32), position)
+    angle = position * inverse
+    sine = jnp.sin(angle)
+    lane = lax.broadcasted_iota(jnp.int32, shape, 1)
+    cos_ref[...] = jnp.cos(angle)
+    sin_ref[...] = jnp.where(lane % HEAD_SIZE < half, -sine, sine)
 
 
 def mark_live(len_ref, pos_ref, mask_ref, slot_pos_ref, live_ref):
@@ -377,13 +386,14 @@
         live_ref[r : r + 1, :] = live.astype(jnp.int32)
 
 
-def call(kernel, out, inputs, specs=None, scratch=(), limit=6, name=None, flops=0):
+def call(kernel, out, inputs, specs=None, scratch=(), limit=6, name=None, flops=0, aliases={}):
     return pl.pallas_call(
         kernel,
         out_shape=out,
         in_specs=specs or [VMEM_SPEC] * len(inputs),
         out_specs=jax.tree.map(lambda _: VMEM_SPEC, out),
         scratch_shapes=scratch,
+        input_output_aliases=aliases,
         compiler_params=pltpu.CompilerParams(vmem_limit_bytes=limit * MIB),
         name=name,
         cost_estimate=pl.CostEstimate(
@@ -422,10 +432,9 @@
 
     chips = groups // 2
     turn = sds((batch, chunk), F32)
-    query_turn = sds((batch // 2, chunk), F32)
-    cosine, sine, query_cos, query_sin = call(
+    cosine, sine = call(
         functools.partial(prepare_kernel, rows),
-        (turn, turn, query_turn, query_turn),
+        (turn, turn),
         (new_pos,),
         specs=[SMEM_SPEC],
         name="prepare",
@@ -440,41 +449,49 @@
     queries = call(
         functools.partial(query_kernel, rows, chips),
         (query_wire,) * chips,
-        (*column, attn_gain, w_qkv, w_peer, query_cos, query_sin),
+        (*column, attn_gain, w_qkv, w_peer, cosine, sine),
         name="query",
         flops=QKV_FLOPS,
     )
+    same = jnp.stack(column)
+    peer = lax.ppermute(same, "tensor", across)
+    same, *queries = lax.optimization_barrier((same, *queries))
     queries = [queries[0]] + [
         lax.ppermute(query, "tensor", hop) for query, hop in zip(queries[1:], hops)
     ]
-    same = jnp.stack(column)
-    peer = lax.ppermute(same, "tensor", across)
-    side = sds((batch, width // 2), F32)
     wire = sds((groups, wire_rows, chunk), F32)
-    flat = sds((batch, lanes), BF16)
-    new_keys, new_values, new_part, own_side, live = call(
+    new_part, key_part, live = call(
         functools.partial(new_token_kernel, rows),
-        (flat, flat, wire, side, sds(slot_mask.shape, jnp.int32)),
+        (wire, wire, sds(slot_mask.shape, jnp.int32)),
         (cache_len, new_pos, slot_mask, slot_pos, same, peer, attn_gain, w_qkv, cosine, sine),
         specs=[SMEM_SPEC] * 2 + [VMEM_SPEC] * 8,
-        scratch=[pltpu.VMEM((groups, 8, width), F32), pltpu.VMEM((batch, width), F32)],
         name="new_token",
         flops=QKV_FLOPS,
     )
-    queries, new_part = lax.optimization_barrier((queries, new_part))
     sink_keys = jnp.transpose(sink_keys, (0, 2, 1))
     sink_values = jnp.transpose(sink_values, (0, 2, 1))
-    part = call(
-        functools.partial(attention_kernel, lanes, chips),
-        sds((shards, groups, wire_rows, chunk), F32),
-        (*queries, key_cache, value_cache, sink_keys, sink_values, live),
-        limit=8,
-        name="attention",
-        flops=ATT_FLOPS,
+
+    def attention(steps, arrays, aliases, name):
+        return call(
+            functools.partial(attention_kernel, lanes, chips, steps),
+            sds((shards, groups, wire_rows, chunk), F32),
+            arrays,
+            limit=8,
+            name=name,
+            flops=ATT_FLOPS,
+            aliases=aliases,
+        )
+
+    cache = (key_cache, value_cache, sink_keys, sink_values, live)
+    part = attention((0,), (queries[0], *cache), {}, "own_heads")
+    queries, new_part, part = lax.optimization_barrier((queries, new_part, part))
+    part = attention(
+        tuple(range(1, chips)), (*queries[1:], *cache, part), {chips + 4: 0}, "other_heads"
     )
     part = lax.all_to_all(
         part.reshape(shards * groups, wire_rows, chunk), ("seq", "tensor"), 0, 0, tiled=True
     ).reshape(shards, groups, wire_rows, chunk)
+    side = sds((batch, width // 2), F32)
     mine, other = call(
         functools.partial(merge_kernel, rows),
         (side, side),
@@ -484,6 +501,17 @@
         flops=MERGE_FLOPS,
     )
     chip = (mine + lax.ppermute(other, "tensor", across)).astype(BF16)
+    flat = sds((batch, lanes), BF16)
+    chip, same, peer, new_part, key_part = lax.optimization_barrier(
+        (chip, same, peer, new_part, key_part)
+    )
+    new_keys, new_values, own_side = call(
+        outputs_kernel,
+        (flat, flat, side),
+        (same, peer, new_part, key_part),
+        scratch=[pltpu.VMEM((groups, 8, width), F32), pltpu.VMEM((batch, width), F32)],
+        name="outputs",
+    )
     total = chip.astype(F32)
     for hop in hops:
         total = total + lax.ppermute(chip, "tensor", hop).astype(F32)

time: 56.5 us -> 55.7 us (0.986)
  starting transfers between devices: 15.4 us -> 14.5 us
    ppermute x3, starting transfers between devices: 7.49 us -> 6.57 us  [per_device(): column = [states] + [lax.ppermute(states, 'tensor', hop) for hop in hops]]
    ppermute x3, waiting for transfers between devices: 0.52 us -> 1.19 us  [per_device(): column = [states] + [lax.ppermute(states, 'tensor', hop) for hop in hops]]
    ppermute x3, waiting for transfers between devices: 1.59 us -> 0.92 us  [per_device(): lax.ppermute(query, 'tensor', hop)]
    pallas_call x7 -> x9, Pallas kernels: 9.61 us -> 9.89 us  [call(): pl.pallas_call(kernel, out_shape=out, in_specs=specs or [VMEM_SPEC] * len...]
  transfers between devices with their start and end apart: 13 -> 13, of which waited for: 7 -> 6; matrix products, arithmetic and copies ran while one was open for 0% -> 0% of each run, Pallas kernels for 7% -> 10%
where the time goes in v5:
time: 55.7 us; the launch traced here: 55.5 us
  blocking collectives  20.4 us (37%)
  starting transfers between devices  14.5 us (26%)
  Pallas kernels  9.89 us (18%)
  waiting for transfers between devices  8.18 us (15%)
  between operations  0.98 us (2%)
  other arithmetic  0.76 us (1%)
  local copies, waits for them, and re-layouts  0.73 us (1%)
    all_to_all x1, blocking collectives, per_device(): lax.all_to_all(part.reshape(shards * groups, wire_rows, chunk), ('seq', '...  12.1 us
    pallas_call x9, Pallas kernels, call(): pl.pallas_call(kernel, out_shape=out, in_specs=specs or [VMEM_SPEC] * len...  9.89 us
    all_to_all x1, blocking collectives, per_device(): partial = lax.all_to_all(partial, 'tensor', 0, 0, tiled=True)  8.29 us
    ppermute x3, starting transfers between devices, per_device(): column = [states] + [lax.ppermute(states, 'tensor', hop) for hop in hops]  6.57 us
    ppermute x3, waiting for transfers between devices, per_device(): total = total + lax.ppermute(chip, 'tensor', hop).astype(F32)  5.03 us
    ppermute x3, starting transfers between devices, per_device(): lax.ppermute(query, 'tensor', hop)  3.88 us
    ppermute x3, starting transfers between devices, per_device(): total = total + lax.ppermute(chip, 'tensor', hop).astype(F32)  3.01 us
    ppermute x3, waiting for transfers between devices, per_device(): column = [states] + [lax.ppermute(states, 'tensor', hop) for hop in hops]  1.19 us
  transfers between devices with their start and end apart: 13, of which 6 were waited for; matrix products, arithmetic and copies ran while one was open for 0% of the time, Pallas kernels for 10%

profile of v5, /device:TPU:0, one launch (start us, length us, event | category | flops | bytes accessed | tf_op | source)
XLA Modules:
  0.0 55.5 jit_solution(7013146302481945905)
XLA Ops:
  0.6 0.0 slice-start.2
  0.6 0.0 slice-start.4
  0.7 0.0 slice-start.3
  0.7 0.0 slice-start.5
  0.7 0.5 collective-permute-start.3
  1.3 2.6 %collective-permute-start = (bf16[2,2048]{1,0:T(2,128)(2,1)}, bf16[2,2048]{1,0:T(2,128)(2,1)S(1)}, u32[]{:S(2)}, u32[]{:S(2)}) collective-permute-start(bf16[2,2048]{1,0:T(2,128)(2,1)} %refs_0_.1), channel_id=1, source_target_pairs={{0,2},{1,3},{2,4},{3,5},{4,6},{5,7},{6,0},{7,1},{8,10},{9,11},{10,... | collective-permute-start | bytes 24584 | tf_op jit(solution)/shard_map/ppermute | solution.py:445
  3.9 2.6 %collective-permute-start.1 = (bf16[2,2048]{1,0:T(2,128)(2,1)}, bf16[2,2048]{1,0:T(2,128)(2,1)S(1)}, u32[]{:S(2)}, u32[]{:S(2)}) collective-permute-start(bf16[2,2048]{1,0:T(2,128)(2,1)} %refs_0_.1), channel_id=1, source_target_pairs={{0,4},{1,5},{2,6},{3,7},{4,0},{5,1},{6,2},{7,3},{8,12},{9,13},{10,... | collective-permute-start | bytes 24584 | tf_op jit(solution)/shard_map/ppermute | solution.py:445
  6.5 1.3 %collective-permute-start.2 = (bf16[2,2048]{1,0:T(2,128)(2,1)}, bf16[2,2048]{1,0:T(2,128)(2,1)S(1)}, u32[]{:S(2)}, u32[]{:S(2)}) collective-permute-start(bf16[2,2048]{1,0:T(2,128)(2,1)} %refs_0_.1), channel_id=1, source_target_pairs={{0,6},{1,7},{2,0},{3,1},{4,2},{5,3},{6,4},{7,5},{8,14},{9,15},{10,... | collective-permute-start | bytes 24584 | tf_op jit(solution)/shard_map/ppermute | solution.py:445
  7.8 0.7 %copy-done.11 = s32[16]{0:T(128)S(1)} copy-done((s32[16]{0:T(128)S(1)}, s32[16]{0:T(128)}, u32[]{:S(2)}) %copy-start.11) | copy-done | bytes 88
  8.5 0.6 %prepare.1 = (f32[16,128]{1,0:T(8,128)S(1)}, f32[16,128]{1,0:T(8,128)S(1)}) custom-call(s32[16]{0:T(128)S(1)} %copy-done.11), custom_call_target="tpu_custom_call" | custom-call | flops 20000000000 | bytes 64 | tf_op jit(solution)/shard_map/prepare/pallas_call | solution.py:390
  9.1 0.0 copy-start.5
  9.1 0.0 copy-start.6
  9.1 0.0 collective-permute-done.refs_1_
  9.2 0.0 collective-permute-done.1.refs_2_
  9.2 1.2 %collective-permute-done.2.refs_3_ = bf16[2,2048]{1,0:T(2,128)(2,1)S(1)} collective-permute-done((bf16[2,2048]{1,0:T(2,128)(2,1)}, bf16[2,2048]{1,0:T(2,128)(2,1)S(1)}, u32[]{:S(2)}, u32[]{:S(2)}) %collective-permute-start.2) | collective-permute-done | bytes 8224 | tf_op jit(solution)/shard_map/ppermute | solution.py:445
  10.3 0.0 copy-done.2
  10.3 0.1 pad_maximum_fusion.same_ref
  10.4 0.1 collective-permute-start.7
  10.5 0.0 collective-permute-done.3.refs_6_
  10.5 0.6 %query.1 = (f32[8,128]{1,0:T(8,128)S(1)}, f32[8,128]{1,0:T(8,128)S(1)}, f32[8,128]{1,0:T(8,128)S(1)}, f32[8,128]{1,0:T(8,128)S(1)}) custom-call(bf16[2,2048]{1,0:T(2,128)(2,1)S(1)} %copy-done.2, bf16[2,2048]{1,0:T(2,128)(2,1)S(1)} %collective-permute-done.refs_1_, bf16[2,2048]{1,0:T(2,128)(2,1)S(1)} %collective-permute-done.1.refs_2_, ...), custom_call_target="tpu_custom_call" | custom-call | flops 2000000000 | bytes 6344704 | tf_op jit(solution)/shard_map/query/pallas_call | solution.py:390
  11.1 0.3 collective-permute-start.4
  11.4 3.4 %collective-permute-start.5 = (f32[8,128]{1,0:T(8,128)S(1)}, f32[8,128]{1,0:T(8,128)S(1)}, u32[]{:S(2)}, u32[]{:S(2)}) collective-permute-start(f32[8,128]{1,0:T(8,128)S(1)} %get-tuple-element.44), channel_id=1, source_target_pairs={{0,4},{1,5},{2,6},{3,7},{4,0},{5,1},{6,2},{7,3},{8,12},{9,13},{10,... | collective-permute-start | bytes 12296 | tf_op jit(solution)/shard_map/ppermute | solution.py:460
  14.8 0.1 collective-permute-start.6
  15.0 0.0 collective-permute-done.7.peer_ref
  15.0 1.5 %new_token.1 = (f32[8,8,128]{2,1,0:T(8,128)S(1)}, f32[8,8,128]{2,1,0:T(8,128)S(1)}, s32[2,1024]{1,0:T(2,128)S(1)}) custom-call(s32[16]{0:T(128)S(1)} %copy-done.10, s32[16]{0:T(128)S(1)} %copy-done.12, s32[2,1024]{1,0:T(2,128)S(1)} %copy-done.7, s32[2,1024]{1,0:T(2,128)S(1)} %copy-done.8, bf16[4,2,2048]{2,1,0:T(2,128)(2,1)S(1)} %pad_maximum_fusion.same_ref, ...), custom_call_target="tpu_custom_call" | custom-call | flops 2000000000 | bytes 3248256 | tf_op jit(solution)/shard_map/new_token/pallas_call | solution.py:390
  16.5 1.0 %own_heads.1.refs_8_ = f32[4,8,8,128]{3,2,1,0:T(8,128)S(1)} custom-call(f32[8,128]{1,0:T(8,128)S(1)} %get-tuple-element.42.refs_0_, bf16[2,2048,1024]{2,1,0:T(8,128)(2,1)S(1)} %bitcast.18, bf16[2,2048,1024]{2,1,0:T(8,128)(2,1)S(1)} %bitcast.20, bf16[2,4,2048]{2,1,0:T(4,128)(2,1)S(1)} %bitcast.24, bf16[2,4,2048]{2,1,0:T(4,128)(2,1)S(1)} %bitcast.26, ...), custom_call_target="tpu_custom_call" | custom-call | flops 10000000000 | bytes 16855040 | tf_op jit(solution)/shard_map/own_heads/pallas_call | solution.py:390
  17.5 0.0 collective-permute-done.4.refs_0_
  17.5 0.0 collective-permute-done.5.refs_1_
  17.5 0.9 %collective-permute-done.6.refs_2_ = f32[8,128]{1,0:T(8,128)S(1)} collective-permute-done((f32[8,128]{1,0:T(8,128)S(1)}, f32[8,128]{1,0:T(8,128)S(1)}, u32[]{:S(2)}, u32[]{:S(2)}) %collective-permute-start.6) | collective-permute-done | bytes 4128 | tf_op jit(solution)/shard_map/ppermute | solution.py:460
  18.5 2.6 %other_heads.1 = f32[4,8,8,128]{3,2,1,0:T(8,128)S(1)} custom-call(f32[8,128]{1,0:T(8,128)S(1)} %collective-permute-done.4.refs_0_, f32[8,128]{1,0:T(8,128)S(1)} %collective-permute-done.5.refs_1_, f32[8,128]{1,0:T(8,128)S(1)} %collective-permute-done.6.refs_2_, bf16[2,2048,1024]{2,1,0:T(8,128)(2,1)S(1)} %bitcast.18, ...), custom_call_target="tpu_custom_call", output_to_operand_aliasing={{}: (8, {})} | custom-call | flops 10000000000 | bytes 16994304 | tf_op jit(solution)/shard_map/other_heads/pallas_call | solution.py:390
  21.1 12.1 %all_to_all.10 = f32[32,8,128]{2,1,0:T(8,128)S(1)} all-to-all(f32[32,8,128]{2,1,0:T(8,128)S(1)} %bitcast.11), channel_id=1, replica_groups=mesh['seq'=4,'tensor'=8] {'seq','tensor'}, dimensions={0} | all-to-all | bytes 262144 | tf_op jit(solution)/shard_map/all_to_all | solution.py:491
  33.2 0.3 merge.1
  33.5 0.4 collective-permute-start.8
  33.9 0.9 %collective-permute-done.8 = f32[16,1024]{1,0:T(8,128)S(1)} collective-permute-done((f32[16,1024]{1,0:T(8,128)S(1)}, f32[16,1024]{1,0:T(8,128)S(1)}, u32[]{:S(2)}, u32[]{:S(2)}) %collective-permute-start.8) | collective-permute-done | bytes 65568 | tf_op jit(solution)/shard_map/ppermute | solution.py:503
  34.9 0.5 collective-permute-start.10
  35.3 2.6 %collective-permute-start.11 = (bf16[16,1024]{1,0:T(8,128)(2,1)S(1)}, bf16[16,1024]{1,0:T(8,128)(2,1)S(1)}, u32[]{:S(2)}, u32[]{:S(2)}) collective-permute-start(bf16[16,1024]{1,0:T(8,128)(2,1)S(1)} %add_convert_fusion.1), channel_id=1, source_target_pairs={{0,6},{1,7},{2,0},{3,1},{4,2},{5,3},{6,4},{7,5},{8,14},{9,15},{10,... | collective-permute-start | bytes 98312 | tf_op jit(solution)/shard_map/ppermute | solution.py:517
  37.9 0.0 collective-permute-start.9
  37.9 0.7 %outputs.1 = (bf16[16,256]{1,0:T(8,128)(2,1)}, bf16[16,256]{1,0:T(8,128)(2,1)}, f32[16,1024]{1,0:T(8,128)S(1)}) custom-call(bf16[4,2,2048]{2,1,0:T(2,128)(2,1)S(1)} %pad_maximum_fusion.same_ref, bf16[4,2,2048]{2,1,0:T(2,128)(2,1)S(1)} %collective-permute-done.7.peer_ref, f32[8,8,128]{2,1,0:T(8,128)S(1)} %get-tuple-element.59.new_ref, ...), custom_call_target="tpu_custom_call" | custom-call | bytes 131072 | tf_op jit(solution)/shard_map/outputs/pallas_call | solution.py:390
  38.6 1.8 %collective-permute-done.10 = bf16[16,1024]{1,0:T(8,128)(2,1)S(1)} collective-permute-done((bf16[16,1024]{1,0:T(8,128)(2,1)S(1)}, bf16[16,1024]{1,0:T(8,128)(2,1)S(1)}, u32[]{:S(2)}, u32[]{:S(2)}) %collective-permute-start.10) | collective-permute-done | bytes 32800 | tf_op jit(solution)/shard_map/ppermute | solution.py:517
  40.4 0.0 collective-permute-done.11
  40.4 3.2 %collective-permute-done.9 = bf16[16,1024]{1,0:T(8,128)(2,1)S(1)} collective-permute-done((bf16[16,1024]{1,0:T(8,128)(2,1)S(1)}, bf16[16,1024]{1,0:T(8,128)(2,1)S(1)}, u32[]{:S(2)}, u32[]{:S(2)}) %collective-permute-start.9) | collective-permute-done | bytes 32800 | tf_op jit(solution)/shard_map/ppermute | solution.py:517
  43.6 0.1 collective-permute-start.12
  43.7 1.1 %first_half.1 = (f32[32,1024]{1,0:T(8,128)S(1)}, f32[16,128]{1,0:T(8,128)S(1)}) custom-call(bf16[16,1024]{1,0:T(8,128)(2,1)S(1)} %add_convert_fusion.side_ref.mine_ref, bf16[2048]{0:T(1024)(128)(2,1)S(1)} %copy-done.1, bf16[2048,2,1024]{2,1,0:T(2,128)(2,1)S(1)} %bitcast.10), custom_call_target="tpu_custom_call" | custom-call | flops 67108864 | bytes 8425472 | tf_op jit(solution)/shard_map/first_half/pallas_call | solution.py:390
  44.8 0.1 collective-permute-done.12.other_ref
  44.9 1.6 %mlp.1 = (bf16[8,2,2048]{2,1,0:T(2,128)(2,1)S(1)}, f32[2,2048]{1,0:T(2,128)S(1)}) custom-call(bf16[16,1024]{1,0:T(8,128)(2,1)S(1)} %add_convert_fusion.side_ref.mine_ref, bf16[16,1024]{1,0:T(8,128)(2,1)S(1)} %collective-permute-done.12.other_ref, bf16[2048]{0:T(1024)(128)(2,1)S(1)} %copy-done.1, bf16[2048,2,1024]{2,1,0:T(2,128)(2,1)S(1)} %bitcast.10, ...), custom_call_target="tpu_custom_call" | custom-call | flops 134217728 | bytes 12791808 | tf_op jit(solution)/shard_map/mlp/pallas_call | solution.py:390
  46.5 8.3 %all_to_all.11 = bf16[8,2,2048]{2,1,0:T(2,128)(2,1)S(1)} all-to-all(bf16[8,2,2048]{2,1,0:T(2,128)(2,1)S(1)} %get-tuple-element.66), channel_id=1, replica_groups=mesh['seq'=4,'tensor'=8] {'tensor'}, dimensions={0} | all-to-all | bytes 131072 | tf_op jit(solution)/shard_map/all_to_all | solution.py:539
  54.8 0.1 convert_reduce_fusion
  54.9 0.6 %add_convert_fusion.2 = bf16[2,2048]{1,0:T(2,128)(2,1)} fusion(f32[2,2048]{1,0:T(2,128)S(1)} %get-tuple-element.65, f32[2,2048]{1,0:T(2,128)S(1)} %convert_reduce_fusion), kind=kLoop, calls=%fused_computation.4 | loop fusion | flops 8192 | bytes 40960 | tf_op jit(solution)/shard_map/convert_element_type | solution.py:540
  (35 shorter events, 0.1 us)
Async XLA Ops:
  0.6 15.8 %slice-start.2 = ((s8[8388608]{0:T(1024)(128)(4,1)}), s8[4194304]{0:T(1024)(128)(4,1)S(1)}, s32[]{:S(2)}) async-start(s8[8388608]{0:T(1024)(128)(4,1)} %bitcast.17), calls=%async_computation.4 | async-start | bytes 8388608
  0.6 15.8 %slice-start.4 = ((s8[8388608]{0:T(1024)(128)(4,1)}), s8[4194304]{0:T(1024)(128)(4,1)S(1)}, s32[]{:S(2)}) async-start(s8[8388608]{0:T(1024)(128)(4,1)} %bitcast.19), calls=%async_computation.6 | async-start | bytes 8388608
  0.7 9.7 %copy-start.2 = (bf16[2,2048]{1,0:T(2,128)(2,1)S(1)}, bf16[2,2048]{1,0:T(2,128)(2,1)}, u32[]{:S(2)}) copy-start(bf16[2,2048]{1,0:T(2,128)(2,1)} %refs_0_.1) | copy-start | bytes 24580
  0.7 9.8 %copy-start.3 = (bf16[2048,3,256]{2,0,1:T(8,128)(2,1)S(1)}, bf16[2048,3,256]{2,0,1:T(8,128)(2,1)}, u32[]{:S(2)}) copy-start(bf16[2048,3,256]{2,0,1:T(8,128)(2,1)} %param.17) | copy-start | bytes 9437188
  0.7 9.8 %copy-start.9 = (bf16[2048]{0:T(1024)(128)(2,1)S(1)}, bf16[2048]{0:T(1024)(128)(2,1)}, u32[]{:S(2)}) copy-start(bf16[2048]{0:T(1024)(128)(2,1)} %gain_ref.3) | copy-start | bytes 12292
  0.7 14.3 %copy-start.7 = (s32[2,1024]{1,0:T(2,128)S(1)}, s32[2,1024]{1,0:T(2,128)}, u32[]{:S(2)}) copy-start(s32[2,1024]{1,0:T(2,128)} %mask_ref.1) | copy-start | bytes 24580
  0.7 14.3 %copy-start.8 = (s32[2,1024]{1,0:T(2,128)S(1)}, s32[2,1024]{1,0:T(2,128)}, u32[]{:S(2)}) copy-start(s32[2,1024]{1,0:T(2,128)} %slot_pos_ref.1) | copy-start | bytes 24580
  0.7 14.3 %copy-start.10 = (s32[16]{0:T(128)S(1)}, s32[16]{0:T(128)}, u32[]{:S(2)}) copy-start(s32[16]{0:T(128)} %len_ref.1) | copy-start | bytes 196
  0.7 15.8 %slice-start.3 = ((s8[8388608]{0:T(1024)(128)(4,1)}), s8[4194304]{0:T(1024)(128)(4,1)S(1)}, s32[]{:S(2)}) async-start(s8[8388608]{0:T(1024)(128)(4,1)} %bitcast.17), calls=%async_computation.5 | async-start | bytes 8388608
  0.7 15.8 %slice-start.5 = ((s8[8388608]{0:T(1024)(128)(4,1)}), s8[4194304]{0:T(1024)(128)(4,1)S(1)}, s32[]{:S(2)}) async-start(s8[8388608]{0:T(1024)(128)(4,1)} %bitcast.19), calls=%async_computation.7 | async-start | bytes 8388608
  0.7 9.8 %collective-permute-start.3 = (bf16[3,2048,256]{2,1,0:T(8,128)(2,1)}, bf16[3,2048,256]{2,1,0:T(8,128)(2,1)S(1)}, u32[]{:S(2)}, u32[]{:S(2)}) collective-permute-start(bf16[3,2048,256]{2,1,0:T(8,128)(2,1)} %bitcast.21), channel_id=1, source_target_pairs={{0,1},{1,0},{2,3},{3,2},{4,5},{5,4},{6,7},{7,6},{8,9},{9,8},{10,11... | collective-permute-start | bytes 9437192 | tf_op jit(solution)/shard_map/ppermute | solution.py:447
  1.3 7.9 %collective-permute-start = (bf16[2,2048]{1,0:T(2,128)(2,1)}, bf16[2,2048]{1,0:T(2,128)(2,1)S(1)}, u32[]{:S(2)}, u32[]{:S(2)}) collective-permute-start(bf16[2,2048]{1,0:T(2,128)(2,1)} %refs_0_.1), channel_id=1, source_target_pairs={{0,2},{1,3},{2,4},{3,5},{4,6},{5,7},{6,0},{7,1},{8,10},{9,11},{10,... | collective-permute-start | bytes 24584 | tf_op jit(solution)/shard_map/ppermute | solution.py:445
  3.9 5.3 %collective-permute-start.1 = (bf16[2,2048]{1,0:T(2,128)(2,1)}, bf16[2,2048]{1,0:T(2,128)(2,1)S(1)}, u32[]{:S(2)}, u32[]{:S(2)}) collective-permute-start(bf16[2,2048]{1,0:T(2,128)(2,1)} %refs_0_.1), channel_id=1, source_target_pairs={{0,4},{1,5},{2,6},{3,7},{4,0},{5,1},{6,2},{7,3},{8,12},{9,13},{10,... | collective-permute-start | bytes 24584 | tf_op jit(solution)/shard_map/ppermute | solution.py:445
  6.5 3.9 %collective-permute-start.2 = (bf16[2,2048]{1,0:T(2,128)(2,1)}, bf16[2,2048]{1,0:T(2,128)(2,1)S(1)}, u32[]{:S(2)}, u32[]{:S(2)}) collective-permute-start(bf16[2,2048]{1,0:T(2,128)(2,1)} %refs_0_.1), channel_id=1, source_target_pairs={{0,6},{1,7},{2,0},{3,1},{4,2},{5,3},{6,4},{7,5},{8,14},{9,15},{10,... | collective-permute-start | bytes 24584 | tf_op jit(solution)/shard_map/ppermute | solution.py:445
  7.8 0.7 %copy-start.11 = (s32[16]{0:T(128)S(1)}, s32[16]{0:T(128)}, u32[]{:S(2)}) copy-start(s32[16]{0:T(128)} %pos_ref.3) | copy-start | bytes 196
  8.5 6.5 %copy-start.12 = (s32[16]{0:T(128)S(1)}, s32[16]{0:T(128)}, u32[]{:S(2)}) copy-start(s32[16]{0:T(128)} %pos_ref.3) | copy-start | bytes 196
  9.1 7.4 %copy-start.5 = (bf16[2,2048,4]{1,2,0:T(4,128)(2,1)S(1)}, bf16[2,2048,4]{1,2,0:T(4,128)(2,1)}, u32[]{:S(2)}) copy-start(bf16[2,2048,4]{1,2,0:T(4,128)(2,1)} %param.24) | copy-start | bytes 98308
  9.1 7.4 %copy-start.6 = (bf16[2,2048,4]{1,2,0:T(4,128)(2,1)S(1)}, bf16[2,2048,4]{1,2,0:T(4,128)(2,1)}, u32[]{:S(2)}) copy-start(bf16[2,2048,4]{1,2,0:T(4,128)(2,1)} %param.25) | copy-start | bytes 98308
  10.4 4.6 %collective-permute-start.7 = (bf16[4,2,2048]{2,1,0:T(2,128)(2,1)S(1)}, bf16[4,2,2048]{2,1,0:T(2,128)(2,1)S(1)}, u32[]{:S(2)}, u32[]{:S(2)}) collective-permute-start(bf16[4,2,2048]{2,1,0:T(2,128)(2,1)S(1)} %pad_maximum_fusion.same_ref), channel_id=1, source_target_pairs={{0,1},{1,0},{2,3},{3,2},{4,5},{5,4},{6,7},{7,6},{8,9},{9,8},{10,11... | collective-permute-start | bytes 98312 | tf_op jit(solution)/shard_map/ppermute | solution.py:457
  11.1 6.4 %collective-permute-start.4 = (f32[8,128]{1,0:T(8,128)S(1)}, f32[8,128]{1,0:T(8,128)S(1)}, u32[]{:S(2)}, u32[]{:S(2)}) collective-permute-start(f32[8,128]{1,0:T(8,128)S(1)} %get-tuple-element.43), channel_id=1, source_target_pairs={{0,2},{1,3},{2,4},{3,5},{4,6},{5,7},{6,0},{7,1},{8,10},{9,11},{10,... | collective-permute-start | bytes 12296 | tf_op jit(solution)/shard_map/ppermute | solution.py:460
  11.4 6.1 %collective-permute-start.5 = (f32[8,128]{1,0:T(8,128)S(1)}, f32[8,128]{1,0:T(8,128)S(1)}, u32[]{:S(2)}, u32[]{:S(2)}) collective-permute-start(f32[8,128]{1,0:T(8,128)S(1)} %get-tuple-element.44), channel_id=1, source_target_pairs={{0,4},{1,5},{2,6},{3,7},{4,0},{5,1},{6,2},{7,3},{8,12},{9,13},{10,... | collective-permute-start | bytes 12296 | tf_op jit(solution)/shard_map/ppermute | solution.py:460
  14.8 3.6 %collective-permute-start.6 = (f32[8,128]{1,0:T(8,128)S(1)}, f32[8,128]{1,0:T(8,128)S(1)}, u32[]{:S(2)}, u32[]{:S(2)}) collective-permute-start(f32[8,128]{1,0:T(8,128)S(1)} %get-tuple-element.45), channel_id=1, source_target_pairs={{0,6},{1,7},{2,0},{3,1},{4,2},{5,3},{6,4},{7,5},{8,14},{9,15},{10,... | collective-permute-start | bytes 12296 | tf_op jit(solution)/shard_map/ppermute | solution.py:460
  18.4 14.8 %copy-start.4 = (bf16[256,2048]{1,0:T(8,128)(2,1)S(1)}, bf16[256,2048]{1,0:T(8,128)(2,1)}, u32[]{:S(2)}) copy-start(bf16[256,2048]{1,0:T(8,128)(2,1)} %w_ref.1) | copy-start | bytes 3145732
  18.5 25.2 %slice-start = ((s8[8388608]{0:T(1024)(128)(4,1)}), s8[4194304]{0:T(1024)(128)(4,1)S(1)}, s32[]{:S(2)}) async-start(s8[8388608]{0:T(1024)(128)(4,1)} %bitcast.9), calls=%async_computation.2 | async-start | bytes 8388608
  33.2 10.5 %slice-start.1 = ((s8[8388608]{0:T(1024)(128)(4,1)}), s8[4194304]{0:T(1024)(128)(4,1)S(1)}, s32[]{:S(2)}) async-start(s8[8388608]{0:T(1024)(128)(4,1)} %bitcast.9), calls=%async_computation.3 | async-start | bytes 8388608
  33.2 10.5 %copy-start.1 = (bf16[2048]{0:T(1024)(128)(2,1)S(1)}, bf16[2048]{0:T(1024)(128)(2,1)}, u32[]{:S(2)}) copy-start(bf16[2048]{0:T(1024)(128)(2,1)} %gain_ref.5) | copy-start | bytes 12292
  33.5 11.4 %copy-start = (bf16[1024,2048]{1,0:T(8,128)(2,1)S(1)}, bf16[1024,2048]{1,0:T(8,128)(2,1)}, u32[]{:S(2)}) copy-start(bf16[1024,2048]{1,0:T(8,128)(2,1)} %down_ref.1) | copy-start | bytes 12582916
  33.5 1.3 %collective-permute-start.8 = (f32[16,1024]{1,0:T(8,128)S(1)}, f32[16,1024]{1,0:T(8,128)S(1)}, u32[]{:S(2)}, u32[]{:S(2)}) collective-permute-start(f32[16,1024]{1,0:T(8,128)S(1)} %get-tuple-element.55), channel_id=1, source_target_pairs={{0,1},{1,0},{2,3},{3,2},{4,5},{5,4},{6,7},{7,6},{8,9},{9,8},{10,11... | collective-permute-start | bytes 196616 | tf_op jit(solution)/shard_map/ppermute | solution.py:503
  34.9 5.5 %collective-permute-start.10 = (bf16[16,1024]{1,0:T(8,128)(2,1)S(1)}, bf16[16,1024]{1,0:T(8,128)(2,1)S(1)}, u32[]{:S(2)}, u32[]{:S(2)}) collective-permute-start(bf16[16,1024]{1,0:T(8,128)(2,1)S(1)} %add_convert_fusion.1), channel_id=1, source_target_pairs={{0,4},{1,5},{2,6},{3,7},{4,0},{5,1},{6,2},{7,3},{8,12},{9,13},{10,... | collective-permute-start | bytes 98312 | tf_op jit(solution)/shard_map/ppermute | solution.py:517
  35.3 5.0 %collective-permute-start.11 = (bf16[16,1024]{1,0:T(8,128)(2,1)S(1)}, bf16[16,1024]{1,0:T(8,128)(2,1)S(1)}, u32[]{:S(2)}, u32[]{:S(2)}) collective-permute-start(bf16[16,1024]{1,0:T(8,128)(2,1)S(1)} %add_convert_fusion.1), channel_id=1, source_target_pairs={{0,6},{1,7},{2,0},{3,1},{4,2},{5,3},{6,4},{7,5},{8,14},{9,15},{10,... | collective-permute-start | bytes 98312 | tf_op jit(solution)/shard_map/ppermute | solution.py:517
  37.9 5.7 %collective-permute-start.9 = (bf16[16,1024]{1,0:T(8,128)(2,1)S(1)}, bf16[16,1024]{1,0:T(8,128)(2,1)S(1)}, u32[]{:S(2)}, u32[]{:S(2)}) collective-permute-start(bf16[16,1024]{1,0:T(8,128)(2,1)S(1)} %add_convert_fusion.1), channel_id=1, source_target_pairs={{0,2},{1,3},{2,4},{3,5},{4,6},{5,7},{6,0},{7,1},{8,10},{9,11},{10,... | collective-permute-start | bytes 98312 | tf_op jit(solution)/shard_map/ppermute | solution.py:517
  43.6 1.3 %collective-permute-start.12 = (bf16[16,1024]{1,0:T(8,128)(2,1)S(1)}, bf16[16,1024]{1,0:T(8,128)(2,1)S(1)}, u32[]{:S(2)}, u32[]{:S(2)}) collective-permute-start(bf16[16,1024]{1,0:T(8,128)(2,1)S(1)} %add_convert_fusion.side_ref.mine_ref), channel_id=1, source_target_pairs={{0,1},{1,0},{2,3},{3,2},{4,5},{5,4},{6,7},{7,6},{8,9},{9,8},{10,11... | collective-permute-start | bytes 98312 | tf_op jit(solution)/shard_map/ppermute | solution.py:519

commit v6 on v5

--- a/solution.py
+++ b/solution.py
@@ -513,8 +513,8 @@
         name="outputs",
     )
     total = chip.astype(F32)
-    for hop in hops:
-        total = total + lax.ppermute(chip, "tensor", hop).astype(F32)
+    for which in range(0, -len(hops), -1):
+        total = total + lax.ppermute(chip, "tensor", hops[which]).astype(F32)
     side_resid = (own_side + total).astype(BF16)
     other_resid = lax.ppermute(side_resid, "tensor", across)
     units = w_gate_up.shape[2]

time: 55.7 us -> 54.8 us (0.984)
  transfers between devices with their start and end apart: 13 -> 13, of which waited for: 6 -> 7; matrix products, arithmetic and copies ran while one was open for 0% -> 0% of each run, Pallas kernels for 10% -> 10%
where the time goes in v6:
time: 54.8 us; the launch traced here: 54.6 us
  blocking collectives  20.4 us (37%)
  starting transfers between devices  14 us (26%)
  Pallas kernels  9.89 us (18%)
  waiting for transfers between devices  7.82 us (14%)
  between operations  0.98 us (2%)
  other arithmetic  0.76 us (1%)
  local copies, waits for them, and re-layouts  0.73 us (1%)
    all_to_all x1, blocking collectives, per_device(): lax.all_to_all(part.reshape(shards * groups, wire_rows, chunk), ('seq', '...  12.1 us
    pallas_call x9, Pallas kernels, call(): pl.pallas_call(kernel, out_shape=out, in_specs=specs or [VMEM_SPEC] * len...  9.89 us
    all_to_all x1, blocking collectives, per_device(): partial = lax.all_to_all(partial, 'tensor', 0, 0, tiled=True)  8.29 us
    ppermute x3, starting transfers between devices, per_device(): column = [states] + [lax.ppermute(states, 'tensor', hop) for hop in hops]  6.57 us
    ppermute x3, waiting for transfers between devices, per_device(): total = total + lax.ppermute(chip, 'tensor', hops[which]).astype(F32)  4.67 us
    ppermute x3, starting transfers between devices, per_device(): lax.ppermute(query, 'tensor', hop)  3.88 us
    ppermute x3, starting transfers between devices, per_device(): total = total + lax.ppermute(chip, 'tensor', hops[which]).astype(F32)  2.46 us
    ppermute x3, waiting for transfers between devices, per_device(): column = [states] + [lax.ppermute(states, 'tensor', hop) for hop in hops]  1.19 us
  transfers between devices with their start and end apart: 13, of which 7 were waited for; matrix products, arithmetic and copies ran while one was open for 0% of the time, Pallas kernels for 10%

profile of v6, /device:TPU:0, one launch (start us, length us, event | category | flops | bytes accessed | tf_op | source)
XLA Modules:
  0.0 54.6 jit_solution(12072256602182165733)
XLA Ops:
  0.6 0.0 slice-start.2
  0.6 0.0 slice-start.4
  0.7 0.0 slice-start.3
  0.7 0.0 slice-start.5
  0.7 0.5 collective-permute-start.3
  1.3 2.6 %collective-permute-start = (bf16[2,2048]{1,0:T(2,128)(2,1)}, bf16[2,2048]{1,0:T(2,128)(2,1)S(1)}, u32[]{:S(2)}, u32[]{:S(2)}) collective-permute-start(bf16[2,2048]{1,0:T(2,128)(2,1)} %refs_0_.1), channel_id=1, source_target_pairs={{0,2},{1,3},{2,4},{3,5},{4,6},{5,7},{6,0},{7,1},{8,10},{9,11},{10,... | collective-permute-start | bytes 24584 | tf_op jit(solution)/shard_map/ppermute | solution.py:445
  3.9 2.6 %collective-permute-start.1 = (bf16[2,2048]{1,0:T(2,128)(2,1)}, bf16[2,2048]{1,0:T(2,128)(2,1)S(1)}, u32[]{:S(2)}, u32[]{:S(2)}) collective-permute-start(bf16[2,2048]{1,0:T(2,128)(2,1)} %refs_0_.1), channel_id=1, source_target_pairs={{0,4},{1,5},{2,6},{3,7},{4,0},{5,1},{6,2},{7,3},{8,12},{9,13},{10,... | collective-permute-start | bytes 24584 | tf_op jit(solution)/shard_map/ppermute | solution.py:445
  6.5 1.3 %collective-permute-start.2 = (bf16[2,2048]{1,0:T(2,128)(2,1)}, bf16[2,2048]{1,0:T(2,128)(2,1)S(1)}, u32[]{:S(2)}, u32[]{:S(2)}) collective-permute-start(bf16[2,2048]{1,0:T(2,128)(2,1)} %refs_0_.1), channel_id=1, source_target_pairs={{0,6},{1,7},{2,0},{3,1},{4,2},{5,3},{6,4},{7,5},{8,14},{9,15},{10,... | collective-permute-start | bytes 24584 | tf_op jit(solution)/shard_map/ppermute | solution.py:445
  7.8 0.7 %copy-done.11 = s32[16]{0:T(128)S(1)} copy-done((s32[16]{0:T(128)S(1)}, s32[16]{0:T(128)}, u32[]{:S(2)}) %copy-start.11) | copy-done | bytes 88
  8.5 0.6 %prepare.1 = (f32[16,128]{1,0:T(8,128)S(1)}, f32[16,128]{1,0:T(8,128)S(1)}) custom-call(s32[16]{0:T(128)S(1)} %copy-done.11), custom_call_target="tpu_custom_call" | custom-call | flops 20000000000 | bytes 64 | tf_op jit(solution)/shard_map/prepare/pallas_call | solution.py:390
  9.1 0.0 copy-start.5
  9.1 0.0 copy-start.6
  9.1 0.0 collective-permute-done.refs_1_
  9.2 0.0 collective-permute-done.1.refs_2_
  9.2 1.2 %collective-permute-done.2.refs_3_ = bf16[2,2048]{1,0:T(2,128)(2,1)S(1)} collective-permute-done((bf16[2,2048]{1,0:T(2,128)(2,1)}, bf16[2,2048]{1,0:T(2,128)(2,1)S(1)}, u32[]{:S(2)}, u32[]{:S(2)}) %collective-permute-start.2) | collective-permute-done | bytes 8224 | tf_op jit(solution)/shard_map/ppermute | solution.py:445
  10.3 0.0 copy-done.2
  10.3 0.1 pad_maximum_fusion.same_ref
  10.4 0.1 collective-permute-start.7
  10.5 0.0 collective-permute-done.3.refs_6_
  10.5 0.6 %query.1 = (f32[8,128]{1,0:T(8,128)S(1)}, f32[8,128]{1,0:T(8,128)S(1)}, f32[8,128]{1,0:T(8,128)S(1)}, f32[8,128]{1,0:T(8,128)S(1)}) custom-call(bf16[2,2048]{1,0:T(2,128)(2,1)S(1)} %copy-done.2, bf16[2,2048]{1,0:T(2,128)(2,1)S(1)} %collective-permute-done.refs_1_, bf16[2,2048]{1,0:T(2,128)(2,1)S(1)} %collective-permute-done.1.refs_2_, ...), custom_call_target="tpu_custom_call" | custom-call | flops 2000000000 | bytes 6344704 | tf_op jit(solution)/shard_map/query/pallas_call | solution.py:390
  11.1 0.3 collective-permute-start.4
  11.4 3.4 %collective-permute-start.5 = (f32[8,128]{1,0:T(8,128)S(1)}, f32[8,128]{1,0:T(8,128)S(1)}, u32[]{:S(2)}, u32[]{:S(2)}) collective-permute-start(f32[8,128]{1,0:T(8,128)S(1)} %get-tuple-element.44), channel_id=1, source_target_pairs={{0,4},{1,5},{2,6},{3,7},{4,0},{5,1},{6,2},{7,3},{8,12},{9,13},{10,... | collective-permute-start | bytes 12296 | tf_op jit(solution)/shard_map/ppermute | solution.py:460
  14.8 0.1 collective-permute-start.6
  15.0 0.0 collective-permute-done.7.peer_ref
  15.0 1.5 %new_token.1 = (f32[8,8,128]{2,1,0:T(8,128)S(1)}, f32[8,8,128]{2,1,0:T(8,128)S(1)}, s32[2,1024]{1,0:T(2,128)S(1)}) custom-call(s32[16]{0:T(128)S(1)} %copy-done.10, s32[16]{0:T(128)S(1)} %copy-done.12, s32[2,1024]{1,0:T(2,128)S(1)} %copy-done.7, s32[2,1024]{1,0:T(2,128)S(1)} %copy-done.8, bf16[4,2,2048]{2,1,0:T(2,128)(2,1)S(1)} %pad_maximum_fusion.same_ref, ...), custom_call_target="tpu_custom_call" | custom-call | flops 2000000000 | bytes 3248256 | tf_op jit(solution)/shard_map/new_token/pallas_call | solution.py:390
  16.5 1.0 %own_heads.1.refs_8_ = f32[4,8,8,128]{3,2,1,0:T(8,128)S(1)} custom-call(f32[8,128]{1,0:T(8,128)S(1)} %get-tuple-element.42.refs_0_, bf16[2,2048,1024]{2,1,0:T(8,128)(2,1)S(1)} %bitcast.18, bf16[2,2048,1024]{2,1,0:T(8,128)(2,1)S(1)} %bitcast.20, bf16[2,4,2048]{2,1,0:T(4,128)(2,1)S(1)} %bitcast.24, bf16[2,4,2048]{2,1,0:T(4,128)(2,1)S(1)} %bitcast.26, ...), custom_call_target="tpu_custom_call" | custom-call | flops 10000000000 | bytes 16855040 | tf_op jit(solution)/shard_map/own_heads/pallas_call | solution.py:390
  17.5 0.0 collective-permute-done.4.refs_0_
  17.5 0.0 collective-permute-done.5.refs_1_
  17.5 0.9 %collective-permute-done.6.refs_2_ = f32[8,128]{1,0:T(8,128)S(1)} collective-permute-done((f32[8,128]{1,0:T(8,128)S(1)}, f32[8,128]{1,0:T(8,128)S(1)}, u32[]{:S(2)}, u32[]{:S(2)}) %collective-permute-start.6) | collective-permute-done | bytes 4128 | tf_op jit(solution)/shard_map/ppermute | solution.py:460
  18.5 2.6 %other_heads.1 = f32[4,8,8,128]{3,2,1,0:T(8,128)S(1)} custom-call(f32[8,128]{1,0:T(8,128)S(1)} %collective-permute-done.4.refs_0_, f32[8,128]{1,0:T(8,128)S(1)} %collective-permute-done.5.refs_1_, f32[8,128]{1,0:T(8,128)S(1)} %collective-permute-done.6.refs_2_, bf16[2,2048,1024]{2,1,0:T(8,128)(2,1)S(1)} %bitcast.18, ...), custom_call_target="tpu_custom_call", output_to_operand_aliasing={{}: (8, {})} | custom-call | flops 10000000000 | bytes 16994304 | tf_op jit(solution)/shard_map/other_heads/pallas_call | solution.py:390
  21.1 12.1 %all_to_all.10 = f32[32,8,128]{2,1,0:T(8,128)S(1)} all-to-all(f32[32,8,128]{2,1,0:T(8,128)S(1)} %bitcast.11), channel_id=1, replica_groups=mesh['seq'=4,'tensor'=8] {'seq','tensor'}, dimensions={0} | all-to-all | bytes 262144 | tf_op jit(solution)/shard_map/all_to_all | solution.py:491
  33.2 0.3 merge.1
  33.5 0.4 collective-permute-start.8
  33.9 0.9 %collective-permute-done.8 = f32[16,1024]{1,0:T(8,128)S(1)} collective-permute-done((f32[16,1024]{1,0:T(8,128)S(1)}, f32[16,1024]{1,0:T(8,128)S(1)}, u32[]{:S(2)}, u32[]{:S(2)}) %collective-permute-start.8) | collective-permute-done | bytes 65568 | tf_op jit(solution)/shard_map/ppermute | solution.py:503
  34.9 1.0 %collective-permute-start.10 = (bf16[16,1024]{1,0:T(8,128)(2,1)S(1)}, bf16[16,1024]{1,0:T(8,128)(2,1)S(1)}, u32[]{:S(2)}, u32[]{:S(2)}) collective-permute-start(bf16[16,1024]{1,0:T(8,128)(2,1)S(1)} %add_convert_fusion.1), channel_id=1, source_target_pairs={{0,6},{1,7},{2,0},{3,1},{4,2},{5,3},{6,4},{7,5},{8,14},{9,15},{10,... | collective-permute-start | bytes 98312 | tf_op jit(solution)/shard_map/ppermute | solution.py:517
  35.9 1.1 %collective-permute-start.11 = (bf16[16,1024]{1,0:T(8,128)(2,1)S(1)}, bf16[16,1024]{1,0:T(8,128)(2,1)S(1)}, u32[]{:S(2)}, u32[]{:S(2)}) collective-permute-start(bf16[16,1024]{1,0:T(8,128)(2,1)S(1)} %add_convert_fusion.1), channel_id=1, source_target_pairs={{0,4},{1,5},{2,6},{3,7},{4,0},{5,1},{6,2},{7,3},{8,12},{9,13},{10,... | collective-permute-start | bytes 98312 | tf_op jit(solution)/shard_map/ppermute | solution.py:517
  37.0 0.4 collective-permute-start.9
  37.3 0.7 %outputs.1 = (bf16[16,256]{1,0:T(8,128)(2,1)}, bf16[16,256]{1,0:T(8,128)(2,1)}, f32[16,1024]{1,0:T(8,128)S(1)}) custom-call(bf16[4,2,2048]{2,1,0:T(2,128)(2,1)S(1)} %pad_maximum_fusion.same_ref, bf16[4,2,2048]{2,1,0:T(2,128)(2,1)S(1)} %collective-permute-done.7.peer_ref, f32[8,8,128]{2,1,0:T(8,128)S(1)} %get-tuple-element.59.new_ref, ...), custom_call_target="tpu_custom_call" | custom-call | bytes 131072 | tf_op jit(solution)/shard_map/outputs/pallas_call | solution.py:390
  38.0 0.8 %collective-permute-done.10 = bf16[16,1024]{1,0:T(8,128)(2,1)S(1)} collective-permute-done((bf16[16,1024]{1,0:T(8,128)(2,1)S(1)}, bf16[16,1024]{1,0:T(8,128)(2,1)S(1)}, u32[]{:S(2)}, u32[]{:S(2)}) %collective-permute-start.10) | collective-permute-done | bytes 32800 | tf_op jit(solution)/shard_map/ppermute | solution.py:517
  38.8 1.9 %collective-permute-done.11 = bf16[16,1024]{1,0:T(8,128)(2,1)S(1)} collective-permute-done((bf16[16,1024]{1,0:T(8,128)(2,1)S(1)}, bf16[16,1024]{1,0:T(8,128)(2,1)S(1)}, u32[]{:S(2)}, u32[]{:S(2)}) %collective-permute-start.11) | collective-permute-done | bytes 32800 | tf_op jit(solution)/shard_map/ppermute | solution.py:517
  40.7 2.0 %collective-permute-done.9 = bf16[16,1024]{1,0:T(8,128)(2,1)S(1)} collective-permute-done((bf16[16,1024]{1,0:T(8,128)(2,1)S(1)}, bf16[16,1024]{1,0:T(8,128)(2,1)S(1)}, u32[]{:S(2)}, u32[]{:S(2)}) %collective-permute-start.9) | collective-permute-done | bytes 32800 | tf_op jit(solution)/shard_map/ppermute | solution.py:517
  42.7 0.1 collective-permute-start.12
  42.8 1.1 %first_half.1 = (f32[32,1024]{1,0:T(8,128)S(1)}, f32[16,128]{1,0:T(8,128)S(1)}) custom-call(bf16[16,1024]{1,0:T(8,128)(2,1)S(1)} %add_convert_fusion.side_ref.mine_ref, bf16[2048]{0:T(1024)(128)(2,1)S(1)} %copy-done.1, bf16[2048,2,1024]{2,1,0:T(2,128)(2,1)S(1)} %bitcast.10), custom_call_target="tpu_custom_call" | custom-call | flops 67108864 | bytes 8425472 | tf_op jit(solution)/shard_map/first_half/pallas_call | solution.py:390
  43.9 0.1 collective-permute-done.12.other_ref
  44.0 1.6 %mlp.1 = (bf16[8,2,2048]{2,1,0:T(2,128)(2,1)S(1)}, f32[2,2048]{1,0:T(2,128)S(1)}) custom-call(bf16[16,1024]{1,0:T(8,128)(2,1)S(1)} %add_convert_fusion.side_ref.mine_ref, bf16[16,1024]{1,0:T(8,128)(2,1)S(1)} %collective-permute-done.12.other_ref, bf16[2048]{0:T(1024)(128)(2,1)S(1)} %copy-done.1, bf16[2048,2,1024]{2,1,0:T(2,128)(2,1)S(1)} %bitcast.10, ...), custom_call_target="tpu_custom_call" | custom-call | flops 134217728 | bytes 12791808 | tf_op jit(solution)/shard_map/mlp/pallas_call | solution.py:390
  45.6 8.3 %all_to_all.11 = bf16[8,2,2048]{2,1,0:T(2,128)(2,1)S(1)} all-to-all(bf16[8,2,2048]{2,1,0:T(2,128)(2,1)S(1)} %get-tuple-element.66), channel_id=1, replica_groups=mesh['seq'=4,'tensor'=8] {'tensor'}, dimensions={0} | all-to-all | bytes 131072 | tf_op jit(solution)/shard_map/all_to_all | solution.py:539
  53.9 0.1 convert_reduce_fusion
  54.0 0.6 %add_convert_fusion.2 = bf16[2,2048]{1,0:T(2,128)(2,1)} fusion(f32[2,2048]{1,0:T(2,128)S(1)} %get-tuple-element.65, f32[2,2048]{1,0:T(2,128)S(1)} %convert_reduce_fusion), kind=kLoop, calls=%fused_computation.4 | loop fusion | flops 8192 | bytes 40960 | tf_op jit(solution)/shard_map/convert_element_type | solution.py:540
  (35 shorter events, 0.1 us)
Async XLA Ops:
  0.6 15.8 %slice-start.2 = ((s8[8388608]{0:T(1024)(128)(4,1)}), s8[4194304]{0:T(1024)(128)(4,1)S(1)}, s32[]{:S(2)}) async-start(s8[8388608]{0:T(1024)(128)(4,1)} %bitcast.17), calls=%async_computation.4 | async-start | bytes 8388608
  0.6 15.8 %slice-start.4 = ((s8[8388608]{0:T(1024)(128)(4,1)}), s8[4194304]{0:T(1024)(128)(4,1)S(1)}, s32[]{:S(2)}) async-start(s8[8388608]{0:T(1024)(128)(4,1)} %bitcast.19), calls=%async_computation.6 | async-start | bytes 8388608
  0.7 9.7 %copy-start.2 = (bf16[2,2048]{1,0:T(2,128)(2,1)S(1)}, bf16[2,2048]{1,0:T(2,128)(2,1)}, u32[]{:S(2)}) copy-start(bf16[2,2048]{1,0:T(2,128)(2,1)} %refs_0_.1) | copy-start | bytes 24580
  0.7 9.8 %copy-start.3 = (bf16[2048,3,256]{2,0,1:T(8,128)(2,1)S(1)}, bf16[2048,3,256]{2,0,1:T(8,128)(2,1)}, u32[]{:S(2)}) copy-start(bf16[2048,3,256]{2,0,1:T(8,128)(2,1)} %param.17) | copy-start | bytes 9437188
  0.7 9.8 %copy-start.9 = (bf16[2048]{0:T(1024)(128)(2,1)S(1)}, bf16[2048]{0:T(1024)(128)(2,1)}, u32[]{:S(2)}) copy-start(bf16[2048]{0:T(1024)(128)(2,1)} %gain_ref.3) | copy-start | bytes 12292
  0.7 14.3 %copy-start.7 = (s32[2,1024]{1,0:T(2,128)S(1)}, s32[2,1024]{1,0:T(2,128)}, u32[]{:S(2)}) copy-start(s32[2,1024]{1,0:T(2,128)} %mask_ref.1) | copy-start | bytes 24580
  0.7 14.3 %copy-start.8 = (s32[2,1024]{1,0:T(2,128)S(1)}, s32[2,1024]{1,0:T(2,128)}, u32[]{:S(2)}) copy-start(s32[2,1024]{1,0:T(2,128)} %slot_pos_ref.1) | copy-start | bytes 24580
  0.7 14.3 %copy-start.10 = (s32[16]{0:T(128)S(1)}, s32[16]{0:T(128)}, u32[]{:S(2)}) copy-start(s32[16]{0:T(128)} %len_ref.1) | copy-start | bytes 196
  0.7 15.8 %slice-start.3 = ((s8[8388608]{0:T(1024)(128)(4,1)}), s8[4194304]{0:T(1024)(128)(4,1)S(1)}, s32[]{:S(2)}) async-start(s8[8388608]{0:T(1024)(128)(4,1)} %bitcast.17), calls=%async_computation.5 | async-start | bytes 8388608
  0.7 15.8 %slice-start.5 = ((s8[8388608]{0:T(1024)(128)(4,1)}), s8[4194304]{0:T(1024)(128)(4,1)S(1)}, s32[]{:S(2)}) async-start(s8[8388608]{0:T(1024)(128)(4,1)} %bitcast.19), calls=%async_computation.7 | async-start | bytes 8388608
  0.7 9.8 %collective-permute-start.3 = (bf16[3,2048,256]{2,1,0:T(8,128)(2,1)}, bf16[3,2048,256]{2,1,0:T(8,128)(2,1)S(1)}, u32[]{:S(2)}, u32[]{:S(2)}) collective-permute-start(bf16[3,2048,256]{2,1,0:T(8,128)(2,1)} %bitcast.21), channel_id=1, source_target_pairs={{0,1},{1,0},{2,3},{3,2},{4,5},{5,4},{6,7},{7,6},{8,9},{9,8},{10,11... | collective-permute-start | bytes 9437192 | tf_op jit(solution)/shard_map/ppermute | solution.py:447
  1.3 7.9 %collective-permute-start = (bf16[2,2048]{1,0:T(2,128)(2,1)}, bf16[2,2048]{1,0:T(2,128)(2,1)S(1)}, u32[]{:S(2)}, u32[]{:S(2)}) collective-permute-start(bf16[2,2048]{1,0:T(2,128)(2,1)} %refs_0_.1), channel_id=1, source_target_pairs={{0,2},{1,3},{2,4},{3,5},{4,6},{5,7},{6,0},{7,1},{8,10},{9,11},{10,... | collective-permute-start | bytes 24584 | tf_op jit(solution)/shard_map/ppermute | solution.py:445
  3.9 5.3 %collective-permute-start.1 = (bf16[2,2048]{1,0:T(2,128)(2,1)}, bf16[2,2048]{1,0:T(2,128)(2,1)S(1)}, u32[]{:S(2)}, u32[]{:S(2)}) collective-permute-start(bf16[2,2048]{1,0:T(2,128)(2,1)} %refs_0_.1), channel_id=1, source_target_pairs={{0,4},{1,5},{2,6},{3,7},{4,0},{5,1},{6,2},{7,3},{8,12},{9,13},{10,... | collective-permute-start | bytes 24584 | tf_op jit(solution)/shard_map/ppermute | solution.py:445
  6.5 3.9 %collective-permute-start.2 = (bf16[2,2048]{1,0:T(2,128)(2,1)}, bf16[2,2048]{1,0:T(2,128)(2,1)S(1)}, u32[]{:S(2)}, u32[]{:S(2)}) collective-permute-start(bf16[2,2048]{1,0:T(2,128)(2,1)} %refs_0_.1), channel_id=1, source_target_pairs={{0,6},{1,7},{2,0},{3,1},{4,2},{5,3},{6,4},{7,5},{8,14},{9,15},{10,... | collective-permute-start | bytes 24584 | tf_op jit(solution)/shard_map/ppermute | solution.py:445
  7.8 0.7 %copy-start.11 = (s32[16]{0:T(128)S(1)}, s32[16]{0:T(128)}, u32[]{:S(2)}) copy-start(s32[16]{0:T(128)} %pos_ref.3) | copy-start | bytes 196
  8.5 6.5 %copy-start.12 = (s32[16]{0:T(128)S(1)}, s32[16]{0:T(128)}, u32[]{:S(2)}) copy-start(s32[16]{0:T(128)} %pos_ref.3) | copy-start | bytes 196
  9.1 7.4 %copy-start.5 = (bf16[2,2048,4]{1,2,0:T(4,128)(2,1)S(1)}, bf16[2,2048,4]{1,2,0:T(4,128)(2,1)}, u32[]{:S(2)}) copy-start(bf16[2,2048,4]{1,2,0:T(4,128)(2,1)} %param.24) | copy-start | bytes 98308
  9.1 7.4 %copy-start.6 = (bf16[2,2048,4]{1,2,0:T(4,128)(2,1)S(1)}, bf16[2,2048,4]{1,2,0:T(4,128)(2,1)}, u32[]{:S(2)}) copy-start(bf16[2,2048,4]{1,2,0:T(4,128)(2,1)} %param.25) | copy-start | bytes 98308
  10.4 4.6 %collective-permute-start.7 = (bf16[4,2,2048]{2,1,0:T(2,128)(2,1)S(1)}, bf16[4,2,2048]{2,1,0:T(2,128)(2,1)S(1)}, u32[]{:S(2)}, u32[]{:S(2)}) collective-permute-start(bf16[4,2,2048]{2,1,0:T(2,128)(2,1)S(1)} %pad_maximum_fusion.same_ref), channel_id=1, source_target_pairs={{0,1},{1,0},{2,3},{3,2},{4,5},{5,4},{6,7},{7,6},{8,9},{9,8},{10,11... | collective-permute-start | bytes 98312 | tf_op jit(solution)/shard_map/ppermute | solution.py:457
  11.1 6.4 %collective-permute-start.4 = (f32[8,128]{1,0:T(8,128)S(1)}, f32[8,128]{1,0:T(8,128)S(1)}, u32[]{:S(2)}, u32[]{:S(2)}) collective-permute-start(f32[8,128]{1,0:T(8,128)S(1)} %get-tuple-element.43), channel_id=1, source_target_pairs={{0,2},{1,3},{2,4},{3,5},{4,6},{5,7},{6,0},{7,1},{8,10},{9,11},{10,... | collective-permute-start | bytes 12296 | tf_op jit(solution)/shard_map/ppermute | solution.py:460
  11.4 6.1 %collective-permute-start.5 = (f32[8,128]{1,0:T(8,128)S(1)}, f32[8,128]{1,0:T(8,128)S(1)}, u32[]{:S(2)}, u32[]{:S(2)}) collective-permute-start(f32[8,128]{1,0:T(8,128)S(1)} %get-tuple-element.44), channel_id=1, source_target_pairs={{0,4},{1,5},{2,6},{3,7},{4,0},{5,1},{6,2},{7,3},{8,12},{9,13},{10,... | collective-permute-start | bytes 12296 | tf_op jit(solution)/shard_map/ppermute | solution.py:460
  14.8 3.6 %collective-permute-start.6 = (f32[8,128]{1,0:T(8,128)S(1)}, f32[8,128]{1,0:T(8,128)S(1)}, u32[]{:S(2)}, u32[]{:S(2)}) collective-permute-start(f32[8,128]{1,0:T(8,128)S(1)} %get-tuple-element.45), channel_id=1, source_target_pairs={{0,6},{1,7},{2,0},{3,1},{4,2},{5,3},{6,4},{7,5},{8,14},{9,15},{10,... | collective-permute-start | bytes 12296 | tf_op jit(solution)/shard_map/ppermute | solution.py:460
  18.4 14.8 %copy-start.4 = (bf16[256,2048]{1,0:T(8,128)(2,1)S(1)}, bf16[256,2048]{1,0:T(8,128)(2,1)}, u32[]{:S(2)}) copy-start(bf16[256,2048]{1,0:T(8,128)(2,1)} %w_ref.1) | copy-start | bytes 3145732
  18.5 24.3 %slice-start = ((s8[8388608]{0:T(1024)(128)(4,1)}), s8[4194304]{0:T(1024)(128)(4,1)S(1)}, s32[]{:S(2)}) async-start(s8[8388608]{0:T(1024)(128)(4,1)} %bitcast.9), calls=%async_computation.2 | async-start | bytes 8388608
  33.2 9.6 %slice-start.1 = ((s8[8388608]{0:T(1024)(128)(4,1)}), s8[4194304]{0:T(1024)(128)(4,1)S(1)}, s32[]{:S(2)}) async-start(s8[8388608]{0:T(1024)(128)(4,1)} %bitcast.9), calls=%async_computation.3 | async-start | bytes 8388608
  33.2 9.6 %copy-start.1 = (bf16[2048]{0:T(1024)(128)(2,1)S(1)}, bf16[2048]{0:T(1024)(128)(2,1)}, u32[]{:S(2)}) copy-start(bf16[2048]{0:T(1024)(128)(2,1)} %gain_ref.5) | copy-start | bytes 12292
  33.5 10.5 %copy-start = (bf16[1024,2048]{1,0:T(8,128)(2,1)S(1)}, bf16[1024,2048]{1,0:T(8,128)(2,1)}, u32[]{:S(2)}) copy-start(bf16[1024,2048]{1,0:T(8,128)(2,1)} %down_ref.1) | copy-start | bytes 12582916
  33.5 1.3 %collective-permute-start.8 = (f32[16,1024]{1,0:T(8,128)S(1)}, f32[16,1024]{1,0:T(8,128)S(1)}, u32[]{:S(2)}, u32[]{:S(2)}) collective-permute-start(f32[16,1024]{1,0:T(8,128)S(1)} %get-tuple-element.55), channel_id=1, source_target_pairs={{0,1},{1,0},{2,3},{3,2},{4,5},{5,4},{6,7},{7,6},{8,9},{9,8},{10,11... | collective-permute-start | bytes 196616 | tf_op jit(solution)/shard_map/ppermute | solution.py:503
  34.9 4.0 %collective-permute-start.10 = (bf16[16,1024]{1,0:T(8,128)(2,1)S(1)}, bf16[16,1024]{1,0:T(8,128)(2,1)S(1)}, u32[]{:S(2)}, u32[]{:S(2)}) collective-permute-start(bf16[16,1024]{1,0:T(8,128)(2,1)S(1)} %add_convert_fusion.1), channel_id=1, source_target_pairs={{0,6},{1,7},{2,0},{3,1},{4,2},{5,3},{6,4},{7,5},{8,14},{9,15},{10,... | collective-permute-start | bytes 98312 | tf_op jit(solution)/shard_map/ppermute | solution.py:517
  35.9 4.8 %collective-permute-start.11 = (bf16[16,1024]{1,0:T(8,128)(2,1)S(1)}, bf16[16,1024]{1,0:T(8,128)(2,1)S(1)}, u32[]{:S(2)}, u32[]{:S(2)}) collective-permute-start(bf16[16,1024]{1,0:T(8,128)(2,1)S(1)} %add_convert_fusion.1), channel_id=1, source_target_pairs={{0,4},{1,5},{2,6},{3,7},{4,0},{5,1},{6,2},{7,3},{8,12},{9,13},{10,... | collective-permute-start | bytes 98312 | tf_op jit(solution)/shard_map/ppermute | solution.py:517
  37.0 5.7 %collective-permute-start.9 = (bf16[16,1024]{1,0:T(8,128)(2,1)S(1)}, bf16[16,1024]{1,0:T(8,128)(2,1)S(1)}, u32[]{:S(2)}, u32[]{:S(2)}) collective-permute-start(bf16[16,1024]{1,0:T(8,128)(2,1)S(1)} %add_convert_fusion.1), channel_id=1, source_target_pairs={{0,2},{1,3},{2,4},{3,5},{4,6},{5,7},{6,0},{7,1},{8,10},{9,11},{10,... | collective-permute-start | bytes 98312 | tf_op jit(solution)/shard_map/ppermute | solution.py:517
  42.7 1.3 %collective-permute-start.12 = (bf16[16,1024]{1,0:T(8,128)(2,1)S(1)}, bf16[16,1024]{1,0:T(8,128)(2,1)S(1)}, u32[]{:S(2)}, u32[]{:S(2)}) collective-permute-start(bf16[16,1024]{1,0:T(8,128)(2,1)S(1)} %add_convert_fusion.side_ref.mine_ref), channel_id=1, source_target_pairs={{0,1},{1,0},{2,3},{3,2},{4,5},{5,4},{6,7},{7,6},{8,9},{9,8},{10,11... | collective-permute-start | bytes 98312 | tf_op jit(solution)/shard_map/ppermute | solution.py:519

commit v7 on v6

--- a/solution.py
+++ b/solution.py
@@ -15,6 +15,7 @@
 LANE = 128
 MIB = 2**20
 AHEAD = 1
+LEVEL_ROW = 4
 PREP_FLOPS = 20_000_000_000
 QKV_FLOPS = 2_000_000_000
 ATT_FLOPS = 10_000_000_000
@@ -162,12 +163,14 @@
 def attention_kernel(lanes, chips, steps, *refs):
     queries, refs = dict(zip(steps, refs)), refs[len(steps) :]
     k_ref, v_ref, sink_k_ref, sink_v_ref, live_ref = refs[:5]
-    out_ref = refs[-1]
+    out_ref, tile_ref = refs[-2:]
     rows, features, slots = k_ref.shape
     sinks = sink_k_ref.shape[1]
     copies = out_ref.shape[0]
-    half, chunk = out_ref.shape[2] // 2, out_ref.shape[3]
+    chunk = out_ref.shape[3]
     block = 2 * lanes
+    group_heads = lanes // HEAD_SIZE
+    repeat = chunk // (rows * group_heads)
     heads = max(8, block // HEAD_SIZE)
     seq_index = lax.axis_index("seq")
     chip = lax.axis_index("tensor") // 2
@@ -224,15 +227,31 @@
         level = jnp.where(some, top + jnp.log(jnp.where(some, total, 1.0)), NEG)
         mixture = mixture / jnp.where(some, total, 1.0)
         mixture = jnp.sum(jnp.where(own, mixture, 0.0), axis=0, keepdims=True)
-        level = jnp.sum(jnp.where(own, level, 0.0), axis=0, keepdims=True)
-        for f in range(block // chunk):
-            t, c = divmod(f, lanes // chunk)
-            row = wire_row(rows, c, r)
-            at = slice(f * chunk, (f + 1) * chunk)
+        for t in range(2):
+            tile = steps.index(step) * 2 + t
+            for c in range(lanes // chunk):
+                row = wire_row(rows, c, r)
+                start = t * lanes + c * chunk
+                tile_ref[tile, row : row + 1, :] = mixture[:, start : start + chunk]
+            here = head_row == head_lane + (t - r) * group_heads
+            here = here & (head_row // group_heads == t)
+            one = jnp.sum(jnp.where(here, level, 0.0), axis=0, keepdims=True)
+            if r > 0:
+                one = one + tile_ref[tile, LEVEL_ROW : LEVEL_ROW + 1, :]
+            if r < rows - 1:
+                tile_ref[tile, LEVEL_ROW : LEVEL_ROW + 1, :] = one
+                continue
+            for term in range(3):
+                rounded = one.astype(BF16).astype(F32)
+                tile_ref[tile, LEVEL_ROW + term : LEVEL_ROW + term + 1, :] = rounded
+                one = one - rounded
+            parts = tile_ref[tile].astype(BF16)
             for copy in range(copies):
-                out_ref[copy, 2 * source + t, row : row + 1, :] = mixture[:, at]
-                out_ref[copy, 2 * source + t, half + row : half + row + 1, :] = level[:, at]
-
+                out_ref[copy, 2 * source + t] = parts
+
+    tile_ref[...] = jnp.zeros_like(tile_ref)
+    head_row = lax.broadcasted_iota(jnp.int32, (heads, chunk), 0)
+    head_lane = lax.broadcasted_iota(jnp.int32, (heads, chunk), 1) // repeat
     todo = [(r, step) for step in steps for r in range(rows)]
     ahead = [scores(*one) for one in todo[:AHEAD]]
     for i, one in enumerate(todo):
@@ -241,34 +260,46 @@
         mix(*one, *ahead[i])
 
 
-def merge_kernel(rows, part_ref, new_ref, w_ref, mine_ref, other_ref, rows_ref, full_ref):
+def merge_kernel(
+    rows, part_ref, new_ref, w_ref, mine_ref, other_ref, rows_ref, attended_ref, full_ref
+):
     copies, groups, wire_rows, chunk = part_ref.shape
-    half = wire_rows // 2
     lanes = w_ref.shape[0]
     flat = groups * wire_rows
-    parts = [part_ref[s].reshape(flat, chunk) for s in range(copies)]
-    parts.append(new_ref[...].reshape(flat, chunk))
-    levels = [pltpu.roll(part, flat - half, 0) for part in parts]
-    top = functools.reduce(jnp.maximum, levels)
-    mixture = jnp.zeros((flat, chunk), F32)
-    total = jnp.zeros((flat, chunk), F32)
-    for part, level in zip(parts, levels):
-        share = jnp.exp(level - top)
-        mixture = mixture + share * part
-        total = total + share
-    rows_ref[...] = mixture / total
-    attended = []
-    for c in range(lanes // chunk):
-        start = wire_row(rows, c, 0)
-        attended.append(
-            jnp.concatenate(
-                [
-                    rows_ref[g * wire_rows + start : g * wire_rows + start + rows, :]
-                    for g in range(groups)
-                ],
-                axis=0,
-            )
-        )
+    for s in range(copies):
+        rows_ref[s * flat : (s + 1) * flat, :] = part_ref[s].astype(F32).reshape(flat, chunk)
+    rows_ref[copies * flat :, :] = new_ref[...].reshape(flat, chunk)
+
+    def every(row, first, count):
+        return rows_ref[pl.ds(first * flat + row, count * groups, stride=wire_rows), :]
+
+    count = rows * lanes // chunk
+    terms = jnp.concatenate([every(LEVEL_ROW + term, 0, copies) for term in range(3)], axis=0)
+    shape = (chunk, count * chunk)
+    to = lax.broadcasted_iota(jnp.int32, shape, 1)
+    to_head = (to // (rows * chunk) * chunk + to % chunk) // HEAD_SIZE
+    group_heads = lanes // HEAD_SIZE
+    at = (to // chunk % rows * group_heads + to_head) * (chunk // (rows * group_heads))
+    spread = (lax.broadcasted_iota(jnp.int32, shape, 0) == at).astype(F32).astype(BF16)
+    terms = jnp.dot(terms.astype(BF16), spread, preferred_element_type=F32)
+    size = copies * groups
+    levels = terms[:size] + terms[size : 2 * size] + terms[2 * size :]
+    for i in range(count):
+        c, r = divmod(i, rows)
+        mine = every(i, 0, copies)
+        parts = [mine[s * groups : (s + 1) * groups] for s in range(copies)]
+        parts.append(every(i, copies, 1))
+        level = [
+            levels[s * groups : (s + 1) * groups, i * chunk : (i + 1) * chunk]
+            for s in range(copies)
+        ]
+        level.append(every(wire_rows // 2 + i, copies, 1))
+        top = functools.reduce(jnp.maximum, level)
+        shares = [jnp.exp(one - top) for one in level]
+        mixture = functools.reduce(jnp.add, [share * part for share, part in zip(shares, parts)])
+        total = functools.reduce(jnp.add, shares)
+        attended_ref[c, pl.ds(r, groups, stride=rows), :] = mixture / total
+    attended = [attended_ref[c] for c in range(lanes // chunk)]
     attended = jnp.concatenate(attended, axis=1).astype(BF16)
     full_ref[...] = jnp.dot(attended, w_ref[...], preferred_element_type=F32)
     width = mine_ref.shape[1]
@@ -474,8 +505,9 @@
     def attention(steps, arrays, aliases, name):
         return call(
             functools.partial(attention_kernel, lanes, chips, steps),
-            sds((shards, groups, wire_rows, chunk), F32),
+            sds((shards, groups, 8, chunk), BF16),
             arrays,
+            scratch=[pltpu.VMEM((2 * len(steps), 8, chunk), F32)],
             limit=8,
             name=name,
             flops=ATT_FLOPS,
@@ -489,14 +521,18 @@
         tuple(range(1, chips)), (*queries[1:], *cache, part), {chips + 4: 0}, "other_heads"
     )
     part = lax.all_to_all(
-        part.reshape(shards * groups, wire_rows, chunk), ("seq", "tensor"), 0, 0, tiled=True
-    ).reshape(shards, groups, wire_rows, chunk)
+        part.reshape(shards * groups, 8, chunk), ("seq", "tensor"), 0, 0, tiled=True
+    ).reshape(shards, groups, 8, chunk)
     side = sds((batch, width // 2), F32)
     mine, other = call(
         functools.partial(merge_kernel, rows),
         (side, side),
         (part, new_part, w_out),
-        scratch=[pltpu.VMEM((groups * wire_rows, chunk), F32), pltpu.VMEM((batch, width), F32)],
+        scratch=[
+            pltpu.VMEM(((shards + 1) * groups * 8, chunk), F32),
+            pltpu.VMEM((lanes // chunk, batch, chunk), F32),
+            pltpu.VMEM((batch, width), F32),
+        ],
         name="merge",
         flops=MERGE_FLOPS,
     )

time: 54.8 us -> 54 us (0.985)
  blocking collectives: 20.4 us -> 19.7 us
    all_to_all x1, blocking collectives: 12.1 us -> 11.4 us  [per_device(): lax.all_to_all(part.reshape(shards * groups, 8, chunk), ('seq', 'tensor')...]
where the time goes in v7:
time: 54 us; the launch traced here: 53.8 us
  blocking collectives  19.7 us (36%)
  starting transfers between devices  13.7 us (25%)
  Pallas kernels  10.1 us (19%)
  waiting for transfers between devices  7.93 us (15%)
  between operations  0.97 us (2%)
  other arithmetic  0.76 us (1%)
  local copies, waits for them, and re-layouts  0.73 us (1%)
    all_to_all x1, blocking collectives, per_device(): lax.all_to_all(part.reshape(shards * groups, 8, chunk), ('seq', 'tensor')...  11.4 us
    pallas_call x9, Pallas kernels, call(): pl.pallas_call(kernel, out_shape=out, in_specs=specs or [VMEM_SPEC] * len...  10.1 us
    all_to_all x1, blocking collectives, per_device(): partial = lax.all_to_all(partial, 'tensor', 0, 0, tiled=True)  8.29 us
    ppermute x3, starting transfers between devices, per_device(): column = [states] + [lax.ppermute(states, 'tensor', hop) for hop in hops]  6.57 us
    ppermute x3, waiting for transfers between devices, per_device(): total = total + lax.ppermute(chip, 'tensor', hops[which]).astype(F32)  4.58 us
    ppermute x3, starting transfers between devices, per_device(): lax.ppermute(query, 'tensor', hop)  3.88 us
    ppermute x3, starting transfers between devices, per_device(): total = total + lax.ppermute(chip, 'tensor', hops[which]).astype(F32)  2.42 us
    ppermute x3, waiting for transfers between devices, per_device(): column = [states] + [lax.ppermute(states, 'tensor', hop) for hop in hops]  1.19 us
  transfers between devices with their start and end apart: 13, of which 7 were waited for; matrix products, arithmetic and copies ran while one was open for 0% of the time, Pallas kernels for 10%

profile of v7, /device:TPU:0, one launch (start us, length us, event | category | flops | bytes accessed | tf_op | source)
XLA Modules:
  0.0 53.8 jit_solution(6995986824495502150)
XLA Ops:
  0.6 0.0 slice-start.2
  0.6 0.0 slice-start.4
  0.7 0.0 slice-start.3
  0.7 0.0 slice-start.5
  0.7 0.5 collective-permute-start.3
  1.3 2.6 %collective-permute-start = (bf16[2,2048]{1,0:T(2,128)(2,1)}, bf16[2,2048]{1,0:T(2,128)(2,1)S(1)}, u32[]{:S(2)}, u32[]{:S(2)}) collective-permute-start(bf16[2,2048]{1,0:T(2,128)(2,1)} %refs_0_.1), channel_id=1, source_target_pairs={{0,2},{1,3},{2,4},{3,5},{4,6},{5,7},{6,0},{7,1},{8,10},{9,11},{10,... | collective-permute-start | bytes 24584 | tf_op jit(solution)/shard_map/ppermute | solution.py:476
  3.9 2.6 %collective-permute-start.1 = (bf16[2,2048]{1,0:T(2,128)(2,1)}, bf16[2,2048]{1,0:T(2,128)(2,1)S(1)}, u32[]{:S(2)}, u32[]{:S(2)}) collective-permute-start(bf16[2,2048]{1,0:T(2,128)(2,1)} %refs_0_.1), channel_id=1, source_target_pairs={{0,4},{1,5},{2,6},{3,7},{4,0},{5,1},{6,2},{7,3},{8,12},{9,13},{10,... | collective-permute-start | bytes 24584 | tf_op jit(solution)/shard_map/ppermute | solution.py:476
  6.5 1.3 %collective-permute-start.2 = (bf16[2,2048]{1,0:T(2,128)(2,1)}, bf16[2,2048]{1,0:T(2,128)(2,1)S(1)}, u32[]{:S(2)}, u32[]{:S(2)}) collective-permute-start(bf16[2,2048]{1,0:T(2,128)(2,1)} %refs_0_.1), channel_id=1, source_target_pairs={{0,6},{1,7},{2,0},{3,1},{4,2},{5,3},{6,4},{7,5},{8,14},{9,15},{10,... | collective-permute-start | bytes 24584 | tf_op jit(solution)/shard_map/ppermute | solution.py:476
  7.8 0.7 %copy-done.11 = s32[16]{0:T(128)S(1)} copy-done((s32[16]{0:T(128)S(1)}, s32[16]{0:T(128)}, u32[]{:S(2)}) %copy-start.11) | copy-done | bytes 88
  8.5 0.6 %prepare.1 = (f32[16,128]{1,0:T(8,128)S(1)}, f32[16,128]{1,0:T(8,128)S(1)}) custom-call(s32[16]{0:T(128)S(1)} %copy-done.11), custom_call_target="tpu_custom_call" | custom-call | flops 20000000000 | bytes 64 | tf_op jit(solution)/shard_map/prepare/pallas_call | solution.py:421
  9.1 0.0 copy-start.5
  9.1 0.0 copy-start.6
  9.1 0.0 collective-permute-done.refs_1_
  9.2 0.0 collective-permute-done.1.refs_2_
  9.2 1.2 %collective-permute-done.2.refs_3_ = bf16[2,2048]{1,0:T(2,128)(2,1)S(1)} collective-permute-done((bf16[2,2048]{1,0:T(2,128)(2,1)}, bf16[2,2048]{1,0:T(2,128)(2,1)S(1)}, u32[]{:S(2)}, u32[]{:S(2)}) %collective-permute-start.2) | collective-permute-done | bytes 8224 | tf_op jit(solution)/shard_map/ppermute | solution.py:476
  10.3 0.0 copy-done.2
  10.3 0.1 pad_maximum_fusion.same_ref
  10.4 0.1 collective-permute-start.7
  10.5 0.0 collective-permute-done.3.refs_6_
  10.5 0.6 %query.1 = (f32[8,128]{1,0:T(8,128)S(1)}, f32[8,128]{1,0:T(8,128)S(1)}, f32[8,128]{1,0:T(8,128)S(1)}, f32[8,128]{1,0:T(8,128)S(1)}) custom-call(bf16[2,2048]{1,0:T(2,128)(2,1)S(1)} %copy-done.2, bf16[2,2048]{1,0:T(2,128)(2,1)S(1)} %collective-permute-done.refs_1_, bf16[2,2048]{1,0:T(2,128)(2,1)S(1)} %collective-permute-done.1.refs_2_, ...), custom_call_target="tpu_custom_call" | custom-call | flops 2000000000 | bytes 6344704 | tf_op jit(solution)/shard_map/query/pallas_call | solution.py:421
  11.1 0.3 collective-permute-start.4
  11.4 3.4 %collective-permute-start.5 = (f32[8,128]{1,0:T(8,128)S(1)}, f32[8,128]{1,0:T(8,128)S(1)}, u32[]{:S(2)}, u32[]{:S(2)}) collective-permute-start(f32[8,128]{1,0:T(8,128)S(1)} %get-tuple-element.44), channel_id=1, source_target_pairs={{0,4},{1,5},{2,6},{3,7},{4,0},{5,1},{6,2},{7,3},{8,12},{9,13},{10,... | collective-permute-start | bytes 12296 | tf_op jit(solution)/shard_map/ppermute | solution.py:491
  14.8 0.1 collective-permute-start.6
  15.0 0.0 collective-permute-done.7.peer_ref
  15.0 1.5 %new_token.1 = (f32[8,8,128]{2,1,0:T(8,128)S(1)}, f32[8,8,128]{2,1,0:T(8,128)S(1)}, s32[2,1024]{1,0:T(2,128)S(1)}) custom-call(s32[16]{0:T(128)S(1)} %copy-done.10, s32[16]{0:T(128)S(1)} %copy-done.12, s32[2,1024]{1,0:T(2,128)S(1)} %copy-done.7, s32[2,1024]{1,0:T(2,128)S(1)} %copy-done.8, bf16[4,2,2048]{2,1,0:T(2,128)(2,1)S(1)} %pad_maximum_fusion.same_ref, ...), custom_call_target="tpu_custom_call" | custom-call | flops 2000000000 | bytes 3248256 | tf_op jit(solution)/shard_map/new_token/pallas_call | solution.py:421
  16.5 1.0 %own_heads.1.refs_8_ = bf16[4,8,8,128]{3,2,1,0:T(8,128)(2,1)S(1)} custom-call(f32[8,128]{1,0:T(8,128)S(1)} %get-tuple-element.42.refs_0_, bf16[2,2048,1024]{2,1,0:T(8,128)(2,1)S(1)} %bitcast.18, bf16[2,2048,1024]{2,1,0:T(8,128)(2,1)S(1)} %bitcast.20, bf16[2,4,2048]{2,1,0:T(4,128)(2,1)S(1)} %bitcast.24, bf16[2,4,2048]{2,1,0:T(4,128)(2,1)S(1)} %bitcast.26, ...), custom_call_target="tpu_custom_call" | custom-call | flops 10000000000 | bytes 16855040 | tf_op jit(solution)/shard_map/own_heads/pallas_call | solution.py:421
  17.5 0.0 collective-permute-done.4.refs_0_
  17.5 0.0 collective-permute-done.5.refs_1_
  17.5 0.9 %collective-permute-done.6.refs_2_ = f32[8,128]{1,0:T(8,128)S(1)} collective-permute-done((f32[8,128]{1,0:T(8,128)S(1)}, f32[8,128]{1,0:T(8,128)S(1)}, u32[]{:S(2)}, u32[]{:S(2)}) %collective-permute-start.6) | collective-permute-done | bytes 4128 | tf_op jit(solution)/shard_map/ppermute | solution.py:491
  18.5 2.6 %other_heads.1 = bf16[4,8,8,128]{3,2,1,0:T(8,128)(2,1)S(1)} custom-call(f32[8,128]{1,0:T(8,128)S(1)} %collective-permute-done.4.refs_0_, f32[8,128]{1,0:T(8,128)S(1)} %collective-permute-done.5.refs_1_, f32[8,128]{1,0:T(8,128)S(1)} %collective-permute-done.6.refs_2_, bf16[2,2048,1024]{2,1,0:T(8,128)(2,1)S(1)} %bitcast.18, ...), custom_call_target="tpu_custom_call", output_to_operand_aliasing={{}: (8, {})} | custom-call | flops 10000000000 | bytes 16928768 | tf_op jit(solution)/shard_map/other_heads/pallas_call | solution.py:421
  21.1 11.4 %all_to_all.10 = bf16[32,8,128]{2,1,0:T(8,128)(2,1)S(1)} all-to-all(bf16[32,8,128]{2,1,0:T(8,128)(2,1)S(1)} %bitcast.11), channel_id=1, replica_groups=mesh['seq'=4,'tensor'=8] {'seq','tensor'}, dimensions={0} | all-to-all | bytes 131072 | tf_op jit(solution)/shard_map/all_to_all | solution.py:523
  32.5 0.5 merge.1
  32.9 0.2 collective-permute-start.8
  33.1 1.1 %collective-permute-done.8 = f32[16,1024]{1,0:T(8,128)S(1)} collective-permute-done((f32[16,1024]{1,0:T(8,128)S(1)}, f32[16,1024]{1,0:T(8,128)S(1)}, u32[]{:S(2)}, u32[]{:S(2)}) %collective-permute-start.8) | collective-permute-done | bytes 65568 | tf_op jit(solution)/shard_map/ppermute | solution.py:539
  34.2 0.8 %collective-permute-start.10 = (bf16[16,1024]{1,0:T(8,128)(2,1)S(1)}, bf16[16,1024]{1,0:T(8,128)(2,1)S(1)}, u32[]{:S(2)}, u32[]{:S(2)}) collective-permute-start(bf16[16,1024]{1,0:T(8,128)(2,1)S(1)} %add_convert_fusion.1), channel_id=1, source_target_pairs={{0,6},{1,7},{2,0},{3,1},{4,2},{5,3},{6,4},{7,5},{8,14},{9,15},{10,... | collective-permute-start | bytes 98312 | tf_op jit(solution)/shard_map/ppermute | solution.py:553
  35.1 1.1 %collective-permute-start.11 = (bf16[16,1024]{1,0:T(8,128)(2,1)S(1)}, bf16[16,1024]{1,0:T(8,128)(2,1)S(1)}, u32[]{:S(2)}, u32[]{:S(2)}) collective-permute-start(bf16[16,1024]{1,0:T(8,128)(2,1)S(1)} %add_convert_fusion.1), channel_id=1, source_target_pairs={{0,4},{1,5},{2,6},{3,7},{4,0},{5,1},{6,2},{7,3},{8,12},{9,13},{10,... | collective-permute-start | bytes 98312 | tf_op jit(solution)/shard_map/ppermute | solution.py:553
  36.2 0.5 collective-permute-start.9
  36.7 0.7 %outputs.1 = (bf16[16,256]{1,0:T(8,128)(2,1)}, bf16[16,256]{1,0:T(8,128)(2,1)}, f32[16,1024]{1,0:T(8,128)S(1)}) custom-call(bf16[4,2,2048]{2,1,0:T(2,128)(2,1)S(1)} %pad_maximum_fusion.same_ref, bf16[4,2,2048]{2,1,0:T(2,128)(2,1)S(1)} %collective-permute-done.7.peer_ref, f32[8,8,128]{2,1,0:T(8,128)S(1)} %get-tuple-element.59.new_ref, ...), custom_call_target="tpu_custom_call" | custom-call | bytes 131072 | tf_op jit(solution)/shard_map/outputs/pallas_call | solution.py:421
  37.3 0.9 %collective-permute-done.10 = bf16[16,1024]{1,0:T(8,128)(2,1)S(1)} collective-permute-done((bf16[16,1024]{1,0:T(8,128)(2,1)S(1)}, bf16[16,1024]{1,0:T(8,128)(2,1)S(1)}, u32[]{:S(2)}, u32[]{:S(2)}) %collective-permute-start.10) | collective-permute-done | bytes 32800 | tf_op jit(solution)/shard_map/ppermute | solution.py:553
  38.2 1.7 %collective-permute-done.11 = bf16[16,1024]{1,0:T(8,128)(2,1)S(1)} collective-permute-done((bf16[16,1024]{1,0:T(8,128)(2,1)S(1)}, bf16[16,1024]{1,0:T(8,128)(2,1)S(1)}, u32[]{:S(2)}, u32[]{:S(2)}) %collective-permute-start.11) | collective-permute-done | bytes 32800 | tf_op jit(solution)/shard_map/ppermute | solution.py:553
  39.9 2.0 %collective-permute-done.9 = bf16[16,1024]{1,0:T(8,128)(2,1)S(1)} collective-permute-done((bf16[16,1024]{1,0:T(8,128)(2,1)S(1)}, bf16[16,1024]{1,0:T(8,128)(2,1)S(1)}, u32[]{:S(2)}, u32[]{:S(2)}) %collective-permute-start.9) | collective-permute-done | bytes 32800 | tf_op jit(solution)/shard_map/ppermute | solution.py:553
  42.0 0.1 collective-permute-start.12
  42.1 1.1 %first_half.1 = (f32[32,1024]{1,0:T(8,128)S(1)}, f32[16,128]{1,0:T(8,128)S(1)}) custom-call(bf16[16,1024]{1,0:T(8,128)(2,1)S(1)} %add_convert_fusion.side_ref.mine_ref, bf16[2048]{0:T(1024)(128)(2,1)S(1)} %copy-done.1, bf16[2048,2,1024]{2,1,0:T(2,128)(2,1)S(1)} %bitcast.10), custom_call_target="tpu_custom_call" | custom-call | flops 67108864 | bytes 8425472 | tf_op jit(solution)/shard_map/first_half/pallas_call | solution.py:421
  43.1 0.1 collective-permute-done.12.other_ref
  43.2 1.6 %mlp.1 = (bf16[8,2,2048]{2,1,0:T(2,128)(2,1)S(1)}, f32[2,2048]{1,0:T(2,128)S(1)}) custom-call(bf16[16,1024]{1,0:T(8,128)(2,1)S(1)} %add_convert_fusion.side_ref.mine_ref, bf16[16,1024]{1,0:T(8,128)(2,1)S(1)} %collective-permute-done.12.other_ref, bf16[2048]{0:T(1024)(128)(2,1)S(1)} %copy-done.1, bf16[2048,2,1024]{2,1,0:T(2,128)(2,1)S(1)} %bitcast.10, ...), custom_call_target="tpu_custom_call" | custom-call | flops 134217728 | bytes 12791808 | tf_op jit(solution)/shard_map/mlp/pallas_call | solution.py:421
  44.9 8.3 %all_to_all.11 = bf16[8,2,2048]{2,1,0:T(2,128)(2,1)S(1)} all-to-all(bf16[8,2,2048]{2,1,0:T(2,128)(2,1)S(1)} %get-tuple-element.66), channel_id=1, replica_groups=mesh['seq'=4,'tensor'=8] {'tensor'}, dimensions={0} | all-to-all | bytes 131072 | tf_op jit(solution)/shard_map/all_to_all | solution.py:575
  53.2 0.1 convert_reduce_fusion
  53.2 0.6 %add_convert_fusion.2 = bf16[2,2048]{1,0:T(2,128)(2,1)} fusion(f32[2,2048]{1,0:T(2,128)S(1)} %get-tuple-element.65, f32[2,2048]{1,0:T(2,128)S(1)} %convert_reduce_fusion), kind=kLoop, calls=%fused_computation.4 | loop fusion | flops 8192 | bytes 40960 | tf_op jit(solution)/shard_map/convert_element_type | solution.py:576
  (35 shorter events, 0.1 us)
Async XLA Ops:
  0.6 15.8 %slice-start.2 = ((s8[8388608]{0:T(1024)(128)(4,1)}), s8[4194304]{0:T(1024)(128)(4,1)S(1)}, s32[]{:S(2)}) async-start(s8[8388608]{0:T(1024)(128)(4,1)} %bitcast.17), calls=%async_computation.4 | async-start | bytes 8388608
  0.6 15.8 %slice-start.4 = ((s8[8388608]{0:T(1024)(128)(4,1)}), s8[4194304]{0:T(1024)(128)(4,1)S(1)}, s32[]{:S(2)}) async-start(s8[8388608]{0:T(1024)(128)(4,1)} %bitcast.19), calls=%async_computation.6 | async-start | bytes 8388608
  0.7 9.7 %copy-start.2 = (bf16[2,2048]{1,0:T(2,128)(2,1)S(1)}, bf16[2,2048]{1,0:T(2,128)(2,1)}, u32[]{:S(2)}) copy-start(bf16[2,2048]{1,0:T(2,128)(2,1)} %refs_0_.1) | copy-start | bytes 24580
  0.7 9.8 %copy-start.3 = (bf16[2048,3,256]{2,0,1:T(8,128)(2,1)S(1)}, bf16[2048,3,256]{2,0,1:T(8,128)(2,1)}, u32[]{:S(2)}) copy-start(bf16[2048,3,256]{2,0,1:T(8,128)(2,1)} %param.17) | copy-start | bytes 9437188
  0.7 9.8 %copy-start.9 = (bf16[2048]{0:T(1024)(128)(2,1)S(1)}, bf16[2048]{0:T(1024)(128)(2,1)}, u32[]{:S(2)}) copy-start(bf16[2048]{0:T(1024)(128)(2,1)} %gain_ref.3) | copy-start | bytes 12292
  0.7 14.3 %copy-start.7 = (s32[2,1024]{1,0:T(2,128)S(1)}, s32[2,1024]{1,0:T(2,128)}, u32[]{:S(2)}) copy-start(s32[2,1024]{1,0:T(2,128)} %mask_ref.1) | copy-start | bytes 24580
  0.7 14.3 %copy-start.8 = (s32[2,1024]{1,0:T(2,128)S(1)}, s32[2,1024]{1,0:T(2,128)}, u32[]{:S(2)}) copy-start(s32[2,1024]{1,0:T(2,128)} %slot_pos_ref.1) | copy-start | bytes 24580
  0.7 14.3 %copy-start.10 = (s32[16]{0:T(128)S(1)}, s32[16]{0:T(128)}, u32[]{:S(2)}) copy-start(s32[16]{0:T(128)} %len_ref.1) | copy-start | bytes 196
  0.7 15.8 %slice-start.3 = ((s8[8388608]{0:T(1024)(128)(4,1)}), s8[4194304]{0:T(1024)(128)(4,1)S(1)}, s32[]{:S(2)}) async-start(s8[8388608]{0:T(1024)(128)(4,1)} %bitcast.17), calls=%async_computation.5 | async-start | bytes 8388608
  0.7 15.8 %slice-start.5 = ((s8[8388608]{0:T(1024)(128)(4,1)}), s8[4194304]{0:T(1024)(128)(4,1)S(1)}, s32[]{:S(2)}) async-start(s8[8388608]{0:T(1024)(128)(4,1)} %bitcast.19), calls=%async_computation.7 | async-start | bytes 8388608
  0.7 9.8 %collective-permute-start.3 = (bf16[3,2048,256]{2,1,0:T(8,128)(2,1)}, bf16[3,2048,256]{2,1,0:T(8,128)(2,1)S(1)}, u32[]{:S(2)}, u32[]{:S(2)}) collective-permute-start(bf16[3,2048,256]{2,1,0:T(8,128)(2,1)} %bitcast.21), channel_id=1, source_target_pairs={{0,1},{1,0},{2,3},{3,2},{4,5},{5,4},{6,7},{7,6},{8,9},{9,8},{10,11... | collective-permute-start | bytes 9437192 | tf_op jit(solution)/shard_map/ppermute | solution.py:478
  1.3 7.9 %collective-permute-start = (bf16[2,2048]{1,0:T(2,128)(2,1)}, bf16[2,2048]{1,0:T(2,128)(2,1)S(1)}, u32[]{:S(2)}, u32[]{:S(2)}) collective-permute-start(bf16[2,2048]{1,0:T(2,128)(2,1)} %refs_0_.1), channel_id=1, source_target_pairs={{0,2},{1,3},{2,4},{3,5},{4,6},{5,7},{6,0},{7,1},{8,10},{9,11},{10,... | collective-permute-start | bytes 24584 | tf_op jit(solution)/shard_map/ppermute | solution.py:476
  3.9 5.3 %collective-permute-start.1 = (bf16[2,2048]{1,0:T(2,128)(2,1)}, bf16[2,2048]{1,0:T(2,128)(2,1)S(1)}, u32[]{:S(2)}, u32[]{:S(2)}) collective-permute-start(bf16[2,2048]{1,0:T(2,128)(2,1)} %refs_0_.1), channel_id=1, source_target_pairs={{0,4},{1,5},{2,6},{3,7},{4,0},{5,1},{6,2},{7,3},{8,12},{9,13},{10,... | collective-permute-start | bytes 24584 | tf_op jit(solution)/shard_map/ppermute | solution.py:476
  6.5 3.9 %collective-permute-start.2 = (bf16[2,2048]{1,0:T(2,128)(2,1)}, bf16[2,2048]{1,0:T(2,128)(2,1)S(1)}, u32[]{:S(2)}, u32[]{:S(2)}) collective-permute-start(bf16[2,2048]{1,0:T(2,128)(2,1)} %refs_0_.1), channel_id=1, source_target_pairs={{0,6},{1,7},{2,0},{3,1},{4,2},{5,3},{6,4},{7,5},{8,14},{9,15},{10,... | collective-permute-start | bytes 24584 | tf_op jit(solution)/shard_map/ppermute | solution.py:476
  7.8 0.7 %copy-start.11 = (s32[16]{0:T(128)S(1)}, s32[16]{0:T(128)}, u32[]{:S(2)}) copy-start(s32[16]{0:T(128)} %pos_ref.3) | copy-start | bytes 196
  8.5 6.5 %copy-start.12 = (s32[16]{0:T(128)S(1)}, s32[16]{0:T(128)}, u32[]{:S(2)}) copy-start(s32[16]{0:T(128)} %pos_ref.3) | copy-start | bytes 196
  9.1 7.4 %copy-start.5 = (bf16[2,2048,4]{1,2,0:T(4,128)(2,1)S(1)}, bf16[2,2048,4]{1,2,0:T(4,128)(2,1)}, u32[]{:S(2)}) copy-start(bf16[2,2048,4]{1,2,0:T(4,128)(2,1)} %param.24) | copy-start | bytes 98308
  9.1 7.4 %copy-start.6 = (bf16[2,2048,4]{1,2,0:T(4,128)(2,1)S(1)}, bf16[2,2048,4]{1,2,0:T(4,128)(2,1)}, u32[]{:S(2)}) copy-start(bf16[2,2048,4]{1,2,0:T(4,128)(2,1)} %param.25) | copy-start | bytes 98308
  10.4 4.6 %collective-permute-start.7 = (bf16[4,2,2048]{2,1,0:T(2,128)(2,1)S(1)}, bf16[4,2,2048]{2,1,0:T(2,128)(2,1)S(1)}, u32[]{:S(2)}, u32[]{:S(2)}) collective-permute-start(bf16[4,2,2048]{2,1,0:T(2,128)(2,1)S(1)} %pad_maximum_fusion.same_ref), channel_id=1, source_target_pairs={{0,1},{1,0},{2,3},{3,2},{4,5},{5,4},{6,7},{7,6},{8,9},{9,8},{10,11... | collective-permute-start | bytes 98312 | tf_op jit(solution)/shard_map/ppermute | solution.py:488
  11.1 6.4 %collective-permute-start.4 = (f32[8,128]{1,0:T(8,128)S(1)}, f32[8,128]{1,0:T(8,128)S(1)}, u32[]{:S(2)}, u32[]{:S(2)}) collective-permute-start(f32[8,128]{1,0:T(8,128)S(1)} %get-tuple-element.43), channel_id=1, source_target_pairs={{0,2},{1,3},{2,4},{3,5},{4,6},{5,7},{6,0},{7,1},{8,10},{9,11},{10,... | collective-permute-start | bytes 12296 | tf_op jit(solution)/shard_map/ppermute | solution.py:491
  11.4 6.1 %collective-permute-start.5 = (f32[8,128]{1,0:T(8,128)S(1)}, f32[8,128]{1,0:T(8,128)S(1)}, u32[]{:S(2)}, u32[]{:S(2)}) collective-permute-start(f32[8,128]{1,0:T(8,128)S(1)} %get-tuple-element.44), channel_id=1, source_target_pairs={{0,4},{1,5},{2,6},{3,7},{4,0},{5,1},{6,2},{7,3},{8,12},{9,13},{10,... | collective-permute-start | bytes 12296 | tf_op jit(solution)/shard_map/ppermute | solution.py:491
  14.8 3.6 %collective-permute-start.6 = (f32[8,128]{1,0:T(8,128)S(1)}, f32[8,128]{1,0:T(8,128)S(1)}, u32[]{:S(2)}, u32[]{:S(2)}) collective-permute-start(f32[8,128]{1,0:T(8,128)S(1)} %get-tuple-element.45), channel_id=1, source_target_pairs={{0,6},{1,7},{2,0},{3,1},{4,2},{5,3},{6,4},{7,5},{8,14},{9,15},{10,... | collective-permute-start | bytes 12296 | tf_op jit(solution)/shard_map/ppermute | solution.py:491
  18.4 14.0 %copy-start.4 = (bf16[256,2048]{1,0:T(8,128)(2,1)S(1)}, bf16[256,2048]{1,0:T(8,128)(2,1)}, u32[]{:S(2)}) copy-start(bf16[256,2048]{1,0:T(8,128)(2,1)} %w_ref.1) | copy-start | bytes 3145732
  18.5 23.6 %slice-start = ((s8[8388608]{0:T(1024)(128)(4,1)}), s8[4194304]{0:T(1024)(128)(4,1)S(1)}, s32[]{:S(2)}) async-start(s8[8388608]{0:T(1024)(128)(4,1)} %bitcast.9), calls=%async_computation.2 | async-start | bytes 8388608
  32.4 9.6 %slice-start.1 = ((s8[8388608]{0:T(1024)(128)(4,1)}), s8[4194304]{0:T(1024)(128)(4,1)S(1)}, s32[]{:S(2)}) async-start(s8[8388608]{0:T(1024)(128)(4,1)} %bitcast.9), calls=%async_computation.3 | async-start | bytes 8388608
  32.5 9.6 %copy-start.1 = (bf16[2048]{0:T(1024)(128)(2,1)S(1)}, bf16[2048]{0:T(1024)(128)(2,1)}, u32[]{:S(2)}) copy-start(bf16[2048]{0:T(1024)(128)(2,1)} %gain_ref.5) | copy-start | bytes 12292
  32.9 10.3 %copy-start = (bf16[1024,2048]{1,0:T(8,128)(2,1)S(1)}, bf16[1024,2048]{1,0:T(8,128)(2,1)}, u32[]{:S(2)}) copy-start(bf16[1024,2048]{1,0:T(8,128)(2,1)} %down_ref.1) | copy-start | bytes 12582916
  32.9 1.3 %collective-permute-start.8 = (f32[16,1024]{1,0:T(8,128)S(1)}, f32[16,1024]{1,0:T(8,128)S(1)}, u32[]{:S(2)}, u32[]{:S(2)}) collective-permute-start(f32[16,1024]{1,0:T(8,128)S(1)} %get-tuple-element.55), channel_id=1, source_target_pairs={{0,1},{1,0},{2,3},{3,2},{4,5},{5,4},{6,7},{7,6},{8,9},{9,8},{10,11... | collective-permute-start | bytes 196616 | tf_op jit(solution)/shard_map/ppermute | solution.py:539
  34.2 4.0 %collective-permute-start.10 = (bf16[16,1024]{1,0:T(8,128)(2,1)S(1)}, bf16[16,1024]{1,0:T(8,128)(2,1)S(1)}, u32[]{:S(2)}, u32[]{:S(2)}) collective-permute-start(bf16[16,1024]{1,0:T(8,128)(2,1)S(1)} %add_convert_fusion.1), channel_id=1, source_target_pairs={{0,6},{1,7},{2,0},{3,1},{4,2},{5,3},{6,4},{7,5},{8,14},{9,15},{10,... | collective-permute-start | bytes 98312 | tf_op jit(solution)/shard_map/ppermute | solution.py:553
  35.1 4.8 %collective-permute-start.11 = (bf16[16,1024]{1,0:T(8,128)(2,1)S(1)}, bf16[16,1024]{1,0:T(8,128)(2,1)S(1)}, u32[]{:S(2)}, u32[]{:S(2)}) collective-permute-start(bf16[16,1024]{1,0:T(8,128)(2,1)S(1)} %add_convert_fusion.1), channel_id=1, source_target_pairs={{0,4},{1,5},{2,6},{3,7},{4,0},{5,1},{6,2},{7,3},{8,12},{9,13},{10,... | collective-permute-start | bytes 98312 | tf_op jit(solution)/shard_map/ppermute | solution.py:553
  36.2 5.7 %collective-permute-start.9 = (bf16[16,1024]{1,0:T(8,128)(2,1)S(1)}, bf16[16,1024]{1,0:T(8,128)(2,1)S(1)}, u32[]{:S(2)}, u32[]{:S(2)}) collective-permute-start(bf16[16,1024]{1,0:T(8,128)(2,1)S(1)} %add_convert_fusion.1), channel_id=1, source_target_pairs={{0,2},{1,3},{2,4},{3,5},{4,6},{5,7},{6,0},{7,1},{8,10},{9,11},{10,... | collective-permute-start | bytes 98312 | tf_op jit(solution)/shard_map/ppermute | solution.py:553
  42.0 1.3 %collective-permute-start.12 = (bf16[16,1024]{1,0:T(8,128)(2,1)S(1)}, bf16[16,1024]{1,0:T(8,128)(2,1)S(1)}, u32[]{:S(2)}, u32[]{:S(2)}) collective-permute-start(bf16[16,1024]{1,0:T(8,128)(2,1)S(1)} %add_convert_fusion.side_ref.mine_ref), channel_id=1, source_target_pairs={{0,1},{1,0},{2,3},{3,2},{4,5},{5,4},{6,7},{7,6},{8,9},{9,8},{10,11... | collective-permute-start | bytes 98312 | tf_op jit(solution)/shard_map/ppermute | solution.py:555

commit v8 on v7

--- a/solution.py
+++ b/solution.py
@@ -261,7 +261,7 @@
 
 
 def merge_kernel(
-    rows, part_ref, new_ref, w_ref, mine_ref, other_ref, rows_ref, attended_ref, full_ref
+    rows, part_ref, new_ref, w_ref, mine_ref, other_ref, rows_ref, attended_ref
 ):
     copies, groups, wire_rows, chunk = part_ref.shape
     lanes = w_ref.shape[0]
@@ -301,11 +301,11 @@
         attended_ref[c, pl.ds(r, groups, stride=rows), :] = mixture / total
     attended = [attended_ref[c] for c in range(lanes // chunk)]
     attended = jnp.concatenate(attended, axis=1).astype(BF16)
-    full_ref[...] = jnp.dot(attended, w_ref[...], preferred_element_type=F32)
     width = mine_ref.shape[1]
     core = lax.axis_index("tensor") % 2
-    mine_ref[...] = full_ref[:, pl.ds(pl.multiple_of(core * width, LANE), width)]
-    other_ref[...] = full_ref[:, pl.ds(pl.multiple_of((1 - core) * width, LANE), width)]
+    for half, to_ref in ((1 - core, other_ref), (core, mine_ref)):
+        weights = w_ref[:, pl.ds(pl.multiple_of(half * width, LANE), width)]
+        to_ref[...] = jnp.dot(attended, weights, preferred_element_type=F32)
 
 
 def spread_rows(values, wide_ref):
@@ -516,10 +516,12 @@
 
     cache = (key_cache, value_cache, sink_keys, sink_values, live)
     part = attention((0,), (queries[0], *cache), {}, "own_heads")
-    queries, new_part, part = lax.optimization_barrier((queries, new_part, part))
-    part = attention(
-        tuple(range(1, chips)), (*queries[1:], *cache, part), {chips + 4: 0}, "other_heads"
-    )
+    first, new_part, part = lax.optimization_barrier((queries[1:-1], new_part, part))
+    queries = [queries[0], *first, queries[-1]]
+    middle = tuple(range(1, chips - 1))
+    part = attention(middle, (*queries[1:-1], *cache, part), {len(middle) + 5: 0}, "middle_heads")
+    last, part = lax.optimization_barrier((queries[-1], part))
+    part = attention((chips - 1,), (last, *cache, part), {6: 0}, "last_heads")
     part = lax.all_to_all(
         part.reshape(shards * groups, 8, chunk), ("seq", "tensor"), 0, 0, tiled=True
     ).reshape(shards, groups, 8, chunk)
@@ -531,7 +533,6 @@
         scratch=[
             pltpu.VMEM(((shards + 1) * groups * 8, chunk), F32),
             pltpu.VMEM((lanes // chunk, batch, chunk), F32),
-            pltpu.VMEM((batch, width), F32),
         ],
         name="merge",
         flops=MERGE_FLOPS,

time: 54 us -> 53.4 us (0.989)
  waiting for transfers between devices: 7.93 us -> 7.02 us
    ppermute x3, waiting for transfers between devices: 0.92 us -> 0.01 us  [per_device(): lax.ppermute(query, 'tensor', hop)]
    pallas_call x9 -> x10, Pallas kernels: 10.1 us -> 10.2 us  [call(): pl.pallas_call(kernel, out_shape=out, in_specs=specs or [VMEM_SPEC] * len...]
  transfers between devices with their start and end apart: 13 -> 13, of which waited for: 7 -> 6; matrix products, arithmetic and copies ran while one was open for 0% -> 0% of each run, Pallas kernels for 10% -> 13%
where the time goes in v8:
time: 53.4 us; the launch traced here: 53.2 us
  blocking collectives  19.8 us (37%)
  starting transfers between devices  13.7 us (26%)
  Pallas kernels  10.2 us (19%)
  waiting for transfers between devices  7.02 us (13%)
  between operations  0.99 us (2%)
  other arithmetic  0.76 us (1%)
  local copies, waits for them, and re-layouts  0.74 us (1%)
    all_to_all x1, blocking collectives, per_device(): lax.all_to_all(part.reshape(shards * groups, 8, chunk), ('seq', 'tensor')...  11.5 us
    pallas_call x10, Pallas kernels, call(): pl.pallas_call(kernel, out_shape=out, in_specs=specs or [VMEM_SPEC] * len...  10.2 us
    all_to_all x1, blocking collectives, per_device(): partial = lax.all_to_all(partial, 'tensor', 0, 0, tiled=True)  8.29 us
    ppermute x3, starting transfers between devices, per_device(): column = [states] + [lax.ppermute(states, 'tensor', hop) for hop in hops]  6.57 us
    ppermute x3, waiting for transfers between devices, per_device(): total = total + lax.ppermute(chip, 'tensor', hops[which]).astype(F32)  4.58 us
    ppermute x3, starting transfers between devices, per_device(): lax.ppermute(query, 'tensor', hop)  3.88 us
    ppermute x3, starting transfers between devices, per_device(): total = total + lax.ppermute(chip, 'tensor', hops[which]).astype(F32)  2.42 us
    ppermute x3, waiting for transfers between devices, per_device(): column = [states] + [lax.ppermute(states, 'tensor', hop) for hop in hops]  1.19 us
  transfers between devices with their start and end apart: 13, of which 6 were waited for; matrix products, arithmetic and copies ran while one was open for 0% of the time, Pallas kernels for 13%

profile of v8, /device:TPU:0, one launch (start us, length us, event | category | flops | bytes accessed | tf_op | source)
XLA Modules:
  0.0 53.2 jit_solution(13936971564030606492)
XLA Ops:
  0.6 0.0 slice-start.2
  0.6 0.0 slice-start.4
  0.7 0.0 slice-start.3
  0.7 0.0 slice-start.5
  0.7 0.5 collective-permute-start.3
  1.3 2.6 %collective-permute-start = (bf16[2,2048]{1,0:T(2,128)(2,1)}, bf16[2,2048]{1,0:T(2,128)(2,1)S(1)}, u32[]{:S(2)}, u32[]{:S(2)}) collective-permute-start(bf16[2,2048]{1,0:T(2,128)(2,1)} %refs_0_.1), channel_id=1, source_target_pairs={{0,2},{1,3},{2,4},{3,5},{4,6},{5,7},{6,0},{7,1},{8,10},{9,11},{10,... | collective-permute-start | bytes 24584 | tf_op jit(solution)/shard_map/ppermute | solution.py:476
  3.9 2.6 %collective-permute-start.1 = (bf16[2,2048]{1,0:T(2,128)(2,1)}, bf16[2,2048]{1,0:T(2,128)(2,1)S(1)}, u32[]{:S(2)}, u32[]{:S(2)}) collective-permute-start(bf16[2,2048]{1,0:T(2,128)(2,1)} %refs_0_.1), channel_id=1, source_target_pairs={{0,4},{1,5},{2,6},{3,7},{4,0},{5,1},{6,2},{7,3},{8,12},{9,13},{10,... | collective-permute-start | bytes 24584 | tf_op jit(solution)/shard_map/ppermute | solution.py:476
  6.5 1.3 %collective-permute-start.2 = (bf16[2,2048]{1,0:T(2,128)(2,1)}, bf16[2,2048]{1,0:T(2,128)(2,1)S(1)}, u32[]{:S(2)}, u32[]{:S(2)}) collective-permute-start(bf16[2,2048]{1,0:T(2,128)(2,1)} %refs_0_.1), channel_id=1, source_target_pairs={{0,6},{1,7},{2,0},{3,1},{4,2},{5,3},{6,4},{7,5},{8,14},{9,15},{10,... | collective-permute-start | bytes 24584 | tf_op jit(solution)/shard_map/ppermute | solution.py:476
  7.8 0.7 %copy-done.11 = s32[16]{0:T(128)S(1)} copy-done((s32[16]{0:T(128)S(1)}, s32[16]{0:T(128)}, u32[]{:S(2)}) %copy-start.11) | copy-done | bytes 88
  8.5 0.6 %prepare.1 = (f32[16,128]{1,0:T(8,128)S(1)}, f32[16,128]{1,0:T(8,128)S(1)}) custom-call(s32[16]{0:T(128)S(1)} %copy-done.11), custom_call_target="tpu_custom_call" | custom-call | flops 20000000000 | bytes 64 | tf_op jit(solution)/shard_map/prepare/pallas_call | solution.py:421
  9.1 0.0 copy-start.5
  9.1 0.0 copy-start.6
  9.1 0.0 collective-permute-done.refs_1_
  9.2 0.0 collective-permute-done.1.refs_2_
  9.2 1.2 %collective-permute-done.2.refs_3_ = bf16[2,2048]{1,0:T(2,128)(2,1)S(1)} collective-permute-done((bf16[2,2048]{1,0:T(2,128)(2,1)}, bf16[2,2048]{1,0:T(2,128)(2,1)S(1)}, u32[]{:S(2)}, u32[]{:S(2)}) %collective-permute-start.2) | collective-permute-done | bytes 8224 | tf_op jit(solution)/shard_map/ppermute | solution.py:476
  10.3 0.1 pad_maximum_fusion.same_ref
  10.4 0.1 collective-permute-start.7
  10.5 0.0 collective-permute-done.3.refs_6_
  10.5 0.6 %query.1 = (f32[8,128]{1,0:T(8,128)S(1)}, f32[8,128]{1,0:T(8,128)S(1)}, f32[8,128]{1,0:T(8,128)S(1)}, f32[8,128]{1,0:T(8,128)S(1)}) custom-call(bf16[2,2048]{1,0:T(2,128)(2,1)S(1)} %copy-done.2, bf16[2,2048]{1,0:T(2,128)(2,1)S(1)} %collective-permute-done.refs_1_, bf16[2,2048]{1,0:T(2,128)(2,1)S(1)} %collective-permute-done.1.refs_2_, ...), custom_call_target="tpu_custom_call" | custom-call | flops 2000000000 | bytes 6344704 | tf_op jit(solution)/shard_map/query/pallas_call | solution.py:421
  11.1 0.3 collective-permute-start.5
  11.4 3.4 %collective-permute-start.6 = (f32[8,128]{1,0:T(8,128)S(1)}, f32[8,128]{1,0:T(8,128)S(1)}, u32[]{:S(2)}, u32[]{:S(2)}) collective-permute-start(f32[8,128]{1,0:T(8,128)S(1)} %get-tuple-element.45), channel_id=1, source_target_pairs={{0,4},{1,5},{2,6},{3,7},{4,0},{5,1},{6,2},{7,3},{8,12},{9,13},{10,... | collective-permute-start | bytes 12296 | tf_op jit(solution)/shard_map/ppermute | solution.py:491
  14.8 0.1 collective-permute-start.4
  15.0 1.5 %new_token.1 = (f32[8,8,128]{2,1,0:T(8,128)S(1)}, f32[8,8,128]{2,1,0:T(8,128)S(1)}, s32[2,1024]{1,0:T(2,128)S(1)}) custom-call(s32[16]{0:T(128)S(1)} %copy-done.10, s32[16]{0:T(128)S(1)} %copy-done.12, s32[2,1024]{1,0:T(2,128)S(1)} %copy-done.7, s32[2,1024]{1,0:T(2,128)S(1)} %copy-done.8, bf16[4,2,2048]{2,1,0:T(2,128)(2,1)S(1)} %pad_maximum_fusion.same_ref, ...), custom_call_target="tpu_custom_call" | custom-call | flops 2000000000 | bytes 3248256 | tf_op jit(solution)/shard_map/new_token/pallas_call | solution.py:421
  16.5 1.0 %own_heads.1.refs_7_ = bf16[4,8,8,128]{3,2,1,0:T(8,128)(2,1)S(1)} custom-call(f32[8,128]{1,0:T(8,128)S(1)} %get-tuple-element.48.refs_0_, bf16[2,2048,1024]{2,1,0:T(8,128)(2,1)S(1)} %bitcast.18, bf16[2,2048,1024]{2,1,0:T(8,128)(2,1)S(1)} %bitcast.20, bf16[2,4,2048]{2,1,0:T(4,128)(2,1)S(1)} %bitcast.24, bf16[2,4,2048]{2,1,0:T(4,128)(2,1)S(1)} %bitcast.27, ...), custom_call_target="tpu_custom_call" | custom-call | flops 10000000000 | bytes 16855040 | tf_op jit(solution)/shard_map/own_heads/pallas_call | solution.py:421
  17.5 0.0 collective-permute-done.5.refs_0_
  17.5 1.8 %middle_heads.1.refs_6_ = bf16[4,8,8,128]{3,2,1,0:T(8,128)(2,1)S(1)} custom-call(f32[8,128]{1,0:T(8,128)S(1)} %collective-permute-done.5.refs_0_, f32[8,128]{1,0:T(8,128)S(1)} %collective-permute-done.6.refs_1_, bf16[2,2048,1024]{2,1,0:T(8,128)(2,1)S(1)} %bitcast.18, bf16[2,2048,1024]{2,1,0:T(8,128)(2,1)S(1)} %bitcast.20, ...), custom_call_target="tpu_custom_call", output_to_operand_aliasing={{}: (7, {})} | custom-call | flops 10000000000 | bytes 16924672 | tf_op jit(solution)/shard_map/middle_heads/pallas_call | solution.py:421
  19.3 0.0 copy-start.4
  19.4 0.0 collective-permute-done.4.refs_0_
  19.4 0.0 slice-start
  19.4 1.0 %last_heads.1 = bf16[4,8,8,128]{3,2,1,0:T(8,128)(2,1)S(1)} custom-call(f32[8,128]{1,0:T(8,128)S(1)} %collective-permute-done.4.refs_0_, bf16[2,2048,1024]{2,1,0:T(8,128)(2,1)S(1)} %bitcast.18, bf16[2,2048,1024]{2,1,0:T(8,128)(2,1)S(1)} %bitcast.20, bf16[2,4,2048]{2,1,0:T(4,128)(2,1)S(1)} %bitcast.26, ...), custom_call_target="tpu_custom_call", output_to_operand_aliasing={{}: (6, {})} | custom-call | flops 10000000000 | bytes 16920576 | tf_op jit(solution)/shard_map/last_heads/pallas_call | solution.py:421
  20.4 11.5 %all_to_all.10 = bf16[32,8,128]{2,1,0:T(8,128)(2,1)S(1)} all-to-all(bf16[32,8,128]{2,1,0:T(8,128)(2,1)S(1)} %bitcast.11), channel_id=1, replica_groups=mesh['seq'=4,'tensor'=8] {'seq','tensor'}, dimensions={0} | all-to-all | bytes 131072 | tf_op jit(solution)/shard_map/all_to_all | solution.py:525
  31.8 0.4 merge.1
  32.3 0.1 collective-permute-start.8
  32.4 1.1 %collective-permute-done.8 = f32[16,1024]{1,0:T(8,128)S(1)} collective-permute-done((f32[16,1024]{1,0:T(8,128)S(1)}, f32[16,1024]{1,0:T(8,128)S(1)}, u32[]{:S(2)}, u32[]{:S(2)}) %collective-permute-start.8) | collective-permute-done | bytes 65568 | tf_op jit(solution)/shard_map/ppermute | solution.py:540
  33.6 0.8 %collective-permute-start.10 = (bf16[16,1024]{1,0:T(8,128)(2,1)S(1)}, bf16[16,1024]{1,0:T(8,128)(2,1)S(1)}, u32[]{:S(2)}, u32[]{:S(2)}) collective-permute-start(bf16[16,1024]{1,0:T(8,128)(2,1)S(1)} %add_convert_fusion.1), channel_id=1, source_target_pairs={{0,6},{1,7},{2,0},{3,1},{4,2},{5,3},{6,4},{7,5},{8,14},{9,15},{10,... | collective-permute-start | bytes 98312 | tf_op jit(solution)/shard_map/ppermute | solution.py:554
  34.4 1.1 %collective-permute-start.11 = (bf16[16,1024]{1,0:T(8,128)(2,1)S(1)}, bf16[16,1024]{1,0:T(8,128)(2,1)S(1)}, u32[]{:S(2)}, u32[]{:S(2)}) collective-permute-start(bf16[16,1024]{1,0:T(8,128)(2,1)S(1)} %add_convert_fusion.1), channel_id=1, source_target_pairs={{0,4},{1,5},{2,6},{3,7},{4,0},{5,1},{6,2},{7,3},{8,12},{9,13},{10,... | collective-permute-start | bytes 98312 | tf_op jit(solution)/shard_map/ppermute | solution.py:554
  35.5 0.5 collective-permute-start.9
  36.0 0.7 %outputs.1 = (bf16[16,256]{1,0:T(8,128)(2,1)}, bf16[16,256]{1,0:T(8,128)(2,1)}, f32[16,1024]{1,0:T(8,128)S(1)}) custom-call(bf16[4,2,2048]{2,1,0:T(2,128)(2,1)S(1)} %pad_maximum_fusion.same_ref, bf16[4,2,2048]{2,1,0:T(2,128)(2,1)S(1)} %collective-permute-done.7.peer_ref, f32[8,8,128]{2,1,0:T(8,128)S(1)} %get-tuple-element.61.new_ref, ...), custom_call_target="tpu_custom_call" | custom-call | bytes 131072 | tf_op jit(solution)/shard_map/outputs/pallas_call | solution.py:421
  36.7 0.9 %collective-permute-done.10 = bf16[16,1024]{1,0:T(8,128)(2,1)S(1)} collective-permute-done((bf16[16,1024]{1,0:T(8,128)(2,1)S(1)}, bf16[16,1024]{1,0:T(8,128)(2,1)S(1)}, u32[]{:S(2)}, u32[]{:S(2)}) %collective-permute-start.10) | collective-permute-done | bytes 32800 | tf_op jit(solution)/shard_map/ppermute | solution.py:554
  37.5 1.7 %collective-permute-done.11 = bf16[16,1024]{1,0:T(8,128)(2,1)S(1)} collective-permute-done((bf16[16,1024]{1,0:T(8,128)(2,1)S(1)}, bf16[16,1024]{1,0:T(8,128)(2,1)S(1)}, u32[]{:S(2)}, u32[]{:S(2)}) %collective-permute-start.11) | collective-permute-done | bytes 32800 | tf_op jit(solution)/shard_map/ppermute | solution.py:554
  39.2 2.0 %collective-permute-done.9 = bf16[16,1024]{1,0:T(8,128)(2,1)S(1)} collective-permute-done((bf16[16,1024]{1,0:T(8,128)(2,1)S(1)}, bf16[16,1024]{1,0:T(8,128)(2,1)S(1)}, u32[]{:S(2)}, u32[]{:S(2)}) %collective-permute-start.9) | collective-permute-done | bytes 32800 | tf_op jit(solution)/shard_map/ppermute | solution.py:554
  41.3 0.1 collective-permute-start.12
  41.4 1.1 %first_half.1 = (f32[32,1024]{1,0:T(8,128)S(1)}, f32[16,128]{1,0:T(8,128)S(1)}) custom-call(bf16[16,1024]{1,0:T(8,128)(2,1)S(1)} %add_convert_fusion.side_ref.mine_ref, bf16[2048]{0:T(1024)(128)(2,1)S(1)} %copy-done.1, bf16[2048,2,1024]{2,1,0:T(2,128)(2,1)S(1)} %bitcast.10), custom_call_target="tpu_custom_call" | custom-call | flops 67108864 | bytes 8425472 | tf_op jit(solution)/shard_map/first_half/pallas_call | solution.py:421
  42.5 0.1 collective-permute-done.12.other_ref
  42.6 1.6 %mlp.1 = (bf16[8,2,2048]{2,1,0:T(2,128)(2,1)S(1)}, f32[2,2048]{1,0:T(2,128)S(1)}) custom-call(bf16[16,1024]{1,0:T(8,128)(2,1)S(1)} %add_convert_fusion.side_ref.mine_ref, bf16[16,1024]{1,0:T(8,128)(2,1)S(1)} %collective-permute-done.12.other_ref, bf16[2048]{0:T(1024)(128)(2,1)S(1)} %copy-done.1, bf16[2048,2,1024]{2,1,0:T(2,128)(2,1)S(1)} %bitcast.10, ...), custom_call_target="tpu_custom_call" | custom-call | flops 134217728 | bytes 12791808 | tf_op jit(solution)/shard_map/mlp/pallas_call | solution.py:421
  44.2 8.3 %all_to_all.11 = bf16[8,2,2048]{2,1,0:T(2,128)(2,1)S(1)} all-to-all(bf16[8,2,2048]{2,1,0:T(2,128)(2,1)S(1)} %get-tuple-element.68), channel_id=1, replica_groups=mesh['seq'=4,'tensor'=8] {'tensor'}, dimensions={0} | all-to-all | bytes 131072 | tf_op jit(solution)/shard_map/all_to_all | solution.py:576
  52.5 0.1 convert_reduce_fusion
  52.6 0.6 %add_convert_fusion.2 = bf16[2,2048]{1,0:T(2,128)(2,1)} fusion(f32[2,2048]{1,0:T(2,128)S(1)} %get-tuple-element.67, f32[2,2048]{1,0:T(2,128)S(1)} %convert_reduce_fusion), kind=kLoop, calls=%fused_computation.4 | loop fusion | flops 8192 | bytes 40960 | tf_op jit(solution)/shard_map/convert_element_type | solution.py:577
  (36 shorter events, 0.1 us)
Async XLA Ops:
  0.6 15.8 %slice-start.2 = ((s8[8388608]{0:T(1024)(128)(4,1)}), s8[4194304]{0:T(1024)(128)(4,1)S(1)}, s32[]{:S(2)}) async-start(s8[8388608]{0:T(1024)(128)(4,1)} %bitcast.17), calls=%async_computation.4 | async-start | bytes 8388608
  0.6 15.8 %slice-start.4 = ((s8[8388608]{0:T(1024)(128)(4,1)}), s8[4194304]{0:T(1024)(128)(4,1)S(1)}, s32[]{:S(2)}) async-start(s8[8388608]{0:T(1024)(128)(4,1)} %bitcast.19), calls=%async_computation.6 | async-start | bytes 8388608
  0.7 9.7 %copy-start.2 = (bf16[2,2048]{1,0:T(2,128)(2,1)S(1)}, bf16[2,2048]{1,0:T(2,128)(2,1)}, u32[]{:S(2)}) copy-start(bf16[2,2048]{1,0:T(2,128)(2,1)} %refs_0_.1) | copy-start | bytes 24580
  0.7 9.8 %copy-start.3 = (bf16[2048,3,256]{2,0,1:T(8,128)(2,1)S(1)}, bf16[2048,3,256]{2,0,1:T(8,128)(2,1)}, u32[]{:S(2)}) copy-start(bf16[2048,3,256]{2,0,1:T(8,128)(2,1)} %param.17) | copy-start | bytes 9437188
  0.7 9.8 %copy-start.9 = (bf16[2048]{0:T(1024)(128)(2,1)S(1)}, bf16[2048]{0:T(1024)(128)(2,1)}, u32[]{:S(2)}) copy-start(bf16[2048]{0:T(1024)(128)(2,1)} %gain_ref.3) | copy-start | bytes 12292
  0.7 14.3 %copy-start.7 = (s32[2,1024]{1,0:T(2,128)S(1)}, s32[2,1024]{1,0:T(2,128)}, u32[]{:S(2)}) copy-start(s32[2,1024]{1,0:T(2,128)} %mask_ref.1) | copy-start | bytes 24580
  0.7 14.3 %copy-start.8 = (s32[2,1024]{1,0:T(2,128)S(1)}, s32[2,1024]{1,0:T(2,128)}, u32[]{:S(2)}) copy-start(s32[2,1024]{1,0:T(2,128)} %slot_pos_ref.1) | copy-start | bytes 24580
  0.7 14.3 %copy-start.10 = (s32[16]{0:T(128)S(1)}, s32[16]{0:T(128)}, u32[]{:S(2)}) copy-start(s32[16]{0:T(128)} %len_ref.1) | copy-start | bytes 196
  0.7 15.8 %slice-start.3 = ((s8[8388608]{0:T(1024)(128)(4,1)}), s8[4194304]{0:T(1024)(128)(4,1)S(1)}, s32[]{:S(2)}) async-start(s8[8388608]{0:T(1024)(128)(4,1)} %bitcast.17), calls=%async_computation.5 | async-start | bytes 8388608
  0.7 15.8 %slice-start.5 = ((s8[8388608]{0:T(1024)(128)(4,1)}), s8[4194304]{0:T(1024)(128)(4,1)S(1)}, s32[]{:S(2)}) async-start(s8[8388608]{0:T(1024)(128)(4,1)} %bitcast.19), calls=%async_computation.7 | async-start | bytes 8388608
  0.7 9.8 %collective-permute-start.3 = (bf16[3,2048,256]{2,1,0:T(8,128)(2,1)}, bf16[3,2048,256]{2,1,0:T(8,128)(2,1)S(1)}, u32[]{:S(2)}, u32[]{:S(2)}) collective-permute-start(bf16[3,2048,256]{2,1,0:T(8,128)(2,1)} %bitcast.21), channel_id=1, source_target_pairs={{0,1},{1,0},{2,3},{3,2},{4,5},{5,4},{6,7},{7,6},{8,9},{9,8},{10,11... | collective-permute-start | bytes 9437192 | tf_op jit(solution)/shard_map/ppermute | solution.py:478
  1.3 7.9 %collective-permute-start = (bf16[2,2048]{1,0:T(2,128)(2,1)}, bf16[2,2048]{1,0:T(2,128)(2,1)S(1)}, u32[]{:S(2)}, u32[]{:S(2)}) collective-permute-start(bf16[2,2048]{1,0:T(2,128)(2,1)} %refs_0_.1), channel_id=1, source_target_pairs={{0,2},{1,3},{2,4},{3,5},{4,6},{5,7},{6,0},{7,1},{8,10},{9,11},{10,... | collective-permute-start | bytes 24584 | tf_op jit(solution)/shard_map/ppermute | solution.py:476
  3.9 5.3 %collective-permute-start.1 = (bf16[2,2048]{1,0:T(2,128)(2,1)}, bf16[2,2048]{1,0:T(2,128)(2,1)S(1)}, u32[]{:S(2)}, u32[]{:S(2)}) collective-permute-start(bf16[2,2048]{1,0:T(2,128)(2,1)} %refs_0_.1), channel_id=1, source_target_pairs={{0,4},{1,5},{2,6},{3,7},{4,0},{5,1},{6,2},{7,3},{8,12},{9,13},{10,... | collective-permute-start | bytes 24584 | tf_op jit(solution)/shard_map/ppermute | solution.py:476
  6.5 3.9 %collective-permute-start.2 = (bf16[2,2048]{1,0:T(2,128)(2,1)}, bf16[2,2048]{1,0:T(2,128)(2,1)S(1)}, u32[]{:S(2)}, u32[]{:S(2)}) collective-permute-start(bf16[2,2048]{1,0:T(2,128)(2,1)} %refs_0_.1), channel_id=1, source_target_pairs={{0,6},{1,7},{2,0},{3,1},{4,2},{5,3},{6,4},{7,5},{8,14},{9,15},{10,... | collective-permute-start | bytes 24584 | tf_op jit(solution)/shard_map/ppermute | solution.py:476
  7.8 0.7 %copy-start.11 = (s32[16]{0:T(128)S(1)}, s32[16]{0:T(128)}, u32[]{:S(2)}) copy-start(s32[16]{0:T(128)} %pos_ref.3) | copy-start | bytes 196
  8.5 6.5 %copy-start.12 = (s32[16]{0:T(128)S(1)}, s32[16]{0:T(128)}, u32[]{:S(2)}) copy-start(s32[16]{0:T(128)} %pos_ref.3) | copy-start | bytes 196
  9.1 7.4 %copy-start.5 = (bf16[2,2048,4]{1,2,0:T(4,128)(2,1)S(1)}, bf16[2,2048,4]{1,2,0:T(4,128)(2,1)}, u32[]{:S(2)}) copy-start(bf16[2,2048,4]{1,2,0:T(4,128)(2,1)} %param.24) | copy-start | bytes 98308
  9.1 7.4 %copy-start.6 = (bf16[2,2048,4]{1,2,0:T(4,128)(2,1)S(1)}, bf16[2,2048,4]{1,2,0:T(4,128)(2,1)}, u32[]{:S(2)}) copy-start(bf16[2,2048,4]{1,2,0:T(4,128)(2,1)} %param.25) | copy-start | bytes 98308
  10.4 4.6 %collective-permute-start.7 = (bf16[4,2,2048]{2,1,0:T(2,128)(2,1)S(1)}, bf16[4,2,2048]{2,1,0:T(2,128)(2,1)S(1)}, u32[]{:S(2)}, u32[]{:S(2)}) collective-permute-start(bf16[4,2,2048]{2,1,0:T(2,128)(2,1)S(1)} %pad_maximum_fusion.same_ref), channel_id=1, source_target_pairs={{0,1},{1,0},{2,3},{3,2},{4,5},{5,4},{6,7},{7,6},{8,9},{9,8},{10,11... | collective-permute-start | bytes 98312 | tf_op jit(solution)/shard_map/ppermute | solution.py:488
  11.1 6.4 %collective-permute-start.5 = (f32[8,128]{1,0:T(8,128)S(1)}, f32[8,128]{1,0:T(8,128)S(1)}, u32[]{:S(2)}, u32[]{:S(2)}) collective-permute-start(f32[8,128]{1,0:T(8,128)S(1)} %get-tuple-element.44), channel_id=1, source_target_pairs={{0,2},{1,3},{2,4},{3,5},{4,6},{5,7},{6,0},{7,1},{8,10},{9,11},{10,... | collective-permute-start | bytes 12296 | tf_op jit(solution)/shard_map/ppermute | solution.py:491
  11.4 6.1 %collective-permute-start.6 = (f32[8,128]{1,0:T(8,128)S(1)}, f32[8,128]{1,0:T(8,128)S(1)}, u32[]{:S(2)}, u32[]{:S(2)}) collective-permute-start(f32[8,128]{1,0:T(8,128)S(1)} %get-tuple-element.45), channel_id=1, source_target_pairs={{0,4},{1,5},{2,6},{3,7},{4,0},{5,1},{6,2},{7,3},{8,12},{9,13},{10,... | collective-permute-start | bytes 12296 | tf_op jit(solution)/shard_map/ppermute | solution.py:491
  14.8 4.5 %collective-permute-start.4 = (f32[8,128]{1,0:T(8,128)S(1)}, f32[8,128]{1,0:T(8,128)S(1)}, u32[]{:S(2)}, u32[]{:S(2)}) collective-permute-start(f32[8,128]{1,0:T(8,128)S(1)} %get-tuple-element.43), channel_id=1, source_target_pairs={{0,6},{1,7},{2,0},{3,1},{4,2},{5,3},{6,4},{7,5},{8,14},{9,15},{10,... | collective-permute-start | bytes 12296 | tf_op jit(solution)/shard_map/ppermute | solution.py:491
  19.3 12.5 %copy-start.4 = (bf16[256,2048]{1,0:T(8,128)(2,1)S(1)}, bf16[256,2048]{1,0:T(8,128)(2,1)}, u32[]{:S(2)}) copy-start(bf16[256,2048]{1,0:T(8,128)(2,1)} %w_ref.1) | copy-start | bytes 3145732
  19.4 22.0 %slice-start = ((s8[8388608]{0:T(1024)(128)(4,1)}), s8[4194304]{0:T(1024)(128)(4,1)S(1)}, s32[]{:S(2)}) async-start(s8[8388608]{0:T(1024)(128)(4,1)} %bitcast.9), calls=%async_computation.2 | async-start | bytes 8388608
  31.8 9.5 %slice-start.1 = ((s8[8388608]{0:T(1024)(128)(4,1)}), s8[4194304]{0:T(1024)(128)(4,1)S(1)}, s32[]{:S(2)}) async-start(s8[8388608]{0:T(1024)(128)(4,1)} %bitcast.9), calls=%async_computation.3 | async-start | bytes 8388608
  31.8 9.6 %copy-start.1 = (bf16[2048]{0:T(1024)(128)(2,1)S(1)}, bf16[2048]{0:T(1024)(128)(2,1)}, u32[]{:S(2)}) copy-start(bf16[2048]{0:T(1024)(128)(2,1)} %gain_ref.5) | copy-start | bytes 12292
  32.3 10.3 %copy-start = (bf16[1024,2048]{1,0:T(8,128)(2,1)S(1)}, bf16[1024,2048]{1,0:T(8,128)(2,1)}, u32[]{:S(2)}) copy-start(bf16[1024,2048]{1,0:T(8,128)(2,1)} %down_ref.1) | copy-start | bytes 12582916
  32.3 1.3 %collective-permute-start.8 = (f32[16,1024]{1,0:T(8,128)S(1)}, f32[16,1024]{1,0:T(8,128)S(1)}, u32[]{:S(2)}, u32[]{:S(2)}) collective-permute-start(f32[16,1024]{1,0:T(8,128)S(1)} %get-tuple-element.57), channel_id=1, source_target_pairs={{0,1},{1,0},{2,3},{3,2},{4,5},{5,4},{6,7},{7,6},{8,9},{9,8},{10,11... | collective-permute-start | bytes 196616 | tf_op jit(solution)/shard_map/ppermute | solution.py:540
  33.6 4.0 %collective-permute-start.10 = (bf16[16,1024]{1,0:T(8,128)(2,1)S(1)}, bf16[16,1024]{1,0:T(8,128)(2,1)S(1)}, u32[]{:S(2)}, u32[]{:S(2)}) collective-permute-start(bf16[16,1024]{1,0:T(8,128)(2,1)S(1)} %add_convert_fusion.1), channel_id=1, source_target_pairs={{0,6},{1,7},{2,0},{3,1},{4,2},{5,3},{6,4},{7,5},{8,14},{9,15},{10,... | collective-permute-start | bytes 98312 | tf_op jit(solution)/shard_map/ppermute | solution.py:554
  34.4 4.8 %collective-permute-start.11 = (bf16[16,1024]{1,0:T(8,128)(2,1)S(1)}, bf16[16,1024]{1,0:T(8,128)(2,1)S(1)}, u32[]{:S(2)}, u32[]{:S(2)}) collective-permute-start(bf16[16,1024]{1,0:T(8,128)(2,1)S(1)} %add_convert_fusion.1), channel_id=1, source_target_pairs={{0,4},{1,5},{2,6},{3,7},{4,0},{5,1},{6,2},{7,3},{8,12},{9,13},{10,... | collective-permute-start | bytes 98312 | tf_op jit(solution)/shard_map/ppermute | solution.py:554
  35.5 5.7 %collective-permute-start.9 = (bf16[16,1024]{1,0:T(8,128)(2,1)S(1)}, bf16[16,1024]{1,0:T(8,128)(2,1)S(1)}, u32[]{:S(2)}, u32[]{:S(2)}) collective-permute-start(bf16[16,1024]{1,0:T(8,128)(2,1)S(1)} %add_convert_fusion.1), channel_id=1, source_target_pairs={{0,2},{1,3},{2,4},{3,5},{4,6},{5,7},{6,0},{7,1},{8,10},{9,11},{10,... | collective-permute-start | bytes 98312 | tf_op jit(solution)/shard_map/ppermute | solution.py:554
  41.3 1.3 %collective-permute-start.12 = (bf16[16,1024]{1,0:T(8,128)(2,1)S(1)}, bf16[16,1024]{1,0:T(8,128)(2,1)S(1)}, u32[]{:S(2)}, u32[]{:S(2)}) collective-permute-start(bf16[16,1024]{1,0:T(8,128)(2,1)S(1)} %add_convert_fusion.side_ref.mine_ref), channel_id=1, source_target_pairs={{0,1},{1,0},{2,3},{3,2},{4,5},{5,4},{6,7},{7,6},{8,9},{9,8},{10,11... | collective-permute-start | bytes 98312 | tf_op jit(solution)/shard_map/ppermute | solution.py:556

commit v9 on v8

--- a/solution.py
+++ b/solution.py
@@ -485,8 +485,8 @@
         flops=QKV_FLOPS,
     )
     same = jnp.stack(column)
+    same, *queries = lax.optimization_barrier((same, *queries))
     peer = lax.ppermute(same, "tensor", across)
-    same, *queries = lax.optimization_barrier((same, *queries))
     queries = [queries[0]] + [
         lax.ppermute(query, "tensor", hop) for query, hop in zip(queries[1:], hops)
     ]

time: 53.4 us -> 53.4 us (level)
  transfers between devices with their start and end apart: 13 -> 13, of which waited for: 6 -> 6; matrix products, arithmetic and copies ran while one was open for 0% -> 0% of each run, Pallas kernels for 13% -> 12%
where the time goes in v9:
time: 53.4 us; the launch traced here: 53.2 us
  blocking collectives  19.8 us (37%)
  starting transfers between devices  13.7 us (26%)
  Pallas kernels  10.2 us (19%)
  waiting for transfers between devices  7.02 us (13%)
  between operations  0.99 us (2%)
  other arithmetic  0.76 us (1%)
  local copies, waits for them, and re-layouts  0.74 us (1%)
    all_to_all x1, blocking collectives, per_device(): lax.all_to_all(part.reshape(shards * groups, 8, chunk), ('seq', 'tensor')...  11.5 us
    pallas_call x10, Pallas kernels, call(): pl.pallas_call(kernel, out_shape=out, in_specs=specs or [VMEM_SPEC] * len...  10.2 us
    all_to_all x1, blocking collectives, per_device(): partial = lax.all_to_all(partial, 'tensor', 0, 0, tiled=True)  8.29 us
    ppermute x3, starting transfers between devices, per_device(): column = [states] + [lax.ppermute(states, 'tensor', hop) for hop in hops]  6.57 us
    ppermute x3, waiting for transfers between devices, per_device(): total = total + lax.ppermute(chip, 'tensor', hops[which]).astype(F32)  4.58 us
    ppermute x3, starting transfers between devices, per_device(): lax.ppermute(query, 'tensor', hop)  3.88 us
    ppermute x3, starting transfers between devices, per_device(): total = total + lax.ppermute(chip, 'tensor', hops[which]).astype(F32)  2.42 us
    ppermute x3, waiting for transfers between devices, per_device(): column = [states] + [lax.ppermute(states, 'tensor', hop) for hop in hops]  1.19 us
  transfers between devices with their start and end apart: 13, of which 6 were waited for; matrix products, arithmetic and copies ran while one was open for 0% of the time, Pallas kernels for 12%

profile of v9, /device:TPU:0, one launch (start us, length us, event | category | flops | bytes accessed | tf_op | source)
XLA Modules:
  0.0 53.2 jit_solution(16892973844201382105)
XLA Ops:
  0.6 0.0 slice-start.2
  0.6 0.0 slice-start.4
  0.7 0.0 slice-start.3
  0.7 0.0 slice-start.5
  0.7 0.5 collective-permute-start.3
  1.3 2.6 %collective-permute-start = (bf16[2,2048]{1,0:T(2,128)(2,1)}, bf16[2,2048]{1,0:T(2,128)(2,1)S(1)}, u32[]{:S(2)}, u32[]{:S(2)}) collective-permute-start(bf16[2,2048]{1,0:T(2,128)(2,1)} %refs_0_.1), channel_id=1, source_target_pairs={{0,2},{1,3},{2,4},{3,5},{4,6},{5,7},{6,0},{7,1},{8,10},{9,11},{10,... | collective-permute-start | bytes 24584 | tf_op jit(solution)/shard_map/ppermute | solution.py:476
  3.9 2.6 %collective-permute-start.1 = (bf16[2,2048]{1,0:T(2,128)(2,1)}, bf16[2,2048]{1,0:T(2,128)(2,1)S(1)}, u32[]{:S(2)}, u32[]{:S(2)}) collective-permute-start(bf16[2,2048]{1,0:T(2,128)(2,1)} %refs_0_.1), channel_id=1, source_target_pairs={{0,4},{1,5},{2,6},{3,7},{4,0},{5,1},{6,2},{7,3},{8,12},{9,13},{10,... | collective-permute-start | bytes 24584 | tf_op jit(solution)/shard_map/ppermute | solution.py:476
  6.5 1.3 %collective-permute-start.2 = (bf16[2,2048]{1,0:T(2,128)(2,1)}, bf16[2,2048]{1,0:T(2,128)(2,1)S(1)}, u32[]{:S(2)}, u32[]{:S(2)}) collective-permute-start(bf16[2,2048]{1,0:T(2,128)(2,1)} %refs_0_.1), channel_id=1, source_target_pairs={{0,6},{1,7},{2,0},{3,1},{4,2},{5,3},{6,4},{7,5},{8,14},{9,15},{10,... | collective-permute-start | bytes 24584 | tf_op jit(solution)/shard_map/ppermute | solution.py:476
  7.8 0.7 %copy-done.11 = s32[16]{0:T(128)S(1)} copy-done((s32[16]{0:T(128)S(1)}, s32[16]{0:T(128)}, u32[]{:S(2)}) %copy-start.11) | copy-done | bytes 88
  8.5 0.6 %prepare.1 = (f32[16,128]{1,0:T(8,128)S(1)}, f32[16,128]{1,0:T(8,128)S(1)}) custom-call(s32[16]{0:T(128)S(1)} %copy-done.11), custom_call_target="tpu_custom_call" | custom-call | flops 20000000000 | bytes 64 | tf_op jit(solution)/shard_map/prepare/pallas_call | solution.py:421
  9.1 0.0 copy-start.5
  9.1 0.0 copy-start.6
  9.1 0.0 collective-permute-done.refs_1_
  9.2 0.0 collective-permute-done.1.refs_2_
  9.2 1.2 %collective-permute-done.2.refs_3_ = bf16[2,2048]{1,0:T(2,128)(2,1)S(1)} collective-permute-done((bf16[2,2048]{1,0:T(2,128)(2,1)}, bf16[2,2048]{1,0:T(2,128)(2,1)S(1)}, u32[]{:S(2)}, u32[]{:S(2)}) %collective-permute-start.2) | collective-permute-done | bytes 8224 | tf_op jit(solution)/shard_map/ppermute | solution.py:476
  10.3 0.1 pad_maximum_fusion.same_ref
  10.4 0.0 collective-permute-done.3.refs_6_
  10.4 0.6 %query.1 = (f32[8,128]{1,0:T(8,128)S(1)}, f32[8,128]{1,0:T(8,128)S(1)}, f32[8,128]{1,0:T(8,128)S(1)}, f32[8,128]{1,0:T(8,128)S(1)}) custom-call(bf16[2,2048]{1,0:T(2,128)(2,1)S(1)} %copy-done.2, bf16[2,2048]{1,0:T(2,128)(2,1)S(1)} %collective-permute-done.refs_1_, bf16[2,2048]{1,0:T(2,128)(2,1)S(1)} %collective-permute-done.1.refs_2_, ...), custom_call_target="tpu_custom_call" | custom-call | flops 2000000000 | bytes 6344704 | tf_op jit(solution)/shard_map/query/pallas_call | solution.py:421
  11.0 0.1 collective-permute-start.7
  11.1 0.3 collective-permute-start.5
  11.4 3.4 %collective-permute-start.6 = (f32[8,128]{1,0:T(8,128)S(1)}, f32[8,128]{1,0:T(8,128)S(1)}, u32[]{:S(2)}, u32[]{:S(2)}) collective-permute-start(f32[8,128]{1,0:T(8,128)S(1)} %get-tuple-element.45), channel_id=1, source_target_pairs={{0,4},{1,5},{2,6},{3,7},{4,0},{5,1},{6,2},{7,3},{8,12},{9,13},{10,... | collective-permute-start | bytes 12296 | tf_op jit(solution)/shard_map/ppermute | solution.py:491
  14.8 0.1 collective-permute-start.4
  15.0 1.5 %new_token.1 = (f32[8,8,128]{2,1,0:T(8,128)S(1)}, f32[8,8,128]{2,1,0:T(8,128)S(1)}, s32[2,1024]{1,0:T(2,128)S(1)}) custom-call(s32[16]{0:T(128)S(1)} %copy-done.10, s32[16]{0:T(128)S(1)} %copy-done.12, s32[2,1024]{1,0:T(2,128)S(1)} %copy-done.7, s32[2,1024]{1,0:T(2,128)S(1)} %copy-done.8, bf16[4,2,2048]{2,1,0:T(2,128)(2,1)S(1)} %pad_maximum_fusion.same_ref, ...), custom_call_target="tpu_custom_call" | custom-call | flops 2000000000 | bytes 3248256 | tf_op jit(solution)/shard_map/new_token/pallas_call | solution.py:421
  16.5 1.0 %own_heads.1.refs_7_ = bf16[4,8,8,128]{3,2,1,0:T(8,128)(2,1)S(1)} custom-call(f32[8,128]{1,0:T(8,128)S(1)} %get-tuple-element.48.refs_0_, bf16[2,2048,1024]{2,1,0:T(8,128)(2,1)S(1)} %bitcast.18, bf16[2,2048,1024]{2,1,0:T(8,128)(2,1)S(1)} %bitcast.20, bf16[2,4,2048]{2,1,0:T(4,128)(2,1)S(1)} %bitcast.24, bf16[2,4,2048]{2,1,0:T(4,128)(2,1)S(1)} %bitcast.27, ...), custom_call_target="tpu_custom_call" | custom-call | flops 10000000000 | bytes 16855040 | tf_op jit(solution)/shard_map/own_heads/pallas_call | solution.py:421
  17.5 0.0 collective-permute-done.5.refs_0_
  17.5 1.8 %middle_heads.1.refs_6_ = bf16[4,8,8,128]{3,2,1,0:T(8,128)(2,1)S(1)} custom-call(f32[8,128]{1,0:T(8,128)S(1)} %collective-permute-done.5.refs_0_, f32[8,128]{1,0:T(8,128)S(1)} %collective-permute-done.6.refs_1_, bf16[2,2048,1024]{2,1,0:T(8,128)(2,1)S(1)} %bitcast.18, bf16[2,2048,1024]{2,1,0:T(8,128)(2,1)S(1)} %bitcast.20, ...), custom_call_target="tpu_custom_call", output_to_operand_aliasing={{}: (7, {})} | custom-call | flops 10000000000 | bytes 16924672 | tf_op jit(solution)/shard_map/middle_heads/pallas_call | solution.py:421
  19.3 0.0 copy-start.4
  19.4 0.0 collective-permute-done.4.refs_0_
  19.4 0.0 slice-start
  19.4 1.0 %last_heads.1 = bf16[4,8,8,128]{3,2,1,0:T(8,128)(2,1)S(1)} custom-call(f32[8,128]{1,0:T(8,128)S(1)} %collective-permute-done.4.refs_0_, bf16[2,2048,1024]{2,1,0:T(8,128)(2,1)S(1)} %bitcast.18, bf16[2,2048,1024]{2,1,0:T(8,128)(2,1)S(1)} %bitcast.20, bf16[2,4,2048]{2,1,0:T(4,128)(2,1)S(1)} %bitcast.26, ...), custom_call_target="tpu_custom_call", output_to_operand_aliasing={{}: (6, {})} | custom-call | flops 10000000000 | bytes 16920576 | tf_op jit(solution)/shard_map/last_heads/pallas_call | solution.py:421
  20.4 11.5 %all_to_all.10 = bf16[32,8,128]{2,1,0:T(8,128)(2,1)S(1)} all-to-all(bf16[32,8,128]{2,1,0:T(8,128)(2,1)S(1)} %bitcast.11), channel_id=1, replica_groups=mesh['seq'=4,'tensor'=8] {'seq','tensor'}, dimensions={0} | all-to-all | bytes 131072 | tf_op jit(solution)/shard_map/all_to_all | solution.py:525
  31.8 0.4 merge.1
  32.3 0.1 collective-permute-start.8
  32.4 1.1 %collective-permute-done.8 = f32[16,1024]{1,0:T(8,128)S(1)} collective-permute-done((f32[16,1024]{1,0:T(8,128)S(1)}, f32[16,1024]{1,0:T(8,128)S(1)}, u32[]{:S(2)}, u32[]{:S(2)}) %collective-permute-start.8) | collective-permute-done | bytes 65568 | tf_op jit(solution)/shard_map/ppermute | solution.py:540
  33.6 0.8 %collective-permute-start.10 = (bf16[16,1024]{1,0:T(8,128)(2,1)S(1)}, bf16[16,1024]{1,0:T(8,128)(2,1)S(1)}, u32[]{:S(2)}, u32[]{:S(2)}) collective-permute-start(bf16[16,1024]{1,0:T(8,128)(2,1)S(1)} %add_convert_fusion.1), channel_id=1, source_target_pairs={{0,6},{1,7},{2,0},{3,1},{4,2},{5,3},{6,4},{7,5},{8,14},{9,15},{10,... | collective-permute-start | bytes 98312 | tf_op jit(solution)/shard_map/ppermute | solution.py:554
  34.4 1.1 %collective-permute-start.11 = (bf16[16,1024]{1,0:T(8,128)(2,1)S(1)}, bf16[16,1024]{1,0:T(8,128)(2,1)S(1)}, u32[]{:S(2)}, u32[]{:S(2)}) collective-permute-start(bf16[16,1024]{1,0:T(8,128)(2,1)S(1)} %add_convert_fusion.1), channel_id=1, source_target_pairs={{0,4},{1,5},{2,6},{3,7},{4,0},{5,1},{6,2},{7,3},{8,12},{9,13},{10,... | collective-permute-start | bytes 98312 | tf_op jit(solution)/shard_map/ppermute | solution.py:554
  35.5 0.5 collective-permute-start.9
  36.0 0.7 %outputs.1 = (bf16[16,256]{1,0:T(8,128)(2,1)}, bf16[16,256]{1,0:T(8,128)(2,1)}, f32[16,1024]{1,0:T(8,128)S(1)}) custom-call(bf16[4,2,2048]{2,1,0:T(2,128)(2,1)S(1)} %pad_maximum_fusion.same_ref, bf16[4,2,2048]{2,1,0:T(2,128)(2,1)S(1)} %collective-permute-done.7.peer_ref, f32[8,8,128]{2,1,0:T(8,128)S(1)} %get-tuple-element.61.new_ref, ...), custom_call_target="tpu_custom_call" | custom-call | bytes 131072 | tf_op jit(solution)/shard_map/outputs/pallas_call | solution.py:421
  36.7 0.9 %collective-permute-done.10 = bf16[16,1024]{1,0:T(8,128)(2,1)S(1)} collective-permute-done((bf16[16,1024]{1,0:T(8,128)(2,1)S(1)}, bf16[16,1024]{1,0:T(8,128)(2,1)S(1)}, u32[]{:S(2)}, u32[]{:S(2)}) %collective-permute-start.10) | collective-permute-done | bytes 32800 | tf_op jit(solution)/shard_map/ppermute | solution.py:554
  37.5 1.7 %collective-permute-done.11 = bf16[16,1024]{1,0:T(8,128)(2,1)S(1)} collective-permute-done((bf16[16,1024]{1,0:T(8,128)(2,1)S(1)}, bf16[16,1024]{1,0:T(8,128)(2,1)S(1)}, u32[]{:S(2)}, u32[]{:S(2)}) %collective-permute-start.11) | collective-permute-done | bytes 32800 | tf_op jit(solution)/shard_map/ppermute | solution.py:554
  39.2 2.0 %collective-permute-done.9 = bf16[16,1024]{1,0:T(8,128)(2,1)S(1)} collective-permute-done((bf16[16,1024]{1,0:T(8,128)(2,1)S(1)}, bf16[16,1024]{1,0:T(8,128)(2,1)S(1)}, u32[]{:S(2)}, u32[]{:S(2)}) %collective-permute-start.9) | collective-permute-done | bytes 32800 | tf_op jit(solution)/shard_map/ppermute | solution.py:554
  41.3 0.1 collective-permute-start.12
  41.4 1.1 %first_half.1 = (f32[32,1024]{1,0:T(8,128)S(1)}, f32[16,128]{1,0:T(8,128)S(1)}) custom-call(bf16[16,1024]{1,0:T(8,128)(2,1)S(1)} %add_convert_fusion.side_ref.mine_ref, bf16[2048]{0:T(1024)(128)(2,1)S(1)} %copy-done.1, bf16[2048,2,1024]{2,1,0:T(2,128)(2,1)S(1)} %bitcast.10), custom_call_target="tpu_custom_call" | custom-call | flops 67108864 | bytes 8425472 | tf_op jit(solution)/shard_map/first_half/pallas_call | solution.py:421
  42.5 0.1 collective-permute-done.12.other_ref
  42.6 1.6 %mlp.1 = (bf16[8,2,2048]{2,1,0:T(2,128)(2,1)S(1)}, f32[2,2048]{1,0:T(2,128)S(1)}) custom-call(bf16[16,1024]{1,0:T(8,128)(2,1)S(1)} %add_convert_fusion.side_ref.mine_ref, bf16[16,1024]{1,0:T(8,128)(2,1)S(1)} %collective-permute-done.12.other_ref, bf16[2048]{0:T(1024)(128)(2,1)S(1)} %copy-done.1, bf16[2048,2,1024]{2,1,0:T(2,128)(2,1)S(1)} %bitcast.10, ...), custom_call_target="tpu_custom_call" | custom-call | flops 134217728 | bytes 12791808 | tf_op jit(solution)/shard_map/mlp/pallas_call | solution.py:421
  44.2 8.3 %all_to_all.11 = bf16[8,2,2048]{2,1,0:T(2,128)(2,1)S(1)} all-to-all(bf16[8,2,2048]{2,1,0:T(2,128)(2,1)S(1)} %get-tuple-element.68), channel_id=1, replica_groups=mesh['seq'=4,'tensor'=8] {'tensor'}, dimensions={0} | all-to-all | bytes 131072 | tf_op jit(solution)/shard_map/all_to_all | solution.py:576
  52.5 0.1 convert_reduce_fusion
  52.6 0.6 %add_convert_fusion.2 = bf16[2,2048]{1,0:T(2,128)(2,1)} fusion(f32[2,2048]{1,0:T(2,128)S(1)} %get-tuple-element.67, f32[2,2048]{1,0:T(2,128)S(1)} %convert_reduce_fusion), kind=kLoop, calls=%fused_computation.4 | loop fusion | flops 8192 | bytes 40960 | tf_op jit(solution)/shard_map/convert_element_type | solution.py:577
  (36 shorter events, 0.1 us)
Async XLA Ops:
  0.6 15.8 %slice-start.2 = ((s8[8388608]{0:T(1024)(128)(4,1)}), s8[4194304]{0:T(1024)(128)(4,1)S(1)}, s32[]{:S(2)}) async-start(s8[8388608]{0:T(1024)(128)(4,1)} %bitcast.17), calls=%async_computation.4 | async-start | bytes 8388608
  0.6 15.8 %slice-start.4 = ((s8[8388608]{0:T(1024)(128)(4,1)}), s8[4194304]{0:T(1024)(128)(4,1)S(1)}, s32[]{:S(2)}) async-start(s8[8388608]{0:T(1024)(128)(4,1)} %bitcast.19), calls=%async_computation.6 | async-start | bytes 8388608
  0.7 9.7 %copy-start.2 = (bf16[2,2048]{1,0:T(2,128)(2,1)S(1)}, bf16[2,2048]{1,0:T(2,128)(2,1)}, u32[]{:S(2)}) copy-start(bf16[2,2048]{1,0:T(2,128)(2,1)} %refs_0_.1) | copy-start | bytes 24580
  0.7 9.8 %copy-start.3 = (bf16[2048,3,256]{2,0,1:T(8,128)(2,1)S(1)}, bf16[2048,3,256]{2,0,1:T(8,128)(2,1)}, u32[]{:S(2)}) copy-start(bf16[2048,3,256]{2,0,1:T(8,128)(2,1)} %param.17) | copy-start | bytes 9437188
  0.7 9.8 %copy-start.9 = (bf16[2048]{0:T(1024)(128)(2,1)S(1)}, bf16[2048]{0:T(1024)(128)(2,1)}, u32[]{:S(2)}) copy-start(bf16[2048]{0:T(1024)(128)(2,1)} %gain_ref.3) | copy-start | bytes 12292
  0.7 14.3 %copy-start.7 = (s32[2,1024]{1,0:T(2,128)S(1)}, s32[2,1024]{1,0:T(2,128)}, u32[]{:S(2)}) copy-start(s32[2,1024]{1,0:T(2,128)} %mask_ref.1) | copy-start | bytes 24580
  0.7 14.3 %copy-start.8 = (s32[2,1024]{1,0:T(2,128)S(1)}, s32[2,1024]{1,0:T(2,128)}, u32[]{:S(2)}) copy-start(s32[2,1024]{1,0:T(2,128)} %slot_pos_ref.1) | copy-start | bytes 24580
  0.7 14.3 %copy-start.10 = (s32[16]{0:T(128)S(1)}, s32[16]{0:T(128)}, u32[]{:S(2)}) copy-start(s32[16]{0:T(128)} %len_ref.1) | copy-start | bytes 196
  0.7 15.8 %slice-start.3 = ((s8[8388608]{0:T(1024)(128)(4,1)}), s8[4194304]{0:T(1024)(128)(4,1)S(1)}, s32[]{:S(2)}) async-start(s8[8388608]{0:T(1024)(128)(4,1)} %bitcast.17), calls=%async_computation.5 | async-start | bytes 8388608
  0.7 15.8 %slice-start.5 = ((s8[8388608]{0:T(1024)(128)(4,1)}), s8[4194304]{0:T(1024)(128)(4,1)S(1)}, s32[]{:S(2)}) async-start(s8[8388608]{0:T(1024)(128)(4,1)} %bitcast.19), calls=%async_computation.7 | async-start | bytes 8388608
  0.7 9.7 %collective-permute-start.3 = (bf16[3,2048,256]{2,1,0:T(8,128)(2,1)}, bf16[3,2048,256]{2,1,0:T(8,128)(2,1)S(1)}, u32[]{:S(2)}, u32[]{:S(2)}) collective-permute-start(bf16[3,2048,256]{2,1,0:T(8,128)(2,1)} %bitcast.21), channel_id=1, source_target_pairs={{0,1},{1,0},{2,3},{3,2},{4,5},{5,4},{6,7},{7,6},{8,9},{9,8},{10,11... | collective-permute-start | bytes 9437192 | tf_op jit(solution)/shard_map/ppermute | solution.py:478
  1.3 7.9 %collective-permute-start = (bf16[2,2048]{1,0:T(2,128)(2,1)}, bf16[2,2048]{1,0:T(2,128)(2,1)S(1)}, u32[]{:S(2)}, u32[]{:S(2)}) collective-permute-start(bf16[2,2048]{1,0:T(2,128)(2,1)} %refs_0_.1), channel_id=1, source_target_pairs={{0,2},{1,3},{2,4},{3,5},{4,6},{5,7},{6,0},{7,1},{8,10},{9,11},{10,... | collective-permute-start | bytes 24584 | tf_op jit(solution)/shard_map/ppermute | solution.py:476
  3.9 5.3 %collective-permute-start.1 = (bf16[2,2048]{1,0:T(2,128)(2,1)}, bf16[2,2048]{1,0:T(2,128)(2,1)S(1)}, u32[]{:S(2)}, u32[]{:S(2)}) collective-permute-start(bf16[2,2048]{1,0:T(2,128)(2,1)} %refs_0_.1), channel_id=1, source_target_pairs={{0,4},{1,5},{2,6},{3,7},{4,0},{5,1},{6,2},{7,3},{8,12},{9,13},{10,... | collective-permute-start | bytes 24584 | tf_op jit(solution)/shard_map/ppermute | solution.py:476
  6.5 3.9 %collective-permute-start.2 = (bf16[2,2048]{1,0:T(2,128)(2,1)}, bf16[2,2048]{1,0:T(2,128)(2,1)S(1)}, u32[]{:S(2)}, u32[]{:S(2)}) collective-permute-start(bf16[2,2048]{1,0:T(2,128)(2,1)} %refs_0_.1), channel_id=1, source_target_pairs={{0,6},{1,7},{2,0},{3,1},{4,2},{5,3},{6,4},{7,5},{8,14},{9,15},{10,... | collective-permute-start | bytes 24584 | tf_op jit(solution)/shard_map/ppermute | solution.py:476
  7.8 0.7 %copy-start.11 = (s32[16]{0:T(128)S(1)}, s32[16]{0:T(128)}, u32[]{:S(2)}) copy-start(s32[16]{0:T(128)} %pos_ref.3) | copy-start | bytes 196
  8.5 6.5 %copy-start.12 = (s32[16]{0:T(128)S(1)}, s32[16]{0:T(128)}, u32[]{:S(2)}) copy-start(s32[16]{0:T(128)} %pos_ref.3) | copy-start | bytes 196
  9.1 7.4 %copy-start.5 = (bf16[2,2048,4]{1,2,0:T(4,128)(2,1)S(1)}, bf16[2,2048,4]{1,2,0:T(4,128)(2,1)}, u32[]{:S(2)}) copy-start(bf16[2,2048,4]{1,2,0:T(4,128)(2,1)} %param.24) | copy-start | bytes 98308
  9.1 7.4 %copy-start.6 = (bf16[2,2048,4]{1,2,0:T(4,128)(2,1)S(1)}, bf16[2,2048,4]{1,2,0:T(4,128)(2,1)}, u32[]{:S(2)}) copy-start(bf16[2,2048,4]{1,2,0:T(4,128)(2,1)} %param.25) | copy-start | bytes 98308
  11.0 4.0 %collective-permute-start.7 = (bf16[4,2,2048]{2,1,0:T(2,128)(2,1)S(1)}, bf16[4,2,2048]{2,1,0:T(2,128)(2,1)S(1)}, u32[]{:S(2)}, u32[]{:S(2)}) collective-permute-start(bf16[4,2,2048]{2,1,0:T(2,128)(2,1)S(1)} %pad_maximum_fusion.same_ref), channel_id=1, source_target_pairs={{0,1},{1,0},{2,3},{3,2},{4,5},{5,4},{6,7},{7,6},{8,9},{9,8},{10,11... | collective-permute-start | bytes 98312 | tf_op jit(solution)/shard_map/ppermute | solution.py:489
  11.1 6.4 %collective-permute-start.5 = (f32[8,128]{1,0:T(8,128)S(1)}, f32[8,128]{1,0:T(8,128)S(1)}, u32[]{:S(2)}, u32[]{:S(2)}) collective-permute-start(f32[8,128]{1,0:T(8,128)S(1)} %get-tuple-element.44), channel_id=1, source_target_pairs={{0,2},{1,3},{2,4},{3,5},{4,6},{5,7},{6,0},{7,1},{8,10},{9,11},{10,... | collective-permute-start | bytes 12296 | tf_op jit(solution)/shard_map/ppermute | solution.py:491
  11.4 6.1 %collective-permute-start.6 = (f32[8,128]{1,0:T(8,128)S(1)}, f32[8,128]{1,0:T(8,128)S(1)}, u32[]{:S(2)}, u32[]{:S(2)}) collective-permute-start(f32[8,128]{1,0:T(8,128)S(1)} %get-tuple-element.45), channel_id=1, source_target_pairs={{0,4},{1,5},{2,6},{3,7},{4,0},{5,1},{6,2},{7,3},{8,12},{9,13},{10,... | collective-permute-start | bytes 12296 | tf_op jit(solution)/shard_map/ppermute | solution.py:491
  14.8 4.5 %collective-permute-start.4 = (f32[8,128]{1,0:T(8,128)S(1)}, f32[8,128]{1,0:T(8,128)S(1)}, u32[]{:S(2)}, u32[]{:S(2)}) collective-permute-start(f32[8,128]{1,0:T(8,128)S(1)} %get-tuple-element.43), channel_id=1, source_target_pairs={{0,6},{1,7},{2,0},{3,1},{4,2},{5,3},{6,4},{7,5},{8,14},{9,15},{10,... | collective-permute-start | bytes 12296 | tf_op jit(solution)/shard_map/ppermute | solution.py:491
  19.3 12.5 %copy-start.4 = (bf16[256,2048]{1,0:T(8,128)(2,1)S(1)}, bf16[256,2048]{1,0:T(8,128)(2,1)}, u32[]{:S(2)}) copy-start(bf16[256,2048]{1,0:T(8,128)(2,1)} %w_ref.1) | copy-start | bytes 3145732
  19.4 22.0 %slice-start = ((s8[8388608]{0:T(1024)(128)(4,1)}), s8[4194304]{0:T(1024)(128)(4,1)S(1)}, s32[]{:S(2)}) async-start(s8[8388608]{0:T(1024)(128)(4,1)} %bitcast.9), calls=%async_computation.2 | async-start | bytes 8388608
  31.8 9.5 %slice-start.1 = ((s8[8388608]{0:T(1024)(128)(4,1)}), s8[4194304]{0:T(1024)(128)(4,1)S(1)}, s32[]{:S(2)}) async-start(s8[8388608]{0:T(1024)(128)(4,1)} %bitcast.9), calls=%async_computation.3 | async-start | bytes 8388608
  31.8 9.6 %copy-start.1 = (bf16[2048]{0:T(1024)(128)(2,1)S(1)}, bf16[2048]{0:T(1024)(128)(2,1)}, u32[]{:S(2)}) copy-start(bf16[2048]{0:T(1024)(128)(2,1)} %gain_ref.5) | copy-start | bytes 12292
  32.3 10.3 %copy-start = (bf16[1024,2048]{1,0:T(8,128)(2,1)S(1)}, bf16[1024,2048]{1,0:T(8,128)(2,1)}, u32[]{:S(2)}) copy-start(bf16[1024,2048]{1,0:T(8,128)(2,1)} %down_ref.1) | copy-start | bytes 12582916
  32.3 1.3 %collective-permute-start.8 = (f32[16,1024]{1,0:T(8,128)S(1)}, f32[16,1024]{1,0:T(8,128)S(1)}, u32[]{:S(2)}, u32[]{:S(2)}) collective-permute-start(f32[16,1024]{1,0:T(8,128)S(1)} %get-tuple-element.57), channel_id=1, source_target_pairs={{0,1},{1,0},{2,3},{3,2},{4,5},{5,4},{6,7},{7,6},{8,9},{9,8},{10,11... | collective-permute-start | bytes 196616 | tf_op jit(solution)/shard_map/ppermute | solution.py:540
  33.6 4.0 %collective-permute-start.10 = (bf16[16,1024]{1,0:T(8,128)(2,1)S(1)}, bf16[16,1024]{1,0:T(8,128)(2,1)S(1)}, u32[]{:S(2)}, u32[]{:S(2)}) collective-permute-start(bf16[16,1024]{1,0:T(8,128)(2,1)S(1)} %add_convert_fusion.1), channel_id=1, source_target_pairs={{0,6},{1,7},{2,0},{3,1},{4,2},{5,3},{6,4},{7,5},{8,14},{9,15},{10,... | collective-permute-start | bytes 98312 | tf_op jit(solution)/shard_map/ppermute | solution.py:554
  34.4 4.8 %collective-permute-start.11 = (bf16[16,1024]{1,0:T(8,128)(2,1)S(1)}, bf16[16,1024]{1,0:T(8,128)(2,1)S(1)}, u32[]{:S(2)}, u32[]{:S(2)}) collective-permute-start(bf16[16,1024]{1,0:T(8,128)(2,1)S(1)} %add_convert_fusion.1), channel_id=1, source_target_pairs={{0,4},{1,5},{2,6},{3,7},{4,0},{5,1},{6,2},{7,3},{8,12},{9,13},{10,... | collective-permute-start | bytes 98312 | tf_op jit(solution)/shard_map/ppermute | solution.py:554
  35.5 5.7 %collective-permute-start.9 = (bf16[16,1024]{1,0:T(8,128)(2,1)S(1)}, bf16[16,1024]{1,0:T(8,128)(2,1)S(1)}, u32[]{:S(2)}, u32[]{:S(2)}) collective-permute-start(bf16[16,1024]{1,0:T(8,128)(2,1)S(1)} %add_convert_fusion.1), channel_id=1, source_target_pairs={{0,2},{1,3},{2,4},{3,5},{4,6},{5,7},{6,0},{7,1},{8,10},{9,11},{10,... | collective-permute-start | bytes 98312 | tf_op jit(solution)/shard_map/ppermute | solution.py:554
  41.3 1.3 %collective-permute-start.12 = (bf16[16,1024]{1,0:T(8,128)(2,1)S(1)}, bf16[16,1024]{1,0:T(8,128)(2,1)S(1)}, u32[]{:S(2)}, u32[]{:S(2)}) collective-permute-start(bf16[16,1024]{1,0:T(8,128)(2,1)S(1)} %add_convert_fusion.side_ref.mine_ref), channel_id=1, source_target_pairs={{0,1},{1,0},{2,3},{3,2},{4,5},{5,4},{6,7},{7,6},{8,9},{9,8},{10,11... | collective-permute-start | bytes 98312 | tf_op jit(solution)/shard_map/ppermute | solution.py:556

commit v10 on v9

--- a/solution.py
+++ b/solution.py
@@ -305,7 +305,7 @@
     core = lax.axis_index("tensor") % 2
     for half, to_ref in ((1 - core, other_ref), (core, mine_ref)):
         weights = w_ref[:, pl.ds(pl.multiple_of(half * width, LANE), width)]
-        to_ref[...] = jnp.dot(attended, weights, preferred_element_type=F32)
+        to_ref[...] = jnp.dot(attended, weights, preferred_element_type=F32).astype(to_ref.dtype)
 
 
 def spread_rows(values, wide_ref):
@@ -528,7 +528,7 @@
     side = sds((batch, width // 2), F32)
     mine, other = call(
         functools.partial(merge_kernel, rows),
-        (side, side),
+        (side, sds(side.shape, BF16)),
         (part, new_part, w_out),
         scratch=[
             pltpu.VMEM(((shards + 1) * groups * 8, chunk), F32),
@@ -537,7 +537,7 @@
         name="merge",
         flops=MERGE_FLOPS,
     )
-    chip = (mine + lax.ppermute(other, "tensor", across)).astype(BF16)
+    chip = (mine + lax.ppermute(other, "tensor", across).astype(F32)).astype(BF16)
     flat = sds((batch, lanes), BF16)
     chip, same, peer, new_part, key_part = lax.optimization_barrier(
         (chip, same, peer, new_part, key_part)

time: 53.4 us -> 53.3 us (level)
  no operation moved by 1% of the time
where the time goes in v10:
time: 53.3 us; the launch traced here: 53.1 us
  blocking collectives  19.8 us (37%)
  starting transfers between devices  13.7 us (26%)
  Pallas kernels  10.2 us (19%)
  waiting for transfers between devices  6.97 us (13%)
  between operations  0.99 us (2%)
  other arithmetic  0.77 us (1%)
  local copies, waits for them, and re-layouts  0.74 us (1%)
    all_to_all x1, blocking collectives, per_device(): lax.all_to_all(part.reshape(shards * groups, 8, chunk), ('seq', 'tensor')...  11.5 us
    pallas_call x10, Pallas kernels, call(): pl.pallas_call(kernel, out_shape=out, in_specs=specs or [VMEM_SPEC] * len...  10.2 us
    all_to_all x1, blocking collectives, per_device(): partial = lax.all_to_all(partial, 'tensor', 0, 0, tiled=True)  8.29 us
    ppermute x3, starting transfers between devices, per_device(): column = [states] + [lax.ppermute(states, 'tensor', hop) for hop in hops]  6.57 us
    ppermute x3, waiting for transfers between devices, per_device(): total = total + lax.ppermute(chip, 'tensor', hops[which]).astype(F32)  4.58 us
    ppermute x3, starting transfers between devices, per_device(): lax.ppermute(query, 'tensor', hop)  3.88 us
    ppermute x3, starting transfers between devices, per_device(): total = total + lax.ppermute(chip, 'tensor', hops[which]).astype(F32)  2.42 us
    ppermute x3, waiting for transfers between devices, per_device(): column = [states] + [lax.ppermute(states, 'tensor', hop) for hop in hops]  1.19 us
  transfers between devices with their start and end apart: 13, of which 6 were waited for; matrix products, arithmetic and copies ran while one was open for 0% of the time, Pallas kernels for 12%

profile of v10, /device:TPU:0, one launch (start us, length us, event | category | flops | bytes accessed | tf_op | source)
XLA Modules:
  0.0 53.1 jit_solution(4871442665679030986)
XLA Ops:
  0.6 0.0 slice-start.2
  0.6 0.0 slice-start.4
  0.7 0.0 slice-start.3
  0.7 0.0 slice-start.5
  0.7 0.5 collective-permute-start.3
  1.3 2.6 %collective-permute-start = (bf16[2,2048]{1,0:T(2,128)(2,1)}, bf16[2,2048]{1,0:T(2,128)(2,1)S(1)}, u32[]{:S(2)}, u32[]{:S(2)}) collective-permute-start(bf16[2,2048]{1,0:T(2,128)(2,1)} %refs_0_.1), channel_id=1, source_target_pairs={{0,2},{1,3},{2,4},{3,5},{4,6},{5,7},{6,0},{7,1},{8,10},{9,11},{10,... | collective-permute-start | bytes 24584 | tf_op jit(solution)/shard_map/ppermute | solution.py:476
  3.9 2.6 %collective-permute-start.1 = (bf16[2,2048]{1,0:T(2,128)(2,1)}, bf16[2,2048]{1,0:T(2,128)(2,1)S(1)}, u32[]{:S(2)}, u32[]{:S(2)}) collective-permute-start(bf16[2,2048]{1,0:T(2,128)(2,1)} %refs_0_.1), channel_id=1, source_target_pairs={{0,4},{1,5},{2,6},{3,7},{4,0},{5,1},{6,2},{7,3},{8,12},{9,13},{10,... | collective-permute-start | bytes 24584 | tf_op jit(solution)/shard_map/ppermute | solution.py:476
  6.5 1.3 %collective-permute-start.2 = (bf16[2,2048]{1,0:T(2,128)(2,1)}, bf16[2,2048]{1,0:T(2,128)(2,1)S(1)}, u32[]{:S(2)}, u32[]{:S(2)}) collective-permute-start(bf16[2,2048]{1,0:T(2,128)(2,1)} %refs_0_.1), channel_id=1, source_target_pairs={{0,6},{1,7},{2,0},{3,1},{4,2},{5,3},{6,4},{7,5},{8,14},{9,15},{10,... | collective-permute-start | bytes 24584 | tf_op jit(solution)/shard_map/ppermute | solution.py:476
  7.8 0.7 %copy-done.11 = s32[16]{0:T(128)S(1)} copy-done((s32[16]{0:T(128)S(1)}, s32[16]{0:T(128)}, u32[]{:S(2)}) %copy-start.11) | copy-done | bytes 88
  8.5 0.6 %prepare.1 = (f32[16,128]{1,0:T(8,128)S(1)}, f32[16,128]{1,0:T(8,128)S(1)}) custom-call(s32[16]{0:T(128)S(1)} %copy-done.11), custom_call_target="tpu_custom_call" | custom-call | flops 20000000000 | bytes 64 | tf_op jit(solution)/shard_map/prepare/pallas_call | solution.py:421
  9.1 0.0 copy-start.5
  9.1 0.0 copy-start.6
  9.1 0.0 collective-permute-done.refs_1_
  9.2 0.0 collective-permute-done.1.refs_2_
  9.2 1.2 %collective-permute-done.2.refs_3_ = bf16[2,2048]{1,0:T(2,128)(2,1)S(1)} collective-permute-done((bf16[2,2048]{1,0:T(2,128)(2,1)}, bf16[2,2048]{1,0:T(2,128)(2,1)S(1)}, u32[]{:S(2)}, u32[]{:S(2)}) %collective-permute-start.2) | collective-permute-done | bytes 8224 | tf_op jit(solution)/shard_map/ppermute | solution.py:476
  10.3 0.1 pad_maximum_fusion.same_ref
  10.4 0.0 collective-permute-done.3.refs_6_
  10.4 0.6 %query.1 = (f32[8,128]{1,0:T(8,128)S(1)}, f32[8,128]{1,0:T(8,128)S(1)}, f32[8,128]{1,0:T(8,128)S(1)}, f32[8,128]{1,0:T(8,128)S(1)}) custom-call(bf16[2,2048]{1,0:T(2,128)(2,1)S(1)} %copy-done.2, bf16[2,2048]{1,0:T(2,128)(2,1)S(1)} %collective-permute-done.refs_1_, bf16[2,2048]{1,0:T(2,128)(2,1)S(1)} %collective-permute-done.1.refs_2_, ...), custom_call_target="tpu_custom_call" | custom-call | flops 2000000000 | bytes 6344704 | tf_op jit(solution)/shard_map/query/pallas_call | solution.py:421
  11.0 0.1 collective-permute-start.7
  11.1 0.3 collective-permute-start.5
  11.4 3.4 %collective-permute-start.6 = (f32[8,128]{1,0:T(8,128)S(1)}, f32[8,128]{1,0:T(8,128)S(1)}, u32[]{:S(2)}, u32[]{:S(2)}) collective-permute-start(f32[8,128]{1,0:T(8,128)S(1)} %get-tuple-element.45), channel_id=1, source_target_pairs={{0,4},{1,5},{2,6},{3,7},{4,0},{5,1},{6,2},{7,3},{8,12},{9,13},{10,... | collective-permute-start | bytes 12296 | tf_op jit(solution)/shard_map/ppermute | solution.py:491
  14.8 0.1 collective-permute-start.4
  15.0 1.5 %new_token.1 = (f32[8,8,128]{2,1,0:T(8,128)S(1)}, f32[8,8,128]{2,1,0:T(8,128)S(1)}, s32[2,1024]{1,0:T(2,128)S(1)}) custom-call(s32[16]{0:T(128)S(1)} %copy-done.10, s32[16]{0:T(128)S(1)} %copy-done.12, s32[2,1024]{1,0:T(2,128)S(1)} %copy-done.7, s32[2,1024]{1,0:T(2,128)S(1)} %copy-done.8, bf16[4,2,2048]{2,1,0:T(2,128)(2,1)S(1)} %pad_maximum_fusion.same_ref, ...), custom_call_target="tpu_custom_call" | custom-call | flops 2000000000 | bytes 3248256 | tf_op jit(solution)/shard_map/new_token/pallas_call | solution.py:421
  16.5 1.0 %own_heads.1.refs_7_ = bf16[4,8,8,128]{3,2,1,0:T(8,128)(2,1)S(1)} custom-call(f32[8,128]{1,0:T(8,128)S(1)} %get-tuple-element.48.refs_0_, bf16[2,2048,1024]{2,1,0:T(8,128)(2,1)S(1)} %bitcast.18, bf16[2,2048,1024]{2,1,0:T(8,128)(2,1)S(1)} %bitcast.20, bf16[2,4,2048]{2,1,0:T(4,128)(2,1)S(1)} %bitcast.24, bf16[2,4,2048]{2,1,0:T(4,128)(2,1)S(1)} %bitcast.27, ...), custom_call_target="tpu_custom_call" | custom-call | flops 10000000000 | bytes 16855040 | tf_op jit(solution)/shard_map/own_heads/pallas_call | solution.py:421
  17.5 0.0 collective-permute-done.5.refs_0_
  17.5 1.8 %middle_heads.1.refs_6_ = bf16[4,8,8,128]{3,2,1,0:T(8,128)(2,1)S(1)} custom-call(f32[8,128]{1,0:T(8,128)S(1)} %collective-permute-done.5.refs_0_, f32[8,128]{1,0:T(8,128)S(1)} %collective-permute-done.6.refs_1_, bf16[2,2048,1024]{2,1,0:T(8,128)(2,1)S(1)} %bitcast.18, bf16[2,2048,1024]{2,1,0:T(8,128)(2,1)S(1)} %bitcast.20, ...), custom_call_target="tpu_custom_call", output_to_operand_aliasing={{}: (7, {})} | custom-call | flops 10000000000 | bytes 16924672 | tf_op jit(solution)/shard_map/middle_heads/pallas_call | solution.py:421
  19.3 0.0 copy-start.4
  19.4 0.0 collective-permute-done.4.refs_0_
  19.4 0.0 slice-start
  19.4 1.0 %last_heads.1 = bf16[4,8,8,128]{3,2,1,0:T(8,128)(2,1)S(1)} custom-call(f32[8,128]{1,0:T(8,128)S(1)} %collective-permute-done.4.refs_0_, bf16[2,2048,1024]{2,1,0:T(8,128)(2,1)S(1)} %bitcast.18, bf16[2,2048,1024]{2,1,0:T(8,128)(2,1)S(1)} %bitcast.20, bf16[2,4,2048]{2,1,0:T(4,128)(2,1)S(1)} %bitcast.26, ...), custom_call_target="tpu_custom_call", output_to_operand_aliasing={{}: (6, {})} | custom-call | flops 10000000000 | bytes 16920576 | tf_op jit(solution)/shard_map/last_heads/pallas_call | solution.py:421
  20.4 11.5 %all_to_all.10 = bf16[32,8,128]{2,1,0:T(8,128)(2,1)S(1)} all-to-all(bf16[32,8,128]{2,1,0:T(8,128)(2,1)S(1)} %bitcast.11), channel_id=1, replica_groups=mesh['seq'=4,'tensor'=8] {'seq','tensor'}, dimensions={0} | all-to-all | bytes 131072 | tf_op jit(solution)/shard_map/all_to_all | solution.py:525
  31.8 0.4 merge.1
  32.3 0.1 collective-permute-start.8
  32.4 1.1 %collective-permute-done.8 = bf16[16,1024]{1,0:T(8,128)(2,1)S(1)} collective-permute-done((bf16[16,1024]{1,0:T(8,128)(2,1)S(1)}, bf16[16,1024]{1,0:T(8,128)(2,1)S(1)}, u32[]{:S(2)}, u32[]{:S(2)}) %collective-permute-start.8) | collective-permute-done | bytes 32800 | tf_op jit(solution)/shard_map/ppermute | solution.py:540
  33.5 0.8 %collective-permute-start.10 = (bf16[16,1024]{1,0:T(8,128)(2,1)S(1)}, bf16[16,1024]{1,0:T(8,128)(2,1)S(1)}, u32[]{:S(2)}, u32[]{:S(2)}) collective-permute-start(bf16[16,1024]{1,0:T(8,128)(2,1)S(1)} %add_convert_fusion.1), channel_id=1, source_target_pairs={{0,6},{1,7},{2,0},{3,1},{4,2},{5,3},{6,4},{7,5},{8,14},{9,15},{10,... | collective-permute-start | bytes 98312 | tf_op jit(solution)/shard_map/ppermute | solution.py:554
  34.4 1.1 %collective-permute-start.11 = (bf16[16,1024]{1,0:T(8,128)(2,1)S(1)}, bf16[16,1024]{1,0:T(8,128)(2,1)S(1)}, u32[]{:S(2)}, u32[]{:S(2)}) collective-permute-start(bf16[16,1024]{1,0:T(8,128)(2,1)S(1)} %add_convert_fusion.1), channel_id=1, source_target_pairs={{0,4},{1,5},{2,6},{3,7},{4,0},{5,1},{6,2},{7,3},{8,12},{9,13},{10,... | collective-permute-start | bytes 98312 | tf_op jit(solution)/shard_map/ppermute | solution.py:554
  35.5 0.5 collective-permute-start.9
  36.0 0.7 %outputs.1 = (bf16[16,256]{1,0:T(8,128)(2,1)}, bf16[16,256]{1,0:T(8,128)(2,1)}, f32[16,1024]{1,0:T(8,128)S(1)}) custom-call(bf16[4,2,2048]{2,1,0:T(2,128)(2,1)S(1)} %pad_maximum_fusion.same_ref, bf16[4,2,2048]{2,1,0:T(2,128)(2,1)S(1)} %collective-permute-done.7.peer_ref, f32[8,8,128]{2,1,0:T(8,128)S(1)} %get-tuple-element.61.new_ref, ...), custom_call_target="tpu_custom_call" | custom-call | bytes 131072 | tf_op jit(solution)/shard_map/outputs/pallas_call | solution.py:421
  36.6 0.9 %collective-permute-done.10 = bf16[16,1024]{1,0:T(8,128)(2,1)S(1)} collective-permute-done((bf16[16,1024]{1,0:T(8,128)(2,1)S(1)}, bf16[16,1024]{1,0:T(8,128)(2,1)S(1)}, u32[]{:S(2)}, u32[]{:S(2)}) %collective-permute-start.10) | collective-permute-done | bytes 32800 | tf_op jit(solution)/shard_map/ppermute | solution.py:554
  37.5 1.7 %collective-permute-done.11 = bf16[16,1024]{1,0:T(8,128)(2,1)S(1)} collective-permute-done((bf16[16,1024]{1,0:T(8,128)(2,1)S(1)}, bf16[16,1024]{1,0:T(8,128)(2,1)S(1)}, u32[]{:S(2)}, u32[]{:S(2)}) %collective-permute-start.11) | collective-permute-done | bytes 32800 | tf_op jit(solution)/shard_map/ppermute | solution.py:554
  39.2 2.0 %collective-permute-done.9 = bf16[16,1024]{1,0:T(8,128)(2,1)S(1)} collective-permute-done((bf16[16,1024]{1,0:T(8,128)(2,1)S(1)}, bf16[16,1024]{1,0:T(8,128)(2,1)S(1)}, u32[]{:S(2)}, u32[]{:S(2)}) %collective-permute-start.9) | collective-permute-done | bytes 32800 | tf_op jit(solution)/shard_map/ppermute | solution.py:554
  41.2 0.1 collective-permute-start.12
  41.4 1.1 %first_half.1 = (f32[32,1024]{1,0:T(8,128)S(1)}, f32[16,128]{1,0:T(8,128)S(1)}) custom-call(bf16[16,1024]{1,0:T(8,128)(2,1)S(1)} %add_convert_fusion.side_ref.mine_ref, bf16[2048]{0:T(1024)(128)(2,1)S(1)} %copy-done.1, bf16[2048,2,1024]{2,1,0:T(2,128)(2,1)S(1)} %bitcast.10), custom_call_target="tpu_custom_call" | custom-call | flops 67108864 | bytes 8425472 | tf_op jit(solution)/shard_map/first_half/pallas_call | solution.py:421
  42.4 0.1 collective-permute-done.12.other_ref
  42.5 1.6 %mlp.1 = (bf16[8,2,2048]{2,1,0:T(2,128)(2,1)S(1)}, f32[2,2048]{1,0:T(2,128)S(1)}) custom-call(bf16[16,1024]{1,0:T(8,128)(2,1)S(1)} %add_convert_fusion.side_ref.mine_ref, bf16[16,1024]{1,0:T(8,128)(2,1)S(1)} %collective-permute-done.12.other_ref, bf16[2048]{0:T(1024)(128)(2,1)S(1)} %copy-done.1, bf16[2048,2,1024]{2,1,0:T(2,128)(2,1)S(1)} %bitcast.10, ...), custom_call_target="tpu_custom_call" | custom-call | flops 134217728 | bytes 12791808 | tf_op jit(solution)/shard_map/mlp/pallas_call | solution.py:421
  44.2 8.3 %all_to_all.11 = bf16[8,2,2048]{2,1,0:T(2,128)(2,1)S(1)} all-to-all(bf16[8,2,2048]{2,1,0:T(2,128)(2,1)S(1)} %get-tuple-element.68), channel_id=1, replica_groups=mesh['seq'=4,'tensor'=8] {'tensor'}, dimensions={0} | all-to-all | bytes 131072 | tf_op jit(solution)/shard_map/all_to_all | solution.py:576
  52.5 0.1 convert_reduce_fusion
  52.5 0.6 %add_convert_fusion.2 = bf16[2,2048]{1,0:T(2,128)(2,1)} fusion(f32[2,2048]{1,0:T(2,128)S(1)} %get-tuple-element.67, f32[2,2048]{1,0:T(2,128)S(1)} %convert_reduce_fusion), kind=kLoop, calls=%fused_computation.4 | loop fusion | flops 8192 | bytes 40960 | tf_op jit(solution)/shard_map/convert_element_type | solution.py:577
  (36 shorter events, 0.1 us)
Async XLA Ops:
  0.6 15.8 %slice-start.2 = ((s8[8388608]{0:T(1024)(128)(4,1)}), s8[4194304]{0:T(1024)(128)(4,1)S(1)}, s32[]{:S(2)}) async-start(s8[8388608]{0:T(1024)(128)(4,1)} %bitcast.17), calls=%async_computation.4 | async-start | bytes 8388608
  0.6 15.8 %slice-start.4 = ((s8[8388608]{0:T(1024)(128)(4,1)}), s8[4194304]{0:T(1024)(128)(4,1)S(1)}, s32[]{:S(2)}) async-start(s8[8388608]{0:T(1024)(128)(4,1)} %bitcast.19), calls=%async_computation.6 | async-start | bytes 8388608
  0.7 9.7 %copy-start.2 = (bf16[2,2048]{1,0:T(2,128)(2,1)S(1)}, bf16[2,2048]{1,0:T(2,128)(2,1)}, u32[]{:S(2)}) copy-start(bf16[2,2048]{1,0:T(2,128)(2,1)} %refs_0_.1) | copy-start | bytes 24580
  0.7 9.8 %copy-start.3 = (bf16[2048,3,256]{2,0,1:T(8,128)(2,1)S(1)}, bf16[2048,3,256]{2,0,1:T(8,128)(2,1)}, u32[]{:S(2)}) copy-start(bf16[2048,3,256]{2,0,1:T(8,128)(2,1)} %param.17) | copy-start | bytes 9437188
  0.7 9.8 %copy-start.9 = (bf16[2048]{0:T(1024)(128)(2,1)S(1)}, bf16[2048]{0:T(1024)(128)(2,1)}, u32[]{:S(2)}) copy-start(bf16[2048]{0:T(1024)(128)(2,1)} %gain_ref.3) | copy-start | bytes 12292
  0.7 14.3 %copy-start.7 = (s32[2,1024]{1,0:T(2,128)S(1)}, s32[2,1024]{1,0:T(2,128)}, u32[]{:S(2)}) copy-start(s32[2,1024]{1,0:T(2,128)} %mask_ref.1) | copy-start | bytes 24580
  0.7 14.3 %copy-start.8 = (s32[2,1024]{1,0:T(2,128)S(1)}, s32[2,1024]{1,0:T(2,128)}, u32[]{:S(2)}) copy-start(s32[2,1024]{1,0:T(2,128)} %slot_pos_ref.1) | copy-start | bytes 24580
  0.7 14.3 %copy-start.10 = (s32[16]{0:T(128)S(1)}, s32[16]{0:T(128)}, u32[]{:S(2)}) copy-start(s32[16]{0:T(128)} %len_ref.1) | copy-start | bytes 196
  0.7 15.8 %slice-start.3 = ((s8[8388608]{0:T(1024)(128)(4,1)}), s8[4194304]{0:T(1024)(128)(4,1)S(1)}, s32[]{:S(2)}) async-start(s8[8388608]{0:T(1024)(128)(4,1)} %bitcast.17), calls=%async_computation.5 | async-start | bytes 8388608
  0.7 15.8 %slice-start.5 = ((s8[8388608]{0:T(1024)(128)(4,1)}), s8[4194304]{0:T(1024)(128)(4,1)S(1)}, s32[]{:S(2)}) async-start(s8[8388608]{0:T(1024)(128)(4,1)} %bitcast.19), calls=%async_computation.7 | async-start | bytes 8388608
  0.7 9.7 %collective-permute-start.3 = (bf16[3,2048,256]{2,1,0:T(8,128)(2,1)}, bf16[3,2048,256]{2,1,0:T(8,128)(2,1)S(1)}, u32[]{:S(2)}, u32[]{:S(2)}) collective-permute-start(bf16[3,2048,256]{2,1,0:T(8,128)(2,1)} %bitcast.21), channel_id=1, source_target_pairs={{0,1},{1,0},{2,3},{3,2},{4,5},{5,4},{6,7},{7,6},{8,9},{9,8},{10,11... | collective-permute-start | bytes 9437192 | tf_op jit(solution)/shard_map/ppermute | solution.py:478
  1.3 7.9 %collective-permute-start = (bf16[2,2048]{1,0:T(2,128)(2,1)}, bf16[2,2048]{1,0:T(2,128)(2,1)S(1)}, u32[]{:S(2)}, u32[]{:S(2)}) collective-permute-start(bf16[2,2048]{1,0:T(2,128)(2,1)} %refs_0_.1), channel_id=1, source_target_pairs={{0,2},{1,3},{2,4},{3,5},{4,6},{5,7},{6,0},{7,1},{8,10},{9,11},{10,... | collective-permute-start | bytes 24584 | tf_op jit(solution)/shard_map/ppermute | solution.py:476
  3.9 5.3 %collective-permute-start.1 = (bf16[2,2048]{1,0:T(2,128)(2,1)}, bf16[2,2048]{1,0:T(2,128)(2,1)S(1)}, u32[]{:S(2)}, u32[]{:S(2)}) collective-permute-start(bf16[2,2048]{1,0:T(2,128)(2,1)} %refs_0_.1), channel_id=1, source_target_pairs={{0,4},{1,5},{2,6},{3,7},{4,0},{5,1},{6,2},{7,3},{8,12},{9,13},{10,... | collective-permute-start | bytes 24584 | tf_op jit(solution)/shard_map/ppermute | solution.py:476
  6.5 3.9 %collective-permute-start.2 = (bf16[2,2048]{1,0:T(2,128)(2,1)}, bf16[2,2048]{1,0:T(2,128)(2,1)S(1)}, u32[]{:S(2)}, u32[]{:S(2)}) collective-permute-start(bf16[2,2048]{1,0:T(2,128)(2,1)} %refs_0_.1), channel_id=1, source_target_pairs={{0,6},{1,7},{2,0},{3,1},{4,2},{5,3},{6,4},{7,5},{8,14},{9,15},{10,... | collective-permute-start | bytes 24584 | tf_op jit(solution)/shard_map/ppermute | solution.py:476
  7.8 0.7 %copy-start.11 = (s32[16]{0:T(128)S(1)}, s32[16]{0:T(128)}, u32[]{:S(2)}) copy-start(s32[16]{0:T(128)} %pos_ref.3) | copy-start | bytes 196
  8.5 6.5 %copy-start.12 = (s32[16]{0:T(128)S(1)}, s32[16]{0:T(128)}, u32[]{:S(2)}) copy-start(s32[16]{0:T(128)} %pos_ref.3) | copy-start | bytes 196
  9.1 7.4 %copy-start.5 = (bf16[2,2048,4]{1,2,0:T(4,128)(2,1)S(1)}, bf16[2,2048,4]{1,2,0:T(4,128)(2,1)}, u32[]{:S(2)}) copy-start(bf16[2,2048,4]{1,2,0:T(4,128)(2,1)} %param.24) | copy-start | bytes 98308
  9.1 7.4 %copy-start.6 = (bf16[2,2048,4]{1,2,0:T(4,128)(2,1)S(1)}, bf16[2,2048,4]{1,2,0:T(4,128)(2,1)}, u32[]{:S(2)}) copy-start(bf16[2,2048,4]{1,2,0:T(4,128)(2,1)} %param.25) | copy-start | bytes 98308
  11.0 4.0 %collective-permute-start.7 = (bf16[4,2,2048]{2,1,0:T(2,128)(2,1)S(1)}, bf16[4,2,2048]{2,1,0:T(2,128)(2,1)S(1)}, u32[]{:S(2)}, u32[]{:S(2)}) collective-permute-start(bf16[4,2,2048]{2,1,0:T(2,128)(2,1)S(1)} %pad_maximum_fusion.same_ref), channel_id=1, source_target_pairs={{0,1},{1,0},{2,3},{3,2},{4,5},{5,4},{6,7},{7,6},{8,9},{9,8},{10,11... | collective-permute-start | bytes 98312 | tf_op jit(solution)/shard_map/ppermute | solution.py:489
  11.1 6.4 %collective-permute-start.5 = (f32[8,128]{1,0:T(8,128)S(1)}, f32[8,128]{1,0:T(8,128)S(1)}, u32[]{:S(2)}, u32[]{:S(2)}) collective-permute-start(f32[8,128]{1,0:T(8,128)S(1)} %get-tuple-element.44), channel_id=1, source_target_pairs={{0,2},{1,3},{2,4},{3,5},{4,6},{5,7},{6,0},{7,1},{8,10},{9,11},{10,... | collective-permute-start | bytes 12296 | tf_op jit(solution)/shard_map/ppermute | solution.py:491
  11.4 6.1 %collective-permute-start.6 = (f32[8,128]{1,0:T(8,128)S(1)}, f32[8,128]{1,0:T(8,128)S(1)}, u32[]{:S(2)}, u32[]{:S(2)}) collective-permute-start(f32[8,128]{1,0:T(8,128)S(1)} %get-tuple-element.45), channel_id=1, source_target_pairs={{0,4},{1,5},{2,6},{3,7},{4,0},{5,1},{6,2},{7,3},{8,12},{9,13},{10,... | collective-permute-start | bytes 12296 | tf_op jit(solution)/shard_map/ppermute | solution.py:491
  14.8 4.5 %collective-permute-start.4 = (f32[8,128]{1,0:T(8,128)S(1)}, f32[8,128]{1,0:T(8,128)S(1)}, u32[]{:S(2)}, u32[]{:S(2)}) collective-permute-start(f32[8,128]{1,0:T(8,128)S(1)} %get-tuple-element.43), channel_id=1, source_target_pairs={{0,6},{1,7},{2,0},{3,1},{4,2},{5,3},{6,4},{7,5},{8,14},{9,15},{10,... | collective-permute-start | bytes 12296 | tf_op jit(solution)/shard_map/ppermute | solution.py:491
  19.3 12.5 %copy-start.4 = (bf16[256,2048]{1,0:T(8,128)(2,1)S(1)}, bf16[256,2048]{1,0:T(8,128)(2,1)}, u32[]{:S(2)}) copy-start(bf16[256,2048]{1,0:T(8,128)(2,1)} %w_ref.1) | copy-start | bytes 3145732
  19.4 22.0 %slice-start = ((s8[8388608]{0:T(1024)(128)(4,1)}), s8[4194304]{0:T(1024)(128)(4,1)S(1)}, s32[]{:S(2)}) async-start(s8[8388608]{0:T(1024)(128)(4,1)} %bitcast.9), calls=%async_computation.2 | async-start | bytes 8388608
  31.8 9.5 %slice-start.1 = ((s8[8388608]{0:T(1024)(128)(4,1)}), s8[4194304]{0:T(1024)(128)(4,1)S(1)}, s32[]{:S(2)}) async-start(s8[8388608]{0:T(1024)(128)(4,1)} %bitcast.9), calls=%async_computation.3 | async-start | bytes 8388608
  31.8 9.5 %copy-start.1 = (bf16[2048]{0:T(1024)(128)(2,1)S(1)}, bf16[2048]{0:T(1024)(128)(2,1)}, u32[]{:S(2)}) copy-start(bf16[2048]{0:T(1024)(128)(2,1)} %gain_ref.5) | copy-start | bytes 12292
  32.3 10.2 %copy-start = (bf16[1024,2048]{1,0:T(8,128)(2,1)S(1)}, bf16[1024,2048]{1,0:T(8,128)(2,1)}, u32[]{:S(2)}) copy-start(bf16[1024,2048]{1,0:T(8,128)(2,1)} %down_ref.1) | copy-start | bytes 12582916
  32.3 1.2 %collective-permute-start.8 = (bf16[16,1024]{1,0:T(8,128)(2,1)S(1)}, bf16[16,1024]{1,0:T(8,128)(2,1)S(1)}, u32[]{:S(2)}, u32[]{:S(2)}) collective-permute-start(bf16[16,1024]{1,0:T(8,128)(2,1)S(1)} %get-tuple-element.57), channel_id=1, source_target_pairs={{0,1},{1,0},{2,3},{3,2},{4,5},{5,4},{6,7},{7,6},{8,9},{9,8},{10,11... | collective-permute-start | bytes 98312 | tf_op jit(solution)/shard_map/ppermute | solution.py:540
  33.5 4.0 %collective-permute-start.10 = (bf16[16,1024]{1,0:T(8,128)(2,1)S(1)}, bf16[16,1024]{1,0:T(8,128)(2,1)S(1)}, u32[]{:S(2)}, u32[]{:S(2)}) collective-permute-start(bf16[16,1024]{1,0:T(8,128)(2,1)S(1)} %add_convert_fusion.1), channel_id=1, source_target_pairs={{0,6},{1,7},{2,0},{3,1},{4,2},{5,3},{6,4},{7,5},{8,14},{9,15},{10,... | collective-permute-start | bytes 98312 | tf_op jit(solution)/shard_map/ppermute | solution.py:554
  34.4 4.8 %collective-permute-start.11 = (bf16[16,1024]{1,0:T(8,128)(2,1)S(1)}, bf16[16,1024]{1,0:T(8,128)(2,1)S(1)}, u32[]{:S(2)}, u32[]{:S(2)}) collective-permute-start(bf16[16,1024]{1,0:T(8,128)(2,1)S(1)} %add_convert_fusion.1), channel_id=1, source_target_pairs={{0,4},{1,5},{2,6},{3,7},{4,0},{5,1},{6,2},{7,3},{8,12},{9,13},{10,... | collective-permute-start | bytes 98312 | tf_op jit(solution)/shard_map/ppermute | solution.py:554
  35.5 5.7 %collective-permute-start.9 = (bf16[16,1024]{1,0:T(8,128)(2,1)S(1)}, bf16[16,1024]{1,0:T(8,128)(2,1)S(1)}, u32[]{:S(2)}, u32[]{:S(2)}) collective-permute-start(bf16[16,1024]{1,0:T(8,128)(2,1)S(1)} %add_convert_fusion.1), channel_id=1, source_target_pairs={{0,2},{1,3},{2,4},{3,5},{4,6},{5,7},{6,0},{7,1},{8,10},{9,11},{10,... | collective-permute-start | bytes 98312 | tf_op jit(solution)/shard_map/ppermute | solution.py:554
  41.2 1.3 %collective-permute-start.12 = (bf16[16,1024]{1,0:T(8,128)(2,1)S(1)}, bf16[16,1024]{1,0:T(8,128)(2,1)S(1)}, u32[]{:S(2)}, u32[]{:S(2)}) collective-permute-start(bf16[16,1024]{1,0:T(8,128)(2,1)S(1)} %add_convert_fusion.side_ref.mine_ref), channel_id=1, source_target_pairs={{0,1},{1,0},{2,3},{3,2},{4,5},{5,4},{6,7},{7,6},{8,9},{9,8},{10,11... | collective-permute-start | bytes 98312 | tf_op jit(solution)/shard_map/ppermute | solution.py:556
